TPU v7x, 32 devices: a whole 2x2x4 slice. The times are simulated.
32 devices in a mesh: dp: 2 (over core), ctx: 8 (over z, x), tp: 2 (over y).
Axes of the slice: x: 2, y: 2, z: 4, core: 2. Of those that a mesh axis runs over, the one named last changes fastest.
Arguments:
- tokens: bfloat16 [8, 16, 256, 1152], P('dp', 'ctx', 'tp'), may hold values from -6 to 6
- condition: bfloat16 [8, 1152], P('dp'), may hold values from -6 to 6
- micro_ids: int32 [8], P('dp'), may hold values from 0 to 2, as said below
- w_qkv: float32 [2, 3, 1152, 1152], P(None, None, ('dp', 'ctx'), 'tp'), may hold values from -0.1875 to 0.1875
- w_out: float32 [2, 1152, 1152], P(None, 'tp', ('dp', 'ctx')), may hold values from -1 to 1
- w_up: float32 [2, 1152, 4608], P(None, ('dp', 'ctx'), 'tp'), may hold values from -0.1875 to 0.1875
- w_down: float32 [2, 4608, 1152], P(None, 'tp', ('dp', 'ctx')), may hold values from -0.09375 to 0.09375
- w_ada: float32 [2, 1152, 6912], P(None, ('dp', 'ctx'), 'tp'), may hold values from -0.1875 to 0.1875
- cotangent: bfloat16 [8, 16, 256, 1152], P('dp', 'ctx', 'tp'), may hold values from -6 to 6
Outputs:
- output: bfloat16 [8, 16, 256, 1152], P('dp', 'ctx', 'tp')
- grad_tokens: float32 [8, 16, 256, 1152], P('dp', 'ctx', 'tp')
- grad_condition: float32 [8, 1152], P('dp')
- grad_qkv: float32 [2, 3, 1152, 1152], P(None, None, ('dp', 'ctx'), 'tp')
- grad_out: float32 [2, 1152, 1152], P(None, 'tp', ('dp', 'ctx'))
- grad_up: float32 [2, 1152, 4608], P(None, ('dp', 'ctx'), 'tp')
- grad_down: float32 [2, 4608, 1152], P(None, 'tp', ('dp', 'ctx'))
- grad_ada: float32 [2, 1152, 6912], P(None, ('dp', 'ctx'), 'tp')
Inputs may be any that keep to these rules, and one draw needn't show every extreme that they name: `micro_ids`: in each aligned block of 4 clips (one data group) one micro-batch id is held by exactly two clips and every other id of 0 to 2 by exactly one clip.
All inputs are finite; a program needn't handle non-finite values.
Results may differ from a plain program's by a relative error of at most 0.02125.
The roundings to bfloat16 on the way count: a program that leaves them out, or rounds other values in their place, can miss the bound.
Values may be sent and summed in bfloat16 or wider, within the bound.
No kernel may reach another device: no remote copies, remote signals or barrier semaphores. Data moves between devices by JAX's collectives and lax.ppermute only.
A program may use at most 640 MiB of HBM per device.

v0:
```python
import jax
import jax.numpy as jnp
from jax import lax
from jax.sharding import PartitionSpec as P

HEAD_DIM = 72
LAYERS = 2


eps_norm = 1e-06
highest = lax.Precision.HIGHEST


def layer_norm(values):
    centred = values - jnp.mean(values, axis=-1, keepdims=True)
    spread_sq = jnp.mean(centred * centred, axis=-1, keepdims=True)
    return centred * lax.rsqrt(spread_sq + eps_norm)


def modulate(values, shifts, scales):
    return layer_norm(values) * (1.0 + scales[:, None, None, :]) + shifts[:, None, None, :]


def gelu_tanh(values):
    return jax.nn.gelu(values, approximate=True)


def attend(queries, key_rows, values):
    score_scale = HEAD_DIM ** (-0.5)
    scores = (
        jnp.einsum("bqhe,bkhe->bhqk", queries, key_rows, preferred_element_type=jnp.float32)
        * score_scale
    )
    largest = jnp.max(scores, axis=-1, keepdims=True)
    raised = jnp.exp(scores - largest)
    totals = jnp.sum(raised, axis=-1, keepdims=True)
    chances = (raised / totals).astype(jnp.bfloat16)
    result = jnp.einsum("bhqk,bkhe->bqhe", chances, values, preferred_element_type=jnp.float32)
    return (result, largest + jnp.log(totals))


def attend_back(queries, key_rows, values, log_total, grad_result):
    score_scale = HEAD_DIM ** (-0.5)
    scores = (
        jnp.einsum("bqhe,bkhe->bhqk", queries, key_rows, preferred_element_type=jnp.float32)
        * score_scale
    )
    chances = jnp.exp(scores - log_total)
    grad_chances = jnp.einsum(
        "bqhe,bkhe->bhqk", grad_result, values, preferred_element_type=jnp.float32
    )
    row_dot = jnp.sum(chances * grad_chances, axis=-1, keepdims=True)
    grad_scores = (chances * (grad_chances - row_dot)).astype(jnp.bfloat16)
    grad_queries = (
        jnp.einsum("bhqk,bkhe->bqhe", grad_scores, key_rows, preferred_element_type=jnp.float32)
        * score_scale
    )
    grad_keys = (
        jnp.einsum("bhqk,bqhe->bkhe", grad_scores, queries, preferred_element_type=jnp.float32)
        * score_scale
    )
    grad_values = jnp.einsum(
        "bhqk,bqhe->bkhe",
        chances.astype(jnp.bfloat16),
        grad_result,
        preferred_element_type=jnp.float32,
    )
    return (grad_queries, grad_keys, grad_values)


def heads_of(arranged, heads_here):
    return arranged.reshape(arranged.shape[:-1] + (heads_here, HEAD_DIM))


def frame_rows(arranged, heads_here):
    clip_count, frames_here, patches = arranged.shape[:3]
    return heads_of(arranged, heads_here).reshape(
        clip_count * frames_here, patches, heads_here, HEAD_DIM
    )


def by_position(arranged, heads_here):
    clip_count, frames, patches = arranged.shape[:3]
    shaped = heads_of(arranged, heads_here).transpose(0, 2, 1, 3, 4)
    return shaped.reshape(clip_count * patches, frames, heads_here, HEAD_DIM)


def from_position(arranged, clip_count):
    rows_all, frames = arranged.shape[:2]
    shaped = arranged.reshape(clip_count, rows_all // clip_count, frames, -1)
    return shaped.transpose(0, 2, 1, 3)


def spread(values):
    return lax.all_gather(values, "tp", axis=2, tiled=True)


def collect(values):
    return lax.psum_scatter(values, "tp", scatter_dimension=2, tiled=True)


def spread_grad(values):
    return lax.all_gather(values, "tp", axis=2, tiled=True)


def collect_grad(values):
    return lax.psum_scatter(values, "tp", scatter_dimension=2, tiled=True)


def spatial_forward(projected, heads_here):
    result, log_total = attend(
        frame_rows(projected[:, :, :, 0], heads_here),
        frame_rows(projected[:, :, :, 1], heads_here),
        frame_rows(projected[:, :, :, 2], heads_here),
    )
    return (result.reshape(projected.shape[:3] + (-1,)).astype(jnp.bfloat16), log_total)


def spatial_back(projected, attn_saved, grad_heads, heads_here):
    partials = attend_back(
        frame_rows(projected[:, :, :, 0], heads_here),
        frame_rows(projected[:, :, :, 1], heads_here),
        frame_rows(projected[:, :, :, 2], heads_here),
        attn_saved,
        frame_rows(grad_heads, heads_here),
    )
    return jnp.stack(
        [part_grad.reshape(grad_heads.shape[:3] + (-1,)) for part_grad in partials], axis=3
    ).astype(jnp.bfloat16)


def temporal_forward(projected, heads_here):
    clip_count, frames_here, patches = projected.shape[:3]
    key_pairs = lax.all_gather(projected[:, :, :, 1:], "ctx", axis=1, tiled=True)
    result, log_total = attend(
        by_position(projected[:, :, :, 0], heads_here),
        by_position(key_pairs[:, :, :, 0], heads_here),
        by_position(key_pairs[:, :, :, 1], heads_here),
    )
    return (from_position(result, clip_count).astype(jnp.bfloat16), (key_pairs, log_total))


def temporal_back(projected, attn_saved, grad_heads, heads_here):
    clip_count, frames_here, patches, head_cols = grad_heads.shape
    key_pairs, log_total = attn_saved
    partials = attend_back(
        by_position(projected[:, :, :, 0], heads_here),
        by_position(key_pairs[:, :, :, 0], heads_here),
        by_position(key_pairs[:, :, :, 1], heads_here),
        log_total,
        by_position(grad_heads, heads_here),
    )
    key_sums = lax.psum_scatter(
        jnp.stack(
            [from_position(partials[1], clip_count), from_position(partials[2], clip_count)], axis=3
        ),
        "ctx",
        scatter_dimension=1,
        tiled=True,
    )
    own_rows = from_position(partials[0], clip_count)[:, :, :, None]
    return jnp.concatenate([own_rows, key_sums], axis=3).astype(jnp.bfloat16)


def local(tokens, condition, micro_ids, w_qkv, w_out, w_up, w_down, w_ada, cotangent):
    heads_here = w_qkv.shape[3] // HEAD_DIM
    cond_full = condition.astype(jnp.float32)
    cond_low = jax.nn.silu(cond_full).astype(jnp.bfloat16)
    residual = tokens.astype(jnp.float32)
    records = []
    for level_id in range(LAYERS):
        gathered = (
            lax.all_gather(w_qkv[level_id].astype(jnp.bfloat16), ("dp", "ctx"), axis=1, tiled=True),
            lax.all_gather(w_out[level_id].astype(jnp.bfloat16), ("dp", "ctx"), axis=1, tiled=True),
            lax.all_gather(w_up[level_id].astype(jnp.bfloat16), ("dp", "ctx"), axis=0, tiled=True),
            lax.all_gather(
                w_down[level_id].astype(jnp.bfloat16), ("dp", "ctx"), axis=1, tiled=True
            ),
            lax.all_gather(w_ada[level_id].astype(jnp.bfloat16), ("dp", "ctx"), axis=0, tiled=True),
        )
        mod_share = jnp.dot(cond_low, gathered[4], preferred_element_type=jnp.float32)
        modulation = lax.all_gather(mod_share, "tp", axis=1, tiled=True)
        shift_a, scale_a, gate_a, shift_m, scale_m, gate_m = jnp.split(modulation, 6, axis=1)
        normed = spread(modulate(residual, shift_a, scale_a).astype(jnp.bfloat16))
        projected = jnp.einsum(
            "cfsd,kde->cfske", normed, gathered[0], preferred_element_type=jnp.float32
        ).astype(jnp.bfloat16)
        if level_id % 2 == 0:
            out_low, attn_saved = spatial_forward(projected, heads_here)
        else:
            out_low, attn_saved = temporal_forward(projected, heads_here)
        branch = collect(
            jnp.einsum("cfsh,hd->cfsd", out_low, gathered[1], preferred_element_type=jnp.float32)
        )
        middle = residual + gate_a[:, None, None, :] * branch
        normed_mlp = spread(modulate(middle, shift_m, scale_m).astype(jnp.bfloat16))
        pre_act = jnp.einsum(
            "cfsd,dh->cfsh", normed_mlp, gathered[2], preferred_element_type=jnp.float32
        )
        activated = gelu_tanh(pre_act).astype(jnp.bfloat16)
        branch_mlp = collect(
            jnp.einsum("cfsh,hd->cfsd", activated, gathered[3], preferred_element_type=jnp.float32)
        )
        records.append(
            (
                gathered,
                modulation,
                residual,
                normed,
                projected,
                attn_saved,
                out_low,
                branch,
                middle,
                normed_mlp,
                pre_act,
                activated,
                branch_mlp,
            )
        )
        residual = middle + gate_m[:, None, None, :] * branch_mlp
    matched = (micro_ids[:, None] == micro_ids[None, :]).astype(jnp.float32)
    gradient = cotangent.astype(jnp.float32) / jnp.sum(matched, axis=1)[:, None, None, None]
    grad_cond = jnp.zeros_like(cond_full)
    weight_grads = []
    for level_id in reversed(range(LAYERS)):
        (
            gathered,
            modulation,
            residual_in,
            normed,
            projected,
            attn_saved,
            out_low,
            branch,
            middle,
            normed_mlp,
            pre_act,
            activated,
            branch_mlp,
        ) = records[level_id]
        shift_a, scale_a, gate_a, shift_m, scale_m, gate_m = jnp.split(modulation, 6, axis=1)
        grad_gate_m = jnp.sum(gradient * branch_mlp, axis=(1, 2))
        grad_branch = spread_grad((gradient * gate_m[:, None, None, :]).astype(jnp.bfloat16))
        grad_act = jnp.einsum(
            "cfsd,hd->cfsh", grad_branch, gathered[3], preferred_element_type=jnp.float32
        )
        layer_down = jnp.einsum(
            "cfsh,cfsd->hd", activated, grad_branch, preferred_element_type=jnp.float32
        )
        grad_pre = jax.vjp(gelu_tanh, pre_act)[1](grad_act)[0].astype(jnp.bfloat16)
        layer_up = jnp.einsum(
            "cfsd,cfsh->dh", normed_mlp, grad_pre, preferred_element_type=jnp.float32
        )
        grad_normed = collect_grad(
            jnp.einsum("cfsh,dh->cfsd", grad_pre, gathered[2], preferred_element_type=jnp.float32)
        )
        grad_middle, grad_shift_m, grad_scale_m = jax.vjp(modulate, middle, shift_m, scale_m)[1](
            grad_normed
        )
        gradient = gradient + grad_middle
        grad_gate_a = jnp.sum(gradient * branch, axis=(1, 2))
        grad_branch = spread_grad((gradient * gate_a[:, None, None, :]).astype(jnp.bfloat16))
        grad_heads = jnp.einsum(
            "cfsd,hd->cfsh", grad_branch, gathered[1], preferred_element_type=jnp.float32
        ).astype(jnp.bfloat16)
        layer_proj = jnp.einsum(
            "cfsh,cfsd->hd", out_low, grad_branch, preferred_element_type=jnp.float32
        )
        if level_id % 2 == 0:
            grad_projected = spatial_back(projected, attn_saved, grad_heads, heads_here)
        else:
            grad_projected = temporal_back(projected, attn_saved, grad_heads, heads_here)
        layer_qkv = jnp.einsum(
            "cfsd,cfske->kde", normed, grad_projected, preferred_element_type=jnp.float32
        )
        grad_normed = collect_grad(
            jnp.einsum(
                "cfske,kde->cfsd", grad_projected, gathered[0], preferred_element_type=jnp.float32
            )
        )
        grad_input, grad_shift_a, grad_scale_a = jax.vjp(modulate, residual_in, shift_a, scale_a)[
            1
        ](grad_normed)
        gradient = gradient + grad_input
        grad_mod = jnp.concatenate(
            [grad_shift_a, grad_scale_a, grad_gate_a, grad_shift_m, grad_scale_m, grad_gate_m],
            axis=1,
        )
        mod_part = lax.psum_scatter(
            grad_mod.astype(jnp.bfloat16), "tp", scatter_dimension=1, tiled=True
        ).astype(jnp.float32)
        layer_ada = jnp.dot(cond_low.astype(jnp.float32).T, mod_part, precision=highest)
        grad_cond = grad_cond + jnp.dot(
            mod_part, gathered[4].astype(jnp.float32).T, precision=highest
        )
        weight_grads.insert(0, (layer_qkv, layer_proj, layer_up, layer_down, layer_ada))
    silu_grad = jax.vjp(jax.nn.silu, cond_full)[1](grad_cond)[0]
    grad_condition = lax.psum(silu_grad, ("ctx", "tp"))
    stack_qkv = jnp.stack([layer_entry[0] for layer_entry in weight_grads])
    stack_proj = jnp.stack([layer_entry[1] for layer_entry in weight_grads])
    stack_up = jnp.stack([layer_entry[2] for layer_entry in weight_grads])
    stack_down = jnp.stack([layer_entry[3] for layer_entry in weight_grads])
    stack_ada = jnp.stack([layer_entry[4] for layer_entry in weight_grads])
    shards = (
        lax.psum_scatter(
            stack_qkv.astype(jnp.bfloat16), ("dp", "ctx"), scatter_dimension=2, tiled=True
        ).astype(jnp.float32),
        lax.psum_scatter(
            stack_proj.astype(jnp.bfloat16), ("dp", "ctx"), scatter_dimension=2, tiled=True
        ).astype(jnp.float32),
        lax.psum_scatter(
            stack_up.astype(jnp.bfloat16), ("dp", "ctx"), scatter_dimension=1, tiled=True
        ).astype(jnp.float32),
        lax.psum_scatter(
            stack_down.astype(jnp.bfloat16), ("dp", "ctx"), scatter_dimension=2, tiled=True
        ).astype(jnp.float32),
        lax.psum_scatter(
            stack_ada.astype(jnp.bfloat16), ("dp", "ctx"), scatter_dimension=1, tiled=True
        ).astype(jnp.float32),
    )
    return (
        residual.astype(jnp.bfloat16),
        gradient,
        grad_condition,
        shards[0],
        shards[1],
        shards[2],
        shards[3],
        shards[4],
    )


def solution(mesh):
    placed = (
        P("dp", "ctx", "tp", None),
        P("dp", None),
        P("dp"),
        P(None, None, ("dp", "ctx"), "tp"),
        P(None, "tp", ("dp", "ctx")),
        P(None, ("dp", "ctx"), "tp"),
        P(None, "tp", ("dp", "ctx")),
        P(None, ("dp", "ctx"), "tp"),
        P("dp", "ctx", "tp", None),
    )
    return jax.shard_map(
        local,
        mesh=mesh,
        in_specs=placed,
        out_specs=(
            P("dp", "ctx", "tp", None),
            P("dp", "ctx", "tp", None),
            P("dp", None),
            P(None, None, ("dp", "ctx"), "tp"),
            P(None, "tp", ("dp", "ctx")),
            P(None, ("dp", "ctx"), "tp"),
            P(None, "tp", ("dp", "ctx")),
            P(None, ("dp", "ctx"), "tp"),
        ),
        check_vma=False,
    )
```

profile of v0, /device:TPU:0, one launch (start us, length us, event | category | flops | bytes accessed | tf_op | source)
XLA Modules:
  0.0 7285.7 jit_solution(16824187302110068093)
XLA Ops:
  12.4 73.3 %all-gather.48.cloned.1.call-done = bf16[1,1152,3456]{2,1,0:T(8,128)(2,1)} async-done(((bf16[1,72,3456]{2,1,0:T(8,128)(2,1)}), bf16[1,1152,3456]{2,1,0:T(8,128)(2,1)}) %all-gather.48.cloned.1.call-update) | async-done | bytes 7962640 | tf_op jit(solution)/shard_map/all_gather | solution.py:179
  99.5 39.1 all-gather.50.cloned.1.call-done
  138.6 63.3 all-gather.30.cloned.1.call-done
  246.4 21.8 fusion.102
  270.7 108.4 %reduce-scatter.24.cloned.1.call-done = f32[4,2,128,1152]{3,2,1,0:T(8,128)} async-done(((f32[4,2,256,1152]{3,2,1,0:T(8,128)}), f32[4,2,128,1152]{3,2,1,0:T(8,128)}) %reduce-scatter.24.cloned.1.call-update) | async-done | bytes 4718608 | tf_op jit(solution)/shard_map/reduce_scatter | solution.py:99
  389.6 48.5 all-gather.54.cloned.1.call-done
  438.1 63.4 all-gather.32.cloned.1.call-done
  501.5 18.4 fusion.53
  519.9 40.8 all-gather.56.cloned.1.call-done
  560.7 23.3 fusion.49
  584.7 49.5 all-gather.58.cloned.1.call-done
  645.4 100.8 %reduce-scatter.26.cloned.1.call-done = f32[4,2,128,1152]{3,2,1,0:T(8,128)} async-done(((f32[4,2,256,1152]{3,2,1,0:T(8,128)}), f32[4,2,128,1152]{3,2,1,0:T(8,128)}) %reduce-scatter.26.cloned.1.call-update) | async-done | bytes 4718608 | tf_op jit(solution)/shard_map/reduce_scatter | solution.py:99
  756.3 43.1 all-gather.60.cloned.1.call-done
  799.3 63.2 all-gather.34.cloned.1.call-done
  889.8 707.2 %all-gather.36.cloned.1.call-done = bf16[4,16,256,2,576]{2,4,3,1,0:T(8,128)(2,1)} async-done(((bf16[4,2,256,2,576]{2,4,3,1,0:T(8,128)(2,1)}), bf16[4,16,256,2,576]{2,4,3,1,0:T(8,128)(2,1)}) %all-gather.36.cloned.1.call-update) | async-done | bytes 37748752 | tf_op jit(solution)/shard_map/all_gather | solution.py:134
  1597.0 26.4 fusion.138
  1623.4 40.6 copy.112
  1664.0 40.7 copy.114
  1704.8 25.2 fusion.147
  1730.0 22.7 fusion.74
  1752.7 27.9 fusion.69
  1803.6 110.2 %reduce-scatter.28.cloned.1.call-done = f32[4,2,128,1152]{3,2,1,0:T(8,128)} async-done(((f32[4,2,256,1152]{3,2,1,0:T(8,128)}), f32[4,2,128,1152]{3,2,1,0:T(8,128)}) %reduce-scatter.28.cloned.1.call-update) | async-done | bytes 4718608 | tf_op jit(solution)/shard_map/reduce_scatter | solution.py:99
  1926.8 46.1 all-gather.64.cloned.1.call-done
  1972.9 63.2 all-gather.38.cloned.1.call-done
  2036.1 18.6 fusion.57
  2054.7 40.5 all-gather.66.cloned.1.call-done
  2095.1 62.8 all-gather.40.cloned.1.call-done
  2157.9 27.2 fusion.13
  2188.8 17.6 fusion.55
  2206.5 23.4 fusion.46
  2229.9 87.2 %reduce-scatter.32.cloned.1.call-done = f32[4,2,128,1152]{3,2,1,0:T(8,128)} async-done(((f32[4,2,256,1152]{3,2,1,0:T(8,128)}), f32[4,2,128,1152]{3,2,1,0:T(8,128)}) %reduce-scatter.32.cloned.1.call-update) | async-done | bytes 4718608 | tf_op jit(solution)/shard_map/reduce_scatter | solution.py:107
  2326.8 103.2 %reduce-scatter.30.cloned.1.call-done = f32[4,2,128,1152]{3,2,1,0:T(8,128)} async-done(((f32[4,2,256,1152]{3,2,1,0:T(8,128)}), f32[4,2,128,1152]{3,2,1,0:T(8,128)}) %reduce-scatter.30.cloned.1.call-update) | async-done | bytes 4718608 | tf_op jit(solution)/shard_map/reduce_scatter | solution.py:99
  2451.3 55.5 all-gather.42.cloned.1.call-done
  2520.7 29.4 multiply_reduce_fusion.2
  2550.1 43.3 convolution_bitcast_fusion
  2593.5 22.0 multiply_convert_fusion.4
  2615.4 16.7 fusion.68
  2632.1 23.4 multiply_bitcast_fusion
  2671.1 56.9 copy.123
  2728.0 45.0 reshape.226
  2773.0 57.1 copy.122
  2830.0 45.0 reshape.225
  2875.0 49.8 pad_maximum_fusion
  2924.8 49.5 copy.124
  2974.3 2866.8 %all-reduce.9 = bf16[4,16,256,2,576]{2,4,3,1,0:T(8,128)(2,1)} all-reduce(f32[4,16,256,2,576]{2,4,3,1,0:T(8,128)} %copy.124), channel_id=17, replica_groups=mesh['dp'=2,'ctx'=8,'tp'=2] {'ctx'}, use_global_device_ids=true, to_apply=%region_21.22.clone | all-reduce | flops 18874368 | bytes 113246208
  5862.0 108.6 %reduce-scatter.34.cloned.1.call-done = f32[4,2,128,1152]{3,2,1,0:T(8,128)} async-done(((f32[4,2,256,1152]{3,2,1,0:T(8,128)}), f32[4,2,128,1152]{3,2,1,0:T(8,128)}) %reduce-scatter.34.cloned.1.call-update) | async-done | bytes 4718608 | tf_op jit(solution)/shard_map/reduce_scatter | solution.py:107
  5989.6 62.8 all-gather.44.cloned.1.call-done
  6052.3 27.4 fusion.6
  6083.4 17.2 fusion.51
  6100.7 110.6 %reduce-scatter.36.cloned.1.call-done = f32[4,2,128,1152]{3,2,1,0:T(8,128)} async-done(((f32[4,2,256,1152]{3,2,1,0:T(8,128)}), f32[4,2,128,1152]{3,2,1,0:T(8,128)}) %reduce-scatter.36.cloned.1.call-update) | async-done | bytes 4718608 | tf_op jit(solution)/shard_map/reduce_scatter | solution.py:107
  6229.8 62.7 all-gather.46.cloned.1.call-done
  6337.1 15.8 convolution_bitcast_fusion.5
  6353.1 17.3 fusion.24
  6372.3 17.5 fusion.25
  6389.9 73.8 %reduce-scatter.38.cloned.1.call-done = f32[4,2,128,1152]{3,2,1,0:T(8,128)} async-done(((f32[4,2,256,1152]{3,2,1,0:T(8,128)}), f32[4,2,128,1152]{3,2,1,0:T(8,128)}) %reduce-scatter.38.cloned.1.call-update) | async-done | bytes 4718608 | tf_op jit(solution)/shard_map/reduce_scatter | solution.py:107
  6477.9 75.8 %copy.176 = bf16[2,1152,2304]{2,0,1:T(2,128)(2,1)S(1)} copy(bf16[2,1152,2304]{2,1,0:T(8,128)(2,1)S(1)} %pad_maximum_fusion.2) | data formatting | bytes 21233664
  6558.7 20.2 fusion.22
  6600.2 18.4 fusion.23
  6623.4 29.8 copy.138
  6684.2 28.4 copy.131
  6734.0 71.9 copy.178
  6831.4 266.7 %all-reduce.8.cloned.1.call-done = (bf16[2,3,1152,576]{3,0,1,2:T(2,128)(2,1)}, bf16[2,576,1152]{1,0,2:T(2,128)(2,1)}, bf16[2,2304,1152]{1,0,2:T(2,128)(2,1)}) async-done(((bf16[2,3,1152,576]{3,0,1,2:T(2,128)(2,1)}, bf16[2,576,1152]{1,0,2:T(2,128)(2,1)}, bf16[2,2304,1152]{1,0,2:T(2,128)(2,1)}), (bf16[2,3,1152,576]{3,0,1,2:T(2,128)(2,1)}, bf16[2,576,1152]{1,0,2:T(2,128)(2,1)}, ...) | async-done | bytes 21233680
  7116.1 77.9 %psum.7 = f32[4,1152]{1,0:T(4,128)} all-reduce(f32[4,1152]{1,0:T(4,128)S(1)} %fusion.116), channel_id=1, replica_groups=mesh['dp'=2,'ctx'=8,'tp'=2] {'ctx','tp'}, use_global_device_ids=true, to_apply=%region_46.47 | all-reduce | flops 4608 | bytes 36864 | tf_op jit(solution)/shard_map/psum | solution.py:299
  7193.9 80.9 %reduce-scatter.46.cloned.1.call-done = bf16[72,6912]{1,0:T(8,128)(2,1)} async-done(((bf16[1152,6912]{1,0:T(8,128)(2,1)}), bf16[72,6912]{1,0:T(8,128)(2,1)}) %reduce-scatter.46.cloned.1.call-update) | async-done | bytes 995344
  (422 shorter events, 476.6 us)
Async XLA Ops:
  7.2 78.5 %all-gather.48.cloned.1.call-start = ((), (), s32[]{:S(2)}) async-start(), calls=%async_computation.29 | async-start | bytes 8460288 | tf_op jit(solution)/shard_map/all_gather | solution.py:179
  9.0 76.7 %copy-start.39 = (bf16[4,1152]{1,0:T(4,128)(2,1)S(1)}, bf16[4,1152]{1,0:T(4,128)(2,1)}, u32[]{:S(2)}) copy-start(bf16[4,1152]{1,0:T(4,128)(2,1)} %param.10) | copy-start | bytes 27652
  10.1 128.5 %all-gather.50.cloned.1.call-start = ((), (), s32[]{:S(2)}) async-start(), calls=%async_computation.30 | async-start | bytes 4700160 | tf_op jit(solution)/shard_map/all_gather | solution.py:173
  11.1 190.9 %all-gather.30.cloned.1.call-start = ((), (), s32[]{:S(2)}) async-start(), calls=%async_computation.12 | async-start | bytes 7077888 | tf_op jit(solution)/shard_map/all_gather | solution.py:95
  11.6 83.6 %copy-start.62 = (f32[4,2,128]{2,1,0:T(2,128)}, f32[4,2,128]{2,1,0:T(2,128)S(1)}, u32[]{:S(2)}) copy-start(f32[4,2,128]{2,1,0:T(2,128)S(1)} %broadcast_multiply_fusion.3) | copy-start | bytes 12292
  12.3 77.8 %copy-start.82 = (f32[4,2,128]{2,1,0:T(2,128)}, f32[4,2,128]{2,1,0:T(2,128)S(1)}, u32[]{:S(2)}) copy-start(f32[4,2,128]{2,1,0:T(2,128)S(1)} %fusion.62) | copy-start | bytes 12292
  12.4 82.8 %copy-start.70 = (f32[4,2,128]{2,1,0:T(2,128)}, f32[4,2,128]{2,1,0:T(2,128)S(1)}, u32[]{:S(2)}) copy-start(f32[4,2,128]{2,1,0:T(2,128)S(1)} %fusion.121) | copy-start | bytes 12292
  95.1 119.7 %copy-start.41 = (f32[4,1152]{1,0:T(4,128)}, f32[4,1152]{1,0:T(4,128)S(1)}, u32[]{:S(2)}) copy-start(f32[4,1152]{1,0:T(4,128)S(1)} %get-tuple-element.96) | copy-start | bytes 55300
  95.1 284.0 %copy-start.56 = (f32[4,1152]{1,0:T(4,128)}, f32[4,1152]{1,0:T(4,128)S(1)}, u32[]{:S(2)}) copy-start(f32[4,1152]{1,0:T(4,128)S(1)} %get-tuple-element.97) | copy-start | bytes 55300
  95.1 287.7 %copy-start.44 = (f32[4,1152]{1,0:T(4,128)}, f32[4,1152]{1,0:T(4,128)S(1)}, u32[]{:S(2)}) copy-start(f32[4,1152]{1,0:T(4,128)S(1)} %get-tuple-element.94) | copy-start | bytes 55300
  95.1 651.0 %copy-start.52 = (f32[4,1152]{1,0:T(4,128)}, f32[4,1152]{1,0:T(4,128)S(1)}, u32[]{:S(2)}) copy-start(f32[4,1152]{1,0:T(4,128)S(1)} %get-tuple-element.92) | copy-start | bytes 55300
  98.7 147.7 %all-gather.52.cloned.1.call-start = ((), (), s32[]{:S(2)}) async-start(), calls=%async_computation.31 | async-start | bytes 1566720 | tf_op jit(solution)/shard_map/all_gather | solution.py:174
  99.5 279.6 %reduce-scatter.24.cloned.1.call-start = ((), (), s32[]{:S(2)}) async-start(), calls=%async_computation.13 | async-start | bytes 14155776 | tf_op jit(solution)/shard_map/reduce_scatter | solution.py:99
  268.3 169.8 %all-gather.54.cloned.1.call-start = ((), (), s32[]{:S(2)}) async-start(), calls=%async_computation.32 | async-start | bytes 5640192 | tf_op jit(solution)/shard_map/all_gather | solution.py:175
  270.6 230.8 %all-gather.32.cloned.1.call-start = ((), (), s32[]{:S(2)}) async-start(), calls=%async_computation.14 | async-start | bytes 7077888 | tf_op jit(solution)/shard_map/all_gather | solution.py:95
  387.8 172.9 %all-gather.56.cloned.1.call-start = ((), (), s32[]{:S(2)}) async-start(), calls=%async_computation.33 | async-start | bytes 5640192 | tf_op jit(solution)/shard_map/all_gather | solution.py:176
  388.8 245.4 %all-gather.58.cloned.1.call-start = ((), (), s32[]{:S(2)}) async-start(), calls=%async_computation.34 | async-start | bytes 8460288 | tf_op jit(solution)/shard_map/all_gather | solution.py:179
  389.5 356.6 %reduce-scatter.26.cloned.1.call-start = ((), (), s32[]{:S(2)}) async-start(), calls=%async_computation.15 | async-start | bytes 14155776 | tf_op jit(solution)/shard_map/reduce_scatter | solution.py:99
  584.0 215.4 %all-gather.60.cloned.1.call-start = ((), (), s32[]{:S(2)}) async-start(), calls=%async_computation.35 | async-start | bytes 4700160 | tf_op jit(solution)/shard_map/all_gather | solution.py:173
  584.7 277.8 %all-gather.34.cloned.1.call-start = ((), (), s32[]{:S(2)}) async-start(), calls=%async_computation.16 | async-start | bytes 7077888 | tf_op jit(solution)/shard_map/all_gather | solution.py:95
  645.4 106.9 %copy-start.46 = (f32[4,1152]{1,0:T(4,128)}, f32[4,1152]{1,0:T(4,128)S(1)}, u32[]{:S(2)}) copy-start(f32[4,1152]{1,0:T(4,128)S(1)} %get-tuple-element.90) | copy-start | bytes 55300
  756.2 840.8 %all-gather.36.cloned.1.call-start = ((), (), s32[]{:S(2)}) async-start(), calls=%async_computation.17 | async-start | bytes 42467328 | tf_op jit(solution)/shard_map/all_gather | solution.py:134
  880.5 912.5 %all-gather.62.cloned.1.call-start = ((), (), s32[]{:S(2)}) async-start(), calls=%async_computation.36 | async-start | bytes 1566720 | tf_op jit(solution)/shard_map/all_gather | solution.py:174
  881.1 1032.7 %reduce-scatter.28.cloned.1.call-start = ((), (), s32[]{:S(2)}) async-start(), calls=%async_computation.18 | async-start | bytes 14155776 | tf_op jit(solution)/shard_map/reduce_scatter | solution.py:99
  1730.0 22.7 copy-start.15
  1802.9 110.9 %copy-start.54 = (f32[4,1152]{1,0:T(4,128)S(1)}, f32[4,1152]{1,0:T(4,128)}, u32[]{:S(2)}) copy-start(f32[4,1152]{1,0:T(4,128)} %get-tuple-element.91) | copy-start | bytes 55300
  1803.0 169.9 %all-gather.64.cloned.1.call-start = ((), (), s32[]{:S(2)}) async-start(), calls=%async_computation.37 | async-start | bytes 5640192 | tf_op jit(solution)/shard_map/all_gather | solution.py:175
  1803.5 232.5 %all-gather.38.cloned.1.call-start = ((), (), s32[]{:S(2)}) async-start(), calls=%async_computation.19 | async-start | bytes 7077888 | tf_op jit(solution)/shard_map/all_gather | solution.py:95
  1923.8 171.4 %all-gather.66.cloned.1.call-start = ((), (), s32[]{:S(2)}) async-start(), calls=%async_computation.38 | async-start | bytes 5640192 | tf_op jit(solution)/shard_map/all_gather | solution.py:176
  1924.3 233.6 %all-gather.40.cloned.1.call-start = ((), (), s32[]{:S(2)}) async-start(), calls=%async_computation.21 | async-start | bytes 7077888 | tf_op jit(solution)/shard_map/all_gather | solution.py:103
  1926.7 390.4 %reduce-scatter.32.cloned.1.call-start = ((), (), s32[]{:S(2)}) async-start(), calls=%async_computation.22 | async-start | bytes 14155776 | tf_op jit(solution)/shard_map/reduce_scatter | solution.py:107
  2206.4 223.6 %reduce-scatter.30.cloned.1.call-start = ((), (), s32[]{:S(2)}) async-start(), calls=%async_computation.20 | async-start | bytes 14155776 | tf_op jit(solution)/shard_map/reduce_scatter | solution.py:99
  2229.9 276.9 %all-gather.42.cloned.1.call-start = ((), (), s32[]{:S(2)}) async-start(), calls=%async_computation.23 | async-start | bytes 7077888 | tf_op jit(solution)/shard_map/all_gather | solution.py:103
  2444.0 3526.6 %reduce-scatter.34.cloned.1.call-start = ((), (), s32[]{:S(2)}) async-start(), calls=%async_computation.24 | async-start | bytes 14155776 | tf_op jit(solution)/shard_map/reduce_scatter | solution.py:107
  2550.1 43.3 copy-start.6
  5861.9 108.7 %copy-start.47 = (f32[4,1152]{1,0:T(4,128)S(1)}, f32[4,1152]{1,0:T(4,128)}, u32[]{:S(2)}) copy-start(f32[4,1152]{1,0:T(4,128)} %copy-done.46) | copy-start | bytes 55300
  5861.9 108.7 %copy-start.61 = (f32[4,2,128]{2,1,0:T(2,128)S(1)}, f32[4,2,128]{2,1,0:T(2,128)}, u32[]{:S(2)}) copy-start(f32[4,2,128]{2,1,0:T(2,128)} %copy-done.60) | copy-start | bytes 12292
  5861.9 113.4 %copy-start.87 = (f32[4,2,128]{2,1,0:T(2,128)S(1)}, f32[4,2,128]{2,1,0:T(2,128)}, u32[]{:S(2)}) copy-start(f32[4,2,128]{2,1,0:T(2,128)} %copy-done.86) | copy-start | bytes 12292
  5861.9 113.4 %copy-start.69 = (f32[4,2,128]{2,1,0:T(2,128)S(1)}, f32[4,2,128]{2,1,0:T(2,128)}, u32[]{:S(2)}) copy-start(f32[4,2,128]{2,1,0:T(2,128)} %copy-done.68) | copy-start | bytes 12292
  5861.9 190.4 %all-gather.44.cloned.1.call-start = ((), (), s32[]{:S(2)}) async-start(), calls=%async_computation.25 | async-start | bytes 7077888 | tf_op jit(solution)/shard_map/all_gather | solution.py:103
  5989.5 221.8 %reduce-scatter.36.cloned.1.call-start = ((), (), s32[]{:S(2)}) async-start(), calls=%async_computation.26 | async-start | bytes 14155776 | tf_op jit(solution)/shard_map/reduce_scatter | solution.py:107
  6100.6 110.7 %copy-start.45 = (f32[4,1152]{1,0:T(4,128)S(1)}, f32[4,1152]{1,0:T(4,128)}, u32[]{:S(2)}) copy-start(f32[4,1152]{1,0:T(4,128)} %copy-done.44) | copy-start | bytes 55300
  6100.6 110.7 %copy-start.59 = (f32[4,2,128]{2,1,0:T(2,128)S(1)}, f32[4,2,128]{2,1,0:T(2,128)}, u32[]{:S(2)}) copy-start(f32[4,2,128]{2,1,0:T(2,128)} %copy-done.58) | copy-start | bytes 12292
  6100.6 115.4 %copy-start.85 = (f32[4,2,128]{2,1,0:T(2,128)S(1)}, f32[4,2,128]{2,1,0:T(2,128)}, u32[]{:S(2)}) copy-start(f32[4,2,128]{2,1,0:T(2,128)} %copy-done.84) | copy-start | bytes 12292
  6100.6 115.4 %copy-start.67 = (f32[4,2,128]{2,1,0:T(2,128)S(1)}, f32[4,2,128]{2,1,0:T(2,128)}, u32[]{:S(2)}) copy-start(f32[4,2,128]{2,1,0:T(2,128)} %copy-done.66) | copy-start | bytes 12292
  6100.7 191.8 %all-gather.46.cloned.1.call-start = ((), (), s32[]{:S(2)}) async-start(), calls=%async_computation.27 | async-start | bytes 7077888 | tf_op jit(solution)/shard_map/all_gather | solution.py:103
  6227.8 64.7 copy-start.89
  6229.7 234.0 %reduce-scatter.38.cloned.1.call-start = ((), (), s32[]{:S(2)}) async-start(), calls=%async_computation.28 | async-start | bytes 14155776 | tf_op jit(solution)/shard_map/reduce_scatter | solution.py:107
  6307.1 28.6 copy-start.33
  6353.0 17.5 copy-start.75
  6353.0 17.5 copy-start.77
  6353.0 359.6 %reduce-scatter.40.cloned.1.call-start = ((), (), s32[]{:S(2)}) async-start(), calls=%async_computation.39 | async-start | bytes 2654208
  6372.2 91.4 %copy-start.4 = (bf16[4,2,128,1152]{3,2,1,0:T(8,128)(2,1)S(1)}, bf16[4,2,128,1152]{3,2,1,0:T(8,128)(2,1)}, u32[]{:S(2)}) copy-start(bf16[4,2,128,1152]{3,2,1,0:T(8,128)(2,1)} %param.9) | copy-start | bytes 7077892
  6372.3 91.4 %copy-start.42 = (f32[4,1152]{1,0:T(4,128)S(1)}, f32[4,1152]{1,0:T(4,128)}, u32[]{:S(2)}) copy-start(f32[4,1152]{1,0:T(4,128)} %copy-done.41) | copy-start | bytes 55300
  6372.3 91.4 %copy-start.63 = (f32[4,2,128]{2,1,0:T(2,128)S(1)}, f32[4,2,128]{2,1,0:T(2,128)}, u32[]{:S(2)}) copy-start(f32[4,2,128]{2,1,0:T(2,128)} %copy-done.62) | copy-start | bytes 12292
  6372.3 348.5 %reduce-scatter.42.cloned.1.call-start = ((), (), s32[]{:S(2)}) async-start(), calls=%async_computation.40 | async-start | bytes 2654208
  6389.9 77.2 %copy-start.83 = (f32[4,2,128]{2,1,0:T(2,128)S(1)}, f32[4,2,128]{2,1,0:T(2,128)}, u32[]{:S(2)}) copy-start(f32[4,2,128]{2,1,0:T(2,128)} %copy-done.82) | copy-start | bytes 12292
  6389.9 77.2 %copy-start.71 = (f32[4,2,128]{2,1,0:T(2,128)S(1)}, f32[4,2,128]{2,1,0:T(2,128)}, u32[]{:S(2)}) copy-start(f32[4,2,128]{2,1,0:T(2,128)} %copy-done.70) | copy-start | bytes 12292
  6472.1 356.0 %reduce-scatter.44.cloned.1.call-start = ((), (), s32[]{:S(2)}) async-start(), calls=%async_computation.41 | async-start | bytes 11280384
  6558.6 20.3 copy-start.30
  6558.6 539.6 %all-reduce.8.cloned.1.call-start = ((), (), s32[]{:S(2)}) async-start(), calls=%async_computation.43 | async-start | bytes 44826624
  6578.9 21.3 slice-start.11
  6623.4 29.8 copy-start.91
  6712.6 562.3 %reduce-scatter.46.cloned.1.call-start = ((), (), s32[]{:S(2)}) async-start(), calls=%async_computation.42 | async-start | bytes 16920576
  (77 other events, 466.2 us)
Sparse Core Ops, SparseCore 0:
  10.8 74.8 all-gather.47
  88.5 50.0 all-gather.49
  140.8 61.1 all-gather.29
  204.6 39.4 all-gather.51
  268.4 110.5 reduce-scatter.23
  381.7 56.3 all-gather.53
  440.2 61.2 all-gather.31
  504.3 56.3 all-gather.55
  563.4 70.7 all-gather.57
  636.4 109.7 reduce-scatter.25
  748.4 50.8 all-gather.59
  801.3 61.1 all-gather.33
  880.6 716.3 all-gather.35
  1599.1 39.3 all-gather.61
  1803.1 110.6 reduce-scatter.27
  1916.5 56.3 all-gather.63
  1974.8 61.2 all-gather.37
  2038.7 56.3 all-gather.65
  2096.7 61.2 all-gather.39
  2206.5 110.5 reduce-scatter.31
  2319.4 110.5 reduce-scatter.29
  2444.1 62.6 all-gather.41
  5862.0 108.5 reduce-scatter.33
  5989.7 62.6 all-gather.43
  6100.8 110.5 reduce-scatter.35
  6229.8 62.6 all-gather.45
  6353.1 110.5 reduce-scatter.37
  6466.5 28.2 reduce-scatter.39
  6497.1 28.2 reduce-scatter.41
  6558.7 120.3 reduce-scatter.43
  6712.7 385.4 all-reduce.7
  7102.9 171.9 reduce-scatter.45
where the time goes:
time: 7300 us; the launch traced here: 7290 us
  blocking collectives  2960 us (41%)
  waiting for transfers between devices  2740 us (38%)
  local copies, waits for them, and re-layouts  691 us (9%)
  matrix products  630 us (9%)
  other arithmetic  252 us (3%)
    unnamed x1, blocking collectives  2870 us
    all_gather x1, waiting for transfers between devices, temporal_forward(): lax.all_gather(projected[:, :, :, 1:], 'ctx', axis=1, tiled=True)  707 us
    reduce_scatter x4, waiting for transfers between devices, collect(): return lax.psum_scatter(values, 'tp', scatter_dimension=2, tiled=True)  423 us
    reduce_scatter x4, waiting for transfers between devices, collect_grad(): return lax.psum_scatter(values, 'tp', scatter_dimension=2, tiled=True)  380 us
    unnamed x37, waiting for transfers between devices  351 us
    all_gather x4, waiting for transfers between devices, spread(): return lax.all_gather(values, 'tp', axis=2, tiled=True)  253 us
    all_gather x4, waiting for transfers between devices, spread_grad(): return lax.all_gather(values, 'tp', axis=2, tiled=True)  244 us
    unnamed x239, local copies, waits for them, and re-layouts  208 us
  transfers between devices with their start and end apart: 32, of which 27 were waited for; matrix products, arithmetic and copies ran while one was open for 11% of the time, Pallas kernels for 0%

commit v1 on v0

v1 whole, which is shorter than its diff:
```python
import functools

import jax
import jax.numpy as jnp
from jax import lax
from jax.experimental import pallas as pl
from jax.experimental.pallas import tpu as pltpu
from jax.sharding import PartitionSpec as P

HEAD_DIM = 72
LAYERS = 2
LANES = 128
EPS = 1e-06
SCALE = HEAD_DIM ** (-0.5)
HIGHEST = lax.Precision.HIGHEST
BF16 = jnp.bfloat16
F32 = jnp.float32

NN = (((1,), (0,)), ((), ()))
NT = (((1,), (1,)), ((), ()))
TN = (((0,), (0,)), ((), ()))


def dot(a, b, dims=NN):
    return lax.dot_general(a, b, dims, preferred_element_type=F32)


def swap_with(v, axis_name, n, k):
    return lax.ppermute(v, axis_name, [(i, i ^ k) for i in range(n)])


def flip_to(v, axis, n, me):
    shape = v.shape
    bit = 1
    while bit < n:
        split = shape[:axis] + (n // (2 * bit), 2, bit) + shape[axis + 1 :]
        parts = v.reshape(split)
        first = lax.slice_in_dim(parts, 0, 1, axis=axis + 1)
        second = lax.slice_in_dim(parts, 1, 2, axis=axis + 1)
        turned = jnp.concatenate([second, first], axis=axis + 1)
        v = jnp.where((me & bit) != 0, turned, parts).reshape(shape)
        bit *= 2
    return v


class Moves:
    def __init__(self, mesh):
        self.n_dp = mesh.shape["dp"]
        self.n_ctx = mesh.shape["ctx"]
        self.n_tp = mesh.shape["tp"]
        self.n_line = self.n_ctx // 2

    def here(self):
        self.dp = lax.axis_index("dp")
        self.ctx = lax.axis_index("ctx")
        self.tp = lax.axis_index("tp")
        self.line = self.ctx // 2
        self.side = self.ctx % 2

    def halves(self, v):
        half = v.shape[-1] // 2
        turned = jnp.concatenate([v[..., half:], v[..., :half]], axis=-1)
        return jnp.where(self.dp == 0, v, turned)

    def line_gather(self, v):
        blocks = [v] + [swap_with(v, "ctx", self.n_ctx, 2 * k) for k in range(1, self.n_line)]
        return flip_to(jnp.stack(blocks), 0, self.n_line, self.line)

    def line_scatter(self, v):
        total = lax.dynamic_index_in_dim(v, self.line, 0, keepdims=False).astype(F32)
        for k in range(1, self.n_line):
            sent = lax.dynamic_index_in_dim(v, self.line ^ k, 0, keepdims=False)
            total = total + swap_with(sent, "ctx", self.n_ctx, 2 * k).astype(F32)
        return total

    def pair_gather(self, v):
        other = swap_with(v, "ctx", self.n_ctx, 1)
        first = jnp.where(self.side == 0, v, other)
        second = jnp.where(self.side == 0, other, v)
        return jnp.stack([first, second], axis=1).reshape(-1, v.shape[-1])

    def pair_scatter(self, v):
        parts = v.reshape(self.n_line, 2, -1, v.shape[-1])
        sent = lax.dynamic_index_in_dim(parts, 1 - self.side, 1, keepdims=False)
        kept = lax.dynamic_index_in_dim(parts, self.side, 1, keepdims=False)
        got = swap_with(sent, "ctx", self.n_ctx, 1)
        return (kept.astype(F32) + got.astype(F32)).astype(BF16)

    def gather_weights(self, shards):
        gathered = []
        line = strip = None
        for index, v in enumerate(shards):
            if line is not None:
                v, line = lax.optimization_barrier((v, line))
            line = self.line_gather(v)
            if index % 2 == 1:
                if strip is not None:
                    line, strip = lax.optimization_barrier((line, strip))
                lines = [line]
                lines += [swap_with(line, "tp", self.n_tp, r) for r in range(1, self.n_tp)]
                strip = lines[-1]
                blocks = [self.pair_gather(entry) for entry in lines]
            else:
                block = self.pair_gather(line)
                if strip is not None:
                    block, strip = lax.optimization_barrier((block, strip))
                blocks = [block]
                blocks += [swap_with(block, "tp", self.n_tp, r) for r in range(1, self.n_tp)]
                strip = blocks[-1]
            gathered.append(
                [
                    jnp.concatenate([entry, swap_with(entry, "dp", self.n_dp, 1)], axis=0)
                    for entry in blocks
                ]
            )
        return gathered

    def gather_whole(self, v):
        whole = lax.all_gather(v, ("tp", "dp", "ctx"), axis=0, tiled=True)
        whole = whole.reshape(self.n_tp, -1, v.shape[-1])
        return [whole[t] for t in range(self.n_tp)]

    def scatter_whole(self, left, rights):
        parts = jnp.concatenate([dot(left, v, TN).astype(BF16) for v in rights], axis=0)
        shard = lax.psum_scatter(parts, ("tp", "dp", "ctx"), scatter_dimension=0, tiled=True)
        return shard.astype(F32)

    def scatter_weight(self, left, rights, tp_first):
        half = left.shape[1] // 2
        mine, theirs = left[:, :half], left[:, half:]
        blocks = [None] * self.n_tp
        for r in list(range(1, self.n_tp)) + [0]:
            sent = dot(theirs, rights[r], TN).astype(BF16)
            got = swap_with(sent, "dp", self.n_dp, 1)
            total = dot(mine, rights[r], TN) + got.astype(F32)
            if tp_first and r == 0:
                for q in range(1, self.n_tp):
                    total = total + swap_with(blocks[q], "tp", self.n_tp, q).astype(F32)
            blocks[r] = total.astype(BF16)
        if tp_first:
            line = self.pair_scatter(blocks[0])
        else:
            lines = [self.pair_scatter(entry) for entry in blocks]
            total = lines[0].astype(F32)
            for q in range(1, self.n_tp):
                total = total + swap_with(lines[q], "tp", self.n_tp, q).astype(F32)
            line = total.astype(BF16) if self.n_tp > 1 else lines[0]
        return self.line_scatter(line)


def window(head):
    start = head * HEAD_DIM
    return start // LANES * LANES, -(-(start + HEAD_DIM) // LANES) * LANES


def in_head(head, rows, low, high):
    lanes = lax.broadcasted_iota(jnp.int32, (rows, high - low), 1) + low
    return (lanes >= head * HEAD_DIM) & (lanes < (head + 1) * HEAD_DIM)


def spread_parts(x_ref, parts, width):
    for index, part in enumerate(parts):
        padded = part.shape[1]
        if padded != width:
            part[:, padded - LANES :] = jnp.zeros((part.shape[0], LANES), part.dtype)
        part[:, :width] = x_ref[:, index * width : (index + 1) * width]


def same_sequence(rows, stride):
    row = lax.broadcasted_iota(jnp.int32, (rows, rows), 0)
    column = lax.broadcasted_iota(jnp.int32, (rows, rows), 1)
    return lax.rem(row, stride) == lax.rem(column, stride)


def attend_kernel(heads, stride, x_ref, o_ref, lse_ref, q_s, k_s, v_s, o_s):
    rows, width = x_ref.shape[0], heads * HEAD_DIM
    spread_parts(x_ref, (q_s, k_s, v_s), width)
    lane = lax.broadcasted_iota(jnp.int32, (rows, LANES), 1)
    logs = jnp.zeros((rows, LANES), F32)
    if stride > 1:
        allowed = same_sequence(rows, stride)
    for head in range(heads):
        low, high = window(head)
        mask = in_head(head, rows, low, high)
        queries = jnp.where(mask, q_s[:, low:high], jnp.zeros((), BF16))
        scores = dot(queries, k_s[:, low:high], NT) * SCALE
        if stride > 1:
            scores = jnp.where(allowed, scores, -jnp.inf)
        largest = jnp.max(scores, axis=-1, keepdims=True)
        raised = jnp.exp(scores - largest)
        total = jnp.sum(raised, axis=-1, keepdims=True)
        chances = (raised * (1.0 / total)).astype(BF16)
        result = dot(chances, v_s[:, low:high])
        o_s[:, low:high] = jnp.where(mask, result, o_s[:, low:high])
        logs = jnp.where(lane == head, largest + jnp.log(total), logs)
    o_ref[...] = o_s[:, :width].astype(BF16)
    lse_ref[...] = logs


def attend_back_kernel(
    heads, stride, x_ref, g_ref, lse_ref, dx_ref, q_s, k_s, v_s, g_s, dq_s, dk_s, dv_s
):
    rows, width = x_ref.shape[0], heads * HEAD_DIM
    spread_parts(x_ref, (q_s, k_s, v_s), width)
    spread_parts(g_ref, (g_s,), width)
    if stride > 1:
        allowed = same_sequence(rows, stride)
    for head in range(heads):
        low, high = window(head)
        mask = in_head(head, rows, low, high)
        zero = jnp.zeros((), BF16)
        q, k, v, g = q_s[:, low:high], k_s[:, low:high], v_s[:, low:high], g_s[:, low:high]
        scores = dot(jnp.where(mask, q, zero), k, NT) * SCALE
        if stride > 1:
            scores = jnp.where(allowed, scores, -jnp.inf)
        chances = jnp.exp(scores - lse_ref[:, head : head + 1])
        grad_chances = dot(jnp.where(mask, g, zero), v, NT)
        row_dot = jnp.sum(chances * grad_chances, axis=-1, keepdims=True)
        grad_scores = (chances * (grad_chances - row_dot)).astype(BF16)
        dq = dot(grad_scores, k) * SCALE
        dk = dot(grad_scores, q, TN) * SCALE
        dv = dot(chances.astype(BF16), g, TN)
        dq_s[:, low:high] = jnp.where(mask, dq, dq_s[:, low:high])
        dk_s[:, low:high] = jnp.where(mask, dk, dk_s[:, low:high])
        dv_s[:, low:high] = jnp.where(mask, dv, dv_s[:, low:high])
    for index, part in enumerate((dq_s, dk_s, dv_s)):
        dx_ref[:, index * width : (index + 1) * width] = part[:, :width].astype(BF16)


def row_block(rows, columns):
    return pl.BlockSpec((rows, columns), lambda i: (i, 0))


def attend(x, rows, stride):
    count, width = x.shape[0], x.shape[1] // 3
    heads = width // HEAD_DIM
    padded = -(-width // LANES) * LANES
    return pl.pallas_call(
        functools.partial(attend_kernel, heads, stride),
        grid=(count // rows,),
        in_specs=[row_block(rows, 3 * width)],
        out_specs=[row_block(rows, width), row_block(rows, LANES)],
        out_shape=[
            jax.ShapeDtypeStruct((count, width), BF16),
            jax.ShapeDtypeStruct((count, LANES), F32),
        ],
        scratch_shapes=[pltpu.VMEM((rows, padded), BF16)] * 3 + [pltpu.VMEM((rows, padded), F32)],
        cost_estimate=pl.CostEstimate(
            flops=heads * count * rows * 1024,
            bytes_accessed=count * width * 8,
            transcendentals=heads * count * rows,
        ),
        compiler_params=pltpu.CompilerParams(vmem_limit_bytes=32 * 1024 * 1024),
    )(x)


def attend_back(x, grad, lse, rows, stride):
    count, width = grad.shape
    heads = width // HEAD_DIM
    padded = -(-width // LANES) * LANES
    return pl.pallas_call(
        functools.partial(attend_back_kernel, heads, stride),
        grid=(count // rows,),
        in_specs=[row_block(rows, 3 * width), row_block(rows, width), row_block(rows, LANES)],
        out_specs=row_block(rows, 3 * width),
        out_shape=jax.ShapeDtypeStruct((count, 3 * width), BF16),
        scratch_shapes=[pltpu.VMEM((rows, padded), BF16)] * 4
        + [pltpu.VMEM((rows, padded), F32)] * 3,
        cost_estimate=pl.CostEstimate(
            flops=heads * count * rows * 2560,
            bytes_accessed=count * width * 14,
            transcendentals=heads * count * rows,
        ),
        compiler_params=pltpu.CompilerParams(vmem_limit_bytes=32 * 1024 * 1024),
    )(x, grad, lse)


def split_frames(v, frames, width):
    return v.reshape(frames, -1, width // HEAD_DIM, HEAD_DIM)


def attend_shared(x, frames):
    width = x.shape[1] // 3
    shaped = x.reshape(frames, -1, 3, width)
    pairs = lax.all_gather(shaped[:, :, 1:], "tp", axis=1, tiled=True)
    q = split_frames(shaped[:, :, 0], frames, width)
    k = split_frames(pairs[:, :, 0], frames, width)
    v = split_frames(pairs[:, :, 1], frames, width)
    scores = jnp.einsum("bqhe,bkhe->bhqk", q, k, preferred_element_type=F32) * SCALE
    chances = jax.nn.softmax(scores, axis=-1)
    result = jnp.einsum("bhqk,bkhe->bqhe", chances.astype(BF16), v, preferred_element_type=F32)
    return result.reshape(-1, width).astype(BF16), (q, k, v, chances)


def attend_shared_back(saved, grad):
    q, k, v, chances = saved
    frames, width = q.shape[0], grad.shape[1]
    grad = split_frames(grad, frames, width)
    grad_chances = jnp.einsum("bqhe,bkhe->bhqk", grad, v, preferred_element_type=F32)
    row_dot = jnp.sum(chances * grad_chances, axis=-1, keepdims=True)
    grad_scores = (chances * (grad_chances - row_dot)).astype(BF16)
    dq = jnp.einsum("bhqk,bkhe->bqhe", grad_scores, k, preferred_element_type=F32) * SCALE
    dk = jnp.einsum("bhqk,bqhe->bkhe", grad_scores, q, preferred_element_type=F32) * SCALE
    dv = jnp.einsum("bhqk,bqhe->bkhe", chances.astype(BF16), grad, preferred_element_type=F32)
    sums = lax.psum_scatter(jnp.stack([dk, dv], axis=2), "tp", scatter_dimension=1, tiled=True)
    parts = jnp.concatenate([dq[:, :, None], sums], axis=2)
    return parts.reshape(-1, 3 * width).astype(BF16)


def normalise(v):
    centred = v - jnp.mean(v, axis=-1, keepdims=True)
    inverse = lax.rsqrt(jnp.mean(centred * centred, axis=-1, keepdims=True) + EPS)
    return centred * inverse, inverse


def modulate(v, shift, scale):
    return (normalise(v)[0] * (1.0 + scale[:, None]) + shift[:, None]).astype(BF16)


def modulate_back(grad, v, scale):
    normed, inverse = normalise(v)
    shift_grad = jnp.sum(grad, axis=1)
    scale_grad = jnp.sum(grad * normed, axis=1)
    scaled = grad * (1.0 + scale[:, None])
    mean_one = jnp.mean(scaled, axis=-1, keepdims=True)
    mean_two = jnp.mean(scaled * normed, axis=-1, keepdims=True)
    return inverse * (scaled - mean_one - normed * mean_two), shift_grad, scale_grad


def gelu(v):
    return jax.nn.gelu(v, approximate=True)


def gelu_slope(v, grad):
    return jax.vjp(gelu, v)[1](grad)[0]


def local(moves, tokens, condition, micro_ids, w_qkv, w_out, w_up, w_down, w_ada, cotangent):
    moves.here()
    n_dp, n_ctx, n_tp = moves.n_dp, moves.n_ctx, moves.n_tp
    clips, frames_here, patches_here, width = tokens.shape
    rows_here, head_cols = w_qkv.shape[2:]
    whole_frames = frames_here % n_tp == 0
    spread_tp = n_tp if whole_frames else 1
    groups = frames_here // spread_tp
    piece = patches_here // n_ctx

    cond_full = condition.astype(F32)
    cond_low = jax.nn.silu(cond_full).astype(BF16)
    cond_all = jnp.concatenate([cond_low, swap_with(cond_low, "dp", n_dp, 1)], axis=0)
    first_row = (moves.dp * n_ctx + moves.ctx) * rows_here
    cond_rows = lax.dynamic_slice_in_dim(cond_all, first_row, rows_here, axis=1)
    ada_low = w_ada.astype(BF16)
    shares = jnp.stack([dot(cond_rows, ada_low[level]) for level in range(LAYERS)], axis=1)
    sums = shares[:clips] + swap_with(shares[clips:], "dp", n_dp, 1)
    step = 1
    while step < n_ctx:
        sums = sums + swap_with(sums, "ctx", n_ctx, step)
        step *= 2
    strips = [sums] + [swap_with(sums, "tp", n_tp, r) for r in range(1, n_tp)]
    strips = flip_to(jnp.stack(strips, axis=2), 2, n_tp, moves.tp)
    mods = strips.reshape(clips, LAYERS, 6, width)
    mods = [moves.halves(mods[:, 0]), mods[:, 1]]

    pieces = []
    for level in range(LAYERS):
        attention = [w_qkv[level, 0], w_qkv[level, 1], w_qkv[level, 2], w_out[level].T]
        pieces.append(jnp.concatenate(attention, axis=1).astype(BF16))
        pieces.append(w_up[level].astype(BF16))
        pieces.append(w_down[level].T.astype(BF16))
    gathered = moves.gather_weights(pieces[:3])
    later, gathered[0] = lax.optimization_barrier((pieces[3:], gathered[0]))
    gathered += [moves.gather_whole(v) for v in later]

    def to_frames(v):
        v = v.reshape(clips, frames_here, n_ctx, piece, width)
        v = flip_to(v, 2, n_ctx, moves.ctx)
        if spread_tp == 1:
            return v.reshape(clips, groups * patches_here, width)
        v = v.reshape(clips, spread_tp, groups, patches_here, width)
        v = flip_to(v, 1, spread_tp, moves.tp)
        blocks = [v[:, 0]]
        blocks += [swap_with(v[:, r], "tp", n_tp, r) for r in range(1, spread_tp)]
        return jnp.stack(blocks, axis=2).reshape(clips, -1, width)

    def from_frames(v):
        if spread_tp > 1:
            v = v.reshape(clips, groups, spread_tp, patches_here, width)
            blocks = [v[:, :, 0]]
            blocks += [swap_with(v[:, :, r], "tp", n_tp, r) for r in range(1, spread_tp)]
            v = flip_to(jnp.stack(blocks, axis=1), 1, spread_tp, moves.tp)
        v = v.reshape(clips, frames_here, n_ctx, piece, width)
        v = flip_to(v, 2, n_ctx, moves.ctx)
        return v.reshape(clips, frames_here, patches_here, width)

    def trade(get, planes):
        sides = []
        for dx, dr in planes:
            block = get(dx, dr)
            if dx or dr:
                pairs = [
                    (c * n_tp + t, (c ^ dx) * n_tp + (t ^ dr))
                    for c in range(n_ctx)
                    for t in range(n_tp)
                ]
                block = lax.ppermute(block, ("ctx", "tp"), pairs)
            sides.append(block)
        lines = []
        for dz in range(n_ctx // 2):
            block = jnp.stack([v[:, dz] for v in sides], axis=1)
            lines.append(swap_with(block, "ctx", n_ctx, 2 * dz) if dz else block)
        return jnp.stack(lines, axis=1)

    all_planes = [(dx, dr) for dx in range(2) for dr in range(spread_tp)]
    own_planes = [(0, 0), (1, 0)]

    def frames_to_clips(v):
        v = v.reshape(clips, groups, spread_tp, n_ctx // 2, 2, piece, width)
        got = trade(lambda dx, dr: v[:, :, dr, :, dx].swapaxes(1, 2), all_planes)
        return got.reshape(clips, -1, width)

    def clips_to_frames(v):
        v = v.reshape(clips, n_ctx // 2, 2, spread_tp, groups, piece, width)
        got = trade(lambda dx, dr: v[:, :, dx, dr], all_planes)
        got = got.reshape(clips, n_ctx, spread_tp, groups, piece, width)
        return got.transpose(0, 3, 2, 1, 4, 5).reshape(clips, -1, width)

    def here_to_clips(v):
        v = v.reshape(clips, spread_tp, groups, n_ctx, piece, width)
        v = flip_to(flip_to(v, 3, n_ctx, moves.ctx), 1, spread_tp, moves.tp % spread_tp)
        v = v.reshape(clips, spread_tp, groups, n_ctx // 2, 2, piece, width)
        got = trade(lambda dx, dr: v[:, :, :, :, dx].transpose(0, 3, 1, 2, 4, 5), own_planes)
        return got.reshape(clips, -1, width)

    def clips_to_here(v):
        v = v.reshape(clips, n_ctx // 2, 2, spread_tp, groups, piece, width)
        got = trade(lambda dx, dr: v[:, :, dx], own_planes)
        v = got.reshape(clips, n_ctx, spread_tp, groups, piece, width).transpose(0, 2, 3, 1, 4, 5)
        v = flip_to(flip_to(v, 3, n_ctx, moves.ctx), 1, spread_tp, moves.tp % spread_tp)
        return v.reshape(clips, frames_here, patches_here, width)

    def flat(v):
        return v.reshape(-1, v.shape[-1])

    def shaped(v):
        return v.reshape(clips, -1, v.shape[-1])

    residual = to_frames(moves.halves(tokens)).astype(F32)
    qkv_cols = 3 * head_cols
    records = []
    for level in range(LAYERS):
        spatial = level % 2 == 0
        joined, ups, downs = gathered[3 * level : 3 * level + 3]
        qkvs = [v[:, :qkv_cols] for v in joined]
        outs = [v[:, qkv_cols:] for v in joined]
        shift_a, scale_a, gate_a, shift_m, scale_m, gate_m = [mods[level][:, i] for i in range(6)]
        if not spatial:
            residual = frames_to_clips(moves.halves(residual.astype(BF16))).astype(F32)
        block_rows = groups * spread_tp * patches_here if not spatial else spread_tp * patches_here
        block_rows = residual.shape[1] if not spatial else block_rows
        stride = 1 if spatial else piece
        normed = flat(modulate(residual, shift_a, scale_a))
        projected = [dot(normed, v).astype(BF16) for v in qkvs]
        if spatial and not whole_frames:
            attended = [attend_shared(v, clips * frames_here) for v in projected]
        else:
            attended = [attend(v, block_rows, stride) for v in projected]
        results = [entry[0] for entry in attended]
        branch = sum(dot(v, w, NT) for v, w in zip(results, outs))
        branch = shaped(branch)
        middle = residual + gate_a[:, None] * branch
        normed_mlp = flat(modulate(middle, shift_m, scale_m))
        pre_acts = [dot(normed_mlp, w) for w in ups]
        acts = [gelu(v).astype(BF16) for v in pre_acts]
        branch_mlp = shaped(sum(dot(v, w, NT) for v, w in zip(acts, downs)))
        records.append(
            (residual, normed, projected, attended, results, branch, middle, normed_mlp)
            + (pre_acts, acts, branch_mlp, qkvs, outs, ups, downs, block_rows, stride)
        )
        residual = middle + gate_m[:, None] * branch_mlp
    output = clips_to_here(residual.astype(BF16))

    matched = (micro_ids[:, None] == micro_ids[None, :]).astype(F32)
    share = 1.0 / jnp.sum(matched, axis=1)
    gradient = here_to_clips(cotangent).astype(F32) * share[:, None, None]
    grads = [None] * LAYERS
    mod_grads = [None] * LAYERS
    for level in reversed(range(LAYERS)):
        spatial = level % 2 == 0

        def scatter(left, rights, tp_first, level=level):
            if level:
                return moves.scatter_whole(left, rights)
            return moves.scatter_weight(left, rights, tp_first)

        (residual, normed, projected, attended, results, branch, middle, normed_mlp) = records[
            level
        ][:8]
        (pre_acts, acts, branch_mlp, qkvs, outs, ups, downs, block_rows, stride) = records[level][
            8:
        ]
        shift_a, scale_a, gate_a, shift_m, scale_m, gate_m = [mods[level][:, i] for i in range(6)]
        gate_m_grad = jnp.sum(gradient * branch_mlp, axis=1)
        low_grad = flat((gradient * gate_m[:, None]).astype(BF16))
        grad_pre = [
            gelu_slope(u, dot(low_grad, w)).astype(BF16) for u, w in zip(pre_acts, downs)
        ]
        grad_down = scatter(low_grad, acts, True)
        grad_normed = shaped(sum(dot(v, w, NT) for v, w in zip(grad_pre, ups)))
        grad_up = scatter(normed_mlp, grad_pre, False)
        added, shift_m_grad, scale_m_grad = modulate_back(grad_normed, middle, scale_m)
        gradient = gradient + added
        gate_a_grad = jnp.sum(gradient * branch, axis=1)
        low_grad = flat((gradient * gate_a[:, None]).astype(BF16))
        grad_heads = [dot(low_grad, w).astype(BF16) for w in outs]
        grad_out = scatter(low_grad, results, True)
        if spatial and not whole_frames:
            grad_qkv = [attend_shared_back(e[1], g) for e, g in zip(attended, grad_heads)]
        else:
            grad_qkv = [
                attend_back(v, g, e[1], block_rows, stride)
                for v, g, e in zip(projected, grad_heads, attended)
            ]
        grad_normed = shaped(sum(dot(v, w, NT) for v, w in zip(grad_qkv, qkvs)))
        grad_in = scatter(normed, grad_qkv, False)
        added, shift_a_grad, scale_a_grad = modulate_back(grad_normed, residual, scale_a)
        gradient = gradient + added
        if not spatial:
            gradient = moves.halves(clips_to_frames(gradient.astype(BF16))).astype(F32)
        mod_grads[level] = jnp.stack(
            [shift_a_grad, scale_a_grad, gate_a_grad, shift_m_grad, scale_m_grad, gate_m_grad],
            axis=1,
        )
        grads[level] = (
            grad_in.reshape(rows_here, 3, head_cols).transpose(1, 0, 2),
            grad_out.T,
            grad_up,
            grad_down.T,
        )
    grad_tokens = from_frames(moves.halves(gradient.astype(BF16))).astype(F32)

    ada_grads = []
    cond_part = 0.0
    for level in range(LAYERS):
        whole = mod_grads[level] if level else moves.halves(mod_grads[level])
        whole = whole.reshape(clips, n_tp, -1)
        whole = flip_to(whole, 1, n_tp, moves.tp)
        strip = whole[:, 0]
        for r in range(1, n_tp):
            strip = strip + swap_with(whole[:, r], "tp", n_tp, r)
        step = 1
        while step < n_ctx:
            strip = strip + swap_with(strip, "ctx", n_ctx, step)
            step *= 2
        strip = jnp.concatenate([strip, swap_with(strip, "dp", n_dp, 1)], axis=0)
        ada_grads.append(
            lax.dot_general(cond_rows.astype(F32), strip, TN, precision=HIGHEST)
        )
        cond_part = cond_part + lax.dot_general(
            strip, ada_low[level].astype(F32), NT, precision=HIGHEST
        )
    step = 1
    while step < n_tp:
        cond_part = cond_part + swap_with(cond_part, "tp", n_tp, step)
        step *= 2
    cond_grad = jnp.stack(
        [cond_part[:clips], swap_with(cond_part[clips:], "dp", n_dp, 1)], axis=1
    )[:, :, None]
    step = 1
    while step < n_ctx:
        cond_grad = jnp.concatenate(
            [cond_grad, swap_with(cond_grad, "ctx", n_ctx, step)], axis=2
        )
        step *= 2
    cond_grad = flip_to(cond_grad, 2, n_ctx, moves.ctx).reshape(clips, width)
    cond_grad = moves.halves(cond_grad)
    grad_condition = jax.vjp(jax.nn.silu, cond_full)[1](cond_grad)[0]

    stacked = [jnp.stack([grads[level][i] for level in range(LAYERS)]) for i in range(4)]
    return (output, grad_tokens, grad_condition, *stacked, jnp.stack(ada_grads))


def solution(mesh):
    placed = (
        P("dp", "ctx", "tp", None),
        P("dp", None),
        P("dp"),
        P(None, None, ("dp", "ctx"), "tp"),
        P(None, "tp", ("dp", "ctx")),
        P(None, ("dp", "ctx"), "tp"),
        P(None, "tp", ("dp", "ctx")),
        P(None, ("dp", "ctx"), "tp"),
        P("dp", "ctx", "tp", None),
    )
    return jax.shard_map(
        functools.partial(local, Moves(mesh)),
        mesh=mesh,
        in_specs=placed,
        out_specs=(
            P("dp", "ctx", "tp", None),
            P("dp", "ctx", "tp", None),
            P("dp", None),
            P(None, None, ("dp", "ctx"), "tp"),
            P(None, "tp", ("dp", "ctx")),
            P(None, ("dp", "ctx"), "tp"),
            P(None, "tp", ("dp", "ctx")),
            P(None, ("dp", "ctx"), "tp"),
        ),
        check_vma=False,
    )
```

time: 7300 us -> 1710 us (0.23)
  blocking collectives: 2960 us -> 0 us
  waiting for transfers between devices: 2740 us -> 664 us
  local copies, waits for them, and re-layouts: 691 us -> 172 us
  matrix products: 630 us -> 406 us
  starting transfers between devices: 1.72 us -> 163 us
  Pallas kernels: 0 us -> 90.2 us
    unnamed x1 -> x0, blocking collectives: 2870 us -> none
    all_gather x19 -> x3, waiting for transfers between devices: 1580 us -> 0.02 us  [gather_whole(): whole = lax.all_gather(v, ('tp', 'dp', 'ctx'), axis=0, tiled=True)]
    reduce_scatter x8 -> x3, waiting for transfers between devices: 803 us -> 0.02 us  [scatter_whole(): lax.psum_scatter(parts, ('tp', 'dp', 'ctx'), scatter_dimension=0, tiled=T...]
    ppermute x0 -> x95, waiting for transfers between devices: none -> 664 us  [the longest x87 616 us: swap_with(): return lax.ppermute(v, axis_name, [(i, i ^ k) for i in range(n)])]
    unnamed x37 -> x8, waiting for transfers between devices: 351 us -> 0.14 us
    dot_general x42 -> x62, matrix products: 630 us -> 406 us  [the longest x58 402 us: dot(): return lax.dot_general(a, b, dims, preferred_element_type=F32)]
    ppermute x0 -> x95, starting transfers between devices: none -> 163 us  [the longest x87 150 us: swap_with(): return lax.ppermute(v, axis_name, [(i, i ^ k) for i in range(n)])]
    transpose x5 -> x3, local copies, waits for them, and re-layouts: 154 us -> 2.05 us  [the longest x1 1.65 us: here_to_clips(): v[:, :, :, :, dx].transpose(0, 3, 1, 2, 4, 5)]
  transfers between devices with their start and end apart: 32 -> 102, of which waited for: 27 -> 46; matrix products, arithmetic and copies ran while one was open for 11% -> 37% of each run, Pallas kernels for 0% -> 5%
where the time goes in v1:
time: 1710 us; the launch traced here: 1700 us
  waiting for transfers between devices  664 us (39%)
  matrix products  406 us (24%)
  other arithmetic  186 us (11%)
  local copies, waits for them, and re-layouts  172 us (10%)
  starting transfers between devices  163 us (10%)
  Pallas kernels  90.2 us (5%)
  between operations  19.4 us (1%)
    ppermute x87, waiting for transfers between devices, swap_with(): return lax.ppermute(v, axis_name, [(i, i ^ k) for i in range(n)])  616 us
    dot_general x58, matrix products, dot(): return lax.dot_general(a, b, dims, preferred_element_type=F32)  402 us
    ppermute x87, starting transfers between devices, swap_with(): return lax.ppermute(v, axis_name, [(i, i ^ k) for i in range(n)])  150 us
    unnamed x534, local copies, waits for them, and re-layouts  74.9 us
    pallas_call x4, Pallas kernels, attend_back(): pl.pallas_call(functools.partial(attend_back_kernel, heads, stride), grid...  60.8 us
    ppermute x8, waiting for transfers between devices, trade(): block = lax.ppermute(block, ('ctx', 'tp'), pairs)  48.6 us
    concatenate x4, other arithmetic, scatter_whole(): jnp.concatenate([dot(left, v, TN).astype(BF16) for v in rights], axis=0)  35.1 us
  transfers between devices with their start and end apart: 102, of which 46 were waited for; matrix products, arithmetic and copies ran while one was open for 37% of the time, Pallas kernels for 5%

profile of v1, /device:TPU:0, one launch (start us, length us, event | category | flops | bytes accessed | tf_op | source)
XLA Modules:
  0.0 1700.1 jit_solution(6997836783521268235)
XLA Ops:
  15.5 11.4 collective-permute-done.7
  26.8 11.7 collective-permute-done.8
  41.3 26.9 %collective-permute-done.10 = bf16[4,72,2304]{2,1,0:T(8,128)(2,1)S(1)} collective-permute-done((bf16[4,72,2304]{2,1,0:T(8,128)(2,1)S(1)}, bf16[4,72,2304]{2,1,0:T(8,128)(2,1)S(1)}, u32[]{:S(2)}, u32[]{:S(2)}) %collective-permute-start.10) | collective-permute-done | bytes 1327136 | tf_op jit(solution)/shard_map/ppermute | solution.py:29
  70.3 54.5 %collective-permute-done.12 = bf16[576,2304]{1,0:T(8,128)(2,1)} collective-permute-done((bf16[576,2304]{1,0:T(8,128)(2,1)S(1)}, bf16[576,2304]{1,0:T(8,128)(2,1)}, u32[]{:S(2)}, u32[]{:S(2)}) %collective-permute-start.12) | collective-permute-done | bytes 2654240 | tf_op jit(solution)/shard_map/ppermute | solution.py:29
  186.4 24.2 %collective-permute-done.3 = f32[4,2,3456]{2,0,1:T(4,128)S(1)} collective-permute-done((f32[4,2,3456]{2,0,1:T(4,128)S(1)}, f32[4,2,3456]{2,0,1:T(4,128)S(1)}, u32[]{:S(2)}, u32[]{:S(2)}) %collective-permute-start.3) | collective-permute-done | bytes 110624 | tf_op jit(solution)/shard_map/ppermute | solution.py:29
  210.6 9.7 collective-permute-start.4
  220.6 8.2 collective-permute-done.4
  229.4 14.8 collective-permute-done.5
  258.3 15.4 collective-permute-done.14
  297.9 45.6 %collective-permute-done.19 = bf16[72,2304]{1,0:T(8,128)(2,1)S(1)} collective-permute-done((bf16[72,2304]{1,0:T(8,128)(2,1)S(1)}, bf16[72,2304]{1,0:T(8,128)(2,1)S(1)}, u32[]{:S(2)}, u32[]{:S(2)}) %collective-permute-start.19) | collective-permute-done | bytes 331808 | tf_op jit(solution)/shard_map/ppermute | solution.py:29
  344.3 21.5 %collective-permute-done.20 = bf16[72,2304]{1,0:T(8,128)(2,1)S(1)} collective-permute-done((bf16[72,2304]{1,0:T(8,128)(2,1)S(1)}, bf16[72,2304]{1,0:T(8,128)(2,1)S(1)}, u32[]{:S(2)}, u32[]{:S(2)}) %collective-permute-start.20) | collective-permute-done | bytes 331808 | tf_op jit(solution)/shard_map/ppermute | solution.py:29
  371.1 26.8 %collective-permute-done.17 = bf16[4,72,2304]{2,1,0:T(8,128)(2,1)S(1)} collective-permute-done((bf16[4,72,2304]{2,1,0:T(8,128)(2,1)S(1)}, bf16[4,72,2304]{2,1,0:T(8,128)(2,1)S(1)}, u32[]{:S(2)}, u32[]{:S(2)}) %collective-permute-start.17) | collective-permute-done | bytes 1327136 | tf_op jit(solution)/shard_map/ppermute | solution.py:29
  400.0 22.7 %collective-permute-done.22 = bf16[4,72,2304]{2,1,0:T(8,128)(2,1)S(1)} collective-permute-done((bf16[4,72,2304]{2,1,0:T(8,128)(2,1)S(1)}, bf16[4,72,2304]{2,1,0:T(8,128)(2,1)S(1)}, u32[]{:S(2)}, u32[]{:S(2)}) %collective-permute-start.22) | collective-permute-done | bytes 1327136 | tf_op jit(solution)/shard_map/ppermute | solution.py:29
  429.8 11.6 collective-permute-done.25
  486.0 11.9 multiply_convert_fusion.3
  514.6 9.5 multiply_convert_fusion.2
  527.2 10.7 convolution_add_fusion.5
  547.8 25.1 %collective-permute-done.29 = bf16[4,4,1,16,1152]{4,3,1,0,2:T(8,128)(2,1)S(1)} collective-permute-done((bf16[4,4,1,16,1152]{4,3,1,0,2:T(8,128)(2,1)S(1)}, bf16[4,4,1,16,1152]{4,3,1,0,2:T(8,128)(2,1)S(1)}, u32[]{:S(2)}, u32[]{:S(2)}) %collective-permute-start.29) | collective-permute-done | bytes 589856 | tf_op jit(solution)/shard_map/ppermute | solution.py:406
  575.3 19.3 %collective-permute-done.31 = bf16[4,4,1,16,1152]{4,3,1,0,2:T(8,128)(2,1)S(1)} collective-permute-done((bf16[4,4,1,16,1152]{4,3,1,0,2:T(8,128)(2,1)S(1)}, bf16[4,4,1,16,1152]{4,3,1,0,2:T(8,128)(2,1)S(1)}, u32[]{:S(2)}, u32[]{:S(2)}) %collective-permute-start.31) | collective-permute-done | bytes 589856 | tf_op jit(solution)/shard_map/ppermute | solution.py:406
  605.6 18.9 %collective-permute-done.32 = bf16[4,4,1,16,1152]{4,3,1,0,2:T(8,128)(2,1)S(1)} collective-permute-done((bf16[4,4,1,16,1152]{4,3,1,0,2:T(8,128)(2,1)S(1)}, bf16[4,4,1,16,1152]{4,3,1,0,2:T(8,128)(2,1)S(1)}, u32[]{:S(2)}, u32[]{:S(2)}) %collective-permute-start.32) | collective-permute-done | bytes 589856 | tf_op jit(solution)/shard_map/ppermute | solution.py:29
  624.4 14.6 collective-permute-done.34
  686.8 11.6 fusion.105
  698.3 9.1 fusion.95
  707.4 15.6 fusion.20
  723.1 13.7 fusion.27
  736.9 8.2 fusion.93
  745.1 11.2 fusion.116
  782.9 15.4 shard_map.156
  805.2 15.2 shard_map.157
  836.2 11.5 copy.791
  855.8 9.1 convolution_convert_fusion.1
  864.9 9.1 convolution_convert_fusion
  874.0 12.2 pad_maximum_fusion.1
  886.3 13.9 fusion.89
  900.2 13.7 fusion.110
  913.9 8.9 fusion.119
  923.0 10.7 fusion.114
  933.7 11.9 fusion.53
  961.4 9.5 fusion.33
  992.8 12.4 pad_maximum_fusion
  1011.8 18.1 %collective-permute-start.46 = (bf16[4,4,1,16,1152]{4,3,0,1,2:T(8,128)(2,1)S(1)}, bf16[4,4,1,16,1152]{4,3,0,1,2:T(8,128)(2,1)S(1)}, u32[]{:S(2)}, u32[]{:S(2)}) collective-permute-start(bf16[4,4,1,16,1152]{4,3,0,1,2:T(8,128)(2,1)S(1)} %pad_maximum_fusion.59), channel_id=1, source_target_pairs={{0,4},{2,6},{4,0},{6,2},{8,12},{10,14},{12,8},{14,10},{1,5},{3,7},... | collective-permute-start | bytes 1769480 | tf_op jit(solution)/shard_map/ppermute | solution.py:29
  1033.8 30.5 %collective-permute-done.46 = bf16[4,4,1,16,1152]{4,3,0,1,2:T(8,128)(2,1)S(1)} collective-permute-done((bf16[4,4,1,16,1152]{4,3,0,1,2:T(8,128)(2,1)S(1)}, bf16[4,4,1,16,1152]{4,3,0,1,2:T(8,128)(2,1)S(1)}, u32[]{:S(2)}, u32[]{:S(2)}) %collective-permute-start.46) | collective-permute-done | bytes 589856 | tf_op jit(solution)/shard_map/ppermute | solution.py:29
  1064.3 19.4 %collective-permute-done.47 = bf16[4,4,1,16,1152]{4,3,0,1,2:T(8,128)(2,1)S(1)} collective-permute-done((bf16[4,4,1,16,1152]{4,3,0,1,2:T(8,128)(2,1)S(1)}, bf16[4,4,1,16,1152]{4,3,0,1,2:T(8,128)(2,1)S(1)}, u32[]{:S(2)}, u32[]{:S(2)}) %collective-permute-start.47) | collective-permute-done | bytes 589856 | tf_op jit(solution)/shard_map/ppermute | solution.py:29
  1090.8 11.3 fusion.6
  1102.1 13.5 fusion.13
  1117.7 8.3 fusion.127
  1126.1 15.6 fusion.115
  1162.0 15.0 shard_map.158
  1177.0 10.2 fusion.124
  1187.3 15.2 shard_map.159
  1204.3 17.8 %fusion.54 = (f32[4,1152]{1,0:T(4,128)S(1)}, f32[4,1152]{1,0:T(4,128)S(1)}, f32[4,1152]{1,0:T(4,128)S(1)}, f32[4,1152]{1,0:T(4,128)S(1)}, f32[4,1152]{1,0:T(4,12...) fusion(f32[1024,1152]{1,0:T(8,128)} %get-tuple-element.350, ...), kind=kOutput, calls=%fused_computation.109 | convolution fusion | flops 4111045632 | bytes 43491328 | tf_op jit(solution)/shard_map/dot_general | solution.py:25
  1262.5 10.8 add_convert_fusion.4
  1305.5 16.5 collective-permute-start.57
  1331.6 24.3 %collective-permute-done.52 = f32[4,3456]{1,0:T(4,128)S(1)} collective-permute-done((f32[4,3456]{1,0:T(4,128)S(1)}, f32[4,3456]{1,0:T(4,128)S(1)}, u32[]{:S(2)}, u32[]{:S(2)}) %collective-permute-start.52) | collective-permute-done | bytes 55328 | tf_op jit(solution)/shard_map/ppermute | solution.py:29
  1380.1 23.6 %collective-permute-done.64 = f32[4,2,4,72]{3,0,1,2:T(4,128)S(1)} collective-permute-done((f32[4,2,4,72]{3,0,1,2:T(4,128)S(1)}, f32[4,2,4,72]{3,0,1,2:T(4,128)S(1)}, u32[]{:S(2)}, u32[]{:S(2)}) %collective-permute-start.64) | collective-permute-done | bytes 9248 | tf_op jit(solution)/shard_map/ppermute | solution.py:29
  1408.2 16.5 collective-permute-done.38
  1439.1 13.2 collective-permute-done.49
  1458.2 11.1 collective-permute-done.75
  1481.7 10.7 collective-permute-start.77
  1528.1 27.9 %collective-permute-done.68 = bf16[4,72,1728]{2,1,0:T(8,128)(2,1)} collective-permute-done((bf16[4,72,1728]{2,1,0:T(8,128)(2,1)}, bf16[4,72,1728]{2,1,0:T(8,128)(2,1)}, u32[]{:S(2)}, u32[]{:S(2)}) %collective-permute-start.68) | collective-permute-done | bytes 995360 | tf_op jit(solution)/shard_map/ppermute | solution.py:29
  1560.2 23.0 %collective-permute-done.83 = bf16[4,72,2304]{2,1,0:T(8,128)(2,1)S(1)} collective-permute-done((bf16[4,72,2304]{2,1,0:T(8,128)(2,1)S(1)}, bf16[4,72,2304]{2,1,0:T(8,128)(2,1)S(1)}, u32[]{:S(2)}, u32[]{:S(2)}) %collective-permute-start.83) | collective-permute-done | bytes 1327136 | tf_op jit(solution)/shard_map/ppermute | solution.py:29
  1587.6 14.2 collective-permute-done.69
  1648.8 8.6 collective-permute-done.86
  1661.1 24.7 %collective-permute-done.93 = bf16[72,2304]{1,0:T(8,128)(2,1)S(1)} collective-permute-done((bf16[72,2304]{1,0:T(8,128)(2,1)S(1)}, bf16[72,2304]{1,0:T(8,128)(2,1)S(1)}, u32[]{:S(2)}, u32[]{:S(2)}) %collective-permute-start.93) | collective-permute-done | bytes 331808 | tf_op jit(solution)/shard_map/ppermute | solution.py:29
  (1108 shorter events, 642.8 us)
Async XLA Ops:
  7.2 638.8 %all-gather.4.cloned.1.call-start = ((), (), s32[]{:S(2)}) async-start(), calls=%async_computation.3 | async-start | bytes 10948608 | tf_op jit(solution)/shard_map/all_gather | solution.py:119
  39.7 28.5 %collective-permute-start.10 = (bf16[4,72,2304]{2,1,0:T(8,128)(2,1)S(1)}, bf16[4,72,2304]{2,1,0:T(8,128)(2,1)S(1)}, u32[]{:S(2)}, u32[]{:S(2)}) collective-permute-start(bf16[4,72,2304]{2,1,0:T(8,128)(2,1)S(1)} %fusion.156), channel_id=1, source_target_pairs={{0,2},{2,0},{4,6},{6,4},{8,10},{10,8},{12,14},{14,12},{1,3},{3,1},... | collective-permute-start | bytes 3981320 | tf_op jit(solution)/shard_map/ppermute | solution.py:29
  68.7 56.1 %collective-permute-start.12 = (bf16[576,2304]{1,0:T(8,128)(2,1)S(1)}, bf16[576,2304]{1,0:T(8,128)(2,1)}, u32[]{:S(2)}, u32[]{:S(2)}) collective-permute-start(bf16[576,2304]{1,0:T(8,128)(2,1)S(1)} %bitcast.968), channel_id=1, source_target_pairs={{0,1},{1,0},{2,3},{3,2},{4,5},{5,4},{6,7},{7,6},{8,9},{9,8},{10,11... | collective-permute-start | bytes 7962632 | tf_op jit(solution)/shard_map/ppermute | solution.py:29
  70.3 61.0 %collective-permute-start.11 = (bf16[576,2304]{1,0:T(8,128)(2,1)S(1)}, bf16[576,2304]{1,0:T(8,128)(2,1)}, u32[]{:S(2)}, u32[]{:S(2)}) collective-permute-start(bf16[576,2304]{1,0:T(8,128)(2,1)S(1)} %bitcast.969), channel_id=1, source_target_pairs={{0,16},{16,0},{1,17},{17,1},{2,18},{18,2},{3,19},{19,3},{4,20},{20... | collective-permute-start | bytes 7962632 | tf_op jit(solution)/shard_map/ppermute | solution.py:29
  141.1 545.7 %all-gather.6.cloned.1.call-start = ((), (), s32[]{:S(2)}) async-start(), calls=%async_computation.4 | async-start | bytes 10948608 | tf_op jit(solution)/shard_map/all_gather | solution.py:119
  167.2 110.0 %collective-permute-start.39 = (bf16[4,4,2,1,16,1152]{5,4,2,1,0,3:T(8,128)(2,1)}, bf16[4,4,2,1,16,1152]{5,4,2,1,0,3:T(8,128)(2,1)}, u32[]{:S(2)}, u32[]{:S(2)}) collective-permute-start(bf16[4,4,2,1,16,1152]{5,4,2,1,0,3:T(8,128)(2,1)} %get-tuple-element.155), channel_id=1, source_target_pairs={{0,2},{1,3},{2,0},{3,1},{4,6},{5,7},{6,4},{7,5},{8,10},{9,11},{10,... | collective-permute-start | bytes 3538952 | tf_op jit(solution)/shard_map/ppermute | solution.py:406
  183.1 104.9 %collective-permute-start = (bf16[4,1,128,1152]{3,2,0,1:T(8,128)(2,1)}, bf16[4,1,128,1152]{3,2,0,1:T(8,128)(2,1)S(1)}, u32[]{:S(2)}, u32[]{:S(2)}) collective-permute-start(bf16[4,1,128,1152]{3,2,0,1:T(8,128)(2,1)} %slice_bitcast_fusion.5), channel_id=1, source_target_pairs={{0,1},{1,0},{2,3},{3,2},{4,5},{5,4},{6,7},{7,6},{8,9},{9,8},{10,11... | collective-permute-start | bytes 3538952 | tf_op jit(solution)/shard_map/ppermute | solution.py:29
  184.7 25.9 %collective-permute-start.3 = (f32[4,2,3456]{2,0,1:T(4,128)S(1)}, f32[4,2,3456]{2,0,1:T(4,128)S(1)}, u32[]{:S(2)}, u32[]{:S(2)}) collective-permute-start(f32[4,2,3456]{2,0,1:T(4,128)S(1)} %fusion.217), channel_id=1, source_target_pairs={{0,2},{2,0},{4,6},{6,4},{8,10},{10,8},{12,14},{14,12},{1,3},{3,1},... | collective-permute-start | bytes 331784 | tf_op jit(solution)/shard_map/ppermute | solution.py:29
  245.9 27.8 %collective-permute-start.14 = (bf16[72,2304]{1,0:T(8,128)(2,1)S(1)}, bf16[72,2304]{1,0:T(8,128)(2,1)}, u32[]{:S(2)}, u32[]{:S(2)}) collective-permute-start(bf16[72,2304]{1,0:T(8,128)(2,1)S(1)} %copy-done.91), channel_id=1, source_target_pairs={{0,4},{2,6},{4,0},{6,2},{8,12},{10,14},{12,8},{14,10},{1,5},{3,7},... | collective-permute-start | bytes 995336 | tf_op jit(solution)/shard_map/ppermute | solution.py:29
  246.0 27.8 %collective-permute-start.15 = (bf16[72,2304]{1,0:T(8,128)(2,1)S(1)}, bf16[72,2304]{1,0:T(8,128)(2,1)}, u32[]{:S(2)}, u32[]{:S(2)}) collective-permute-start(bf16[72,2304]{1,0:T(8,128)(2,1)S(1)} %copy-done.91), channel_id=1, source_target_pairs={{0,8},{2,10},{4,12},{6,14},{8,0},{10,2},{12,4},{14,6},{1,9},{3,11}... | collective-permute-start | bytes 995336 | tf_op jit(solution)/shard_map/ppermute | solution.py:29
  250.6 456.8 %all-gather.8.cloned.1.call-start = ((), (), s32[]{:S(2)}) async-start(), calls=%async_computation.5 | async-start | bytes 10948608 | tf_op jit(solution)/shard_map/all_gather | solution.py:119
  280.2 317.1 %collective-permute-start.40 = (bf16[4,2,2,1,16,1152]{5,4,2,1,0,3:T(8,128)(2,1)}, bf16[4,2,2,1,16,1152]{5,4,2,1,0,3:T(8,128)(2,1)S(1)}, u32[]{:S(2)}, u32[]{:S(2)}) collective-permute-start(bf16[4,2,2,1,16,1152]{5,4,2,1,0,3:T(8,128)(2,1)} %pad_maximum_fusion.56), channel_id=1, source_target_pairs={{0,4},{2,6},{4,0},{6,2},{8,12},{10,14},{12,8},{14,10},{1,5},{3,7},... | collective-permute-start | bytes 1769480 | tf_op jit(solution)/shard_map/ppermute | solution.py:29
  287.6 312.0 %collective-permute-start.41 = (bf16[4,2,2,1,16,1152]{5,4,2,1,0,3:T(8,128)(2,1)}, bf16[4,2,2,1,16,1152]{5,4,2,1,0,3:T(8,128)(2,1)}, u32[]{:S(2)}, u32[]{:S(2)}) collective-permute-start(bf16[4,2,2,1,16,1152]{5,4,2,1,0,3:T(8,128)(2,1)} %pad_maximum_fusion.57), channel_id=1, source_target_pairs={{0,8},{2,10},{4,12},{6,14},{8,0},{10,2},{12,4},{14,6},{1,9},{3,11}... | collective-permute-start | bytes 1769480 | tf_op jit(solution)/shard_map/ppermute | solution.py:29
  292.4 51.1 %collective-permute-start.19 = (bf16[72,2304]{1,0:T(8,128)(2,1)S(1)}, bf16[72,2304]{1,0:T(8,128)(2,1)S(1)}, u32[]{:S(2)}, u32[]{:S(2)}) collective-permute-start(bf16[72,2304]{1,0:T(8,128)(2,1)S(1)} %copy-done.90), channel_id=1, source_target_pairs={{0,4},{2,6},{4,0},{6,2},{8,12},{10,14},{12,8},{14,10},{1,5},{3,7},... | collective-permute-start | bytes 995336 | tf_op jit(solution)/shard_map/ppermute | solution.py:29
  294.4 71.4 %collective-permute-start.20 = (bf16[72,2304]{1,0:T(8,128)(2,1)S(1)}, bf16[72,2304]{1,0:T(8,128)(2,1)S(1)}, u32[]{:S(2)}, u32[]{:S(2)}) collective-permute-start(bf16[72,2304]{1,0:T(8,128)(2,1)S(1)} %copy-done.90), channel_id=1, source_target_pairs={{0,8},{2,10},{4,12},{6,14},{8,0},{10,2},{12,4},{14,6},{1,9},{3,11}... | collective-permute-start | bytes 995336 | tf_op jit(solution)/shard_map/ppermute | solution.py:29
  294.9 70.9 %collective-permute-start.21 = (bf16[72,2304]{1,0:T(8,128)(2,1)S(1)}, bf16[72,2304]{1,0:T(8,128)(2,1)S(1)}, u32[]{:S(2)}, u32[]{:S(2)}) collective-permute-start(bf16[72,2304]{1,0:T(8,128)(2,1)S(1)} %copy-done.90), channel_id=1, source_target_pairs={{0,12},{2,14},{4,8},{6,10},{8,4},{10,6},{12,0},{14,2},{1,13},{3,15... | collective-permute-start | bytes 995336 | tf_op jit(solution)/shard_map/ppermute | solution.py:29
  343.5 56.5 %collective-permute-start.23 = (bf16[4,72,2304]{2,1,0:T(8,128)(2,1)S(1)}, bf16[4,72,2304]{2,1,0:T(8,128)(2,1)S(1)}, u32[]{:S(2)}, u32[]{:S(2)}) collective-permute-start(bf16[4,72,2304]{2,1,0:T(8,128)(2,1)S(1)} %fusion.155), channel_id=1, source_target_pairs={{0,1},{1,0},{2,3},{3,2},{4,5},{5,4},{6,7},{7,6},{8,9},{9,8},{10,11... | collective-permute-start | bytes 3981320 | tf_op jit(solution)/shard_map/ppermute | solution.py:29
  365.8 32.1 %collective-permute-start.17 = (bf16[4,72,2304]{2,1,0:T(8,128)(2,1)S(1)}, bf16[4,72,2304]{2,1,0:T(8,128)(2,1)S(1)}, u32[]{:S(2)}, u32[]{:S(2)}) collective-permute-start(bf16[4,72,2304]{2,1,0:T(8,128)(2,1)S(1)} %fusion.155), channel_id=1, source_target_pairs={{0,2},{2,0},{4,6},{6,4},{8,10},{10,8},{12,14},{14,12},{1,3},{3,1},... | collective-permute-start | bytes 3981320 | tf_op jit(solution)/shard_map/ppermute | solution.py:29
  367.0 55.7 %collective-permute-start.22 = (bf16[4,72,2304]{2,1,0:T(8,128)(2,1)S(1)}, bf16[4,72,2304]{2,1,0:T(8,128)(2,1)S(1)}, u32[]{:S(2)}, u32[]{:S(2)}) collective-permute-start(bf16[4,72,2304]{2,1,0:T(8,128)(2,1)S(1)} %fusion.154), channel_id=1, source_target_pairs={{0,2},{2,0},{4,6},{6,4},{8,10},{10,8},{12,14},{14,12},{1,3},{3,1},... | collective-permute-start | bytes 3981320 | tf_op jit(solution)/shard_map/ppermute | solution.py:29
  399.9 85.5 %collective-permute-start.18 = (bf16[576,2304]{1,0:T(8,128)(2,1)}, bf16[576,2304]{1,0:T(8,128)(2,1)}, u32[]{:S(2)}, u32[]{:S(2)}) collective-permute-start(bf16[576,2304]{1,0:T(8,128)(2,1)} %bitcast.84), channel_id=1, source_target_pairs={{0,16},{16,0},{1,17},{17,1},{2,18},{18,2},{3,19},{19,3},{4,20},{20... | collective-permute-start | bytes 7962632 | tf_op jit(solution)/shard_map/ppermute | solution.py:29
  399.9 41.4 %collective-permute-start.25 = (bf16[4,72,2304]{2,1,0:T(8,128)(2,1)S(1)}, bf16[4,72,2304]{2,1,0:T(8,128)(2,1)S(1)}, u32[]{:S(2)}, u32[]{:S(2)}) collective-permute-start(bf16[4,72,2304]{2,1,0:T(8,128)(2,1)S(1)} %collective-permute-done.23), channel_id=1, source_target_pairs={{0,2},{2,0},{4,6},{6,4},{8,10},{10,8},{12,14},{14,12},{1,3},{3,1},... | collective-permute-start | bytes 3981320 | tf_op jit(solution)/shard_map/ppermute | solution.py:29
  424.9 73.0 %collective-permute-start.27 = (bf16[576,2304]{1,0:T(8,128)(2,1)}, bf16[576,2304]{1,0:T(8,128)(2,1)}, u32[]{:S(2)}, u32[]{:S(2)}) collective-permute-start(bf16[576,2304]{1,0:T(8,128)(2,1)} %bitcast.99), channel_id=1, source_target_pairs={{0,1},{1,0},{2,3},{3,2},{4,5},{5,4},{6,7},{7,6},{8,9},{9,8},{10,11... | collective-permute-start | bytes 7962632 | tf_op jit(solution)/shard_map/ppermute | solution.py:29
  441.4 63.4 %collective-permute-start.24 = (bf16[576,2304]{1,0:T(8,128)(2,1)}, bf16[576,2304]{1,0:T(8,128)(2,1)}, u32[]{:S(2)}, u32[]{:S(2)}) collective-permute-start(bf16[576,2304]{1,0:T(8,128)(2,1)} %bitcast.99), channel_id=1, source_target_pairs={{0,16},{16,0},{1,17},{17,1},{2,18},{18,2},{3,19},{19,3},{4,20},{20... | collective-permute-start | bytes 7962632 | tf_op jit(solution)/shard_map/ppermute | solution.py:29
  481.9 885.3 %all-reduce.3.cloned.1.call-start = ((), (), s32[]{:S(2)}) async-start(), calls=%async_computation.9 | async-start | bytes 5308416
  485.4 29.2 %collective-permute-start.26 = (bf16[576,2304]{1,0:T(8,128)(2,1)S(1)}, bf16[576,2304]{1,0:T(8,128)(2,1)S(1)}, u32[]{:S(2)}, u32[]{:S(2)}) collective-permute-start(bf16[576,2304]{1,0:T(8,128)(2,1)S(1)} %bitcast.1029), channel_id=1, source_target_pairs={{0,16},{16,0},{1,17},{17,1},{2,18},{18,2},{3,19},{19,3},{4,20},{20... | collective-permute-start | bytes 7962632 | tf_op jit(solution)/shard_map/ppermute | solution.py:29
  497.9 101.7 %collective-permute-start.42 = (bf16[4,2,2,1,16,1152]{5,4,2,1,0,3:T(8,128)(2,1)}, bf16[4,2,2,1,16,1152]{5,4,2,1,0,3:T(8,128)(2,1)}, u32[]{:S(2)}, u32[]{:S(2)}) collective-permute-start(bf16[4,2,2,1,16,1152]{5,4,2,1,0,3:T(8,128)(2,1)} %pad_maximum_fusion.58), channel_id=1, source_target_pairs={{0,12},{2,14},{4,8},{6,10},{8,4},{10,6},{12,0},{14,2},{1,13},{3,15... | collective-permute-start | bytes 1769480 | tf_op jit(solution)/shard_map/ppermute | solution.py:29
  545.5 27.4 %collective-permute-start.29 = (bf16[4,4,1,16,1152]{4,3,1,0,2:T(8,128)(2,1)S(1)}, bf16[4,4,1,16,1152]{4,3,1,0,2:T(8,128)(2,1)S(1)}, u32[]{:S(2)}, u32[]{:S(2)}) collective-permute-start(bf16[4,4,1,16,1152]{4,3,1,0,2:T(8,128)(2,1)S(1)} %get-tuple-element.181), channel_id=1, source_target_pairs={{0,1},{1,0},{2,3},{3,2},{4,5},{5,4},{6,7},{7,6},{8,9},{9,8},{10,11... | collective-permute-start | bytes 1769480 | tf_op jit(solution)/shard_map/ppermute | solution.py:406
  547.1 28.2 %collective-permute-start.30 = (bf16[4,4,1,16,1152]{4,3,1,0,2:T(8,128)(2,1)S(1)}, bf16[4,4,1,16,1152]{4,3,1,0,2:T(8,128)(2,1)S(1)}, u32[]{:S(2)}, u32[]{:S(2)}) collective-permute-start(bf16[4,4,1,16,1152]{4,3,1,0,2:T(8,128)(2,1)S(1)} %get-tuple-element.180), channel_id=1, source_target_pairs={{0,2},{1,3},{2,0},{3,1},{4,6},{5,7},{6,4},{7,5},{8,10},{9,11},{10,... | collective-permute-start | bytes 1769480 | tf_op jit(solution)/shard_map/ppermute | solution.py:406
  594.8 29.6 %collective-permute-start.32 = (bf16[4,4,1,16,1152]{4,3,1,0,2:T(8,128)(2,1)S(1)}, bf16[4,4,1,16,1152]{4,3,1,0,2:T(8,128)(2,1)S(1)}, u32[]{:S(2)}, u32[]{:S(2)}) collective-permute-start(bf16[4,4,1,16,1152]{4,3,1,0,2:T(8,128)(2,1)S(1)} %pad_maximum_fusion.50), channel_id=1, source_target_pairs={{0,4},{2,6},{4,0},{6,2},{8,12},{10,14},{12,8},{14,10},{1,5},{3,7},... | collective-permute-start | bytes 1769480 | tf_op jit(solution)/shard_map/ppermute | solution.py:29
  595.0 29.5 %collective-permute-start.33 = (bf16[4,4,1,16,1152]{4,3,1,0,2:T(8,128)(2,1)S(1)}, bf16[4,4,1,16,1152]{4,3,1,0,2:T(8,128)(2,1)S(1)}, u32[]{:S(2)}, u32[]{:S(2)}) collective-permute-start(bf16[4,4,1,16,1152]{4,3,1,0,2:T(8,128)(2,1)S(1)} %pad_maximum_fusion.51), channel_id=1, source_target_pairs={{0,8},{2,10},{4,12},{6,14},{8,0},{10,2},{12,4},{14,6},{1,9},{3,11}... | collective-permute-start | bytes 1769480 | tf_op jit(solution)/shard_map/ppermute | solution.py:29
  597.3 41.7 %collective-permute-start.34 = (bf16[4,4,1,16,1152]{4,3,1,0,2:T(8,128)(2,1)S(1)}, bf16[4,4,1,16,1152]{4,3,1,0,2:T(8,128)(2,1)S(1)}, u32[]{:S(2)}, u32[]{:S(2)}) collective-permute-start(bf16[4,4,1,16,1152]{4,3,1,0,2:T(8,128)(2,1)S(1)} %pad_maximum_fusion.52), channel_id=1, source_target_pairs={{0,12},{2,14},{4,8},{6,10},{8,4},{10,6},{12,0},{14,2},{1,13},{3,15... | collective-permute-start | bytes 1769480 | tf_op jit(solution)/shard_map/ppermute | solution.py:29
  779.8 906.2 %reduce-scatter.11.cloned.1.call-start = ((), (), s32[]{:S(2)}) async-start(), calls=%async_computation.8 | async-start | bytes 8515584 | tf_op jit(solution)/shard_map/reduce_scatter | solution.py:125
  847.8 840.8 %reduce-scatter.9.cloned.1.call-start = ((), (), s32[]{:S(2)}) async-start(), calls=%async_computation.7 | async-start | bytes 10948608 | tf_op jit(solution)/shard_map/reduce_scatter | solution.py:125
  886.2 804.7 %reduce-scatter.7.cloned.1.call-start = ((), (), s32[]{:S(2)}) async-start(), calls=%async_computation.6 | async-start | bytes 10948608 | tf_op jit(solution)/shard_map/reduce_scatter | solution.py:125
  972.2 33.0 %collective-permute-start.43 = (bf16[4,4,1,16,1152]{4,3,0,1,2:T(8,128)(2,1)}, bf16[4,4,1,16,1152]{4,3,0,1,2:T(8,128)(2,1)}, u32[]{:S(2)}, u32[]{:S(2)}) collective-permute-start(bf16[4,4,1,16,1152]{4,3,0,1,2:T(8,128)(2,1)} %get-tuple-element.151), channel_id=1, source_target_pairs={{0,1},{1,0},{2,3},{3,2},{4,5},{5,4},{6,7},{7,6},{8,9},{9,8},{10,11... | collective-permute-start | bytes 1769480 | tf_op jit(solution)/shard_map/ppermute | solution.py:406
  974.5 31.9 %collective-permute-start.44 = (bf16[4,4,1,16,1152]{4,3,0,1,2:T(8,128)(2,1)}, bf16[4,4,1,16,1152]{4,3,0,1,2:T(8,128)(2,1)}, u32[]{:S(2)}, u32[]{:S(2)}) collective-permute-start(bf16[4,4,1,16,1152]{4,3,0,1,2:T(8,128)(2,1)} %get-tuple-element.153), channel_id=1, source_target_pairs={{0,2},{1,3},{2,0},{3,1},{4,6},{5,7},{6,4},{7,5},{8,10},{9,11},{10,... | collective-permute-start | bytes 1769480 | tf_op jit(solution)/shard_map/ppermute | solution.py:406
  974.9 35.6 %collective-permute-start.45 = (bf16[4,4,1,16,1152]{4,3,0,1,2:T(8,128)(2,1)}, bf16[4,4,1,16,1152]{4,3,0,1,2:T(8,128)(2,1)}, u32[]{:S(2)}, u32[]{:S(2)}) collective-permute-start(bf16[4,4,1,16,1152]{4,3,0,1,2:T(8,128)(2,1)} %get-tuple-element.152), channel_id=1, source_target_pairs={{0,3},{1,2},{2,1},{3,0},{4,7},{5,6},{6,5},{7,4},{8,11},{9,10},{10,... | collective-permute-start | bytes 1769480 | tf_op jit(solution)/shard_map/ppermute | solution.py:406
  978.5 318.7 %collective-permute-start.35 = (bf16[4,4,2,1,16,1152]{5,4,2,0,1,3:T(8,128)(2,1)}, bf16[4,4,2,1,16,1152]{5,4,2,0,1,3:T(8,128)(2,1)}, u32[]{:S(2)}, u32[]{:S(2)}) collective-permute-start(bf16[4,4,2,1,16,1152]{5,4,2,0,1,3:T(8,128)(2,1)} %get-tuple-element.177), channel_id=1, source_target_pairs={{0,2},{1,3},{2,0},{3,1},{4,6},{5,7},{6,4},{7,5},{8,10},{9,11},{10,... | collective-permute-start | bytes 3538952 | tf_op jit(solution)/shard_map/ppermute | solution.py:406
  1011.8 52.5 %collective-permute-start.46 = (bf16[4,4,1,16,1152]{4,3,0,1,2:T(8,128)(2,1)S(1)}, bf16[4,4,1,16,1152]{4,3,0,1,2:T(8,128)(2,1)S(1)}, u32[]{:S(2)}, u32[]{:S(2)}) collective-permute-start(bf16[4,4,1,16,1152]{4,3,0,1,2:T(8,128)(2,1)S(1)} %pad_maximum_fusion.59), channel_id=1, source_target_pairs={{0,4},{2,6},{4,0},{6,2},{8,12},{10,14},{12,8},{14,10},{1,5},{3,7},... | collective-permute-start | bytes 1769480 | tf_op jit(solution)/shard_map/ppermute | solution.py:29
  1030.1 53.6 %collective-permute-start.47 = (bf16[4,4,1,16,1152]{4,3,0,1,2:T(8,128)(2,1)S(1)}, bf16[4,4,1,16,1152]{4,3,0,1,2:T(8,128)(2,1)S(1)}, u32[]{:S(2)}, u32[]{:S(2)}) collective-permute-start(bf16[4,4,1,16,1152]{4,3,0,1,2:T(8,128)(2,1)S(1)} %pad_maximum_fusion.60), channel_id=1, source_target_pairs={{0,8},{2,10},{4,12},{6,14},{8,0},{10,2},{12,4},{14,6},{1,9},{3,11}... | collective-permute-start | bytes 1769480 | tf_op jit(solution)/shard_map/ppermute | solution.py:29
  1030.7 53.0 %collective-permute-start.48 = (bf16[4,4,1,16,1152]{4,3,0,1,2:T(8,128)(2,1)S(1)}, bf16[4,4,1,16,1152]{4,3,0,1,2:T(8,128)(2,1)S(1)}, u32[]{:S(2)}, u32[]{:S(2)}) collective-permute-start(bf16[4,4,1,16,1152]{4,3,0,1,2:T(8,128)(2,1)S(1)} %pad_maximum_fusion.61), channel_id=1, source_target_pairs={{0,12},{2,14},{4,8},{6,10},{8,4},{10,6},{12,0},{14,2},{1,13},{3,15... | collective-permute-start | bytes 1769480 | tf_op jit(solution)/shard_map/ppermute | solution.py:29
  1257.6 44.8 %collective-permute-start.50 = (f32[4,3456]{1,0:T(4,128)S(1)}, f32[4,3456]{1,0:T(4,128)S(1)}, u32[]{:S(2)}, u32[]{:S(2)}) collective-permute-start(f32[4,3456]{1,0:T(4,128)S(1)} %bitcast.1120), channel_id=1, source_target_pairs={{0,1},{1,0},{2,3},{3,2},{4,5},{5,4},{6,7},{7,6},{8,9},{9,8},{10,11... | collective-permute-start | bytes 165896 | tf_op jit(solution)/shard_map/ppermute | solution.py:29
  1258.8 42.2 %collective-permute-start.55 = (f32[4,3456]{1,0:T(4,128)S(1)}, f32[4,3456]{1,0:T(4,128)S(1)}, u32[]{:S(2)}, u32[]{:S(2)}) collective-permute-start(f32[4,3456]{1,0:T(4,128)S(1)} %bitcast.1121), channel_id=1, source_target_pairs={{0,1},{1,0},{2,3},{3,2},{4,5},{5,4},{6,7},{7,6},{8,9},{9,8},{10,11... | collective-permute-start | bytes 165896 | tf_op jit(solution)/shard_map/ppermute | solution.py:29
  1259.9 252.9 %collective-permute-start.89 = (bf16[576,2304]{1,0:T(8,128)(2,1)}, bf16[576,2304]{1,0:T(8,128)(2,1)}, u32[]{:S(2)}, u32[]{:S(2)}) collective-permute-start(bf16[576,2304]{1,0:T(8,128)(2,1)} %convolution_convert_fusion.6), channel_id=1, source_target_pairs={{0,16},{16,0},{1,17},{17,1},{2,18},{18,2},{3,19},{19,3},{4,20},{20... | collective-permute-start | bytes 7962632 | tf_op jit(solution)/shard_map/ppermute | solution.py:29
  1259.9 175.4 %collective-permute-start.74 = (bf16[576,576]{1,0:T(8,128)(2,1)}, bf16[576,576]{1,0:T(8,128)(2,1)}, u32[]{:S(2)}, u32[]{:S(2)}) collective-permute-start(bf16[576,576]{1,0:T(8,128)(2,1)} %convolution_convert_fusion.22), channel_id=1, source_target_pairs={{0,16},{16,0},{1,17},{17,1},{2,18},{18,2},{3,19},{19,3},{4,20},{20... | collective-permute-start | bytes 1990664 | tf_op jit(solution)/shard_map/ppermute | solution.py:29
  1322.2 85.2 %collective-permute-start.36 = (bf16[4,2,2,1,16,1152]{5,4,2,0,1,3:T(8,128)(2,1)S(1)}, bf16[4,2,2,1,16,1152]{5,4,2,0,1,3:T(8,128)(2,1)S(1)}, u32[]{:S(2)}, u32[]{:S(2)}) collective-permute-start(bf16[4,2,2,1,16,1152]{5,4,2,0,1,3:T(8,128)(2,1)S(1)} %pad_maximum_fusion.53), channel_id=1, source_target_pairs={{0,4},{2,6},{4,0},{6,2},{8,12},{10,14},{12,8},{14,10},{1,5},{3,7},... | collective-permute-start | bytes 1769480 | tf_op jit(solution)/shard_map/ppermute | solution.py:29
  1322.3 33.6 %collective-permute-start.52 = (f32[4,3456]{1,0:T(4,128)S(1)}, f32[4,3456]{1,0:T(4,128)S(1)}, u32[]{:S(2)}, u32[]{:S(2)}) collective-permute-start(f32[4,3456]{1,0:T(4,128)S(1)} %add.596), channel_id=1, source_target_pairs={{0,4},{2,6},{4,0},{6,2},{8,12},{10,14},{12,8},{14,10},{1,5},{3,7},... | collective-permute-start | bytes 165896 | tf_op jit(solution)/shard_map/ppermute | solution.py:29
  1361.4 46.8 %collective-permute-start.37 = (bf16[4,2,2,1,16,1152]{5,4,2,0,1,3:T(8,128)(2,1)S(1)}, bf16[4,2,2,1,16,1152]{5,4,2,0,1,3:T(8,128)(2,1)}, u32[]{:S(2)}, u32[]{:S(2)}) collective-permute-start(bf16[4,2,2,1,16,1152]{5,4,2,0,1,3:T(8,128)(2,1)S(1)} %pad_maximum_fusion.54), channel_id=1, source_target_pairs={{0,8},{2,10},{4,12},{6,14},{8,0},{10,2},{12,4},{14,6},{1,9},{3,11}... | collective-permute-start | bytes 1769480 | tf_op jit(solution)/shard_map/ppermute | solution.py:29
  1376.8 26.9 %collective-permute-start.64 = (f32[4,2,4,72]{3,0,1,2:T(4,128)S(1)}, f32[4,2,4,72]{3,0,1,2:T(4,128)S(1)}, u32[]{:S(2)}, u32[]{:S(2)}) collective-permute-start(f32[4,2,4,72]{3,0,1,2:T(4,128)S(1)} %pad_maximum_fusion.74), channel_id=1, source_target_pairs={{0,8},{2,10},{4,12},{6,14},{8,0},{10,2},{12,4},{14,6},{1,9},{3,11}... | collective-permute-start | bytes 27656 | tf_op jit(solution)/shard_map/ppermute | solution.py:29
  1407.3 50.8 %collective-permute-start.73 = (bf16[576,576]{1,0:T(8,128)(2,1)}, bf16[576,576]{1,0:T(8,128)(2,1)}, u32[]{:S(2)}, u32[]{:S(2)}) collective-permute-start(bf16[576,576]{1,0:T(8,128)(2,1)} %convolution_convert_fusion.23), channel_id=1, source_target_pairs={{0,16},{16,0},{1,17},{17,1},{2,18},{18,2},{3,19},{19,3},{4,20},{20... | collective-permute-start | bytes 1990664 | tf_op jit(solution)/shard_map/ppermute | solution.py:29
  1408.2 95.7 %collective-permute-start.65 = (bf16[576,1728]{1,0:T(8,128)(2,1)}, bf16[576,1728]{1,0:T(8,128)(2,1)S(1)}, u32[]{:S(2)}, u32[]{:S(2)}) collective-permute-start(bf16[576,1728]{1,0:T(8,128)(2,1)} %convolution_convert_fusion.17), channel_id=1, source_target_pairs={{0,16},{16,0},{1,17},{17,1},{2,18},{18,2},{3,19},{19,3},{4,20},{20... | collective-permute-start | bytes 5971976 | tf_op jit(solution)/shard_map/ppermute | solution.py:29
  1424.6 27.6 %collective-permute-start.49 = (bf16[4,1,128,1152]{3,2,0,1:T(8,128)(2,1)}, bf16[4,1,128,1152]{3,2,0,1:T(8,128)(2,1)S(1)}, u32[]{:S(2)}, u32[]{:S(2)}) collective-permute-start(bf16[4,1,128,1152]{3,2,0,1:T(8,128)(2,1)} %get-tuple-element.145), channel_id=1, source_target_pairs={{0,1},{1,0},{2,3},{3,2},{4,5},{5,4},{6,7},{7,6},{8,9},{9,8},{10,11... | collective-permute-start | bytes 3538952 | tf_op jit(solution)/shard_map/ppermute | solution.py:29
  1436.1 71.7 %collective-permute-start.67 = (bf16[576,1728]{1,0:T(8,128)(2,1)S(1)}, bf16[576,1728]{1,0:T(8,128)(2,1)S(1)}, u32[]{:S(2)}, u32[]{:S(2)}) collective-permute-start(bf16[576,1728]{1,0:T(8,128)(2,1)S(1)} %copy-done.191), channel_id=1, source_target_pairs={{0,16},{16,0},{1,17},{17,1},{2,18},{18,2},{3,19},{19,3},{4,20},{20... | collective-permute-start | bytes 5971976 | tf_op jit(solution)/shard_map/ppermute | solution.py:29
  1502.5 101.3 %collective-permute-start.88 = (bf16[576,2304]{1,0:T(8,128)(2,1)}, bf16[576,2304]{1,0:T(8,128)(2,1)}, u32[]{:S(2)}, u32[]{:S(2)}) collective-permute-start(bf16[576,2304]{1,0:T(8,128)(2,1)} %convolution_convert_fusion.7), channel_id=1, source_target_pairs={{0,16},{16,0},{1,17},{17,1},{2,18},{18,2},{3,19},{19,3},{4,20},{20... | collective-permute-start | bytes 7962632 | tf_op jit(solution)/shard_map/ppermute | solution.py:29
  1507.9 78.3 %collective-permute-start.66 = (bf16[4,72,1728]{2,1,0:T(8,128)(2,1)}, bf16[4,72,1728]{2,1,0:T(8,128)(2,1)}, u32[]{:S(2)}, u32[]{:S(2)}) collective-permute-start(bf16[4,72,1728]{2,1,0:T(8,128)(2,1)} %dynamic-slice_bitcast_fusion.4), channel_id=1, source_target_pairs={{0,2},{2,0},{4,6},{6,4},{8,10},{10,8},{12,14},{14,12},{1,3},{3,1},... | collective-permute-start | bytes 2985992 | tf_op jit(solution)/shard_map/ppermute | solution.py:29
  1512.8 43.2 %collective-permute-start.68 = (bf16[4,72,1728]{2,1,0:T(8,128)(2,1)}, bf16[4,72,1728]{2,1,0:T(8,128)(2,1)}, u32[]{:S(2)}, u32[]{:S(2)}) collective-permute-start(bf16[4,72,1728]{2,1,0:T(8,128)(2,1)} %dynamic-slice_bitcast_fusion.3), channel_id=1, source_target_pairs={{0,2},{2,0},{4,6},{6,4},{8,10},{10,8},{12,14},{14,12},{1,3},{3,1},... | collective-permute-start | bytes 2985992 | tf_op jit(solution)/shard_map/ppermute | solution.py:29
  1519.2 86.5 %collective-permute-start.90 = (bf16[576,2304]{1,0:T(8,128)(2,1)S(1)}, bf16[576,2304]{1,0:T(8,128)(2,1)}, u32[]{:S(2)}, u32[]{:S(2)}) collective-permute-start(bf16[576,2304]{1,0:T(8,128)(2,1)S(1)} %add_convert_fusion.1), channel_id=1, source_target_pairs={{0,1},{1,0},{2,3},{3,2},{4,5},{5,4},{6,7},{7,6},{8,9},{9,8},{10,11... | collective-permute-start | bytes 7962632 | tf_op jit(solution)/shard_map/ppermute | solution.py:29
  1524.0 59.3 %collective-permute-start.83 = (bf16[4,72,2304]{2,1,0:T(8,128)(2,1)S(1)}, bf16[4,72,2304]{2,1,0:T(8,128)(2,1)S(1)}, u32[]{:S(2)}, u32[]{:S(2)}) collective-permute-start(bf16[4,72,2304]{2,1,0:T(8,128)(2,1)S(1)} %dynamic-slice_bitcast_fusion.1), channel_id=1, source_target_pairs={{0,2},{2,0},{4,6},{6,4},{8,10},{10,8},{12,14},{14,12},{1,3},{3,1},... | collective-permute-start | bytes 3981320 | tf_op jit(solution)/shard_map/ppermute | solution.py:29
  1557.5 44.4 %collective-permute-start.69 = (bf16[4,72,1728]{2,1,0:T(8,128)(2,1)S(1)}, bf16[4,72,1728]{2,1,0:T(8,128)(2,1)S(1)}, u32[]{:S(2)}, u32[]{:S(2)}) collective-permute-start(bf16[4,72,1728]{2,1,0:T(8,128)(2,1)S(1)} %fusion.150), channel_id=1, source_target_pairs={{0,1},{1,0},{2,3},{3,2},{4,5},{5,4},{6,7},{7,6},{8,9},{9,8},{10,11... | collective-permute-start | bytes 2985992 | tf_op jit(solution)/shard_map/ppermute | solution.py:29
  1583.3 41.9 %collective-permute-start.81 = (bf16[4,72,2304]{2,1,0:T(8,128)(2,1)}, bf16[4,72,2304]{2,1,0:T(8,128)(2,1)}, u32[]{:S(2)}, u32[]{:S(2)}) collective-permute-start(bf16[4,72,2304]{2,1,0:T(8,128)(2,1)} %dynamic-slice_bitcast_fusion.2), channel_id=1, source_target_pairs={{0,2},{2,0},{4,6},{6,4},{8,10},{10,8},{12,14},{14,12},{1,3},{3,1},... | collective-permute-start | bytes 3981320 | tf_op jit(solution)/shard_map/ppermute | solution.py:29
  1586.1 42.5 %collective-permute-start.84 = (bf16[4,72,2304]{2,1,0:T(8,128)(2,1)}, bf16[4,72,2304]{2,1,0:T(8,128)(2,1)}, u32[]{:S(2)}, u32[]{:S(2)}) collective-permute-start(bf16[4,72,2304]{2,1,0:T(8,128)(2,1)} %fusion.132), channel_id=1, source_target_pairs={{0,1},{1,0},{2,3},{3,2},{4,5},{5,4},{6,7},{7,6},{8,9},{9,8},{10,11... | collective-permute-start | bytes 3981320 | tf_op jit(solution)/shard_map/ppermute | solution.py:29
  1614.8 27.2 %collective-permute-start.91 = (bf16[4,72,2304]{2,1,0:T(8,128)(2,1)}, bf16[4,72,2304]{2,1,0:T(8,128)(2,1)}, u32[]{:S(2)}, u32[]{:S(2)}) collective-permute-start(bf16[4,72,2304]{2,1,0:T(8,128)(2,1)} %dynamic-slice_bitcast_fusion), channel_id=1, source_target_pairs={{0,2},{2,0},{4,6},{6,4},{8,10},{10,8},{12,14},{14,12},{1,3},{3,1},... | collective-permute-start | bytes 3981320 | tf_op jit(solution)/shard_map/ppermute | solution.py:29
  1644.1 41.7 %collective-permute-start.93 = (bf16[72,2304]{1,0:T(8,128)(2,1)S(1)}, bf16[72,2304]{1,0:T(8,128)(2,1)S(1)}, u32[]{:S(2)}, u32[]{:S(2)}) collective-permute-start(bf16[72,2304]{1,0:T(8,128)(2,1)S(1)} %get-tuple-element.198), channel_id=1, source_target_pairs={{0,8},{2,10},{4,12},{6,14},{8,0},{10,2},{12,4},{14,6},{1,9},{3,11}... | collective-permute-start | bytes 995336 | tf_op jit(solution)/shard_map/ppermute | solution.py:29
  1647.3 38.5 %collective-permute-start.94 = (bf16[72,2304]{1,0:T(8,128)(2,1)S(1)}, bf16[72,2304]{1,0:T(8,128)(2,1)S(1)}, u32[]{:S(2)}, u32[]{:S(2)}) collective-permute-start(bf16[72,2304]{1,0:T(8,128)(2,1)S(1)} %get-tuple-element.197), channel_id=1, source_target_pairs={{0,12},{2,14},{4,8},{6,10},{8,4},{10,6},{12,0},{14,2},{1,13},{3,15... | collective-permute-start | bytes 995336 | tf_op jit(solution)/shard_map/ppermute | solution.py:29
  (292 other events, 5513.6 us)
Sparse Core Ops, SparseCore 0:
  141.2 120.8 all-gather.3
  265.1 122.7 all-gather.5
  482.0 123.0 all-gather.7
  779.9 145.4 all-reduce.2
  932.1 169.8 reduce-scatter.10
  1108.0 141.0 reduce-scatter.8
  1255.2 178.3 reduce-scatter.6

commit v2 on v1

v2 whole, which is shorter than its diff:
```python
import functools

import jax
import jax.numpy as jnp
from jax import lax
from jax.experimental import pallas as pl
from jax.experimental.pallas import tpu as pltpu
from jax.sharding import PartitionSpec as P

HEAD_DIM = 72
LAYERS = 2
LANES = 128
EPS = 1e-06
SCALE = HEAD_DIM ** (-0.5)
HIGHEST = lax.Precision.HIGHEST
BF16 = jnp.bfloat16
F32 = jnp.float32

NN = (((1,), (0,)), ((), ()))
NT = (((1,), (1,)), ((), ()))
TN = (((0,), (0,)), ((), ()))


def dot(a, b, dims=NN):
    return lax.dot_general(a, b, dims, preferred_element_type=F32)


def swap_with(v, axis_name, n, k):
    return lax.ppermute(v, axis_name, [(i, i ^ k) for i in range(n)])


def flip_to(v, axis, n, me):
    shape = v.shape
    bit = 1
    while bit < n:
        split = shape[:axis] + (n // (2 * bit), 2, bit) + shape[axis + 1 :]
        parts = v.reshape(split)
        first = lax.slice_in_dim(parts, 0, 1, axis=axis + 1)
        second = lax.slice_in_dim(parts, 1, 2, axis=axis + 1)
        turned = jnp.concatenate([second, first], axis=axis + 1)
        v = jnp.where((me & bit) != 0, turned, parts).reshape(shape)
        bit *= 2
    return v


class Moves:
    def __init__(self, mesh):
        self.n_dp = mesh.shape["dp"]
        self.n_ctx = mesh.shape["ctx"]
        self.n_tp = mesh.shape["tp"]
        self.n_line = self.n_ctx // 2

    def here(self):
        self.dp = lax.axis_index("dp")
        self.ctx = lax.axis_index("ctx")
        self.tp = lax.axis_index("tp")
        self.line = self.ctx // 2
        self.side = self.ctx % 2

    def halves(self, v):
        half = v.shape[-1] // 2
        turned = jnp.concatenate([v[..., half:], v[..., :half]], axis=-1)
        return jnp.where(self.dp == 0, v, turned)

    def pair_stack(self, v, other):
        first = jnp.where(self.side == 0, v, other)
        second = jnp.where(self.side == 0, other, v)
        both = jnp.stack([first, second], axis=-3)
        return both.reshape(v.shape[:-3] + (-1, v.shape[-1]))

    def of_side(self, v, side):
        parts = v.reshape(self.n_line, 2, -1, v.shape[-1])
        return lax.dynamic_index_in_dim(parts, side, 1, keepdims=False)

    def over_tp(self, v, r):
        return swap_with(v, "tp", self.n_tp, r)

    def over_side(self, v):
        return swap_with(v, "ctx", self.n_ctx, 1)

    def over_core(self, v):
        return swap_with(v, "dp", self.n_dp, 1)

    def gather_weight(self, v):
        others = range(1, self.n_tp)
        got = [swap_with(v, "ctx", self.n_ctx, 2 * k) for k in range(1, self.n_line)]
        got = yield got
        half = v.shape[1] // 2
        lines = [
            flip_to(jnp.stack([b[:, cut] for b in [v] + got]), 0, self.n_line, self.line)
            for cut in (slice(0, half), slice(half, None))
        ]
        got = self.over_side(lines[0]), [self.over_tp(lines[1], r) for r in others]
        side_got, tp_got = yield got
        block = self.pair_stack(lines[0], side_got)
        strips = jnp.stack([lines[1]] + tp_got)
        got = [self.over_tp(block, r) for r in others], self.over_side(strips)
        tp_got, side_got = yield got
        first = [block] + tp_got
        second = self.pair_stack(strips, side_got)
        mine = jnp.concatenate(
            [part for r in range(self.n_tp) for part in (first[r], second[r])], axis=1
        )
        return mine, self.over_core(mine)

    def scatter_weight(self, left, rights):
        others = range(1, self.n_tp)
        half_width = left.shape[1] // 2
        mine, theirs = left[:, :half_width], left[:, half_width:]
        got = [self.over_core(dot(theirs, v, TN).astype(BF16)) for v in rights]
        got = yield got
        totals = [(dot(mine, v, TN) + g.astype(F32)).astype(BF16) for v, g in zip(rights, got)]
        if len(totals) == 1:
            totals = jnp.split(totals[0], self.n_tp, axis=1)
        columns = totals[0].shape[1]
        half = max(columns // 2 // LANES, 1) * LANES
        firsts = [v[:, :half] for v in totals]
        seconds = jnp.concatenate([v[:, half:] for v in totals], axis=1)
        got = (
            [self.over_tp(firsts[r], r) for r in others],
            self.over_side(self.of_side(seconds, 1 - self.side)),
        )
        tp_got, side_got = yield got
        first = (firsts[0].astype(F32) + sum(v.astype(F32) for v in tp_got)).astype(BF16)
        second = self.of_side(seconds, self.side).astype(F32) + side_got.astype(F32)
        second = jnp.split(second.astype(BF16), self.n_tp, axis=-1)
        got = (
            self.over_side(self.of_side(first, 1 - self.side)),
            [self.over_tp(second[r], r) for r in others],
        )
        side_got, tp_got = yield got
        first = self.of_side(first, self.side).astype(F32) + side_got.astype(F32)
        second = second[0].astype(F32) + sum(v.astype(F32) for v in tp_got)
        line = jnp.concatenate([first, second], axis=-1).astype(BF16)
        got = yield [
            swap_with(
                lax.dynamic_index_in_dim(line, self.line ^ k, 0, keepdims=False),
                "ctx",
                self.n_ctx,
                2 * k,
            )
            for k in range(1, self.n_line)
        ]
        own = lax.dynamic_index_in_dim(line, self.line, 0, keepdims=False)
        return own.astype(F32) + sum(v.astype(F32) for v in got)


class Task:
    def __init__(self, steps):
        self.steps, self.result = steps, None
        self.pending = next(steps)


class Lanes:
    def __init__(self):
        self.tasks = []

    def start(self, steps):
        task = Task(steps)
        self.tasks.append(task)
        return task

    def fence(self, values=()):
        values, pending = lax.optimization_barrier((values, [t.pending for t in self.tasks]))
        going = []
        for task, done in zip(self.tasks, pending):
            try:
                task.pending = task.steps.send(done)
                going.append(task)
            except StopIteration as stop:
                task.result = stop.value
        self.tasks = going
        return values


def window(head):
    start = head * HEAD_DIM
    return start // LANES * LANES, -(-(start + HEAD_DIM) // LANES) * LANES


def in_head(head, rows, low, high):
    lanes = lax.broadcasted_iota(jnp.int32, (rows, high - low), 1) + low
    return (lanes >= head * HEAD_DIM) & (lanes < (head + 1) * HEAD_DIM)


def spread_parts(x_ref, offset, parts, width):
    for index, part in enumerate(parts):
        padded = part.shape[1]
        start = offset + index * width
        if padded != width:
            part[:, padded - LANES :] = jnp.zeros((part.shape[0], LANES), part.dtype)
        part[:, :width] = x_ref[:, start : start + width]


def same_sequence(rows, stride):
    row = lax.broadcasted_iota(jnp.int32, (rows, rows), 0)
    column = lax.broadcasted_iota(jnp.int32, (rows, rows), 1)
    return lax.rem(row, stride) == lax.rem(column, stride)


def attend_kernel(count, width, stride, *refs):
    x_refs, (o_ref, lse_ref, q_s, k_s, v_s, o_s) = refs[:count], refs[count:]
    heads, rows = width // HEAD_DIM, o_ref.shape[0]
    lane = lax.broadcasted_iota(jnp.int32, (rows, LANES), 1)
    logs = jnp.zeros((rows, LANES), F32)
    if stride > 1:
        allowed = same_sequence(rows, stride)
    for index, x_ref in enumerate(x_refs):
        spread_parts(x_ref, 0, (q_s, k_s, v_s), width)
        for head in range(heads):
            low, high = window(head)
            mask = in_head(head, rows, low, high)
            queries = jnp.where(mask, q_s[:, low:high], jnp.zeros((), BF16))
            scores = dot(queries, k_s[:, low:high], NT) * SCALE
            if stride > 1:
                scores = jnp.where(allowed, scores, -jnp.inf)
            largest = jnp.max(scores, axis=-1, keepdims=True)
            raised = jnp.exp(scores - largest)
            total = jnp.sum(raised, axis=-1, keepdims=True)
            chances = (raised * (1.0 / total)).astype(BF16)
            result = dot(chances, v_s[:, low:high])
            o_s[:, low:high] = jnp.where(mask, result, o_s[:, low:high])
            logs = jnp.where(lane == index * heads + head, largest + jnp.log(total), logs)
        o_ref[:, index * width : (index + 1) * width] = o_s[:, :width].astype(BF16)
    lse_ref[...] = logs


def attend_back_kernel(count, width, stride, *refs):
    x_refs, (g_ref, lse_ref), dx_refs = refs[:count], refs[count : count + 2], refs[count + 2 : -7]
    q_s, k_s, v_s, g_s, dq_s, dk_s, dv_s = refs[-7:]
    heads, rows = width // HEAD_DIM, g_ref.shape[0]
    if stride > 1:
        allowed = same_sequence(rows, stride)
    for index, x_ref in enumerate(x_refs):
        spread_parts(x_ref, 0, (q_s, k_s, v_s), width)
        spread_parts(g_ref, index * width, (g_s,), width)
        for head in range(heads):
            low, high = window(head)
            mask = in_head(head, rows, low, high)
            zero = jnp.zeros((), BF16)
            q, k, v, g = q_s[:, low:high], k_s[:, low:high], v_s[:, low:high], g_s[:, low:high]
            scores = dot(jnp.where(mask, q, zero), k, NT) * SCALE
            if stride > 1:
                scores = jnp.where(allowed, scores, -jnp.inf)
            place = index * heads + head
            chances = jnp.exp(scores - lse_ref[:, place : place + 1])
            grad_chances = dot(jnp.where(mask, g, zero), v, NT)
            row_dot = jnp.sum(chances * grad_chances, axis=-1, keepdims=True)
            grad_scores = (chances * (grad_chances - row_dot)).astype(BF16)
            dq = dot(grad_scores, k) * SCALE
            dk = dot(grad_scores, q, TN) * SCALE
            dv = dot(chances.astype(BF16), g, TN)
            dq_s[:, low:high] = jnp.where(mask, dq, dq_s[:, low:high])
            dk_s[:, low:high] = jnp.where(mask, dk, dk_s[:, low:high])
            dv_s[:, low:high] = jnp.where(mask, dv, dv_s[:, low:high])
        for part_index, part in enumerate((dq_s, dk_s, dv_s)):
            start = part_index * width
            dx_refs[index][:, start : start + width] = part[:, :width].astype(BF16)


def row_block(rows, columns):
    return pl.BlockSpec((rows, columns), lambda i: (i, 0))


def attend(xs, rows, stride):
    count, width = xs[0].shape[0], xs[0].shape[1] // 3
    strips = len(xs)
    heads = strips * width // HEAD_DIM
    padded = -(-width // LANES) * LANES
    return pl.pallas_call(
        functools.partial(attend_kernel, strips, width, stride),
        grid=(count // rows,),
        in_specs=[row_block(rows, 3 * width)] * strips,
        out_specs=[row_block(rows, strips * width), row_block(rows, LANES)],
        out_shape=[
            jax.ShapeDtypeStruct((count, strips * width), BF16),
            jax.ShapeDtypeStruct((count, LANES), F32),
        ],
        scratch_shapes=[pltpu.VMEM((rows, padded), BF16)] * 3 + [pltpu.VMEM((rows, padded), F32)],
        cost_estimate=pl.CostEstimate(
            flops=heads * count * rows * 1024,
            bytes_accessed=count * width * strips * 8,
            transcendentals=heads * count * rows,
        ),
        compiler_params=pltpu.CompilerParams(vmem_limit_bytes=32 * 1024 * 1024),
    )(*xs)


def attend_back(xs, grad, lse, rows, stride):
    count, width = xs[0].shape[0], xs[0].shape[1] // 3
    strips = len(xs)
    heads = strips * width // HEAD_DIM
    padded = -(-width // LANES) * LANES
    return pl.pallas_call(
        functools.partial(attend_back_kernel, strips, width, stride),
        grid=(count // rows,),
        in_specs=[row_block(rows, 3 * width)] * strips
        + [row_block(rows, strips * width), row_block(rows, LANES)],
        out_specs=[row_block(rows, 3 * width)] * strips,
        out_shape=[jax.ShapeDtypeStruct((count, 3 * width), BF16)] * strips,
        scratch_shapes=[pltpu.VMEM((rows, padded), BF16)] * 4
        + [pltpu.VMEM((rows, padded), F32)] * 3,
        cost_estimate=pl.CostEstimate(
            flops=heads * count * rows * 2560,
            bytes_accessed=count * width * strips * 14,
            transcendentals=heads * count * rows,
        ),
        compiler_params=pltpu.CompilerParams(vmem_limit_bytes=32 * 1024 * 1024),
    )(*xs, grad, lse)


def split_frames(v, frames, width):
    return v.reshape(frames, -1, width // HEAD_DIM, HEAD_DIM)


def attend_shared(x, frames):
    width = x.shape[1] // 3
    shaped = x.reshape(frames, -1, 3, width)
    pairs = lax.all_gather(shaped[:, :, 1:], "tp", axis=1, tiled=True)
    q = split_frames(shaped[:, :, 0], frames, width)
    k = split_frames(pairs[:, :, 0], frames, width)
    v = split_frames(pairs[:, :, 1], frames, width)
    scores = jnp.einsum("bqhe,bkhe->bhqk", q, k, preferred_element_type=F32) * SCALE
    chances = jax.nn.softmax(scores, axis=-1)
    result = jnp.einsum("bhqk,bkhe->bqhe", chances.astype(BF16), v, preferred_element_type=F32)
    return result.reshape(-1, width).astype(BF16), (q, k, v, chances)


def attend_shared_back(saved, grad):
    q, k, v, chances = saved
    frames, width = q.shape[0], grad.shape[1]
    grad = split_frames(grad, frames, width)
    grad_chances = jnp.einsum("bqhe,bkhe->bhqk", grad, v, preferred_element_type=F32)
    row_dot = jnp.sum(chances * grad_chances, axis=-1, keepdims=True)
    grad_scores = (chances * (grad_chances - row_dot)).astype(BF16)
    dq = jnp.einsum("bhqk,bkhe->bqhe", grad_scores, k, preferred_element_type=F32) * SCALE
    dk = jnp.einsum("bhqk,bqhe->bkhe", grad_scores, q, preferred_element_type=F32) * SCALE
    dv = jnp.einsum("bhqk,bqhe->bkhe", chances.astype(BF16), grad, preferred_element_type=F32)
    sums = lax.psum_scatter(jnp.stack([dk, dv], axis=2), "tp", scatter_dimension=1, tiled=True)
    parts = jnp.concatenate([dq[:, :, None], sums], axis=2)
    return parts.reshape(-1, 3 * width).astype(BF16)


def normalise(v):
    centred = v - jnp.mean(v, axis=-1, keepdims=True)
    inverse = lax.rsqrt(jnp.mean(centred * centred, axis=-1, keepdims=True) + EPS)
    return centred * inverse, inverse


def modulate(v, shift, scale):
    return (normalise(v)[0] * (1.0 + scale[:, None]) + shift[:, None]).astype(BF16)


def modulate_back(grad, v, scale):
    normed, inverse = normalise(v)
    shift_grad = jnp.sum(grad, axis=1)
    scale_grad = jnp.sum(grad * normed, axis=1)
    scaled = grad * (1.0 + scale[:, None])
    mean_one = jnp.mean(scaled, axis=-1, keepdims=True)
    mean_two = jnp.mean(scaled * normed, axis=-1, keepdims=True)
    return inverse * (scaled - mean_one - normed * mean_two), shift_grad, scale_grad


def gelu(v):
    return jax.nn.gelu(v, approximate=True)


def gelu_slope(v, grad):
    return jax.vjp(gelu, v)[1](grad)[0]


def local(moves, tokens, condition, micro_ids, w_qkv, w_out, w_up, w_down, w_ada, cotangent):
    moves.here()
    n_dp, n_ctx, n_tp = moves.n_dp, moves.n_ctx, moves.n_tp
    clips, frames_here, patches_here, width = tokens.shape
    rows_here, head_cols = w_qkv.shape[2:]
    whole_frames = frames_here % n_tp == 0
    spread_tp = n_tp if whole_frames else 1
    groups = frames_here // spread_tp
    piece = patches_here // n_ctx

    cond_full = condition.astype(F32)
    cond_low = jax.nn.silu(cond_full).astype(BF16)
    cond_all = jnp.concatenate([cond_low, swap_with(cond_low, "dp", n_dp, 1)], axis=0)
    first_row = (moves.dp * n_ctx + moves.ctx) * rows_here
    cond_rows = lax.dynamic_slice_in_dim(cond_all, first_row, rows_here, axis=1)
    ada_low = w_ada.astype(BF16)
    shares = jnp.stack([dot(cond_rows, ada_low[level]) for level in range(LAYERS)], axis=1)
    sums = shares[:clips] + swap_with(shares[clips:], "dp", n_dp, 1)
    step = 1
    while step < n_ctx:
        sums = sums + swap_with(sums, "ctx", n_ctx, step)
        step *= 2
    strips = [sums] + [swap_with(sums, "tp", n_tp, r) for r in range(1, n_tp)]
    strips = flip_to(jnp.stack(strips, axis=2), 2, n_tp, moves.tp)
    mods = strips.reshape(clips, LAYERS, 6, width)
    mods = [moves.halves(mods[:, level]) for level in range(LAYERS)]

    def to_frames(v):
        v = v.reshape(clips, frames_here, n_ctx, piece, width)
        v = flip_to(v, 2, n_ctx, moves.ctx)
        if spread_tp == 1:
            yield ()
            return v.reshape(clips, groups * patches_here, width)
        v = v.reshape(clips, spread_tp, groups, patches_here, width)
        v = flip_to(v, 1, spread_tp, moves.tp)
        got = yield [swap_with(v[:, r], "tp", n_tp, r) for r in range(1, spread_tp)]
        return jnp.stack([v[:, 0]] + got, axis=2).reshape(clips, -1, width)

    def from_frames(v):
        if spread_tp > 1:
            v = v.reshape(clips, groups, spread_tp, patches_here, width)
            blocks = [v[:, :, 0]]
            blocks += [swap_with(v[:, :, r], "tp", n_tp, r) for r in range(1, spread_tp)]
            v = flip_to(jnp.stack(blocks, axis=1), 1, spread_tp, moves.tp)
        v = v.reshape(clips, frames_here, n_ctx, piece, width)
        v = flip_to(v, 2, n_ctx, moves.ctx)
        return v.reshape(clips, frames_here, patches_here, width)

    def trade(get, planes):
        sides = []
        for dx, dr in planes:
            block = get(dx, dr)
            if dx or dr:
                pairs = [
                    (c * n_tp + t, (c ^ dx) * n_tp + (t ^ dr))
                    for c in range(n_ctx)
                    for t in range(n_tp)
                ]
                block = lax.ppermute(block, ("ctx", "tp"), pairs)
            sides.append(block)
        sides = sides[:1] + (yield sides[1:])
        lines = [jnp.stack([v[:, dz] for v in sides], axis=1) for dz in range(n_ctx // 2)]
        got = yield [swap_with(v, "ctx", n_ctx, 2 * dz) for dz, v in enumerate(lines) if dz]
        return jnp.stack(lines[:1] + got, axis=1)

    all_planes = [(dx, dr) for dx in range(2) for dr in range(spread_tp)]
    own_planes = [(0, 0), (1, 0)]

    def frames_to_clips(v):
        v = v.reshape(clips, groups, spread_tp, n_ctx // 2, 2, piece, width)
        got = yield from trade(lambda dx, dr: v[:, :, dr, :, dx].swapaxes(1, 2), all_planes)
        return got.reshape(clips, -1, width)

    def clips_to_frames(v):
        v = v.reshape(clips, n_ctx // 2, 2, spread_tp, groups, piece, width)
        got = yield from trade(lambda dx, dr: v[:, :, dx, dr], all_planes)
        got = got.reshape(clips, n_ctx, spread_tp, groups, piece, width)
        return got.transpose(0, 3, 2, 1, 4, 5).reshape(clips, -1, width)

    def here_to_clips(v):
        v = v.reshape(clips, spread_tp, groups, n_ctx, piece, width)
        v = flip_to(flip_to(v, 3, n_ctx, moves.ctx), 1, spread_tp, moves.tp % spread_tp)
        v = v.reshape(clips, spread_tp, groups, n_ctx // 2, 2, piece, width)
        got = yield from trade(lambda dx, dr: v[:, :, :, :, dx].transpose(0, 3, 1, 2, 4, 5), own_planes)
        return got.reshape(clips, -1, width)

    def clips_to_here(v):
        v = v.reshape(clips, n_ctx // 2, 2, spread_tp, groups, piece, width)
        got = yield from trade(lambda dx, dr: v[:, :, dx], own_planes)
        v = got.reshape(clips, n_ctx, spread_tp, groups, piece, width).transpose(0, 2, 3, 1, 4, 5)
        v = flip_to(flip_to(v, 3, n_ctx, moves.ctx), 1, spread_tp, moves.tp % spread_tp)
        return v.reshape(clips, frames_here, patches_here, width)

    def flat(v):
        return v.reshape(-1, v.shape[-1])

    def shaped(v):
        return v.reshape(clips, -1, v.shape[-1])

    shards = []
    for level in range(LAYERS):
        attention = [w_qkv[level, 0], w_qkv[level, 1], w_qkv[level, 2], w_out[level].T]
        shards.append(jnp.concatenate(attention, axis=1).astype(BF16))
        shards.append(w_up[level].astype(BF16))
        shards.append(w_down[level].T.astype(BF16))
    lanes = Lanes()
    gathers = []

    def tick(values=()):
        rest, values = lanes.fence((shards[len(gathers) :], values))
        if rest:
            gathers.append(lanes.start(moves.gather_weight(rest[0])))
        return values

    def whole(index):
        return jnp.concatenate(gathers[index].result, axis=0)

    def attention_weights(index):
        v = whole(index)
        strips = jnp.split(v, n_tp, axis=1)
        cut = 3 * head_cols
        return [w[:, :cut] for w in strips], jnp.concatenate([w[:, cut:] for w in strips], axis=1)

    def modulations(level):
        return [mods[level][:, i] for i in range(6)]

    moved = lanes.start(to_frames(moves.halves(tokens)))
    gathers.append(lanes.start(moves.gather_weight(shards[0])))
    tick()
    residual = moved.result.astype(F32)
    tick()
    tick()
    records = []
    for level in range(LAYERS):
        spatial = level % 2 == 0
        shift_a, scale_a, gate_a, shift_m, scale_m, gate_m = modulations(level)
        normed = flat(modulate(residual, shift_a, scale_a))
        qkvs, outs = attention_weights(3 * level)
        projected = [dot(normed, v).astype(BF16) for v in qkvs]
        rows, stride = (patches_here * spread_tp, 1) if spatial else (residual.shape[1], piece)
        if spatial and not whole_frames:
            saved = [attend_shared(v, clips * frames_here) for v in projected]
            result = jnp.concatenate([entry[0] for entry in saved], axis=1)
            saved = [entry[1] for entry in saved]
        else:
            result, saved = attend(projected, rows, stride)
        result, saved = tick((result, saved))
        branch = shaped(dot(result, outs, NT))
        middle = residual + gate_a[:, None] * branch
        normed_mlp = flat(modulate(middle, shift_m, scale_m))
        up = whole(3 * level + 1)
        pre_act = dot(normed_mlp, up)
        act = gelu(pre_act).astype(BF16)
        act, pre_act = tick((act, pre_act))
        down = whole(3 * level + 2)
        branch_mlp = shaped(dot(act, down, NT))
        records.append(
            (residual, normed, projected, saved, result, branch, middle, normed_mlp)
            + (pre_act, act, branch_mlp, qkvs, outs, up, down, rows, stride)
        )
        residual = middle + gate_m[:, None] * branch_mlp
        if spatial:
            moved = lanes.start(frames_to_clips(residual.astype(BF16)))
            tick()
            turned = lanes.start(here_to_clips(moves.halves(cotangent)))
            tick()
            residual = moved.result.astype(F32)
    matched = (micro_ids[:, None] == micro_ids[None, :]).astype(F32)
    share = 1.0 / jnp.sum(matched, axis=1)
    gradient = turned.result.astype(F32) * share[:, None, None]
    finished = lanes.start(clips_to_here(moves.halves(residual.astype(BF16))))
    scatters = {}
    mod_grads = [None] * LAYERS
    for level in reversed(range(LAYERS)):
        spatial = level % 2 == 0
        (residual, normed, projected, saved, result, branch, middle, normed_mlp) = records[level][
            :8
        ]
        (pre_act, act, branch_mlp, qkvs, outs, up, down, rows, stride) = records[level][8:]
        shift_a, scale_a, gate_a, shift_m, scale_m, gate_m = modulations(level)
        gate_m_grad = jnp.sum(gradient * branch_mlp, axis=1)
        low_grad = flat((gradient * gate_m[:, None]).astype(BF16))
        grad_pre = gelu_slope(pre_act, dot(low_grad, down)).astype(BF16)
        scatters[level, "down"] = lanes.start(moves.scatter_weight(low_grad, [act]))
        grad_pre = lanes.fence(grad_pre)
        grad_normed = shaped(dot(grad_pre, up, NT))
        scatters[level, "up"] = lanes.start(moves.scatter_weight(normed_mlp, [grad_pre]))
        grad_normed = lanes.fence(grad_normed)
        added, shift_m_grad, scale_m_grad = modulate_back(grad_normed, middle, scale_m)
        gradient = gradient + added
        gate_a_grad = jnp.sum(gradient * branch, axis=1)
        low_grad = flat((gradient * gate_a[:, None]).astype(BF16))
        grad_heads = dot(low_grad, outs).astype(BF16)
        scatters[level, "out"] = lanes.start(moves.scatter_weight(low_grad, [result]))
        grad_heads = lanes.fence(grad_heads)
        if spatial and not whole_frames:
            grad_qkv = [
                attend_shared_back(v, g)
                for v, g in zip(saved, jnp.split(grad_heads, n_tp, axis=1))
            ]
        else:
            grad_qkv = attend_back(projected, grad_heads, saved, rows, stride)
        grad_qkv = lanes.fence(grad_qkv)
        scatters[level, "qkv"] = lanes.start(moves.scatter_weight(normed, grad_qkv))
        grad_normed = shaped(sum(dot(v, w, NT) for v, w in zip(grad_qkv, qkvs)))
        added, shift_a_grad, scale_a_grad = modulate_back(grad_normed, residual, scale_a)
        gradient = gradient + added
        mod_grads[level] = jnp.stack(
            [shift_a_grad, scale_a_grad, gate_a_grad, shift_m_grad, scale_m_grad, gate_m_grad],
            axis=1,
        )
        if not spatial:
            moved = lanes.start(clips_to_frames(gradient.astype(BF16)))
            lanes.fence()
            lanes.fence()
            gradient = moved.result.astype(F32)
    grad_tokens = from_frames(moves.halves(gradient.astype(BF16))).astype(F32)
    while lanes.tasks:
        lanes.fence()
    output = finished.result
    grads = [
        (
            scatters[level, "qkv"].result.reshape(rows_here, 3, head_cols).transpose(1, 0, 2),
            scatters[level, "out"].result.T,
            scatters[level, "up"].result,
            scatters[level, "down"].result.T,
        )
        for level in range(LAYERS)
    ]

    ada_grads = []
    cond_part = 0.0
    for level in range(LAYERS):
        strips = moves.halves(mod_grads[level]).reshape(clips, n_tp, -1)
        strips = flip_to(strips, 1, n_tp, moves.tp)
        strip = strips[:, 0]
        for r in range(1, n_tp):
            strip = strip + swap_with(strips[:, r], "tp", n_tp, r)
        step = 1
        while step < n_ctx:
            strip = strip + swap_with(strip, "ctx", n_ctx, step)
            step *= 2
        strip = jnp.concatenate([strip, swap_with(strip, "dp", n_dp, 1)], axis=0)
        ada_grads.append(
            lax.dot_general(cond_rows.astype(F32), strip, TN, precision=HIGHEST)
        )
        cond_part = cond_part + lax.dot_general(
            strip, ada_low[level].astype(F32), NT, precision=HIGHEST
        )
    step = 1
    while step < n_tp:
        cond_part = cond_part + swap_with(cond_part, "tp", n_tp, step)
        step *= 2
    cond_grad = jnp.stack(
        [cond_part[:clips], swap_with(cond_part[clips:], "dp", n_dp, 1)], axis=1
    )[:, :, None]
    step = 1
    while step < n_ctx:
        cond_grad = jnp.concatenate(
            [cond_grad, swap_with(cond_grad, "ctx", n_ctx, step)], axis=2
        )
        step *= 2
    cond_grad = flip_to(cond_grad, 2, n_ctx, moves.ctx).reshape(clips, width)
    cond_grad = moves.halves(cond_grad)
    grad_condition = jax.vjp(jax.nn.silu, cond_full)[1](cond_grad)[0]

    stacked = [jnp.stack([grads[level][i] for level in range(LAYERS)]) for i in range(4)]
    return (output, grad_tokens, grad_condition, *stacked, jnp.stack(ada_grads))


def solution(mesh):
    placed = (
        P("dp", "ctx", "tp", None),
        P("dp", None),
        P("dp"),
        P(None, None, ("dp", "ctx"), "tp"),
        P(None, "tp", ("dp", "ctx")),
        P(None, ("dp", "ctx"), "tp"),
        P(None, "tp", ("dp", "ctx")),
        P(None, ("dp", "ctx"), "tp"),
        P("dp", "ctx", "tp", None),
    )
    return jax.shard_map(
        functools.partial(local, Moves(mesh)),
        mesh=mesh,
        in_specs=placed,
        out_specs=(
            P("dp", "ctx", "tp", None),
            P("dp", "ctx", "tp", None),
            P("dp", None),
            P(None, None, ("dp", "ctx"), "tp"),
            P(None, "tp", ("dp", "ctx")),
            P(None, ("dp", "ctx"), "tp"),
            P(None, "tp", ("dp", "ctx")),
            P(None, ("dp", "ctx"), "tp"),
        ),
        check_vma=False,
    )
```

time: 1710 us -> 1630 us (0.953)
  waiting for transfers between devices: 664 us -> 417 us
  other arithmetic: 186 us -> 393 us
  local copies, waits for them, and re-layouts: 172 us -> 145 us
    ppermute x87 -> x149, waiting for transfers between devices: 616 us -> 373 us  [swap_with(): return lax.ppermute(v, axis_name, [(i, i ^ k) for i in range(n)])]
    concatenate x6 -> x18, other arithmetic: 45 us -> 143 us  [the longest x2 80.4 us: whole(): return jnp.concatenate(gathers[index].result, axis=0)]
    convert_element_type x14 -> x25, other arithmetic: 31.3 us -> 80.1 us  [the longest x2 34.7 us: local(): grad_pre = gelu_slope(pre_act, dot(low_grad, down)).astype(BF16)]
    another operation x32 -> x82, other arithmetic: 11.1 us -> 58.3 us  [the longest x13 5.11 us: trade(): block = jnp.stack([v[:, dz] for v in sides], axis=1)]
    unnamed x534 -> x583, local copies, waits for them, and re-layouts: 74.9 us -> 49.7 us
    ppermute x87 -> x149, starting transfers between devices: 150 us -> 166 us  [swap_with(): return lax.ppermute(v, axis_name, [(i, i ^ k) for i in range(n)])]
    dot_general x58 -> x42, matrix products: 402 us -> 387 us  [dot(): return lax.dot_general(a, b, dims, preferred_element_type=F32)]
    pallas_call x8 -> x4, Pallas kernels: 90.2 us -> 87.9 us  [the longest x2 59.8 us: attend_back(): pl.pallas_call(functools.partial(attend_back_kernel, strips, width, strid...]
  transfers between devices with their start and end apart: 102 -> 157, of which waited for: 46 -> 64; matrix products, arithmetic and copies ran while one was open for 37% -> 45% of each run, Pallas kernels for 5% -> 5%
where the time goes in v2:
time: 1630 us; the launch traced here: 1620 us
  waiting for transfers between devices  417 us (26%)
  other arithmetic  393 us (24%)
  matrix products  392 us (24%)
  starting transfers between devices  176 us (11%)
  local copies, waits for them, and re-layouts  145 us (9%)
  Pallas kernels  87.9 us (5%)
    dot_general x42, matrix products, dot(): return lax.dot_general(a, b, dims, preferred_element_type=F32)  387 us
    ppermute x149, waiting for transfers between devices, swap_with(): return lax.ppermute(v, axis_name, [(i, i ^ k) for i in range(n)])  373 us
    ppermute x149, starting transfers between devices, swap_with(): return lax.ppermute(v, axis_name, [(i, i ^ k) for i in range(n)])  166 us
    concatenate x2, other arithmetic, whole(): return jnp.concatenate(gathers[index].result, axis=0)  80.4 us
    pallas_call x2, Pallas kernels, attend_back(): pl.pallas_call(functools.partial(attend_back_kernel, strips, width, strid...  59.8 us
    unnamed x583, local copies, waits for them, and re-layouts  49.7 us
    ppermute x8, waiting for transfers between devices, trade(): block = lax.ppermute(block, ('ctx', 'tp'), pairs)  44.4 us
    concatenate x2, other arithmetic, attention_weights(): jnp.concatenate([w[:, cut:] for w in strips], axis=1)  43.3 us
  transfers between devices with their start and end apart: 157, of which 64 were waited for; matrix products, arithmetic and copies ran while one was open for 45% of the time, Pallas kernels for 5%

profile of v2, /device:TPU:0, one launch (start us, length us, event | category | flops | bytes accessed | tf_op | source)
XLA Modules:
  0.0 1617.7 jit_solution(11255122073701942824)
XLA Ops:
  84.7 23.0 %collective-permute-done.13 = bf16[72,2304]{1,0:T(8,128)(2,1)S(1)} collective-permute-done((bf16[72,2304]{1,0:T(8,128)(2,1)S(1)}, bf16[72,2304]{1,0:T(8,128)(2,1)S(1)}, u32[]{:S(2)}, u32[]{:S(2)}) %collective-permute-start.13) | collective-permute-done | bytes 331808 | tf_op jit(solution)/shard_map/ppermute | solution.py:29
  118.5 8.5 collective-permute-done.20
  127.1 7.1 collective-permute-done.19
  134.2 10.8 collective-permute-done.17
  162.5 41.3 %pad_maximum_fusion = bf16[1152,4608]{1,0:T(8,128)(2,1)} fusion(bf16[576,4608]{1,0:T(8,128)(2,1)S(1)} %collective-permute-done.22, bf16[576,1152]{1,0:T(8,128)(2,1)S(1)} %bitcast.1334, bf16[576,1152]{1,0:T(8,128)(2,1)S(1)} %collective-permute-done.15, bf16[576,1152]{1,0:T(8,128)(2,1)S(1)} %bitcast.1331, bf16[576,1152]{1,0:T(8,128)(2,1)S(1)} %bitcast.1322), kind=kLoop, calls=%fused_computation.36 | loop fusion | flops 53084160 | bytes 21233664 | tf_op jit(solution)/shard_map/concatenate | solution.py:487
  203.7 7.7 convolution_convert_fusion.8.refs_1_
  213.9 7.3 convolution_convert_fusion.9.refs_0_
  221.3 13.7 shard_map.152
  235.1 9.4 collective-permute-done.23
  261.7 22.2 %fusion.89 = bf16[1152,1152]{1,0:T(8,128)(2,1)S(1)} fusion(bf16[576,4608]{1,0:T(8,128)(2,1)S(1)} %collective-permute-done.22, bf16[576,1152]{1,0:T(8,128)(2,1)S(1)} %bitcast.1335, bf16[576,1152]{1,0:T(8,128)(2,1)S(1)} %collective-permute-done.15, bf16[576,1152]{1,0:T(8,128)(2,1)S(1)} %bitcast.1332, bf16[576,1152]{1,0:T(8,128)(2,1)S(1)} %bitcast.1323), kind=kLoop, calls=%fused_computation.195 | loop fusion | flops 39813120 | bytes 13271040 | tf_op jit(solution)/shard_map/concatenate | solution.py:493
  309.8 36.8 %fusion.21 = (bf16[1024,4608]{1,0:T(8,128)(2,1)}, f32[1024,4608]{1,0:T(8,128)}) fusion(bf16[1024,1152]{1,0:T(8,128)(2,1)S(1)} %fusion.60, bf16[576,4608]{1,0:T(8,128)(2,1)} %collective-permute-done.30, bf16[576,1152]{1,0:T(8,128)(2,1)S(1)} %bitcast.1440, bf16[576,1152]{1,0:T(8,128)(2,1)} %copy-done.152, bf16[576,1152]{1,0:T(8,128)(2,1)S(1)} %bitcast.1437, ...), kind=kOutput, calls=%fused_computation.27 | convolution fusion | flops 10967187456 | bytes 41287680 | tf_op jit(solution)/shard_map/dot_general | solution.py:25
  378.3 21.3 %fusion.287 = f32[1024,1152]{1,0:T(8,128)} fusion(bf16[1024,4608]{1,0:T(8,128)(2,1)} %get-tuple-element.198, bf16[576,4608]{1,0:T(8,128)(2,1)} %copy-done.247, bf16[576,1152]{1,0:T(8,128)(2,1)} %bitcast.1449, bf16[576,1152]{1,0:T(8,128)(2,1)} %collective-permute-done.31, bf16[576,1152]{1,0:T(8,128)(2,1)} %bitcast.1446, bf16[576,1152]{1,0:T(8,128)(2,1)} %bitcast.1441), kind=kOutput, calls=%fused_computation.908 | convolution fusion | flops 10924720128 | bytes 24772608 | tf_op jit(solution)/shard_map/dot_general | solution.py:25
  411.8 24.7 %collective-permute-done.40 = bf16[2,4,72,1152]{3,2,1,0:T(8,128)(2,1)S(1)} collective-permute-done((bf16[2,4,72,1152]{3,2,1,0:T(8,128)(2,1)S(1)}, bf16[2,4,72,1152]{3,2,1,0:T(8,128)(2,1)S(1)}, u32[]{:S(2)}, u32[]{:S(2)}) %collective-permute-start.40) | collective-permute-done | bytes 1327136 | tf_op jit(solution)/shard_map/ppermute | solution.py:29
  437.6 11.6 collective-permute-done.47
  449.2 11.6 collective-permute-done.46
  491.5 15.1 collective-permute-done.54
  510.1 8.7 collective-permute-done.52
  518.7 10.0 collective-permute-done.51
  557.3 39.1 %pad_maximum_fusion.3 = bf16[1152,4608]{1,0:T(8,128)(2,1)S(1)} fusion(bf16[576,4608]{1,0:T(8,128)(2,1)} %collective-permute-done.57, bf16[576,1152]{1,0:T(8,128)(2,1)S(1)} %bitcast.1328, bf16[576,1152]{1,0:T(8,128)(2,1)S(1)} %copy-done.39, bf16[576,1152]{1,0:T(8,128)(2,1)S(1)} %bitcast.1325, bf16[576,1152]{1,0:T(8,128)(2,1)S(1)} %bitcast.1318), kind=kLoop, calls=%fused_computation.39 | loop fusion | flops 53084160 | bytes 21233664 | tf_op jit(solution)/shard_map/concatenate | solution.py:487
  606.9 14.4 shard_map.153
  631.0 21.1 %fusion.93 = bf16[1152,1152]{1,0:T(8,128)(2,1)S(1)} fusion(bf16[576,4608]{1,0:T(8,128)(2,1)} %collective-permute-done.57, bf16[576,1152]{1,0:T(8,128)(2,1)S(1)} %bitcast.1329, bf16[576,1152]{1,0:T(8,128)(2,1)S(1)} %copy-done.39, bf16[576,1152]{1,0:T(8,128)(2,1)S(1)} %bitcast.1326, bf16[576,1152]{1,0:T(8,128)(2,1)S(1)} %bitcast.1319), kind=kLoop, calls=%fused_computation.199 | loop fusion | flops 39813120 | bytes 13271040 | tf_op jit(solution)/shard_map/concatenate | solution.py:493
  672.7 29.1 %fusion.29 = (bf16[1024,4608]{1,0:T(8,128)(2,1)}, f32[1024,4608]{1,0:T(8,128)}) fusion(bf16[1024,1152]{1,0:T(8,128)(2,1)S(1)} %fusion.54, bf16[576,4608]{1,0:T(8,128)(2,1)} %collective-permute-done.63, bf16[576,1152]{1,0:T(8,128)(2,1)} %bitcast.1459, bf16[576,1152]{1,0:T(8,128)(2,1)} %copy-done.154, bf16[576,1152]{1,0:T(8,128)(2,1)} %bitcast.1456, ...), kind=kOutput, calls=%fused_computation.35 | convolution fusion | flops 10967187456 | bytes 41287680 | tf_op jit(solution)/shard_map/dot_general | solution.py:25
  701.8 11.3 convolution_convert_fusion.3
  713.1 8.5 fusion.149
  721.6 21.1 %fusion.283 = f32[1024,1152]{1,0:T(8,128)} fusion(bf16[1024,4608]{1,0:T(8,128)(2,1)} %get-tuple-element.228, bf16[576,4608]{1,0:T(8,128)(2,1)} %collective-permute-done.64, bf16[576,1152]{1,0:T(8,128)(2,1)} %bitcast.1465, bf16[576,1152]{1,0:T(8,128)(2,1)} %collective-permute-done.58, bf16[576,1152]{1,0:T(8,128)(2,1)} %bitcast.1461, ...), kind=kOutput, calls=%fused_computation.904 | convolution fusion | flops 10924720128 | bytes 24772608 | tf_op jit(solution)/shard_map/dot_general | solution.py:25
  742.8 9.2 add_convert_fusion.6
  760.1 20.3 %fusion.282 = f32[1024,4608]{1,0:T(8,128)} fusion(bf16[1024,1152]{1,0:T(8,128)(2,1)} %fusion.52, bf16[576,4608]{1,0:T(8,128)(2,1)} %collective-permute-done.64, bf16[576,1152]{1,0:T(8,128)(2,1)} %bitcast.1466, bf16[576,1152]{1,0:T(8,128)(2,1)} %collective-permute-done.58, bf16[576,1152]{1,0:T(8,128)(2,1)} %bitcast.1462, bf16[576,1152]{1,0:T(8,128)(2,1)} %bitcast.286), kind=kOutput, calls=%fused_computation.903 | convolution fusion | flops 10924720128 | bytes 31850496 | tf_op jit(solution)/shard_map/dot_general | solution.py:25
  780.4 17.3 %fusion.6 = bf16[1024,4608]{1,0:T(8,128)(2,1)S(1)} fusion(f32[1024,4608]{1,0:T(8,128)} %get-tuple-element.234, f32[1024,4608]{1,0:T(8,128)} %fusion.282), kind=kLoop, calls=%fused_computation.12 | loop fusion | flops 94371840 | bytes 47185920 | tf_op jit(solution)/shard_map/convert_element_type | solution.py:554
  808.7 8.2 convolution_convert_fusion.2
  817.0 9.5 add_convert_fusion.3
  835.0 21.2 %fusion.284 = f32[1024,1152]{1,0:T(8,128)} fusion(bf16[1024,4608]{1,0:T(8,128)(2,1)} %copy-done.24, bf16[576,4608]{1,0:T(8,128)(2,1)} %collective-permute-done.63, bf16[576,1152]{1,0:T(8,128)(2,1)} %bitcast.1460, bf16[576,1152]{1,0:T(8,128)(2,1)} %copy-done.154, bf16[576,1152]{1,0:T(8,128)(2,1)} %bitcast.1457, bf16[576,1152]{1,0:T(8,128)(2,1)} %bitcast.1452), kind=kOutput, calls=%fused_computation.905 | convolution fusion | flops 10924720128 | bytes 24772608 | tf_op jit(solution)/shard_map/dot_general | solution.py:25
  858.2 6.4 collective-permute-done.71
  865.5 10.8 add_convert_fusion.2
  917.2 21.8 %collective-permute-done.76 = bf16[4,72,2304]{2,1,0:T(8,128)(2,1)S(1)} collective-permute-done((bf16[4,72,2304]{2,1,0:T(8,128)(2,1)S(1)}, bf16[4,72,2304]{2,1,0:T(8,128)(2,1)S(1)}, u32[]{:S(2)}, u32[]{:S(2)}) %collective-permute-start.76) | collective-permute-done | bytes 1327136 | tf_op jit(solution)/shard_map/ppermute | solution.py:29
  966.8 30.0 %shard_map.154 = (bf16[1024,1728]{1,0:T(8,128)(2,1)S(1)}, bf16[1024,1728]{1,0:T(8,128)(2,1)S(1)}) custom-call(bf16[1024,1728]{1,0:T(8,128)(2,1)S(1)} %copy-done.20, bf16[1024,1728]{1,0:T(8,128)(2,1)S(1)} %copy-done.18, bf16[1024,1152]{1,0:T(8,128)(2,1)S(1)} %convolution_convert_fusion.5.refs_2_, f32[1024,128]{1,0:T(8,128)S(1)} %get-tuple-element.246.refs_3_), custom_call_target="tpu_custom_call" | custom-call | flops 10737418240 | bytes 16515072 | tf_op jit(solution)/shard_map/pallas_call | solution.py:294
  1002.0 8.8 fusion.74
  1014.8 10.1 fusion.73
  1024.9 7.7 fusion.53
  1058.9 7.9 collective-permute-done.87
  1067.6 7.6 collective-permute-done.85
  1076.3 8.0 collective-permute-done.86
  1089.5 13.6 collective-permute-done.92
  1124.0 19.6 %collective-permute-done.100 = bf16[4,4,1,16,1152]{4,3,1,0,2:T(8,128)(2,1)S(1)} collective-permute-done((bf16[4,4,1,16,1152]{4,3,1,0,2:T(8,128)(2,1)S(1)}, bf16[4,4,1,16,1152]{4,3,1,0,2:T(8,128)(2,1)S(1)}, u32[]{:S(2)}, u32[]{:S(2)}) %collective-permute-start.100) | collective-permute-done | bytes 589856 | tf_op jit(solution)/shard_map/ppermute | solution.py:29
  1143.6 17.6 %collective-permute-done.101 = bf16[4,4,1,16,1152]{4,3,1,0,2:T(8,128)(2,1)S(1)} collective-permute-done((bf16[4,4,1,16,1152]{4,3,1,0,2:T(8,128)(2,1)S(1)}, bf16[4,4,1,16,1152]{4,3,1,0,2:T(8,128)(2,1)S(1)}, u32[]{:S(2)}, u32[]{:S(2)}) %collective-permute-start.101) | collective-permute-done | bytes 589856 | tf_op jit(solution)/shard_map/ppermute | solution.py:29
  1172.6 8.0 convolution_convert_fusion.1
  1180.5 19.4 %fusion.286 = f32[1024,4608]{1,0:T(8,128)} fusion(bf16[1024,1152]{1,0:T(8,128)(2,1)S(1)} %fusion.50, bf16[576,4608]{1,0:T(8,128)(2,1)} %copy-done.247, bf16[576,1152]{1,0:T(8,128)(2,1)} %bitcast.1450, bf16[576,1152]{1,0:T(8,128)(2,1)} %collective-permute-done.31, bf16[576,1152]{1,0:T(8,128)(2,1)} %bitcast.1447, bf16[576,1152]{1,0:T(8,128)(2,1)} %bitcast.1442), kind=kOutput, calls=%fused_computation.907 | convolution fusion | flops 10924720128 | bytes 31850496 | tf_op jit(solution)/shard_map/dot_general | solution.py:25
  1200.0 17.4 %fusion.13 = bf16[1024,4608]{1,0:T(8,128)(2,1)S(1)} fusion(f32[1024,4608]{1,0:T(8,128)} %get-tuple-element.270, f32[1024,4608]{1,0:T(8,128)} %fusion.286), kind=kLoop, calls=%fused_computation.19 | loop fusion | flops 94371840 | bytes 47185920 | tf_op jit(solution)/shard_map/convert_element_type | solution.py:554
  1218.2 11.7 add_convert_fusion.1
  1237.2 8.8 collective-permute-start.106
  1246.6 8.5 convolution_convert_fusion
  1260.4 21.1 %fusion.288 = f32[1024,1152]{1,0:T(8,128)} fusion(bf16[1024,4608]{1,0:T(8,128)(2,1)} %copy-done.25, bf16[576,4608]{1,0:T(8,128)(2,1)} %collective-permute-done.30, bf16[576,1152]{1,0:T(8,128)(2,1)} %bitcast.1439, bf16[576,1152]{1,0:T(8,128)(2,1)} %copy-done.152, bf16[576,1152]{1,0:T(8,128)(2,1)} %bitcast.1436, bf16[576,1152]{1,0:T(8,128)(2,1)} %bitcast.110), kind=kOutput, calls=%fused_computation.909 | convolution fusion | flops 10924720128 | bytes 24772608 | tf_op jit(solution)/shard_map/dot_general | solution.py:25
  1281.5 8.3 collective-permute-done.110
  1291.0 11.1 add_convert_fusion
  1320.7 6.4 multiply_reduce_fusion.5
  1340.2 17.4 %collective-permute-done.112 = bf16[4,72,1152]{2,1,0:T(8,128)(2,1)S(1)} collective-permute-done((bf16[4,72,1152]{2,1,0:T(8,128)(2,1)S(1)}, bf16[4,72,1152]{2,1,0:T(8,128)(2,1)S(1)}, u32[]{:S(2)}, u32[]{:S(2)}) %collective-permute-start.112) | collective-permute-done | bytes 663584 | tf_op jit(solution)/shard_map/ppermute | solution.py:29
  1384.0 29.8 %shard_map.155 = (bf16[1024,1728]{1,0:T(8,128)(2,1)S(1)}, bf16[1024,1728]{1,0:T(8,128)(2,1)S(1)}) custom-call(bf16[1024,1728]{1,0:T(8,128)(2,1)S(1)} %copy-done.16, bf16[1024,1728]{1,0:T(8,128)(2,1)S(1)} %copy-done.14, bf16[1024,1152]{1,0:T(8,128)(2,1)S(1)} %convolution_convert_fusion.4.refs_2_, f32[1024,128]{1,0:T(8,128)S(1)} %get-tuple-element.282.refs_3_), custom_call_target="tpu_custom_call" | custom-call | flops 10737418240 | bytes 16515072 | tf_op jit(solution)/shard_map/pallas_call | solution.py:294
  1419.0 7.1 fusion.79
  1426.2 9.7 fusion.72
  1435.9 6.5 fusion.51
  1501.5 13.2 collective-permute-done.124
  1521.5 13.5 collective-permute-done.140
  1560.0 13.3 collective-permute-done.150
  1573.4 6.5 collective-permute-done.151
  1605.5 10.1 collective-permute-done.155
  (1406 shorter events, 672.0 us)
Async XLA Ops:
  5.5 63.3 %collective-permute-start.3 = (bf16[72,2304]{1,0:T(8,128)(2,1)}, bf16[72,2304]{1,0:T(8,128)(2,1)}, u32[]{:S(2)}, u32[]{:S(2)}) collective-permute-start(bf16[72,2304]{1,0:T(8,128)(2,1)} %concatenate.904), channel_id=1, source_target_pairs={{0,12},{2,14},{4,8},{6,10},{8,4},{10,6},{12,0},{14,2},{1,13},{3,15... | collective-permute-start | bytes 995336 | tf_op jit(solution)/shard_map/ppermute | solution.py:29
  10.5 58.3 %collective-permute-start.2 = (bf16[72,2304]{1,0:T(8,128)(2,1)}, bf16[72,2304]{1,0:T(8,128)(2,1)}, u32[]{:S(2)}, u32[]{:S(2)}) collective-permute-start(bf16[72,2304]{1,0:T(8,128)(2,1)} %concatenate.904), channel_id=1, source_target_pairs={{0,8},{2,10},{4,12},{6,14},{8,0},{10,2},{12,4},{14,6},{1,9},{3,11}... | collective-permute-start | bytes 995336 | tf_op jit(solution)/shard_map/ppermute | solution.py:29
  10.5 58.3 %collective-permute-start.1 = (bf16[72,2304]{1,0:T(8,128)(2,1)}, bf16[72,2304]{1,0:T(8,128)(2,1)}, u32[]{:S(2)}, u32[]{:S(2)}) collective-permute-start(bf16[72,2304]{1,0:T(8,128)(2,1)} %concatenate.904), channel_id=1, source_target_pairs={{0,4},{2,6},{4,0},{6,2},{8,12},{10,14},{12,8},{14,10},{1,5},{3,7},... | collective-permute-start | bytes 995336 | tf_op jit(solution)/shard_map/ppermute | solution.py:29
  18.2 50.6 %collective-permute-start = (bf16[4,1,128,1152]{3,2,0,1:T(8,128)(2,1)}, bf16[4,1,128,1152]{3,2,0,1:T(8,128)(2,1)S(1)}, u32[]{:S(2)}, u32[]{:S(2)}) collective-permute-start(bf16[4,1,128,1152]{3,2,0,1:T(8,128)(2,1)} %get-tuple-element.489), channel_id=1, source_target_pairs={{0,1},{1,0},{2,3},{3,2},{4,5},{5,4},{6,7},{7,6},{8,9},{9,8},{10,11... | collective-permute-start | bytes 3538952 | tf_op jit(solution)/shard_map/ppermute | solution.py:29
  145.0 66.5 %collective-permute-start.29 = (bf16[72,2304]{1,0:T(8,128)(2,1)}, bf16[72,2304]{1,0:T(8,128)(2,1)S(1)}, u32[]{:S(2)}, u32[]{:S(2)}) collective-permute-start(bf16[72,2304]{1,0:T(8,128)(2,1)} %concatenate.903), channel_id=1, source_target_pairs={{0,12},{2,14},{4,8},{6,10},{8,4},{10,6},{12,0},{14,2},{1,13},{3,15... | collective-permute-start | bytes 995336 | tf_op jit(solution)/shard_map/ppermute | solution.py:29
  148.4 72.8 %collective-permute-start.28 = (bf16[72,2304]{1,0:T(8,128)(2,1)}, bf16[72,2304]{1,0:T(8,128)(2,1)}, u32[]{:S(2)}, u32[]{:S(2)}) collective-permute-start(bf16[72,2304]{1,0:T(8,128)(2,1)} %concatenate.903), channel_id=1, source_target_pairs={{0,8},{2,10},{4,12},{6,14},{8,0},{10,2},{12,4},{14,6},{1,9},{3,11}... | collective-permute-start | bytes 995336 | tf_op jit(solution)/shard_map/ppermute | solution.py:29
  154.9 80.2 %collective-permute-start.26 = (bf16[4,72,1152]{2,1,0:T(8,128)(2,1)}, bf16[4,72,1152]{2,1,0:T(8,128)(2,1)}, u32[]{:S(2)}, u32[]{:S(2)}) collective-permute-start(bf16[4,72,1152]{2,1,0:T(8,128)(2,1)} %fusion.183), channel_id=1, source_target_pairs={{0,1},{1,0},{2,3},{3,2},{4,5},{5,4},{6,7},{7,6},{8,9},{9,8},{10,11... | collective-permute-start | bytes 1990664 | tf_op jit(solution)/shard_map/ppermute | solution.py:29
  155.9 79.2 %collective-permute-start.25 = (bf16[4,72,1152]{2,1,0:T(8,128)(2,1)S(1)}, bf16[4,72,1152]{2,1,0:T(8,128)(2,1)}, u32[]{:S(2)}, u32[]{:S(2)}) collective-permute-start(bf16[4,72,1152]{2,1,0:T(8,128)(2,1)S(1)} %fusion.184), channel_id=1, source_target_pairs={{0,2},{2,0},{4,6},{6,4},{8,10},{10,8},{12,14},{14,12},{1,3},{3,1},... | collective-permute-start | bytes 1990664 | tf_op jit(solution)/shard_map/ppermute | solution.py:29
  161.0 74.2 %collective-permute-start.24 = (bf16[2,4,72,1152]{3,2,1,0:T(8,128)(2,1)}, bf16[2,4,72,1152]{3,2,1,0:T(8,128)(2,1)S(1)}, u32[]{:S(2)}, u32[]{:S(2)}) collective-permute-start(bf16[2,4,72,1152]{3,2,1,0:T(8,128)(2,1)} %pad_maximum_fusion.49), channel_id=1, source_target_pairs={{0,2},{2,0},{4,6},{6,4},{8,10},{10,8},{12,14},{14,12},{1,3},{3,1},... | collective-permute-start | bytes 3981320 | tf_op jit(solution)/shard_map/ppermute | solution.py:29
  244.5 61.5 %collective-permute-start.37 = (bf16[72,2304]{1,0:T(8,128)(2,1)}, bf16[72,2304]{1,0:T(8,128)(2,1)}, u32[]{:S(2)}, u32[]{:S(2)}) collective-permute-start(bf16[72,2304]{1,0:T(8,128)(2,1)} %get-tuple-element.197), channel_id=1, source_target_pairs={{0,12},{2,14},{4,8},{6,10},{8,4},{10,6},{12,0},{14,2},{1,13},{3,15... | collective-permute-start | bytes 995336 | tf_op jit(solution)/shard_map/ppermute | solution.py:29
  245.5 62.0 %collective-permute-start.36 = (bf16[72,2304]{1,0:T(8,128)(2,1)}, bf16[72,2304]{1,0:T(8,128)(2,1)}, u32[]{:S(2)}, u32[]{:S(2)}) collective-permute-start(bf16[72,2304]{1,0:T(8,128)(2,1)} %get-tuple-element.197), channel_id=1, source_target_pairs={{0,8},{2,10},{4,12},{6,14},{8,0},{10,2},{12,4},{14,6},{1,9},{3,11}... | collective-permute-start | bytes 995336 | tf_op jit(solution)/shard_map/ppermute | solution.py:29
  245.7 101.0 %collective-permute-start.35 = (bf16[72,2304]{1,0:T(8,128)(2,1)}, bf16[72,2304]{1,0:T(8,128)(2,1)}, u32[]{:S(2)}, u32[]{:S(2)}) collective-permute-start(bf16[72,2304]{1,0:T(8,128)(2,1)} %get-tuple-element.197), channel_id=1, source_target_pairs={{0,4},{2,6},{4,0},{6,2},{8,12},{10,14},{12,8},{14,10},{1,5},{3,7},... | collective-permute-start | bytes 995336 | tf_op jit(solution)/shard_map/ppermute | solution.py:29
  257.1 89.6 %collective-permute-start.34 = (bf16[4,72,1152]{2,1,0:T(8,128)(2,1)}, bf16[4,72,1152]{2,1,0:T(8,128)(2,1)}, u32[]{:S(2)}, u32[]{:S(2)}) collective-permute-start(bf16[4,72,1152]{2,1,0:T(8,128)(2,1)} %fusion.181), channel_id=1, source_target_pairs={{0,1},{1,0},{2,3},{3,2},{4,5},{5,4},{6,7},{7,6},{8,9},{9,8},{10,11... | collective-permute-start | bytes 1990664 | tf_op jit(solution)/shard_map/ppermute | solution.py:29
  261.7 46.3 %collective-permute-start.30 = (bf16[576,4608]{1,0:T(8,128)(2,1)}, bf16[576,4608]{1,0:T(8,128)(2,1)}, u32[]{:S(2)}, u32[]{:S(2)}) collective-permute-start(bf16[576,4608]{1,0:T(8,128)(2,1)} %pad_maximum_fusion.7), channel_id=1, source_target_pairs={{0,16},{16,0},{1,17},{17,1},{2,18},{18,2},{3,19},{19,3},{4,20},{20... | collective-permute-start | bytes 15925256 | tf_op jit(solution)/shard_map/ppermute | solution.py:29
  306.0 40.7 %collective-permute-start.33 = (bf16[4,72,1152]{2,1,0:T(8,128)(2,1)S(1)}, bf16[4,72,1152]{2,1,0:T(8,128)(2,1)}, u32[]{:S(2)}, u32[]{:S(2)}) collective-permute-start(bf16[4,72,1152]{2,1,0:T(8,128)(2,1)S(1)} %fusion.182), channel_id=1, source_target_pairs={{0,2},{2,0},{4,6},{6,4},{8,10},{10,8},{12,14},{14,12},{1,3},{3,1},... | collective-permute-start | bytes 1990664 | tf_op jit(solution)/shard_map/ppermute | solution.py:29
  307.5 44.3 %collective-permute-start.32 = (bf16[2,4,72,1152]{3,2,1,0:T(8,128)(2,1)S(1)}, bf16[2,4,72,1152]{3,2,1,0:T(8,128)(2,1)S(1)}, u32[]{:S(2)}, u32[]{:S(2)}) collective-permute-start(bf16[2,4,72,1152]{3,2,1,0:T(8,128)(2,1)S(1)} %pad_maximum_fusion.51), channel_id=1, source_target_pairs={{0,2},{2,0},{4,6},{6,4},{8,10},{10,8},{12,14},{14,12},{1,3},{3,1},... | collective-permute-start | bytes 3981320 | tf_op jit(solution)/shard_map/ppermute | solution.py:29
  308.1 43.7 %collective-permute-start.31 = (bf16[576,1152]{1,0:T(8,128)(2,1)S(1)}, bf16[576,1152]{1,0:T(8,128)(2,1)}, u32[]{:S(2)}, u32[]{:S(2)}) collective-permute-start(bf16[576,1152]{1,0:T(8,128)(2,1)S(1)} %bitcast.1443), channel_id=1, source_target_pairs={{0,1},{1,0},{2,3},{3,2},{4,5},{5,4},{6,7},{7,6},{8,9},{9,8},{10,11... | collective-permute-start | bytes 3981320 | tf_op jit(solution)/shard_map/ppermute | solution.py:29
  351.8 52.7 %collective-permute-start.45 = (bf16[72,2304]{1,0:T(8,128)(2,1)}, bf16[72,2304]{1,0:T(8,128)(2,1)}, u32[]{:S(2)}, u32[]{:S(2)}) collective-permute-start(bf16[72,2304]{1,0:T(8,128)(2,1)} %get-tuple-element.206), channel_id=1, source_target_pairs={{0,12},{2,14},{4,8},{6,10},{8,4},{10,6},{12,0},{14,2},{1,13},{3,15... | collective-permute-start | bytes 995336 | tf_op jit(solution)/shard_map/ppermute | solution.py:29
  352.8 52.7 %collective-permute-start.44 = (bf16[72,2304]{1,0:T(8,128)(2,1)}, bf16[72,2304]{1,0:T(8,128)(2,1)}, u32[]{:S(2)}, u32[]{:S(2)}) collective-permute-start(bf16[72,2304]{1,0:T(8,128)(2,1)} %get-tuple-element.206), channel_id=1, source_target_pairs={{0,8},{2,10},{4,12},{6,14},{8,0},{10,2},{12,4},{14,6},{1,9},{3,11}... | collective-permute-start | bytes 995336 | tf_op jit(solution)/shard_map/ppermute | solution.py:29
  353.3 53.9 %collective-permute-start.43 = (bf16[72,2304]{1,0:T(8,128)(2,1)}, bf16[72,2304]{1,0:T(8,128)(2,1)}, u32[]{:S(2)}, u32[]{:S(2)}) collective-permute-start(bf16[72,2304]{1,0:T(8,128)(2,1)} %get-tuple-element.206), channel_id=1, source_target_pairs={{0,4},{2,6},{4,0},{6,2},{8,12},{10,14},{12,8},{14,10},{1,5},{3,7},... | collective-permute-start | bytes 995336 | tf_op jit(solution)/shard_map/ppermute | solution.py:29
  367.5 40.3 %collective-permute-start.42 = (bf16[4,72,1152]{2,1,0:T(8,128)(2,1)}, bf16[4,72,1152]{2,1,0:T(8,128)(2,1)}, u32[]{:S(2)}, u32[]{:S(2)}) collective-permute-start(bf16[4,72,1152]{2,1,0:T(8,128)(2,1)} %fusion.179), channel_id=1, source_target_pairs={{0,1},{1,0},{2,3},{3,2},{4,5},{5,4},{6,7},{7,6},{8,9},{9,8},{10,11... | collective-permute-start | bytes 1990664 | tf_op jit(solution)/shard_map/ppermute | solution.py:29
  407.2 42.0 %collective-permute-start.47 = (bf16[4,4,1,16,1152]{4,3,1,0,2:T(8,128)(2,1)S(1)}, bf16[4,4,1,16,1152]{4,3,1,0,2:T(8,128)(2,1)S(1)}, u32[]{:S(2)}, u32[]{:S(2)}) collective-permute-start(bf16[4,4,1,16,1152]{4,3,1,0,2:T(8,128)(2,1)S(1)} %get-tuple-element.485), channel_id=1, source_target_pairs={{0,2},{1,3},{2,0},{3,1},{4,6},{5,7},{6,4},{7,5},{8,10},{9,11},{10,... | collective-permute-start | bytes 1769480 | tf_op jit(solution)/shard_map/ppermute | solution.py:430
  407.8 53.0 %collective-permute-start.46 = (bf16[4,4,1,16,1152]{4,3,1,0,2:T(8,128)(2,1)S(1)}, bf16[4,4,1,16,1152]{4,3,1,0,2:T(8,128)(2,1)S(1)}, u32[]{:S(2)}, u32[]{:S(2)}) collective-permute-start(bf16[4,4,1,16,1152]{4,3,1,0,2:T(8,128)(2,1)S(1)} %get-tuple-element.486), channel_id=1, source_target_pairs={{0,1},{1,0},{2,3},{3,2},{4,5},{5,4},{6,7},{7,6},{8,9},{9,8},{10,11... | collective-permute-start | bytes 1769480 | tf_op jit(solution)/shard_map/ppermute | solution.py:430
  409.0 53.2 %collective-permute-start.48 = (bf16[4,4,1,16,1152]{4,3,1,0,2:T(8,128)(2,1)S(1)}, bf16[4,4,1,16,1152]{4,3,1,0,2:T(8,128)(2,1)S(1)}, u32[]{:S(2)}, u32[]{:S(2)}) collective-permute-start(bf16[4,4,1,16,1152]{4,3,1,0,2:T(8,128)(2,1)S(1)} %get-tuple-element.487), channel_id=1, source_target_pairs={{0,3},{1,2},{2,1},{3,0},{4,7},{5,6},{6,5},{7,4},{8,11},{9,10},{10,... | collective-permute-start | bytes 1769480 | tf_op jit(solution)/shard_map/ppermute | solution.py:430
  436.6 50.6 %collective-permute-start.56 = (bf16[4,4,2,1,16,1152]{5,4,1,2,0,3:T(8,128)(2,1)S(1)}, bf16[4,4,2,1,16,1152]{5,4,1,2,0,3:T(8,128)(2,1)S(1)}, u32[]{:S(2)}, u32[]{:S(2)}) collective-permute-start(bf16[4,4,2,1,16,1152]{5,4,1,2,0,3:T(8,128)(2,1)S(1)} %copy-done.164), channel_id=1, source_target_pairs={{0,2},{1,3},{2,0},{3,1},{4,6},{5,7},{6,4},{7,5},{8,10},{9,11},{10,... | collective-permute-start | bytes 3538952 | tf_op jit(solution)/shard_map/ppermute | solution.py:430
  465.7 40.9 %collective-permute-start.54 = (bf16[4,4,1,16,1152]{4,3,1,0,2:T(8,128)(2,1)S(1)}, bf16[4,4,1,16,1152]{4,3,1,0,2:T(8,128)(2,1)S(1)}, u32[]{:S(2)}, u32[]{:S(2)}) collective-permute-start(bf16[4,4,1,16,1152]{4,3,1,0,2:T(8,128)(2,1)S(1)} %pad_maximum_fusion.100), channel_id=1, source_target_pairs={{0,8},{2,10},{4,12},{6,14},{8,0},{10,2},{12,4},{14,6},{1,9},{3,11}... | collective-permute-start | bytes 1769480 | tf_op jit(solution)/shard_map/ppermute | solution.py:29
  475.0 53.8 %collective-permute-start.50 = (bf16[2,4,72,1152]{3,2,1,0:T(8,128)(2,1)S(1)}, bf16[2,4,72,1152]{3,2,1,0:T(8,128)(2,1)S(1)}, u32[]{:S(2)}, u32[]{:S(2)}) collective-permute-start(bf16[2,4,72,1152]{3,2,1,0:T(8,128)(2,1)S(1)} %pad_maximum_fusion.55), channel_id=1, source_target_pairs={{0,2},{2,0},{4,6},{6,4},{8,10},{10,8},{12,14},{14,12},{1,3},{3,1},... | collective-permute-start | bytes 3981320 | tf_op jit(solution)/shard_map/ppermute | solution.py:29
  476.5 52.2 %collective-permute-start.49 = (bf16[576,1152]{1,0:T(8,128)(2,1)S(1)}, bf16[576,1152]{1,0:T(8,128)(2,1)S(1)}, u32[]{:S(2)}, u32[]{:S(2)}) collective-permute-start(bf16[576,1152]{1,0:T(8,128)(2,1)S(1)} %bitcast.1451), channel_id=1, source_target_pairs={{0,1},{1,0},{2,3},{3,2},{4,5},{5,4},{6,7},{7,6},{8,9},{9,8},{10,11... | collective-permute-start | bytes 3981320 | tf_op jit(solution)/shard_map/ppermute | solution.py:29
  510.1 46.0 %collective-permute-start.57 = (bf16[576,4608]{1,0:T(8,128)(2,1)}, bf16[576,4608]{1,0:T(8,128)(2,1)}, u32[]{:S(2)}, u32[]{:S(2)}) collective-permute-start(bf16[576,4608]{1,0:T(8,128)(2,1)} %pad_maximum_fusion.9), channel_id=1, source_target_pairs={{0,16},{16,0},{1,17},{17,1},{2,18},{18,2},{3,19},{19,3},{4,20},{20... | collective-permute-start | bytes 15925256 | tf_op jit(solution)/shard_map/ppermute | solution.py:29
  536.1 85.3 %collective-permute-start.60 = (bf16[4,2,2,1,16,1152]{5,4,1,2,0,3:T(8,128)(2,1)}, bf16[4,2,2,1,16,1152]{5,4,1,2,0,3:T(8,128)(2,1)}, u32[]{:S(2)}, u32[]{:S(2)}) collective-permute-start(bf16[4,2,2,1,16,1152]{5,4,1,2,0,3:T(8,128)(2,1)} %pad_maximum_fusion.102), channel_id=1, source_target_pairs={{0,4},{2,6},{4,0},{6,2},{8,12},{10,14},{12,8},{14,10},{1,5},{3,7},... | collective-permute-start | bytes 1769480 | tf_op jit(solution)/shard_map/ppermute | solution.py:29
  537.0 84.5 %collective-permute-start.61 = (bf16[4,2,2,1,16,1152]{5,4,1,2,0,3:T(8,128)(2,1)}, bf16[4,2,2,1,16,1152]{5,4,1,2,0,3:T(8,128)(2,1)}, u32[]{:S(2)}, u32[]{:S(2)}) collective-permute-start(bf16[4,2,2,1,16,1152]{5,4,1,2,0,3:T(8,128)(2,1)} %pad_maximum_fusion.103), channel_id=1, source_target_pairs={{0,8},{2,10},{4,12},{6,14},{8,0},{10,2},{12,4},{14,6},{1,9},{3,11}... | collective-permute-start | bytes 1769480 | tf_op jit(solution)/shard_map/ppermute | solution.py:29
  539.4 82.1 %collective-permute-start.62 = (bf16[4,2,2,1,16,1152]{5,4,1,2,0,3:T(8,128)(2,1)}, bf16[4,2,2,1,16,1152]{5,4,1,2,0,3:T(8,128)(2,1)}, u32[]{:S(2)}, u32[]{:S(2)}) collective-permute-start(bf16[4,2,2,1,16,1152]{5,4,1,2,0,3:T(8,128)(2,1)} %pad_maximum_fusion.104), channel_id=1, source_target_pairs={{0,12},{2,14},{4,8},{6,10},{8,4},{10,6},{12,0},{14,2},{1,13},{3,15... | collective-permute-start | bytes 1769480 | tf_op jit(solution)/shard_map/ppermute | solution.py:29
  547.1 74.4 %collective-permute-start.59 = (bf16[2,4,72,1152]{3,2,1,0:T(8,128)(2,1)}, bf16[2,4,72,1152]{3,2,1,0:T(8,128)(2,1)}, u32[]{:S(2)}, u32[]{:S(2)}) collective-permute-start(bf16[2,4,72,1152]{3,2,1,0:T(8,128)(2,1)} %pad_maximum_fusion.57), channel_id=1, source_target_pairs={{0,2},{2,0},{4,6},{6,4},{8,10},{10,8},{12,14},{14,12},{1,3},{3,1},... | collective-permute-start | bytes 3981320 | tf_op jit(solution)/shard_map/ppermute | solution.py:29
  556.0 65.5 %collective-permute-start.58 = (bf16[576,1152]{1,0:T(8,128)(2,1)}, bf16[576,1152]{1,0:T(8,128)(2,1)}, u32[]{:S(2)}, u32[]{:S(2)}) collective-permute-start(bf16[576,1152]{1,0:T(8,128)(2,1)} %bitcast.286), channel_id=1, source_target_pairs={{0,1},{1,0},{2,3},{3,2},{4,5},{5,4},{6,7},{7,6},{8,9},{9,8},{10,11... | collective-permute-start | bytes 3981320 | tf_op jit(solution)/shard_map/ppermute | solution.py:29
  621.4 51.3 %collective-permute-start.63 = (bf16[576,4608]{1,0:T(8,128)(2,1)}, bf16[576,4608]{1,0:T(8,128)(2,1)}, u32[]{:S(2)}, u32[]{:S(2)}) collective-permute-start(bf16[576,4608]{1,0:T(8,128)(2,1)} %pad_maximum_fusion.10), channel_id=1, source_target_pairs={{0,16},{16,0},{1,17},{17,1},{2,18},{18,2},{3,19},{19,3},{4,20},{20... | collective-permute-start | bytes 15925256 | tf_op jit(solution)/shard_map/ppermute | solution.py:29
  667.8 53.8 %collective-permute-start.64 = (bf16[576,4608]{1,0:T(8,128)(2,1)S(1)}, bf16[576,4608]{1,0:T(8,128)(2,1)}, u32[]{:S(2)}, u32[]{:S(2)}) collective-permute-start(bf16[576,4608]{1,0:T(8,128)(2,1)S(1)} %pad_maximum_fusion.11), channel_id=1, source_target_pairs={{0,16},{16,0},{1,17},{17,1},{2,18},{18,2},{3,19},{19,3},{4,20},{20... | collective-permute-start | bytes 15925256 | tf_op jit(solution)/shard_map/ppermute | solution.py:29
  713.1 85.6 %collective-permute-start.66 = (bf16[576,4608]{1,0:T(8,128)(2,1)}, bf16[576,4608]{1,0:T(8,128)(2,1)}, u32[]{:S(2)}, u32[]{:S(2)}) collective-permute-start(bf16[576,4608]{1,0:T(8,128)(2,1)} %convolution_convert_fusion.3), channel_id=1, source_target_pairs={{0,16},{16,0},{1,17},{17,1},{2,18},{18,2},{3,19},{19,3},{4,20},{20... | collective-permute-start | bytes 15925256 | tf_op jit(solution)/shard_map/ppermute | solution.py:29
  759.2 39.5 %collective-permute-start.65 = (bf16[4,4,2,1,16,1152]{5,4,2,1,0,3:T(8,128)(2,1)}, bf16[4,4,2,1,16,1152]{5,4,2,1,0,3:T(8,128)(2,1)}, u32[]{:S(2)}, u32[]{:S(2)}) collective-permute-start(bf16[4,4,2,1,16,1152]{5,4,2,1,0,3:T(8,128)(2,1)} %get-tuple-element.465), channel_id=1, source_target_pairs={{0,2},{1,3},{2,0},{3,1},{4,6},{5,7},{6,4},{7,5},{8,10},{9,11},{10,... | collective-permute-start | bytes 3538952 | tf_op jit(solution)/shard_map/ppermute | solution.py:430
  803.4 54.8 %collective-permute-start.68 = (bf16[4,2,2,1,16,1152]{5,4,2,1,0,3:T(8,128)(2,1)}, bf16[4,2,2,1,16,1152]{5,4,2,1,0,3:T(8,128)(2,1)}, u32[]{:S(2)}, u32[]{:S(2)}) collective-permute-start(bf16[4,2,2,1,16,1152]{5,4,2,1,0,3:T(8,128)(2,1)} %pad_maximum_fusion.106), channel_id=1, source_target_pairs={{0,8},{2,10},{4,12},{6,14},{8,0},{10,2},{12,4},{14,6},{1,9},{3,11}... | collective-permute-start | bytes 1769480 | tf_op jit(solution)/shard_map/ppermute | solution.py:29
  805.8 52.4 %collective-permute-start.69 = (bf16[4,2,2,1,16,1152]{5,4,2,1,0,3:T(8,128)(2,1)}, bf16[4,2,2,1,16,1152]{5,4,2,1,0,3:T(8,128)(2,1)}, u32[]{:S(2)}, u32[]{:S(2)}) collective-permute-start(bf16[4,2,2,1,16,1152]{5,4,2,1,0,3:T(8,128)(2,1)} %pad_maximum_fusion.107), channel_id=1, source_target_pairs={{0,12},{2,14},{4,8},{6,10},{8,4},{10,6},{12,0},{14,2},{1,13},{3,15... | collective-permute-start | bytes 1769480 | tf_op jit(solution)/shard_map/ppermute | solution.py:29
  816.9 48.6 %collective-permute-start.72 = (bf16[576,4608]{1,0:T(8,128)(2,1)}, bf16[576,4608]{1,0:T(8,128)(2,1)}, u32[]{:S(2)}, u32[]{:S(2)}) collective-permute-start(bf16[576,4608]{1,0:T(8,128)(2,1)} %convolution_convert_fusion.2), channel_id=1, source_target_pairs={{0,16},{16,0},{1,17},{17,1},{2,18},{18,2},{3,19},{19,3},{4,20},{20... | collective-permute-start | bytes 15925256 | tf_op jit(solution)/shard_map/ppermute | solution.py:29
  952.1 44.7 %collective-permute-start.82 = (bf16[4,72,1152]{2,1,0:T(8,128)(2,1)S(1)}, bf16[4,72,1152]{2,1,0:T(8,128)(2,1)S(1)}, u32[]{:S(2)}, u32[]{:S(2)}) collective-permute-start(bf16[4,72,1152]{2,1,0:T(8,128)(2,1)S(1)} %split.82), channel_id=1, source_target_pairs={{0,1},{1,0},{2,3},{3,2},{4,5},{5,4},{6,7},{7,6},{8,9},{9,8},{10,11... | collective-permute-start | bytes 1990664 | tf_op jit(solution)/shard_map/ppermute | solution.py:29
  953.3 43.5 %collective-permute-start.81 = (bf16[4,72,1152]{2,1,0:T(8,128)(2,1)S(1)}, bf16[4,72,1152]{2,1,0:T(8,128)(2,1)S(1)}, u32[]{:S(2)}, u32[]{:S(2)}) collective-permute-start(bf16[4,72,1152]{2,1,0:T(8,128)(2,1)S(1)} %dynamic-slice_bitcast_fusion.8), channel_id=1, source_target_pairs={{0,2},{2,0},{4,6},{6,4},{8,10},{10,8},{12,14},{14,12},{1,3},{3,1},... | collective-permute-start | bytes 1990664 | tf_op jit(solution)/shard_map/ppermute | solution.py:29
  954.3 42.5 %collective-permute-start.84 = (bf16[4,72,640]{2,1,0:T(8,128)(2,1)S(1)}, bf16[4,72,640]{2,1,0:T(8,128)(2,1)S(1)}, u32[]{:S(2)}, u32[]{:S(2)}) collective-permute-start(bf16[4,72,640]{2,1,0:T(8,128)(2,1)S(1)} %dynamic-slice_bitcast_fusion.13), channel_id=1, source_target_pairs={{0,2},{2,0},{4,6},{6,4},{8,10},{10,8},{12,14},{14,12},{1,3},{3,1},... | collective-permute-start | bytes 1105928 | tf_op jit(solution)/shard_map/ppermute | solution.py:29
  1034.7 68.4 %collective-permute-start.91 = (bf16[576,1728]{1,0:T(8,128)(2,1)}, bf16[576,1728]{1,0:T(8,128)(2,1)S(1)}, u32[]{:S(2)}, u32[]{:S(2)}) collective-permute-start(bf16[576,1728]{1,0:T(8,128)(2,1)} %convolution_convert_fusion.14), channel_id=1, source_target_pairs={{0,16},{16,0},{1,17},{17,1},{2,18},{18,2},{3,19},{19,3},{4,20},{20... | collective-permute-start | bytes 5971976 | tf_op jit(solution)/shard_map/ppermute | solution.py:29
  1041.5 61.6 %collective-permute-start.90 = (bf16[576,1728]{1,0:T(8,128)(2,1)S(1)}, bf16[576,1728]{1,0:T(8,128)(2,1)S(1)}, u32[]{:S(2)}, u32[]{:S(2)}) collective-permute-start(bf16[576,1728]{1,0:T(8,128)(2,1)S(1)} %copy-done.248), channel_id=1, source_target_pairs={{0,16},{16,0},{1,17},{17,1},{2,18},{18,2},{3,19},{19,3},{4,20},{20... | collective-permute-start | bytes 5971976 | tf_op jit(solution)/shard_map/ppermute | solution.py:29
  1115.6 45.6 %collective-permute-start.98 = (bf16[576,768]{1,0:T(8,128)(2,1)S(1)}, bf16[576,768]{1,0:T(8,128)(2,1)S(1)}, u32[]{:S(2)}, u32[]{:S(2)}) collective-permute-start(bf16[576,768]{1,0:T(8,128)(2,1)S(1)} %slice.1543), channel_id=1, source_target_pairs={{0,1},{1,0},{2,3},{3,2},{4,5},{5,4},{6,7},{7,6},{8,9},{9,8},{10,11... | collective-permute-start | bytes 2654216 | tf_op jit(solution)/shard_map/ppermute | solution.py:29
  1117.8 43.4 %collective-permute-start.99 = (bf16[4,72,1920]{2,1,0:T(8,128)(2,1)S(1)}, bf16[4,72,1920]{2,1,0:T(8,128)(2,1)S(1)}, u32[]{:S(2)}, u32[]{:S(2)}) collective-permute-start(bf16[4,72,1920]{2,1,0:T(8,128)(2,1)S(1)} %dynamic-slice_bitcast_fusion.5), channel_id=1, source_target_pairs={{0,2},{2,0},{4,6},{6,4},{8,10},{10,8},{12,14},{14,12},{1,3},{3,1},... | collective-permute-start | bytes 3317768 | tf_op jit(solution)/shard_map/ppermute | solution.py:29
  1118.7 42.4 %collective-permute-start.101 = (bf16[4,4,1,16,1152]{4,3,1,0,2:T(8,128)(2,1)S(1)}, bf16[4,4,1,16,1152]{4,3,1,0,2:T(8,128)(2,1)S(1)}, u32[]{:S(2)}, u32[]{:S(2)}) collective-permute-start(bf16[4,4,1,16,1152]{4,3,1,0,2:T(8,128)(2,1)S(1)} %pad_maximum_fusion.109), channel_id=1, source_target_pairs={{0,8},{2,10},{4,12},{6,14},{8,0},{10,2},{12,4},{14,6},{1,9},{3,11}... | collective-permute-start | bytes 1769480 | tf_op jit(solution)/shard_map/ppermute | solution.py:29
  1120.8 40.4 %collective-permute-start.102 = (bf16[4,4,1,16,1152]{4,3,1,0,2:T(8,128)(2,1)S(1)}, bf16[4,4,1,16,1152]{4,3,1,0,2:T(8,128)(2,1)S(1)}, u32[]{:S(2)}, u32[]{:S(2)}) collective-permute-start(bf16[4,4,1,16,1152]{4,3,1,0,2:T(8,128)(2,1)S(1)} %pad_maximum_fusion.110), channel_id=1, source_target_pairs={{0,12},{2,14},{4,8},{6,10},{8,4},{10,6},{12,0},{14,2},{1,13},{3,15... | collective-permute-start | bytes 1769480 | tf_op jit(solution)/shard_map/ppermute | solution.py:29
  1162.8 55.4 %collective-permute-start.103 = (bf16[4,72,768]{2,1,0:T(8,128)(2,1)}, bf16[4,72,768]{2,1,0:T(8,128)(2,1)}, u32[]{:S(2)}, u32[]{:S(2)}) collective-permute-start(bf16[4,72,768]{2,1,0:T(8,128)(2,1)} %dynamic-slice_bitcast_fusion.11), channel_id=1, source_target_pairs={{0,2},{2,0},{4,6},{6,4},{8,10},{10,8},{12,14},{14,12},{1,3},{3,1},... | collective-permute-start | bytes 1327112 | tf_op jit(solution)/shard_map/ppermute | solution.py:29
  1165.6 52.6 %collective-permute-start.104 = (bf16[4,72,960]{2,1,0:T(8,128)(2,1)}, bf16[4,72,960]{2,1,0:T(8,128)(2,1)}, u32[]{:S(2)}, u32[]{:S(2)}) collective-permute-start(bf16[4,72,960]{2,1,0:T(8,128)(2,1)} %split.86), channel_id=1, source_target_pairs={{0,1},{1,0},{2,3},{3,2},{4,5},{5,4},{6,7},{7,6},{8,9},{9,8},{10,11... | collective-permute-start | bytes 1658888 | tf_op jit(solution)/shard_map/ppermute | solution.py:29
  1180.5 37.7 %collective-permute-start.105 = (bf16[576,4608]{1,0:T(8,128)(2,1)}, bf16[576,4608]{1,0:T(8,128)(2,1)}, u32[]{:S(2)}, u32[]{:S(2)}) collective-permute-start(bf16[576,4608]{1,0:T(8,128)(2,1)} %convolution_convert_fusion.1), channel_id=1, source_target_pairs={{0,16},{16,0},{1,17},{17,1},{2,18},{18,2},{3,19},{19,3},{4,20},{20... | collective-permute-start | bytes 15925256 | tf_op jit(solution)/shard_map/ppermute | solution.py:29
  1237.2 44.3 %collective-permute-start.106 = (bf16[72,1728]{1,0:T(8,128)(2,1)}, bf16[72,1728]{1,0:T(8,128)(2,1)}, u32[]{:S(2)}, u32[]{:S(2)}) collective-permute-start(bf16[72,1728]{1,0:T(8,128)(2,1)} %get-tuple-element.548), channel_id=1, source_target_pairs={{0,4},{2,6},{4,0},{6,2},{8,12},{10,14},{12,8},{14,10},{1,5},{3,7},... | collective-permute-start | bytes 746504 | tf_op jit(solution)/shard_map/ppermute | solution.py:29
  1313.2 44.4 %collective-permute-start.115 = (bf16[4,72,2304]{2,1,0:T(8,128)(2,1)S(1)}, bf16[4,72,2304]{2,1,0:T(8,128)(2,1)}, u32[]{:S(2)}, u32[]{:S(2)}) collective-permute-start(bf16[4,72,2304]{2,1,0:T(8,128)(2,1)S(1)} %dynamic-slice_bitcast_fusion), channel_id=1, source_target_pairs={{0,2},{2,0},{4,6},{6,4},{8,10},{10,8},{12,14},{14,12},{1,3},{3,1},... | collective-permute-start | bytes 3981320 | tf_op jit(solution)/shard_map/ppermute | solution.py:29
  1314.1 43.5 %collective-permute-start.114 = (bf16[576,1152]{1,0:T(8,128)(2,1)}, bf16[576,1152]{1,0:T(8,128)(2,1)}, u32[]{:S(2)}, u32[]{:S(2)}) collective-permute-start(bf16[576,1152]{1,0:T(8,128)(2,1)} %get-tuple-element.393), channel_id=1, source_target_pairs={{0,1},{1,0},{2,3},{3,2},{4,5},{5,4},{6,7},{7,6},{8,9},{9,8},{10,11... | collective-permute-start | bytes 3981320 | tf_op jit(solution)/shard_map/ppermute | solution.py:29
  1369.0 45.0 %collective-permute-start.121 = (bf16[4,72,1152]{2,1,0:T(8,128)(2,1)S(1)}, bf16[4,72,1152]{2,1,0:T(8,128)(2,1)S(1)}, u32[]{:S(2)}, u32[]{:S(2)}) collective-permute-start(bf16[4,72,1152]{2,1,0:T(8,128)(2,1)S(1)} %split.90), channel_id=1, source_target_pairs={{0,1},{1,0},{2,3},{3,2},{4,5},{5,4},{6,7},{7,6},{8,9},{9,8},{10,11... | collective-permute-start | bytes 1990664 | tf_op jit(solution)/shard_map/ppermute | solution.py:29
  1370.0 44.0 %collective-permute-start.120 = (bf16[4,72,1152]{2,1,0:T(8,128)(2,1)S(1)}, bf16[4,72,1152]{2,1,0:T(8,128)(2,1)S(1)}, u32[]{:S(2)}, u32[]{:S(2)}) collective-permute-start(bf16[4,72,1152]{2,1,0:T(8,128)(2,1)S(1)} %dynamic-slice_bitcast_fusion.6), channel_id=1, source_target_pairs={{0,2},{2,0},{4,6},{6,4},{8,10},{10,8},{12,14},{14,12},{1,3},{3,1},... | collective-permute-start | bytes 1990664 | tf_op jit(solution)/shard_map/ppermute | solution.py:29
  1371.2 42.8 %collective-permute-start.123 = (bf16[4,72,640]{2,1,0:T(8,128)(2,1)S(1)}, bf16[4,72,640]{2,1,0:T(8,128)(2,1)S(1)}, u32[]{:S(2)}, u32[]{:S(2)}) collective-permute-start(bf16[4,72,640]{2,1,0:T(8,128)(2,1)S(1)} %dynamic-slice_bitcast_fusion.12), channel_id=1, source_target_pairs={{0,2},{2,0},{4,6},{6,4},{8,10},{10,8},{12,14},{14,12},{1,3},{3,1},... | collective-permute-start | bytes 1105928 | tf_op jit(solution)/shard_map/ppermute | solution.py:29
  1376.1 37.9 %collective-permute-start.117 = (bf16[72,2304]{1,0:T(8,128)(2,1)S(1)}, bf16[72,2304]{1,0:T(8,128)(2,1)S(1)}, u32[]{:S(2)}, u32[]{:S(2)}) collective-permute-start(bf16[72,2304]{1,0:T(8,128)(2,1)S(1)} %get-tuple-element.506), channel_id=1, source_target_pairs={{0,4},{2,6},{4,0},{6,2},{8,12},{10,14},{12,8},{14,10},{1,5},{3,7},... | collective-permute-start | bytes 995336 | tf_op jit(solution)/shard_map/ppermute | solution.py:29
  1446.0 75.5 %collective-permute-start.142 = (bf16[72,2304]{1,0:T(8,128)(2,1)}, bf16[72,2304]{1,0:T(8,128)(2,1)}, u32[]{:S(2)}, u32[]{:S(2)}) collective-permute-start(bf16[72,2304]{1,0:T(8,128)(2,1)} %get-tuple-element.500), channel_id=1, source_target_pairs={{0,12},{2,14},{4,8},{6,10},{8,4},{10,6},{12,0},{14,2},{1,13},{3,15... | collective-permute-start | bytes 995336 | tf_op jit(solution)/shard_map/ppermute | solution.py:29
  1448.4 89.8 %collective-permute-start.146 = (bf16[576,1728]{1,0:T(8,128)(2,1)}, bf16[576,1728]{1,0:T(8,128)(2,1)}, u32[]{:S(2)}, u32[]{:S(2)}) collective-permute-start(bf16[576,1728]{1,0:T(8,128)(2,1)} %convolution_convert_fusion.12), channel_id=1, source_target_pairs={{0,16},{16,0},{1,17},{17,1},{2,18},{18,2},{3,19},{19,3},{4,20},{20... | collective-permute-start | bytes 5971976 | tf_op jit(solution)/shard_map/ppermute | solution.py:29
  1477.7 41.1 %collective-permute-start.143 = (bf16[4,72,256]{2,1,0:T(8,128)(2,1)}, bf16[4,72,256]{2,1,0:T(8,128)(2,1)}, u32[]{:S(2)}, u32[]{:S(2)}) collective-permute-start(bf16[4,72,256]{2,1,0:T(8,128)(2,1)} %dynamic-slice_bitcast_fusion.14), channel_id=1, source_target_pairs={{0,2},{2,0},{4,6},{6,4},{8,10},{10,8},{12,14},{14,12},{1,3},{3,1},... | collective-permute-start | bytes 442376 | tf_op jit(solution)/shard_map/ppermute | solution.py:29
  1479.8 40.5 %collective-permute-start.144 = (bf16[4,72,320]{2,1,0:T(8,128)(2,1)}, bf16[4,72,320]{2,1,0:T(8,128)(2,1)}, u32[]{:S(2)}, u32[]{:S(2)}) collective-permute-start(bf16[4,72,320]{2,1,0:T(8,128)(2,1)} %split.92), channel_id=1, source_target_pairs={{0,1},{1,0},{2,3},{3,2},{4,5},{5,4},{6,7},{7,6},{8,9},{9,8},{10,11... | collective-permute-start | bytes 552968 | tf_op jit(solution)/shard_map/ppermute | solution.py:29
  (377 other events, 4988.2 us)

commit v3 on v2

--- a/solution.py
+++ b/solution.py
@@ -98,10 +98,8 @@
         tp_got, side_got = yield got
         first = [block] + tp_got
         second = self.pair_stack(strips, side_got)
-        mine = jnp.concatenate(
-            [part for r in range(self.n_tp) for part in (first[r], second[r])], axis=1
-        )
-        return mine, self.over_core(mine)
+        mine = first + [second]
+        return mine + [self.over_core(v) for v in mine]
 
     def scatter_weight(self, left, rights):
         others = range(1, self.n_tp)
@@ -160,10 +158,11 @@
         self.tasks.append(task)
         return task
 
-    def fence(self, values=()):
-        values, pending = lax.optimization_barrier((values, [t.pending for t in self.tasks]))
-        going = []
-        for task, done in zip(self.tasks, pending):
+    def fence(self, values=(), but=()):
+        due = [t for t in self.tasks if t not in but]
+        values, pending = lax.optimization_barrier((values, [t.pending for t in due]))
+        going = [t for t in self.tasks if t in but]
+        for task, done in zip(due, pending):
             try:
                 task.pending = task.steps.send(done)
                 going.append(task)
@@ -309,6 +308,397 @@
     )(*xs, grad, lse)
 
 
+def weight_specs(pieces):
+    return [pl.BlockSpec(memory_space=pl.ANY)] * len(pieces)
+
+
+def weight_scratch(pieces):
+    strips = len(pieces) // 2 - 1
+    rows, half = pieces[0].shape
+    return [
+        pltpu.VMEM((2 * rows, strips * 2 * half), BF16),
+        pltpu.SemaphoreType.DMA((2, strips, 2)),
+    ]
+
+
+def weight_copies(refs, w_s, sems):
+    count = len(refs) // 2
+    copies = [([], []) for _ in range(count - 1)]
+    for group in range(2):
+        firsts, seconds = refs[group * count : group * count + count - 1], refs[group * count + count - 1]
+        for strip, first in enumerate(firsts):
+            rows, half = first.shape
+            for part, source in enumerate((first, seconds.at[strip])):
+                target = w_s.at[pl.ds(group * rows, rows), pl.ds((2 * strip + part) * half, half)]
+                copies[strip][part].append(
+                    pltpu.make_async_copy(source, target, sems.at[group, strip, part])
+                )
+    return copies
+
+
+def start_copies(copies):
+    for strip in copies:
+        for part in strip:
+            for copy in part:
+                copy.start()
+
+
+def await_copies(parts):
+    @pl.when(pl.program_id(0) == 0)
+    def _():
+        for part in parts:
+            for copy in part:
+                copy.wait()
+
+
+def turn_copies(parts, w_s, t_s):
+    @pl.when(pl.program_id(0) == 0)
+    def _():
+        low = 0
+        for part in parts:
+            for copy in part:
+                copy.wait()
+            size = w_s.shape[1] // len(parts)
+            t_s[low : low + size] = w_s[:, low : low + size].T
+            low += size
+
+
+def begin_copies(*many):
+    @pl.when(pl.program_id(0) == 0)
+    def _():
+        for copies in many:
+            start_copies(copies)
+
+
+def row_normal(v):
+    centred = v - jnp.mean(v, axis=-1, keepdims=True)
+    inverse = lax.rsqrt(jnp.mean(centred * centred, axis=-1, keepdims=True) + EPS)
+    return centred * inverse, inverse
+
+
+def row_back(grad, normed, inverse, scale):
+    scaled = grad * (1.0 + scale)
+    mean_one = jnp.mean(scaled, axis=-1, keepdims=True)
+    mean_two = jnp.mean(scaled * normed, axis=-1, keepdims=True)
+    return inverse * (scaled - mean_one - normed * mean_two)
+
+
+def head_forward(heads, first, rows, allowed, q_s, k_s, v_s, o_s, lane, logs):
+    for head in range(heads):
+        low, high = window(head)
+        mask = in_head(head, rows, low, high)
+        queries = jnp.where(mask, q_s[:, low:high], jnp.zeros((), BF16))
+        scores = dot(queries, k_s[:, low:high], NT) * SCALE
+        if allowed is not None:
+            scores = jnp.where(allowed, scores, -jnp.inf)
+        largest = jnp.max(scores, axis=-1, keepdims=True)
+        raised = jnp.exp(scores - largest)
+        total = jnp.sum(raised, axis=-1, keepdims=True)
+        chances = (raised * (1.0 / total)).astype(BF16)
+        result = dot(chances, v_s[:, low:high])
+        o_s[:, low:high] = jnp.where(mask, result, o_s[:, low:high])
+        logs = jnp.where(lane == first + head, largest + jnp.log(total), logs)
+    return logs
+
+
+def head_back(heads, first, rows, allowed, q_s, k_s, v_s, g_s, lse_ref, dq_s, dk_s, dv_s):
+    zero = jnp.zeros((), BF16)
+    for head in range(heads):
+        low, high = window(head)
+        mask = in_head(head, rows, low, high)
+        q, k, v, g = q_s[:, low:high], k_s[:, low:high], v_s[:, low:high], g_s[:, low:high]
+        scores = dot(jnp.where(mask, q, zero), k, NT) * SCALE
+        if allowed is not None:
+            scores = jnp.where(allowed, scores, -jnp.inf)
+        place = first + head
+        chances = jnp.exp(scores - lse_ref[:, place : place + 1])
+        grad_chances = dot(jnp.where(mask, g, zero), v, NT)
+        row_dot = jnp.sum(chances * grad_chances, axis=-1, keepdims=True)
+        grad_scores = (chances * (grad_chances - row_dot)).astype(BF16)
+        dq = dot(grad_scores, k) * SCALE
+        dk = dot(grad_scores, q, TN) * SCALE
+        dv = dot(chances.astype(BF16), g, TN)
+        dq_s[:, low:high] = jnp.where(mask, dq, dq_s[:, low:high])
+        dk_s[:, low:high] = jnp.where(mask, dk, dk_s[:, low:high])
+        dv_s[:, low:high] = jnp.where(mask, dv, dv_s[:, low:high])
+
+
+def branch_kernel(strips, stride, x_ref, mod_ref, *refs):
+    count = 2 * (strips + 1)
+    w_refs = refs[:count]
+    h_ref, qkv_ref, lse_ref, o_ref, a_ref, y_ref, g_ref = refs[count : count + 7]
+    w_s, sems, p_s, o_s, z_s = refs[count + 7 :]
+    rows, width = x_ref.shape
+    head_cols = width // strips
+    padded = o_s.shape[1]
+    spare = padded - head_cols
+    columns = w_s.shape[1] // strips
+    copies = weight_copies(w_refs, w_s, sems)
+    begin_copies(copies)
+    x = x_ref[...].astype(F32)
+    shift_a, scale_a, gate_a, shift_m, scale_m = [mod_ref[0, i : i + 1, :] for i in range(5)]
+    h = (row_normal(x)[0] * (1.0 + scale_a) + shift_a).astype(BF16)
+    h_ref[...] = h
+    heads = head_cols // HEAD_DIM
+    lane = lax.broadcasted_iota(jnp.int32, (rows, LANES), 1)
+    logs = jnp.zeros((rows, LANES), F32)
+    allowed = same_sequence(rows, stride) if stride > 1 else None
+    branch = jnp.zeros((rows, width), F32)
+    for strip in range(strips):
+        start = strip * columns
+        await_copies(copies[strip])
+        p_s[...] = dot(h, w_s[:, start : start + p_s.shape[1]]).astype(BF16)
+        parts = []
+        for index in range(3):
+            low = (3 * strip + index) * padded
+            if spare:
+                qkv_ref[:, low + padded - LANES : low + padded] = jnp.zeros((rows, LANES), BF16)
+            qkv_ref[:, low : low + head_cols] = p_s[:, index * head_cols : (index + 1) * head_cols]
+            parts.append(qkv_ref.at[:, pl.ds(low, padded)])
+        logs = head_forward(heads, strip * heads, rows, allowed, *parts, o_s, lane, logs)
+        low = o_s[:, :head_cols].astype(BF16)
+        o_ref[:, strip * head_cols : (strip + 1) * head_cols] = low
+        if spare:
+            z_s[:, :LANES] = jnp.zeros((rows, LANES), BF16)
+        z_s[:, spare:] = low
+        branch = branch + dot(z_s[...], w_s[:, start + columns - padded : start + columns], NT)
+    lse_ref[...] = logs
+    a_ref[...] = branch.astype(BF16)
+    y = x + gate_a * branch
+    y_ref[...] = y
+    g_ref[...] = (row_normal(y)[0] * (1.0 + scale_m) + shift_m).astype(BF16)
+
+
+def branch_back_kernel(strips, stride, x_ref, mod_ref, da_ref, dy_ref, qkv_ref, lse_ref, *refs):
+    count = 2 * (strips + 1)
+    w_refs = refs[:count]
+    dx_ref, sums_ref = refs[count : count + 2]
+    out_refs = refs[count + 2 : count + 2 + strips]
+    w_s, sems, d_s, g_s, dq_s, dk_s, dv_s = refs[count + 2 + strips :]
+    rows, width = x_ref.shape
+    head_cols = width // strips
+    padded = g_s.shape[1]
+    spare = padded - head_cols
+    columns = w_s.shape[1] // strips
+    copies = weight_copies(w_refs, w_s, sems)
+    begin_copies(copies)
+    heads = head_cols // HEAD_DIM
+    allowed = same_sequence(rows, stride) if stride > 1 else None
+    grad = jnp.zeros((rows, width), F32)
+    for strip in range(strips):
+        start = strip * columns
+        await_copies(copies[strip])
+        turned = dot(da_ref[...], w_s[:, start + columns - padded : start + columns]).astype(BF16)
+        if spare:
+            g_s[:, padded - LANES :] = jnp.zeros((rows, LANES), BF16)
+        g_s[:, :head_cols] = turned[:, spare:]
+        parts = [qkv_ref.at[:, pl.ds((3 * strip + i) * padded, padded)] for i in range(3)]
+        head_back(heads, strip * heads, rows, allowed, *parts, g_s, lse_ref, dq_s, dk_s, dv_s)
+        if d_s.shape[1] != 3 * head_cols:
+            d_s[:, d_s.shape[1] - LANES :] = jnp.zeros((rows, LANES), BF16)
+        for index, part in enumerate((dq_s, dk_s, dv_s)):
+            d_s[:, index * head_cols : (index + 1) * head_cols] = part[:, :head_cols].astype(BF16)
+        out_refs[strip][...] = d_s[:, : 3 * head_cols]
+        grad = grad + dot(d_s[...], w_s[:, start : start + d_s.shape[1]], NT)
+    scale_a = mod_ref[0, 1:2, :]
+    normed, inverse = row_normal(x_ref[...].astype(F32))
+    sums_ref[...] = jnp.zeros(sums_ref.shape, F32)
+    sums_ref[0, 0:1, :] = jnp.sum(grad, axis=0, keepdims=True)
+    sums_ref[0, 1:2, :] = jnp.sum(grad * normed, axis=0, keepdims=True)
+    dx_ref[...] = (dy_ref[...] + row_back(grad, normed, inverse, scale_a)).astype(BF16)
+
+
+GELU_A = 0.7978845608028654
+GELU_B = 0.044715
+
+
+def up_kernel(strips, g_ref, *refs):
+    count = 2 * (strips + 1)
+    z_ref, slope_ref, w_s, sems = refs[count:]
+    copies = weight_copies(refs[:count], w_s, sems)
+    begin_copies(copies)
+    half = w_s.shape[1] // (2 * strips)
+    g = g_ref[...]
+    for index in range(2 * strips):
+        await_copies([copies[index // 2][index % 2]])
+        low = index * half
+        u = dot(g, w_s[:, low : low + half])
+        square = u * u
+        bent = jnp.tanh(u * (GELU_A + GELU_A * GELU_B * square))
+        lifted = 0.5 * (1.0 + bent)
+        z_ref[:, low : low + half] = (u * lifted).astype(BF16)
+        inner = GELU_A + 3.0 * GELU_A * GELU_B * square
+        slope = lifted + 0.5 * u * (1.0 - bent * bent) * inner
+        slope_ref[:, low : low + half] = slope.astype(BF16)
+
+
+def down_kernel(strips, z_ref, y_ref, mod_ref, *refs):
+    count = 2 * (strips + 1)
+    m_ref, x_ref, w_s, sems, t_s = refs[count:]
+    copies = weight_copies(refs[:count], w_s, sems)
+    begin_copies(copies)
+    half = w_s.shape[1] // (2 * strips)
+    turn_copies([copies[i // 2][i % 2] for i in range(2 * strips)], w_s, t_s)
+    total = dot(z_ref[...], t_s[...])
+    m_ref[...] = total.astype(BF16)
+    x_ref[...] = (y_ref[...] + mod_ref[0, 5:6, :] * total).astype(BF16)
+
+
+def mlp_back_kernel(strips, dx_ref, mod_ref, m_ref, slope_ref, y_ref, a_ref, *refs):
+    count = 2 * (strips + 1)
+    dm_ref, du_ref, dy_ref, da_ref, sums_ref, up_s, up_sems, down_s, down_sems, t_s = refs[2 * count :]
+    ups = weight_copies(refs[:count], up_s, up_sems)
+    downs = weight_copies(refs[count : 2 * count], down_s, down_sems)
+    begin_copies(downs, ups)
+    half = up_s.shape[1] // (2 * strips)
+    turn_copies([ups[i // 2][i % 2] for i in range(2 * strips)], up_s, t_s)
+    scale_m, gate_m, share, gate_a = [mod_ref[0, i : i + 1, :] for i in (4, 5, 6, 2)]
+    dx = dx_ref[...].astype(F32) * share
+    sums_ref[...] = jnp.zeros(sums_ref.shape, F32)
+    sums_ref[0, 5:6, :] = jnp.sum(dx * m_ref[...].astype(F32), axis=0, keepdims=True)
+    dm = (gate_m * dx).astype(BF16)
+    dm_ref[...] = dm
+    grad = jnp.zeros(y_ref.shape, F32)
+    for index in range(2 * strips):
+        low = index * half
+        await_copies([downs[index // 2][index % 2]])
+        dz = dot(dm, down_s[:, low : low + half])
+        du = (dz * slope_ref[:, low : low + half].astype(F32)).astype(BF16)
+        du_ref[:, low : low + half] = du
+        grad = grad + dot(du, t_s[low : low + half])
+    normed, inverse = row_normal(y_ref[...])
+    sums_ref[0, 3:4, :] = jnp.sum(grad, axis=0, keepdims=True)
+    sums_ref[0, 4:5, :] = jnp.sum(grad * normed, axis=0, keepdims=True)
+    dy = dx + row_back(grad, normed, inverse, scale_m)
+    dy_ref[...] = dy
+    sums_ref[0, 2:3, :] = jnp.sum(dy * a_ref[...].astype(F32), axis=0, keepdims=True)
+    da_ref[...] = (gate_a * dy).astype(BF16)
+
+
+def shape_of(*dims, dtype=BF16):
+    return jax.ShapeDtypeStruct(dims, dtype)
+
+
+def block_call(kernel, clips, rows, arrays, mods, weights, outs, sums, scratch, flops, order):
+    operands, specs = [], []
+    for v in order:
+        if v is None:
+            operands.append(mods)
+            specs.append(pl.BlockSpec((1,) + mods.shape[1:], lambda i: (i, 0, 0)))
+        else:
+            operands.append(arrays[v])
+            specs.append(row_block(rows, arrays[v].shape[1]))
+    for pieces in weights:
+        operands += pieces
+        specs += weight_specs(pieces)
+    out_specs = [row_block(rows, v.shape[1]) for v in outs]
+    out_shape = list(outs)
+    if sums is not None:
+        width = mods.shape[2]
+        out_specs.insert(sums, pl.BlockSpec((1, 8, width), lambda i: (i, 0, 0)))
+        out_shape.insert(sums, shape_of(clips, 8, width, dtype=F32))
+    held = []
+    for pieces in weights:
+        held += weight_scratch(pieces)
+    moved = sum(v.size * v.dtype.itemsize for v in operands)
+    return pl.pallas_call(
+        kernel,
+        grid=(clips,),
+        in_specs=specs,
+        out_specs=out_specs,
+        out_shape=out_shape,
+        scratch_shapes=held + scratch,
+        cost_estimate=pl.CostEstimate(flops=flops, bytes_accessed=moved, transcendentals=0),
+        compiler_params=pltpu.CompilerParams(vmem_limit_bytes=60 * 1024 * 1024),
+    )(*operands)
+
+
+def padded_to(columns):
+    return -(-columns // LANES) * LANES
+
+
+def fused_branch(x, mods, pieces, clips, stride):
+    count, width = x.shape
+    rows, strips = count // clips, len(pieces) // 2 - 1
+    head_cols = width // strips
+    padded = padded_to(head_cols)
+    outs = [
+        shape_of(count, width),
+        shape_of(count, 3 * strips * padded),
+        shape_of(count, LANES, dtype=F32),
+        shape_of(count, width),
+        shape_of(count, width),
+        shape_of(count, width, dtype=F32),
+        shape_of(count, width),
+    ]
+    scratch = [
+        pltpu.VMEM((rows, padded_to(3 * head_cols)), BF16),
+        pltpu.VMEM((rows, padded), F32),
+        pltpu.VMEM((rows, padded), BF16),
+    ]
+    return block_call(
+        functools.partial(branch_kernel, strips, stride),
+        clips, rows, [x], mods, [pieces], outs, None, scratch,
+        12 * count * width * width, [0, None],
+    )
+
+
+def fused_branch_back(x, mods, da, dy, qkv, lse, pieces, clips, stride):
+    count, width = x.shape
+    rows, strips = count // clips, len(pieces) // 2 - 1
+    head_cols = width // strips
+    padded = padded_to(head_cols)
+    outs = [shape_of(count, width)] + [shape_of(count, 3 * head_cols) for _ in range(strips)]
+    scratch = [
+        pltpu.VMEM((rows, padded_to(3 * head_cols)), BF16),
+        pltpu.VMEM((rows, padded), BF16),
+    ] + [pltpu.VMEM((rows, padded), F32)] * 3
+    return block_call(
+        functools.partial(branch_back_kernel, strips, stride),
+        clips, rows, [x, da, dy, qkv, lse], mods, [pieces], outs, 1, scratch,
+        16 * count * width * width, [0, None, 1, 2, 3, 4],
+    )
+
+
+def fused_up(g, mods, pieces, clips):
+    count, width = g.shape
+    rows, strips = count // clips, len(pieces) // 2 - 1
+    units = strips * 2 * pieces[0].shape[1]
+    outs = [shape_of(count, units), shape_of(count, units)]
+    return block_call(
+        functools.partial(up_kernel, strips),
+        clips, rows, [g], mods, [pieces], outs, None, [], 2 * count * width * units, [0],
+    )
+
+
+def fused_down(z, y, mods, pieces, clips):
+    count, width = y.shape
+    rows, strips = count // clips, len(pieces) // 2 - 1
+    outs = [shape_of(count, width), shape_of(count, width)]
+    return block_call(
+        functools.partial(down_kernel, strips),
+        clips, rows, [z, y], mods, [pieces], outs, None, [pltpu.VMEM((z.shape[1], width), BF16)],
+        2 * z.size * width, [0, 1, None],
+    )
+
+
+def fused_mlp_back(dx, mods, m, slope, y, a, ups, downs, clips):
+    count, width = y.shape
+    rows, strips = count // clips, len(ups) // 2 - 1
+    outs = [
+        shape_of(count, width),
+        shape_of(*slope.shape),
+        shape_of(count, width, dtype=F32),
+        shape_of(count, width),
+    ]
+    return block_call(
+        functools.partial(mlp_back_kernel, strips),
+        clips, rows, [dx, m, slope, y, a], mods, [ups, downs], outs, 4,
+        [pltpu.VMEM((slope.shape[1], width), BF16)],
+        4 * slope.size * width, [0, None, 1, 2, 3, 4],
+    )
+
+
 def split_frames(v, frames, width):
     return v.reshape(frames, -1, width // HEAD_DIM, HEAD_DIM)
 
@@ -484,7 +874,13 @@
         return values
 
     def whole(index):
-        return jnp.concatenate(gathers[index].result, axis=0)
+        pieces = gathers[index].result
+        count = len(pieces) // 2
+        groups = []
+        for group in (pieces[:count], pieces[count:]):
+            strips = [v for r in range(n_tp) for v in (group[r], group[-1][r])]
+            groups.append(jnp.concatenate(strips, axis=1))
+        return jnp.concatenate(groups, axis=0)
 
     def attention_weights(index):
         v = whole(index)
@@ -498,93 +894,166 @@
     moved = lanes.start(to_frames(moves.halves(tokens)))
     gathers.append(lanes.start(moves.gather_weight(shards[0])))
     tick()
-    residual = moved.result.astype(F32)
+    residual = moved.result
     tick()
     tick()
-    records = []
-    for level in range(LAYERS):
-        spatial = level % 2 == 0
-        shift_a, scale_a, gate_a, shift_m, scale_m, gate_m = modulations(level)
-        normed = flat(modulate(residual, shift_a, scale_a))
-        qkvs, outs = attention_weights(3 * level)
-        projected = [dot(normed, v).astype(BF16) for v in qkvs]
-        rows, stride = (patches_here * spread_tp, 1) if spatial else (residual.shape[1], piece)
-        if spatial and not whole_frames:
-            saved = [attend_shared(v, clips * frames_here) for v in projected]
-            result = jnp.concatenate([entry[0] for entry in saved], axis=1)
-            saved = [entry[1] for entry in saved]
-        else:
-            result, saved = attend(projected, rows, stride)
-        result, saved = tick((result, saved))
-        branch = shaped(dot(result, outs, NT))
-        middle = residual + gate_a[:, None] * branch
-        normed_mlp = flat(modulate(middle, shift_m, scale_m))
-        up = whole(3 * level + 1)
-        pre_act = dot(normed_mlp, up)
-        act = gelu(pre_act).astype(BF16)
-        act, pre_act = tick((act, pre_act))
-        down = whole(3 * level + 2)
-        branch_mlp = shaped(dot(act, down, NT))
-        records.append(
-            (residual, normed, projected, saved, result, branch, middle, normed_mlp)
-            + (pre_act, act, branch_mlp, qkvs, outs, up, down, rows, stride)
-        )
-        residual = middle + gate_m[:, None] * branch_mlp
-        if spatial:
-            moved = lanes.start(frames_to_clips(residual.astype(BF16)))
-            tick()
-            turned = lanes.start(here_to_clips(moves.halves(cotangent)))
-            tick()
-            residual = moved.result.astype(F32)
+    fused = (
+        whole_frames
+        and head_cols % 32 == 0
+        and w_up.shape[2] % (2 * LANES) == 0
+        and 4 * head_cols == w_up.shape[2]
+        and width % 32 == 0
+    )
     matched = (micro_ids[:, None] == micro_ids[None, :]).astype(F32)
     share = 1.0 / jnp.sum(matched, axis=1)
-    gradient = turned.result.astype(F32) * share[:, None, None]
-    finished = lanes.start(clips_to_here(moves.halves(residual.astype(BF16))))
     scatters = {}
     mod_grads = [None] * LAYERS
-    for level in reversed(range(LAYERS)):
-        spatial = level % 2 == 0
-        (residual, normed, projected, saved, result, branch, middle, normed_mlp) = records[level][
-            :8
-        ]
-        (pre_act, act, branch_mlp, qkvs, outs, up, down, rows, stride) = records[level][8:]
-        shift_a, scale_a, gate_a, shift_m, scale_m, gate_m = modulations(level)
-        gate_m_grad = jnp.sum(gradient * branch_mlp, axis=1)
-        low_grad = flat((gradient * gate_m[:, None]).astype(BF16))
-        grad_pre = gelu_slope(pre_act, dot(low_grad, down)).astype(BF16)
-        scatters[level, "down"] = lanes.start(moves.scatter_weight(low_grad, [act]))
-        grad_pre = lanes.fence(grad_pre)
-        grad_normed = shaped(dot(grad_pre, up, NT))
-        scatters[level, "up"] = lanes.start(moves.scatter_weight(normed_mlp, [grad_pre]))
-        grad_normed = lanes.fence(grad_normed)
-        added, shift_m_grad, scale_m_grad = modulate_back(grad_normed, middle, scale_m)
-        gradient = gradient + added
-        gate_a_grad = jnp.sum(gradient * branch, axis=1)
-        low_grad = flat((gradient * gate_a[:, None]).astype(BF16))
-        grad_heads = dot(low_grad, outs).astype(BF16)
-        scatters[level, "out"] = lanes.start(moves.scatter_weight(low_grad, [result]))
-        grad_heads = lanes.fence(grad_heads)
-        if spatial and not whole_frames:
-            grad_qkv = [
-                attend_shared_back(v, g)
-                for v, g in zip(saved, jnp.split(grad_heads, n_tp, axis=1))
+
+    def start_scatter(level, name, left, rights):
+        scatters[level, name] = lanes.start(moves.scatter_weight(left, rights))
+
+    def fused_passes(v):
+        vectors, saved = [], []
+        for level in range(LAYERS):
+            last = share if level == LAYERS - 1 else jnp.ones_like(share)
+            last = jnp.broadcast_to(last[:, None, None], (clips, 2, width))
+            vectors.append(jnp.concatenate([mods[level], last], axis=1))
+        v = flat(v)
+        for level in range(LAYERS):
+            stride = piece if level % 2 else 1
+            joined = gathers[3 * level].result
+            kept = fused_branch(v, vectors[level], joined, clips, stride)
+            normed, qkv, lse, result, branch, middle, normed_mlp = tick(kept)
+            up = gathers[3 * level + 1].result
+            act, slope = tick(fused_up(normed_mlp, vectors[level], up, clips))
+            down = gathers[3 * level + 2].result
+            branch_mlp, after = fused_down(act, middle, vectors[level], down, clips)
+            saved.append((v, normed, qkv, lse, result, branch, middle, normed_mlp))
+            saved[-1] += (act, slope, branch_mlp, joined, up, down, stride)
+            v = after
+            if level == 0:
+                moved = lanes.start(frames_to_clips(shaped(v)))
+                tick()
+                turned = lanes.start(here_to_clips(moves.halves(cotangent)))
+                tick()
+                v = flat(moved.result)
+        finished = lanes.start(clips_to_here(moves.halves(shaped(v))))
+        grad = flat(turned.result)
+        for level in reversed(range(LAYERS)):
+            v, normed, qkv, lse, result, branch, middle, normed_mlp = saved[level][:8]
+            act, slope, branch_mlp, joined, up, down, stride = saved[level][8:]
+            back = fused_mlp_back(
+                grad, vectors[level], branch_mlp, slope, middle, branch, up, down, clips
+            )
+            grad_branch, grad_pre, grad_middle, grad_out, sums = lanes.fence(back)
+            start_scatter(level, "down", grad_branch, [act])
+            if level == 0:
+                start_scatter(level, "up", normed_mlp, [grad_pre])
+                grad_out = lanes.fence(grad_out)
+            back = fused_branch_back(
+                v, vectors[level], grad_out, grad_middle, qkv, lse, joined, clips, stride
+            )
+            grad, more, *grad_qkv = lanes.fence(back)
+            mod_grads[level] = (sums + more)[:, :6]
+            if level:
+                moved = lanes.start(clips_to_frames(shaped(grad)))
+                start_scatter(level, "up", normed_mlp, [grad_pre])
+                lanes.fence()
+                start_scatter(level, "out", grad_out, [result])
+                start_scatter(level, "qkv", normed, grad_qkv)
+                lanes.fence()
+                grad = flat(moved.result)
+            else:
+                start_scatter(level, "qkv", normed, grad_qkv)
+                start_scatter(level, "out", grad_out, [result])
+        return finished, shaped(grad)
+
+    def plain_passes(residual):
+        residual = residual.astype(F32)
+        records = []
+        for level in range(LAYERS):
+            spatial = level % 2 == 0
+            shift_a, scale_a, gate_a, shift_m, scale_m, gate_m = modulations(level)
+            normed = flat(modulate(residual, shift_a, scale_a))
+            qkvs, outs = attention_weights(3 * level)
+            projected = [dot(normed, v).astype(BF16) for v in qkvs]
+            rows, stride = (patches_here * spread_tp, 1) if spatial else (residual.shape[1], piece)
+            if spatial and not whole_frames:
+                saved = [attend_shared(v, clips * frames_here) for v in projected]
+                result = jnp.concatenate([entry[0] for entry in saved], axis=1)
+                saved = [entry[1] for entry in saved]
+            else:
+                result, saved = attend(projected, rows, stride)
+            result, saved = tick((result, saved))
+            branch = shaped(dot(result, outs, NT))
+            middle = residual + gate_a[:, None] * branch
+            normed_mlp = flat(modulate(middle, shift_m, scale_m))
+            up = whole(3 * level + 1)
+            pre_act = dot(normed_mlp, up)
+            act = gelu(pre_act).astype(BF16)
+            act, pre_act = tick((act, pre_act))
+            down = whole(3 * level + 2)
+            branch_mlp = shaped(dot(act, down, NT))
+            records.append(
+                (residual, normed, projected, saved, result, branch, middle, normed_mlp)
+                + (pre_act, act, branch_mlp, qkvs, outs, up, down, rows, stride)
+            )
+            residual = middle + gate_m[:, None] * branch_mlp
+            if spatial:
+                moved = lanes.start(frames_to_clips(residual.astype(BF16)))
+                tick()
+                turned = lanes.start(here_to_clips(moves.halves(cotangent)))
+                tick()
+                residual = moved.result.astype(F32)
+        gradient = turned.result.astype(F32) * share[:, None, None]
+        finished = lanes.start(clips_to_here(moves.halves(residual.astype(BF16))))
+        for level in reversed(range(LAYERS)):
+            spatial = level % 2 == 0
+            (residual, normed, projected, saved, result, branch, middle, normed_mlp) = records[level][
+                :8
             ]
-        else:
-            grad_qkv = attend_back(projected, grad_heads, saved, rows, stride)
-        grad_qkv = lanes.fence(grad_qkv)
-        scatters[level, "qkv"] = lanes.start(moves.scatter_weight(normed, grad_qkv))
-        grad_normed = shaped(sum(dot(v, w, NT) for v, w in zip(grad_qkv, qkvs)))
-        added, shift_a_grad, scale_a_grad = modulate_back(grad_normed, residual, scale_a)
-        gradient = gradient + added
-        mod_grads[level] = jnp.stack(
-            [shift_a_grad, scale_a_grad, gate_a_grad, shift_m_grad, scale_m_grad, gate_m_grad],
-            axis=1,
-        )
-        if not spatial:
-            moved = lanes.start(clips_to_frames(gradient.astype(BF16)))
-            lanes.fence()
-            lanes.fence()
-            gradient = moved.result.astype(F32)
+            (pre_act, act, branch_mlp, qkvs, outs, up, down, rows, stride) = records[level][8:]
+            shift_a, scale_a, gate_a, shift_m, scale_m, gate_m = modulations(level)
+            gate_m_grad = jnp.sum(gradient * branch_mlp, axis=1)
+            low_grad = flat((gradient * gate_m[:, None]).astype(BF16))
+            grad_pre = gelu_slope(pre_act, dot(low_grad, down)).astype(BF16)
+            start_scatter(level, "down", low_grad, [act])
+            grad_pre = lanes.fence(grad_pre)
+            grad_normed = shaped(dot(grad_pre, up, NT))
+            start_scatter(level, "up", normed_mlp, [grad_pre])
+            grad_normed = lanes.fence(grad_normed)
+            added, shift_m_grad, scale_m_grad = modulate_back(grad_normed, middle, scale_m)
+            gradient = gradient + added
+            gate_a_grad = jnp.sum(gradient * branch, axis=1)
+            low_grad = flat((gradient * gate_a[:, None]).astype(BF16))
+            grad_heads = dot(low_grad, outs).astype(BF16)
+            start_scatter(level, "out", low_grad, [result])
+            grad_heads = lanes.fence(grad_heads)
+            if spatial and not whole_frames:
+                grad_qkv = [
+                    attend_shared_back(v, g)
+                    for v, g in zip(saved, jnp.split(grad_heads, n_tp, axis=1))
+                ]
+            else:
+                grad_qkv = attend_back(projected, grad_heads, saved, rows, stride)
+            grad_qkv = lanes.fence(grad_qkv)
+            start_scatter(level, "qkv", normed, grad_qkv)
+            grad_normed = shaped(sum(dot(v, w, NT) for v, w in zip(grad_qkv, qkvs)))
+            added, shift_a_grad, scale_a_grad = modulate_back(grad_normed, residual, scale_a)
+            gradient = gradient + added
+            mod_grads[level] = jnp.stack(
+                [shift_a_grad, scale_a_grad, gate_a_grad, shift_m_grad, scale_m_grad, gate_m_grad],
+                axis=1,
+            )
+            if not spatial:
+                moved = lanes.start(clips_to_frames(gradient.astype(BF16)))
+                lanes.fence()
+                lanes.fence()
+                gradient = moved.result.astype(F32)
+        return finished, gradient
+
+    passes = fused_passes if fused else plain_passes
+    finished, gradient = passes(residual)
     grad_tokens = from_frames(moves.halves(gradient.astype(BF16))).astype(F32)
     while lanes.tasks:
         lanes.fence()

time: 1630 us -> 1470 us (0.902)
  Pallas kernels: 87.9 us -> 383 us
  other arithmetic: 393 us -> 127 us
  matrix products: 392 us -> 133 us
  starting transfers between devices: 176 us -> 227 us
  waiting for transfers between devices: 417 us -> 444 us
    pallas_call x4 -> x10, Pallas kernels: 87.9 us -> 383 us  [block_call(): pl.pallas_call(kernel, grid=(clips,), in_specs=specs, out_specs=out_specs...]
    dot_general x42 -> x22, matrix products: 387 us -> 128 us  [dot(): return lax.dot_general(a, b, dims, preferred_element_type=F32)]
    concatenate x10 -> x1, other arithmetic: 141 us -> 0.69 us  [fused_passes(): vectors.append(jnp.concatenate([mods[level], last], axis=1))]
    convert_element_type x17 -> x0, other arithmetic: 73.1 us -> none  [the longest x2 34.7 us: local(): grad_pre = gelu_slope(pre_act, dot(low_grad, down)).astype(BF16)]
    ppermute x149 -> x161, starting transfers between devices: 166 us -> 216 us  [swap_with(): return lax.ppermute(v, axis_name, [(i, i ^ k) for i in range(n)])]
    reduce_sum x12 -> x0, other arithmetic: 44.6 us -> none  [the longest x4 21.6 us: modulate_back(): scale_grad = jnp.sum(grad * normed, axis=1)]
    ppermute x149 -> x161, waiting for transfers between devices: 373 us -> 395 us  [swap_with(): return lax.ppermute(v, axis_name, [(i, i ^ k) for i in range(n)])]
    unnamed x583 -> x450, local copies, waits for them, and re-layouts: 49.7 us -> 44.3 us
  transfers between devices with their start and end apart: 157 -> 169, of which waited for: 64 -> 56; matrix products, arithmetic and copies ran while one was open for 45% -> 20% of each run, Pallas kernels for 5% -> 25%
where the time goes in v3:
time: 1470 us; the launch traced here: 1450 us
  waiting for transfers between devices  444 us (30%)
  Pallas kernels  383 us (26%)
  starting transfers between devices  227 us (15%)
  local copies, waits for them, and re-layouts  135 us (9%)
  matrix products  133 us (9%)
  other arithmetic  127 us (9%)
    ppermute x161, waiting for transfers between devices, swap_with(): return lax.ppermute(v, axis_name, [(i, i ^ k) for i in range(n)])  395 us
    pallas_call x10, Pallas kernels, block_call(): pl.pallas_call(kernel, grid=(clips,), in_specs=specs, out_specs=out_specs...  383 us
    ppermute x161, starting transfers between devices, swap_with(): return lax.ppermute(v, axis_name, [(i, i ^ k) for i in range(n)])  216 us
    dot_general x22, matrix products, dot(): return lax.dot_general(a, b, dims, preferred_element_type=F32)  128 us
    ppermute x8, waiting for transfers between devices, trade(): block = lax.ppermute(block, ('ctx', 'tp'), pairs)  48.9 us
    unnamed x450, local copies, waits for them, and re-layouts  44.3 us
  transfers between devices with their start and end apart: 169, of which 56 were waited for; matrix products, arithmetic and copies ran while one was open for 20% of the time, Pallas kernels for 25%

profile of v3, /device:TPU:0, one launch (start us, length us, event | category | flops | bytes accessed | tf_op | source)
XLA Modules:
  0.0 1454.0 jit_solution(13112319839784465539)
XLA Ops:
  54.1 4.0 collective-permute-done.7
  60.5 4.5 collective-permute-done.8
  85.8 11.7 collective-permute-done.13
  97.5 4.2 collective-permute-start.19
  108.5 4.5 collective-permute-done.19
  114.6 5.4 collective-permute-done.20
  120.0 4.6 collective-permute-start.21
  124.6 5.2 collective-permute-done.21
  129.8 17.1 %collective-permute-done.17 = bf16[4,72,1152]{2,1,0:T(8,128)(2,1)S(1)} collective-permute-done((bf16[4,72,1152]{2,1,0:T(8,128)(2,1)S(1)}, bf16[4,72,1152]{2,1,0:T(8,128)(2,1)S(1)}, u32[]{:S(2)}, u32[]{:S(2)}) %collective-permute-start.17) | collective-permute-done | bytes 663584 | tf_op jit(solution)/shard_map/ppermute | solution.py:29
  165.5 39.7 %shard_map.152 = (bf16[1024,1152]{1,0:T(8,128)(2,1)}, bf16[1024,3840]{1,0:T(8,128)(2,1)}, f32[1024,128]{1,0:T(8,128)}, bf16[1024,1152]{1,0:T(8,128)(2,1)}, bf16[...) custom-call(bf16[1024,1152]{1,0:T(8,128)(2,1)} %bitcast.1198, ...), custom_call_target="tpu_custom_call" | custom-call | flops 16307453952 | bytes 13123584 | tf_op jit(solution)/shard_map/pallas_call | solution.py:604
  233.0 28.1 %shard_map.153 = (bf16[1024,4608]{1,0:T(8,128)(2,1)}, bf16[1024,4608]{1,0:T(8,128)(2,1)}) custom-call(bf16[1024,1152]{1,0:T(8,128)(2,1)} %get-tuple-element.243.g_ref, bf16[576,1152]{1,0:T(8,128)(2,1)} %bitcast.103.refs_0_, bf16[576,1152]{1,0:T(8,128)(2,1)} %copy-done.195, bf16[2,576,1152]{2,1,0:T(8,128)(2,1)} %bitcast.1181, bf16[576,1152]{1,0:T(8,128)(2,1)} %copy-done.197, ...), custom_call_target="tpu_custom_call" | custom-call | flops 10871635968 | bytes 12976128 | tf_op jit(solution)/shard_map/pallas_call | solution.py:604
  261.1 9.1 collective-permute-done.38
  291.5 21.3 %shard_map.154 = (bf16[1024,1152]{1,0:T(8,128)(2,1)}, bf16[1024,1152]{1,0:T(8,128)(2,1)}) custom-call(bf16[1024,4608]{1,0:T(8,128)(2,1)} %get-tuple-element.254.z_ref, f32[1024,1152]{1,0:T(8,128)} %get-tuple-element.255.y_ref, f32[4,8,1152]{2,1,0:T(8,128)} %concatenate.847.mod_ref, bf16[576,1152]{1,0:T(8,128)(2,1)} %bitcast.136.refs_0_.refs_6_, ...), custom_call_target="tpu_custom_call" | custom-call | flops 10871635968 | bytes 24920064 | tf_op jit(solution)/shard_map/pallas_call | solution.py:604
  321.7 23.4 %collective-permute-done.46 = bf16[2,4,72,1152]{3,2,1,0:T(8,128)(2,1)S(1)} collective-permute-done((bf16[2,4,72,1152]{3,2,1,0:T(8,128)(2,1)}, bf16[2,4,72,1152]{3,2,1,0:T(8,128)(2,1)S(1)}, u32[]{:S(2)}, u32[]{:S(2)}) %collective-permute-start.46) | collective-permute-done | bytes 1327136 | tf_op jit(solution)/shard_map/ppermute | solution.py:29
  346.5 22.2 %collective-permute-done.52 = bf16[4,4,1,16,1152]{4,3,1,0,2:T(8,128)(2,1)S(1)} collective-permute-done((bf16[4,4,1,16,1152]{4,3,1,0,2:T(8,128)(2,1)S(1)}, bf16[4,4,1,16,1152]{4,3,1,0,2:T(8,128)(2,1)S(1)}, u32[]{:S(2)}, u32[]{:S(2)}) %collective-permute-start.52) | collective-permute-done | bytes 589856 | tf_op jit(solution)/shard_map/ppermute | solution.py:820
  386.3 9.4 collective-permute-done.62
  396.6 23.5 %collective-permute-done.60 = bf16[4,4,1,16,1152]{4,3,1,0,2:T(8,128)(2,1)S(1)} collective-permute-done((bf16[4,4,1,16,1152]{4,3,1,0,2:T(8,128)(2,1)S(1)}, bf16[4,4,1,16,1152]{4,3,1,0,2:T(8,128)(2,1)S(1)}, u32[]{:S(2)}, u32[]{:S(2)}) %collective-permute-start.60) | collective-permute-done | bytes 589856 | tf_op jit(solution)/shard_map/ppermute | solution.py:29
  424.7 11.9 collective-permute-done.57
  457.8 39.8 %shard_map.155 = (bf16[1024,1152]{1,0:T(8,128)(2,1)}, bf16[1024,3840]{1,0:T(8,128)(2,1)}, f32[1024,128]{1,0:T(8,128)}, bf16[1024,1152]{1,0:T(8,128)(2,1)}, bf16[...) custom-call(bf16[1024,1152]{1,0:T(8,128)(2,1)} %bitcast.1200, ...), custom_call_target="tpu_custom_call" | custom-call | flops 16307453952 | bytes 13123584 | tf_op jit(solution)/shard_map/pallas_call | solution.py:604
  507.2 28.1 %shard_map.156 = (bf16[1024,4608]{1,0:T(8,128)(2,1)}, bf16[1024,4608]{1,0:T(8,128)(2,1)}) custom-call(bf16[1024,1152]{1,0:T(8,128)(2,1)} %get-tuple-element.288.g_ref, bf16[576,1152]{1,0:T(8,128)(2,1)} %bitcast.206.refs_0_, bf16[576,1152]{1,0:T(8,128)(2,1)} %collective-permute-done.55.refs_1_, bf16[2,576,1152]{2,1,0:T(8,128)(2,1)} %bitcast.281.refs_2_, ...), custom_call_target="tpu_custom_call" | custom-call | flops 10871635968 | bytes 12976128 | tf_op jit(solution)/shard_map/pallas_call | solution.py:604
  535.3 21.1 %shard_map.157 = (bf16[1024,1152]{1,0:T(8,128)(2,1)}, bf16[1024,1152]{1,0:T(8,128)(2,1)}) custom-call(bf16[1024,4608]{1,0:T(8,128)(2,1)} %get-tuple-element.291.z_ref, f32[1024,1152]{1,0:T(8,128)} %get-tuple-element.292.y_ref, f32[4,8,1152]{2,1,0:T(8,128)} %pad_maximum_fusion.101.mod_ref, bf16[576,1152]{1,0:T(8,128)(2,1)} %bitcast.268.refs_0_.refs_6_, ...), custom_call_target="tpu_custom_call" | custom-call | flops 10871635968 | bytes 24920064 | tf_op jit(solution)/shard_map/pallas_call | solution.py:604
  563.1 46.9 %shard_map.158 = (bf16[1024,1152]{1,0:T(8,128)(2,1)}, bf16[1024,4608]{1,0:T(8,128)(2,1)}, f32[1024,1152]{1,0:T(8,128)}, bf16[1024,1152]{1,0:T(8,128)(2,1)}, f32[4,8,1152]{2,1,0:T(8,128)}) custom-call(bf16[1024,1152]{1,0:T(8,128)(2,1)} %bitcast.1203, f32[4,8,1152]{2,1,0:T(8,128)} %pad_maximum_fusion.101.mod_ref, bf16[1024,1152]{1,0:T(8,128)(2,1)} %get-tuple-element.299.m_ref, ...), custom_call_target="tpu_custom_call" | custom-call | flops 21743271936 | bytes 42614784 | tf_op jit(solution)/shard_map/pallas_call | solution.py:604
  611.6 10.6 convolution_convert_fusion.3
  627.8 22.3 %collective-permute-start.79 = (bf16[4,2,2,1,16,1152]{5,4,2,1,0,3:T(8,128)(2,1)}, bf16[4,2,2,1,16,1152]{5,4,2,1,0,3:T(8,128)(2,1)}, u32[]{:S(2)}, u32[]{:S(2)}) collective-permute-start(bf16[4,2,2,1,16,1152]{5,4,2,1,0,3:T(8,128)(2,1)} %pad_maximum_fusion.94), channel_id=1, source_target_pairs={{0,8},{2,10},{4,12},{6,14},{8,0},{10,2},{12,4},{14,6},{1,9},{3,11}... | collective-permute-start | bytes 1769480 | tf_op jit(solution)/shard_map/ppermute | solution.py:29
  651.0 8.1 convolution_convert_fusion.2
  659.1 56.0 %shard_map.159 = (bf16[1024,1152]{1,0:T(8,128)(2,1)}, f32[4,8,1152]{2,1,0:T(8,128)}, bf16[1024,1728]{1,0:T(8,128)(2,1)}, bf16[1024,1728]{1,0:T(8,128)(2,1)}) custom-call(bf16[1024,1152]{1,0:T(8,128)(2,1)} %bitcast.1201, f32[4,8,1152]{2,1,0:T(8,128)} %pad_maximum_fusion.101.mod_ref, bf16[1024,1152]{1,0:T(8,128)(2,1)} %get-tuple-element.308.da_ref, ...), custom_call_target="tpu_custom_call" | custom-call | flops 21743271936 | bytes 28590080 | tf_op jit(solution)/shard_map/pallas_call | solution.py:604
  715.2 5.2 convolution_convert_fusion.5
  720.9 9.2 add_convert_fusion.3
  751.5 26.2 %collective-permute-done.132 = f32[4,3456]{1,0:T(4,128)S(1)} collective-permute-done((f32[4,3456]{1,0:T(4,128)S(1)}, f32[4,3456]{1,0:T(4,128)S(1)}, u32[]{:S(2)}, u32[]{:S(2)}) %collective-permute-start.132) | collective-permute-done | bytes 55328 | tf_op jit(solution)/shard_map/ppermute | solution.py:29
  788.7 3.9 convolution_convert_fusion.9
  796.5 11.6 collective-permute-done.86
  810.2 8.6 add_convert_fusion.2
  834.3 7.5 collective-permute-done.92
  843.1 33.7 %collective-permute-done.91 = bf16[4,4,1,16,1152]{4,3,1,0,2:T(8,128)(2,1)S(1)} collective-permute-done((bf16[4,4,1,16,1152]{4,3,1,0,2:T(8,128)(2,1)S(1)}, bf16[4,4,1,16,1152]{4,3,1,0,2:T(8,128)(2,1)S(1)}, u32[]{:S(2)}, u32[]{:S(2)}) %collective-permute-start.91) | collective-permute-done | bytes 589856 | tf_op jit(solution)/shard_map/ppermute | solution.py:29
  882.3 38.9 %collective-permute-done.89 = bf16[4,72,1152]{2,1,0:T(8,128)(2,1)} collective-permute-done((bf16[4,72,1152]{2,1,0:T(8,128)(2,1)}, bf16[4,72,1152]{2,1,0:T(8,128)(2,1)}, u32[]{:S(2)}, u32[]{:S(2)}) %collective-permute-start.89) | collective-permute-done | bytes 663584 | tf_op jit(solution)/shard_map/ppermute | solution.py:29
  921.3 4.5 add_convert_fusion.7
  961.8 5.4 collective-permute-done.98
  969.3 6.4 collective-permute-done.99
  976.7 46.7 %shard_map.160 = (bf16[1024,1152]{1,0:T(8,128)(2,1)}, bf16[1024,4608]{1,0:T(8,128)(2,1)}, f32[1024,1152]{1,0:T(8,128)}, bf16[1024,1152]{1,0:T(8,128)(2,1)}, f32[4,8,1152]{2,1,0:T(8,128)}) custom-call(bf16[1024,1152]{1,0:T(8,128)(2,1)} %bitcast.1204, f32[4,8,1152]{2,1,0:T(8,128)} %concatenate.847.mod_ref, bf16[1024,1152]{1,0:T(8,128)(2,1)} %get-tuple-element.336.m_ref, ...), custom_call_target="tpu_custom_call" | custom-call | flops 21743271936 | bytes 42614784 | tf_op jit(solution)/shard_map/pallas_call | solution.py:604
  1023.6 11.0 convolution_convert_fusion
  1034.6 10.5 convolution_convert_fusion.1
  1049.2 4.7 collective-permute-done.136
  1074.3 9.8 collective-permute-done.107
  1091.3 4.8 collective-permute-done.109
  1097.2 8.6 add_convert_fusion
  1111.4 7.8 add_convert_fusion.1
  1125.8 6.5 collective-permute-start.116
  1137.0 4.7 collective-permute-done.117
  1144.1 55.7 %shard_map.161 = (bf16[1024,1152]{1,0:T(8,128)(2,1)}, f32[4,8,1152]{2,1,0:T(8,128)}, bf16[1024,1728]{1,0:T(8,128)(2,1)}, bf16[1024,1728]{1,0:T(8,128)(2,1)}) custom-call(bf16[1024,1152]{1,0:T(8,128)(2,1)} %bitcast.1199, f32[4,8,1152]{2,1,0:T(8,128)} %concatenate.847.mod_ref, bf16[1024,1152]{1,0:T(8,128)(2,1)} %get-tuple-element.360.da_ref, ...), custom_call_target="tpu_custom_call" | custom-call | flops 21743271936 | bytes 28590080 | tf_op jit(solution)/shard_map/pallas_call | solution.py:604
  1203.6 10.2 collective-permute-done.120
  1215.5 4.4 convolution_convert_fusion.4
  1226.1 6.7 convolution_convert_fusion.6
  1281.0 23.7 %collective-permute-done.126 = bf16[4,1,128,1152]{3,2,0,1:T(8,128)(2,1)S(1)} collective-permute-done((bf16[4,1,128,1152]{3,2,0,1:T(8,128)(2,1)}, bf16[4,1,128,1152]{3,2,0,1:T(8,128)(2,1)S(1)}, u32[]{:S(2)}, u32[]{:S(2)}) %collective-permute-start.126) | collective-permute-done | bytes 1179680 | tf_op jit(solution)/shard_map/ppermute | solution.py:29
  1312.1 10.7 collective-permute-done.144
  1323.1 9.7 collective-permute-done.142
  1337.3 4.1 add_convert_fusion.5
  1341.4 4.7 add_convert_fusion.4
  1359.5 7.3 collective-permute-done.152
  1368.0 6.6 collective-permute-done.153
  1375.8 11.5 collective-permute-start.150
  1393.7 9.5 collective-permute-done.150
  1411.3 5.3 collective-permute-done.159
  1416.8 8.1 collective-permute-start.166
  1439.6 11.5 collective-permute-done.164
  (1187 shorter events, 499.9 us)
Async XLA Ops:
  4.5 67.6 %collective-permute-start.1 = (bf16[72,2304]{1,0:T(8,128)(2,1)}, bf16[72,2304]{1,0:T(8,128)(2,1)}, u32[]{:S(2)}, u32[]{:S(2)}) collective-permute-start(bf16[72,2304]{1,0:T(8,128)(2,1)} %concatenate.843), channel_id=1, source_target_pairs={{0,4},{2,6},{4,0},{6,2},{8,12},{10,14},{12,8},{14,10},{1,5},{3,7},... | collective-permute-start | bytes 995336 | tf_op jit(solution)/shard_map/ppermute | solution.py:29
  7.5 64.6 %collective-permute-start.2 = (bf16[72,2304]{1,0:T(8,128)(2,1)}, bf16[72,2304]{1,0:T(8,128)(2,1)}, u32[]{:S(2)}, u32[]{:S(2)}) collective-permute-start(bf16[72,2304]{1,0:T(8,128)(2,1)} %concatenate.843), channel_id=1, source_target_pairs={{0,8},{2,10},{4,12},{6,14},{8,0},{10,2},{12,4},{14,6},{1,9},{3,11}... | collective-permute-start | bytes 995336 | tf_op jit(solution)/shard_map/ppermute | solution.py:29
  10.1 62.0 %collective-permute-start.3 = (bf16[72,2304]{1,0:T(8,128)(2,1)}, bf16[72,2304]{1,0:T(8,128)(2,1)}, u32[]{:S(2)}, u32[]{:S(2)}) collective-permute-start(bf16[72,2304]{1,0:T(8,128)(2,1)} %concatenate.843), channel_id=1, source_target_pairs={{0,12},{2,14},{4,8},{6,10},{8,4},{10,6},{12,0},{14,2},{1,13},{3,15... | collective-permute-start | bytes 995336 | tf_op jit(solution)/shard_map/ppermute | solution.py:29
  19.8 52.3 %collective-permute-start = (bf16[4,1,128,1152]{3,2,0,1:T(8,128)(2,1)}, bf16[4,1,128,1152]{3,2,0,1:T(8,128)(2,1)}, u32[]{:S(2)}, u32[]{:S(2)}) collective-permute-start(bf16[4,1,128,1152]{3,2,0,1:T(8,128)(2,1)} %get-tuple-element.539), channel_id=1, source_target_pairs={{0,1},{1,0},{2,3},{3,2},{4,5},{5,4},{6,7},{7,6},{8,9},{9,8},{10,11... | collective-permute-start | bytes 3538952 | tf_op jit(solution)/shard_map/ppermute | solution.py:29
  104.8 42.0 %collective-permute-start.16 = (bf16[2,4,72,1152]{3,2,1,0:T(8,128)(2,1)S(1)}, bf16[2,4,72,1152]{3,2,1,0:T(8,128)(2,1)S(1)}, u32[]{:S(2)}, u32[]{:S(2)}) collective-permute-start(bf16[2,4,72,1152]{3,2,1,0:T(8,128)(2,1)S(1)} %pad_maximum_fusion.36), channel_id=1, source_target_pairs={{0,2},{2,0},{4,6},{6,4},{8,10},{10,8},{12,14},{14,12},{1,3},{3,1},... | collective-permute-start | bytes 3981320 | tf_op jit(solution)/shard_map/ppermute | solution.py:29
  106.8 40.1 %collective-permute-start.15 = (bf16[576,1152]{1,0:T(8,128)(2,1)S(1)}, bf16[576,1152]{1,0:T(8,128)(2,1)S(1)}, u32[]{:S(2)}, u32[]{:S(2)}) collective-permute-start(bf16[576,1152]{1,0:T(8,128)(2,1)S(1)} %bitcast.1206), channel_id=1, source_target_pairs={{0,1},{1,0},{2,3},{3,2},{4,5},{5,4},{6,7},{7,6},{8,9},{9,8},{10,11... | collective-permute-start | bytes 3981320 | tf_op jit(solution)/shard_map/ppermute | solution.py:29
  158.2 47.1 %collective-permute-start.31 = (bf16[72,2304]{1,0:T(8,128)(2,1)}, bf16[72,2304]{1,0:T(8,128)(2,1)}, u32[]{:S(2)}, u32[]{:S(2)}) collective-permute-start(bf16[72,2304]{1,0:T(8,128)(2,1)} %concatenate.842), channel_id=1, source_target_pairs={{0,12},{2,14},{4,8},{6,10},{8,4},{10,6},{12,0},{14,2},{1,13},{3,15... | collective-permute-start | bytes 995336 | tf_op jit(solution)/shard_map/ppermute | solution.py:29
  160.6 44.8 %collective-permute-start.28 = (bf16[4,72,1152]{2,1,0:T(8,128)(2,1)}, bf16[4,72,1152]{2,1,0:T(8,128)(2,1)}, u32[]{:S(2)}, u32[]{:S(2)}) collective-permute-start(bf16[4,72,1152]{2,1,0:T(8,128)(2,1)} %fusion.70), channel_id=1, source_target_pairs={{0,1},{1,0},{2,3},{3,2},{4,5},{5,4},{6,7},{7,6},{8,9},{9,8},{10,11... | collective-permute-start | bytes 1990664 | tf_op jit(solution)/shard_map/ppermute | solution.py:29
  162.0 43.4 %collective-permute-start.27 = (bf16[4,72,1152]{2,1,0:T(8,128)(2,1)}, bf16[4,72,1152]{2,1,0:T(8,128)(2,1)}, u32[]{:S(2)}, u32[]{:S(2)}) collective-permute-start(bf16[4,72,1152]{2,1,0:T(8,128)(2,1)} %fusion.71), channel_id=1, source_target_pairs={{0,2},{2,0},{4,6},{6,4},{8,10},{10,8},{12,14},{14,12},{1,3},{3,1},... | collective-permute-start | bytes 1990664 | tf_op jit(solution)/shard_map/ppermute | solution.py:29
  163.4 43.7 %collective-permute-start.26 = (bf16[2,4,72,1152]{3,2,1,0:T(8,128)(2,1)}, bf16[2,4,72,1152]{3,2,1,0:T(8,128)(2,1)}, u32[]{:S(2)}, u32[]{:S(2)}) collective-permute-start(bf16[2,4,72,1152]{3,2,1,0:T(8,128)(2,1)} %pad_maximum_fusion.38), channel_id=1, source_target_pairs={{0,2},{2,0},{4,6},{6,4},{8,10},{10,8},{12,14},{14,12},{1,3},{3,1},... | collective-permute-start | bytes 3981320 | tf_op jit(solution)/shard_map/ppermute | solution.py:29
  164.1 43.1 %collective-permute-start.25 = (bf16[576,1152]{1,0:T(8,128)(2,1)}, bf16[576,1152]{1,0:T(8,128)(2,1)S(1)}, u32[]{:S(2)}, u32[]{:S(2)}) collective-permute-start(bf16[576,1152]{1,0:T(8,128)(2,1)} %bitcast.103.refs_0_), channel_id=1, source_target_pairs={{0,1},{1,0},{2,3},{3,2},{4,5},{5,4},{6,7},{7,6},{8,9},{9,8},{10,11... | collective-permute-start | bytes 3981320 | tf_op jit(solution)/shard_map/ppermute | solution.py:29
  223.1 47.2 %collective-permute-start.36 = (bf16[2,4,72,1152]{3,2,1,0:T(8,128)(2,1)}, bf16[2,4,72,1152]{3,2,1,0:T(8,128)(2,1)}, u32[]{:S(2)}, u32[]{:S(2)}) collective-permute-start(bf16[2,4,72,1152]{3,2,1,0:T(8,128)(2,1)} %pad_maximum_fusion.40), channel_id=1, source_target_pairs={{0,2},{2,0},{4,6},{6,4},{8,10},{10,8},{12,14},{14,12},{1,3},{3,1},... | collective-permute-start | bytes 3981320 | tf_op jit(solution)/shard_map/ppermute | solution.py:29
  224.5 45.8 %collective-permute-start.35 = (bf16[576,1152]{1,0:T(8,128)(2,1)}, bf16[576,1152]{1,0:T(8,128)(2,1)}, u32[]{:S(2)}, u32[]{:S(2)}) collective-permute-start(bf16[576,1152]{1,0:T(8,128)(2,1)} %bitcast.136.refs_0_.refs_6_), channel_id=1, source_target_pairs={{0,1},{1,0},{2,3},{3,2},{4,5},{5,4},{6,7},{7,6},{8,9},{9,8},{10,11... | collective-permute-start | bytes 3981320 | tf_op jit(solution)/shard_map/ppermute | solution.py:29
  229.5 40.8 %collective-permute-start.38 = (bf16[4,72,1152]{2,1,0:T(8,128)(2,1)}, bf16[4,72,1152]{2,1,0:T(8,128)(2,1)}, u32[]{:S(2)}, u32[]{:S(2)}) collective-permute-start(bf16[4,72,1152]{2,1,0:T(8,128)(2,1)} %fusion.68), channel_id=1, source_target_pairs={{0,1},{1,0},{2,3},{3,2},{4,5},{5,4},{6,7},{7,6},{8,9},{9,8},{10,11... | collective-permute-start | bytes 1990664 | tf_op jit(solution)/shard_map/ppermute | solution.py:29
  270.3 42.5 %collective-permute-start.49 = (bf16[72,2304]{1,0:T(8,128)(2,1)}, bf16[72,2304]{1,0:T(8,128)(2,1)}, u32[]{:S(2)}, u32[]{:S(2)}) collective-permute-start(bf16[72,2304]{1,0:T(8,128)(2,1)} %get-tuple-element.264), channel_id=1, source_target_pairs={{0,4},{2,6},{4,0},{6,2},{8,12},{10,14},{12,8},{14,10},{1,5},{3,7},... | collective-permute-start | bytes 995336 | tf_op jit(solution)/shard_map/ppermute | solution.py:29
  271.0 43.2 %collective-permute-start.50 = (bf16[72,2304]{1,0:T(8,128)(2,1)}, bf16[72,2304]{1,0:T(8,128)(2,1)}, u32[]{:S(2)}, u32[]{:S(2)}) collective-permute-start(bf16[72,2304]{1,0:T(8,128)(2,1)} %get-tuple-element.264), channel_id=1, source_target_pairs={{0,8},{2,10},{4,12},{6,14},{8,0},{10,2},{12,4},{14,6},{1,9},{3,11}... | collective-permute-start | bytes 995336 | tf_op jit(solution)/shard_map/ppermute | solution.py:29
  317.0 51.7 %collective-permute-start.52 = (bf16[4,4,1,16,1152]{4,3,1,0,2:T(8,128)(2,1)S(1)}, bf16[4,4,1,16,1152]{4,3,1,0,2:T(8,128)(2,1)S(1)}, u32[]{:S(2)}, u32[]{:S(2)}) collective-permute-start(bf16[4,4,1,16,1152]{4,3,1,0,2:T(8,128)(2,1)S(1)} %get-tuple-element.536), channel_id=1, source_target_pairs={{0,1},{1,0},{2,3},{3,2},{4,5},{5,4},{6,7},{7,6},{8,9},{9,8},{10,11... | collective-permute-start | bytes 1769480 | tf_op jit(solution)/shard_map/ppermute | solution.py:820
  318.2 50.5 %collective-permute-start.53 = (bf16[4,4,1,16,1152]{4,3,1,0,2:T(8,128)(2,1)S(1)}, bf16[4,4,1,16,1152]{4,3,1,0,2:T(8,128)(2,1)S(1)}, u32[]{:S(2)}, u32[]{:S(2)}) collective-permute-start(bf16[4,4,1,16,1152]{4,3,1,0,2:T(8,128)(2,1)S(1)} %get-tuple-element.535), channel_id=1, source_target_pairs={{0,2},{1,3},{2,0},{3,1},{4,6},{5,7},{6,4},{7,5},{8,10},{9,11},{10,... | collective-permute-start | bytes 1769480 | tf_op jit(solution)/shard_map/ppermute | solution.py:820
  318.9 51.9 %collective-permute-start.54 = (bf16[4,4,1,16,1152]{4,3,1,0,2:T(8,128)(2,1)S(1)}, bf16[4,4,1,16,1152]{4,3,1,0,2:T(8,128)(2,1)S(1)}, u32[]{:S(2)}, u32[]{:S(2)}) collective-permute-start(bf16[4,4,1,16,1152]{4,3,1,0,2:T(8,128)(2,1)S(1)} %get-tuple-element.537), channel_id=1, source_target_pairs={{0,3},{1,2},{2,1},{3,0},{4,7},{5,6},{6,5},{7,4},{8,11},{9,10},{10,... | collective-permute-start | bytes 1769480 | tf_op jit(solution)/shard_map/ppermute | solution.py:820
  345.1 50.6 %collective-permute-start.62 = (bf16[4,4,2,1,16,1152]{5,4,1,2,0,3:T(8,128)(2,1)S(1)}, bf16[4,4,2,1,16,1152]{5,4,1,2,0,3:T(8,128)(2,1)S(1)}, u32[]{:S(2)}, u32[]{:S(2)}) collective-permute-start(bf16[4,4,2,1,16,1152]{5,4,1,2,0,3:T(8,128)(2,1)S(1)} %copy-done.108), channel_id=1, source_target_pairs={{0,2},{1,3},{2,0},{3,1},{4,6},{5,7},{6,4},{7,5},{8,10},{9,11},{10,... | collective-permute-start | bytes 3538952 | tf_op jit(solution)/shard_map/ppermute | solution.py:820
  373.6 46.5 %collective-permute-start.60 = (bf16[4,4,1,16,1152]{4,3,1,0,2:T(8,128)(2,1)S(1)}, bf16[4,4,1,16,1152]{4,3,1,0,2:T(8,128)(2,1)S(1)}, u32[]{:S(2)}, u32[]{:S(2)}) collective-permute-start(bf16[4,4,1,16,1152]{4,3,1,0,2:T(8,128)(2,1)S(1)} %pad_maximum_fusion.88), channel_id=1, source_target_pairs={{0,8},{2,10},{4,12},{6,14},{8,0},{10,2},{12,4},{14,6},{1,9},{3,11}... | collective-permute-start | bytes 1769480 | tf_op jit(solution)/shard_map/ppermute | solution.py:29
  378.8 57.8 %collective-permute-start.56 = (bf16[2,4,72,1152]{3,2,1,0:T(8,128)(2,1)S(1)}, bf16[2,4,72,1152]{3,2,1,0:T(8,128)(2,1)S(1)}, u32[]{:S(2)}, u32[]{:S(2)}) collective-permute-start(bf16[2,4,72,1152]{3,2,1,0:T(8,128)(2,1)S(1)} %pad_maximum_fusion.44), channel_id=1, source_target_pairs={{0,2},{2,0},{4,6},{6,4},{8,10},{10,8},{12,14},{14,12},{1,3},{3,1},... | collective-permute-start | bytes 3981320 | tf_op jit(solution)/shard_map/ppermute | solution.py:29
  382.8 53.8 %collective-permute-start.55 = (bf16[576,1152]{1,0:T(8,128)(2,1)}, bf16[576,1152]{1,0:T(8,128)(2,1)}, u32[]{:S(2)}, u32[]{:S(2)}) collective-permute-start(bf16[576,1152]{1,0:T(8,128)(2,1)} %bitcast.206.refs_0_), channel_id=1, source_target_pairs={{0,1},{1,0},{2,3},{3,2},{4,5},{5,4},{6,7},{7,6},{8,9},{9,8},{10,11... | collective-permute-start | bytes 3981320 | tf_op jit(solution)/shard_map/ppermute | solution.py:29
  440.9 56.7 %collective-permute-start.69 = (bf16[4,2,2,1,16,1152]{5,4,1,2,0,3:T(8,128)(2,1)}, bf16[4,2,2,1,16,1152]{5,4,1,2,0,3:T(8,128)(2,1)}, u32[]{:S(2)}, u32[]{:S(2)}) collective-permute-start(bf16[4,2,2,1,16,1152]{5,4,1,2,0,3:T(8,128)(2,1)} %pad_maximum_fusion.91), channel_id=1, source_target_pairs={{0,8},{2,10},{4,12},{6,14},{8,0},{10,2},{12,4},{14,6},{1,9},{3,11}... | collective-permute-start | bytes 1769480 | tf_op jit(solution)/shard_map/ppermute | solution.py:29
  449.7 48.1 %collective-permute-start.68 = (bf16[4,2,2,1,16,1152]{5,4,1,2,0,3:T(8,128)(2,1)}, bf16[4,2,2,1,16,1152]{5,4,1,2,0,3:T(8,128)(2,1)}, u32[]{:S(2)}, u32[]{:S(2)}) collective-permute-start(bf16[4,2,2,1,16,1152]{5,4,1,2,0,3:T(8,128)(2,1)} %pad_maximum_fusion.90), channel_id=1, source_target_pairs={{0,4},{2,6},{4,0},{6,2},{8,12},{10,14},{12,8},{14,10},{1,5},{3,7},... | collective-permute-start | bytes 1769480 | tf_op jit(solution)/shard_map/ppermute | solution.py:29
  451.6 46.1 %collective-permute-start.67 = (bf16[2,4,72,1152]{3,2,1,0:T(8,128)(2,1)}, bf16[2,4,72,1152]{3,2,1,0:T(8,128)(2,1)}, u32[]{:S(2)}, u32[]{:S(2)}) collective-permute-start(bf16[2,4,72,1152]{3,2,1,0:T(8,128)(2,1)} %pad_maximum_fusion.46), channel_id=1, source_target_pairs={{0,2},{2,0},{4,6},{6,4},{8,10},{10,8},{12,14},{14,12},{1,3},{3,1},... | collective-permute-start | bytes 3981320 | tf_op jit(solution)/shard_map/ppermute | solution.py:29
  455.7 42.1 %collective-permute-start.66 = (bf16[576,1152]{1,0:T(8,128)(2,1)}, bf16[576,1152]{1,0:T(8,128)(2,1)}, u32[]{:S(2)}, u32[]{:S(2)}) collective-permute-start(bf16[576,1152]{1,0:T(8,128)(2,1)} %bitcast.268.refs_0_.refs_6_), channel_id=1, source_target_pairs={{0,1},{1,0},{2,3},{3,2},{4,5},{5,4},{6,7},{7,6},{8,9},{9,8},{10,11... | collective-permute-start | bytes 3981320 | tf_op jit(solution)/shard_map/ppermute | solution.py:29
  456.3 50.9 %collective-permute-start.73 = (bf16[2,576,1152]{2,1,0:T(8,128)(2,1)}, bf16[2,576,1152]{2,1,0:T(8,128)(2,1)}, u32[]{:S(2)}, u32[]{:S(2)}) collective-permute-start(bf16[2,576,1152]{2,1,0:T(8,128)(2,1)} %bitcast.281.refs_2_), channel_id=1, source_target_pairs={{0,16},{16,0},{1,17},{17,1},{2,18},{18,2},{3,19},{19,3},{4,20},{20... | collective-permute-start | bytes 7962632 | tf_op jit(solution)/shard_map/ppermute | solution.py:29
  561.6 48.5 %collective-permute-start.77 = (bf16[4,4,2,1,16,1152]{5,4,2,1,0,3:T(8,128)(2,1)}, bf16[4,4,2,1,16,1152]{5,4,2,1,0,3:T(8,128)(2,1)}, u32[]{:S(2)}, u32[]{:S(2)}) collective-permute-start(bf16[4,4,2,1,16,1152]{5,4,2,1,0,3:T(8,128)(2,1)} %get-tuple-element.515), channel_id=1, source_target_pairs={{0,2},{1,3},{2,0},{3,1},{4,6},{5,7},{6,4},{7,5},{8,10},{9,11},{10,... | collective-permute-start | bytes 3538952 | tf_op jit(solution)/shard_map/ppermute | solution.py:820
  622.2 98.2 %collective-permute-start.81 = (bf16[576,4608]{1,0:T(8,128)(2,1)}, bf16[576,4608]{1,0:T(8,128)(2,1)}, u32[]{:S(2)}, u32[]{:S(2)}) collective-permute-start(bf16[576,4608]{1,0:T(8,128)(2,1)} %convolution_convert_fusion.3), channel_id=1, source_target_pairs={{0,16},{16,0},{1,17},{17,1},{2,18},{18,2},{3,19},{19,3},{4,20},{20... | collective-permute-start | bytes 15925256 | tf_op jit(solution)/shard_map/ppermute | solution.py:29
  624.5 96.0 %collective-permute-start.80 = (bf16[4,2,2,1,16,1152]{5,4,2,1,0,3:T(8,128)(2,1)}, bf16[4,2,2,1,16,1152]{5,4,2,1,0,3:T(8,128)(2,1)}, u32[]{:S(2)}, u32[]{:S(2)}) collective-permute-start(bf16[4,2,2,1,16,1152]{5,4,2,1,0,3:T(8,128)(2,1)} %pad_maximum_fusion.95), channel_id=1, source_target_pairs={{0,12},{2,14},{4,8},{6,10},{8,4},{10,6},{12,0},{14,2},{1,13},{3,15... | collective-permute-start | bytes 1769480 | tf_op jit(solution)/shard_map/ppermute | solution.py:29
  627.8 92.7 %collective-permute-start.79 = (bf16[4,2,2,1,16,1152]{5,4,2,1,0,3:T(8,128)(2,1)}, bf16[4,2,2,1,16,1152]{5,4,2,1,0,3:T(8,128)(2,1)}, u32[]{:S(2)}, u32[]{:S(2)}) collective-permute-start(bf16[4,2,2,1,16,1152]{5,4,2,1,0,3:T(8,128)(2,1)} %pad_maximum_fusion.94), channel_id=1, source_target_pairs={{0,8},{2,10},{4,12},{6,14},{8,0},{10,2},{12,4},{14,6},{1,9},{3,11}... | collective-permute-start | bytes 1769480 | tf_op jit(solution)/shard_map/ppermute | solution.py:29
  651.0 69.5 %collective-permute-start.78 = (bf16[4,2,2,1,16,1152]{5,4,2,1,0,3:T(8,128)(2,1)}, bf16[4,2,2,1,16,1152]{5,4,2,1,0,3:T(8,128)(2,1)}, u32[]{:S(2)}, u32[]{:S(2)}) collective-permute-start(bf16[4,2,2,1,16,1152]{5,4,2,1,0,3:T(8,128)(2,1)} %pad_maximum_fusion.93), channel_id=1, source_target_pairs={{0,4},{2,6},{4,0},{6,2},{8,12},{10,14},{12,8},{14,10},{1,5},{3,7},... | collective-permute-start | bytes 1769480 | tf_op jit(solution)/shard_map/ppermute | solution.py:29
  659.1 120.9 %collective-permute-start.87 = (bf16[576,4608]{1,0:T(8,128)(2,1)}, bf16[576,4608]{1,0:T(8,128)(2,1)}, u32[]{:S(2)}, u32[]{:S(2)}) collective-permute-start(bf16[576,4608]{1,0:T(8,128)(2,1)} %convolution_convert_fusion.2), channel_id=1, source_target_pairs={{0,16},{16,0},{1,17},{17,1},{2,18},{18,2},{3,19},{19,3},{4,20},{20... | collective-permute-start | bytes 15925256 | tf_op jit(solution)/shard_map/ppermute | solution.py:29
  731.8 76.2 %collective-permute-start.83 = (bf16[4,72,2304]{2,1,0:T(8,128)(2,1)S(1)}, bf16[4,72,2304]{2,1,0:T(8,128)(2,1)}, u32[]{:S(2)}, u32[]{:S(2)}) collective-permute-start(bf16[4,72,2304]{2,1,0:T(8,128)(2,1)S(1)} %dynamic-slice_bitcast_fusion.3), channel_id=1, source_target_pairs={{0,2},{2,0},{4,6},{6,4},{8,10},{10,8},{12,14},{14,12},{1,3},{3,1},... | collective-permute-start | bytes 3981320 | tf_op jit(solution)/shard_map/ppermute | solution.py:29
  732.4 77.7 %collective-permute-start.82 = (bf16[576,1152]{1,0:T(8,128)(2,1)}, bf16[576,1152]{1,0:T(8,128)(2,1)}, u32[]{:S(2)}, u32[]{:S(2)}) collective-permute-start(bf16[576,1152]{1,0:T(8,128)(2,1)} %get-tuple-element.469), channel_id=1, source_target_pairs={{0,1},{1,0},{2,3},{3,2},{4,5},{5,4},{6,7},{7,6},{8,9},{9,8},{10,11... | collective-permute-start | bytes 3981320 | tf_op jit(solution)/shard_map/ppermute | solution.py:29
  735.6 57.1 %collective-permute-start.84 = (bf16[4,4,1,16,1152]{4,3,1,0,2:T(8,128)(2,1)}, bf16[4,4,1,16,1152]{4,3,1,0,2:T(8,128)(2,1)}, u32[]{:S(2)}, u32[]{:S(2)}) collective-permute-start(bf16[4,4,1,16,1152]{4,3,1,0,2:T(8,128)(2,1)} %get-tuple-element.500), channel_id=1, source_target_pairs={{0,1},{1,0},{2,3},{3,2},{4,5},{5,4},{6,7},{7,6},{8,9},{9,8},{10,11... | collective-permute-start | bytes 1769480 | tf_op jit(solution)/shard_map/ppermute | solution.py:820
  737.1 40.6 %collective-permute-start.132 = (f32[4,3456]{1,0:T(4,128)S(1)}, f32[4,3456]{1,0:T(4,128)S(1)}, u32[]{:S(2)}, u32[]{:S(2)}) collective-permute-start(f32[4,3456]{1,0:T(4,128)S(1)} %bitcast.1237), channel_id=1, source_target_pairs={{0,1},{1,0},{2,3},{3,2},{4,5},{5,4},{6,7},{7,6},{8,9},{9,8},{10,11... | collective-permute-start | bytes 165896 | tf_op jit(solution)/shard_map/ppermute | solution.py:29
  792.7 39.4 %collective-permute-start.95 = (bf16[576,1152]{1,0:T(8,128)(2,1)}, bf16[576,1152]{1,0:T(8,128)(2,1)}, u32[]{:S(2)}, u32[]{:S(2)}) collective-permute-start(bf16[576,1152]{1,0:T(8,128)(2,1)} %convolution_convert_fusion.5), channel_id=1, source_target_pairs={{0,16},{16,0},{1,17},{17,1},{2,18},{18,2},{3,19},{19,3},{4,20},{20... | collective-permute-start | bytes 3981320 | tf_op jit(solution)/shard_map/ppermute | solution.py:29
  796.5 82.4 %collective-permute-start.97 = (bf16[576,1728]{1,0:T(8,128)(2,1)}, bf16[576,1728]{1,0:T(8,128)(2,1)}, u32[]{:S(2)}, u32[]{:S(2)}) collective-permute-start(bf16[576,1728]{1,0:T(8,128)(2,1)} %convolution_convert_fusion.8), channel_id=1, source_target_pairs={{0,16},{16,0},{1,17},{17,1},{2,18},{18,2},{3,19},{19,3},{4,20},{20... | collective-permute-start | bytes 5971976 | tf_op jit(solution)/shard_map/ppermute | solution.py:29
  808.1 74.2 %collective-permute-start.96 = (bf16[576,1728]{1,0:T(8,128)(2,1)}, bf16[576,1728]{1,0:T(8,128)(2,1)}, u32[]{:S(2)}, u32[]{:S(2)}) collective-permute-start(bf16[576,1728]{1,0:T(8,128)(2,1)} %convolution_convert_fusion.9), channel_id=1, source_target_pairs={{0,16},{16,0},{1,17},{17,1},{2,18},{18,2},{3,19},{19,3},{4,20},{20... | collective-permute-start | bytes 5971976 | tf_op jit(solution)/shard_map/ppermute | solution.py:29
  832.1 44.7 %collective-permute-start.91 = (bf16[4,4,1,16,1152]{4,3,1,0,2:T(8,128)(2,1)S(1)}, bf16[4,4,1,16,1152]{4,3,1,0,2:T(8,128)(2,1)S(1)}, u32[]{:S(2)}, u32[]{:S(2)}) collective-permute-start(bf16[4,4,1,16,1152]{4,3,1,0,2:T(8,128)(2,1)S(1)} %pad_maximum_fusion.97), channel_id=1, source_target_pairs={{0,8},{2,10},{4,12},{6,14},{8,0},{10,2},{12,4},{14,6},{1,9},{3,11}... | collective-permute-start | bytes 1769480 | tf_op jit(solution)/shard_map/ppermute | solution.py:29
  832.1 45.4 %collective-permute-start.90 = (bf16[4,4,1,16,1152]{4,3,1,0,2:T(8,128)(2,1)S(1)}, bf16[4,4,1,16,1152]{4,3,1,0,2:T(8,128)(2,1)S(1)}, u32[]{:S(2)}, u32[]{:S(2)}) collective-permute-start(bf16[4,4,1,16,1152]{4,3,1,0,2:T(8,128)(2,1)S(1)} %pad_maximum_fusion.96), channel_id=1, source_target_pairs={{0,4},{2,6},{4,0},{6,2},{8,12},{10,14},{12,8},{14,10},{1,5},{3,7},... | collective-permute-start | bytes 1769480 | tf_op jit(solution)/shard_map/ppermute | solution.py:29
  841.9 79.4 %collective-permute-start.94 = (bf16[4,72,2304]{2,1,0:T(8,128)(2,1)S(1)}, bf16[4,72,2304]{2,1,0:T(8,128)(2,1)S(1)}, u32[]{:S(2)}, u32[]{:S(2)}) collective-permute-start(bf16[4,72,2304]{2,1,0:T(8,128)(2,1)S(1)} %dynamic-slice_bitcast_fusion.2), channel_id=1, source_target_pairs={{0,2},{2,0},{4,6},{6,4},{8,10},{10,8},{12,14},{14,12},{1,3},{3,1},... | collective-permute-start | bytes 3981320 | tf_op jit(solution)/shard_map/ppermute | solution.py:29
  876.8 44.4 %collective-permute-start.93 = (bf16[576,1152]{1,0:T(8,128)(2,1)}, bf16[576,1152]{1,0:T(8,128)(2,1)}, u32[]{:S(2)}, u32[]{:S(2)}) collective-permute-start(bf16[576,1152]{1,0:T(8,128)(2,1)} %get-tuple-element.466), channel_id=1, source_target_pairs={{0,1},{1,0},{2,3},{3,2},{4,5},{5,4},{6,7},{7,6},{8,9},{9,8},{10,11... | collective-permute-start | bytes 3981320 | tf_op jit(solution)/shard_map/ppermute | solution.py:29
  877.5 43.7 %collective-permute-start.89 = (bf16[4,72,1152]{2,1,0:T(8,128)(2,1)}, bf16[4,72,1152]{2,1,0:T(8,128)(2,1)}, u32[]{:S(2)}, u32[]{:S(2)}) collective-permute-start(bf16[4,72,1152]{2,1,0:T(8,128)(2,1)} %split.76), channel_id=1, source_target_pairs={{0,1},{1,0},{2,3},{3,2},{4,5},{5,4},{6,7},{7,6},{8,9},{9,8},{10,11... | collective-permute-start | bytes 1990664 | tf_op jit(solution)/shard_map/ppermute | solution.py:29
  878.8 42.4 %collective-permute-start.88 = (bf16[4,72,1152]{2,1,0:T(8,128)(2,1)S(1)}, bf16[4,72,1152]{2,1,0:T(8,128)(2,1)}, u32[]{:S(2)}, u32[]{:S(2)}) collective-permute-start(bf16[4,72,1152]{2,1,0:T(8,128)(2,1)S(1)} %dynamic-slice_bitcast_fusion.9), channel_id=1, source_target_pairs={{0,2},{2,0},{4,6},{6,4},{8,10},{10,8},{12,14},{14,12},{1,3},{3,1},... | collective-permute-start | bytes 1990664 | tf_op jit(solution)/shard_map/ppermute | solution.py:29
  940.8 82.7 %collective-permute-start.106 = (bf16[4,72,1920]{2,1,0:T(8,128)(2,1)}, bf16[4,72,1920]{2,1,0:T(8,128)(2,1)}, u32[]{:S(2)}, u32[]{:S(2)}) collective-permute-start(bf16[4,72,1920]{2,1,0:T(8,128)(2,1)} %dynamic-slice_bitcast_fusion.5), channel_id=1, source_target_pairs={{0,2},{2,0},{4,6},{6,4},{8,10},{10,8},{12,14},{14,12},{1,3},{3,1},... | collective-permute-start | bytes 3317768 | tf_op jit(solution)/shard_map/ppermute | solution.py:29
  957.5 66.1 %collective-permute-start.105 = (bf16[576,768]{1,0:T(8,128)(2,1)}, bf16[576,768]{1,0:T(8,128)(2,1)}, u32[]{:S(2)}, u32[]{:S(2)}) collective-permute-start(bf16[576,768]{1,0:T(8,128)(2,1)} %slice.1361), channel_id=1, source_target_pairs={{0,1},{1,0},{2,3},{3,2},{4,5},{5,4},{6,7},{7,6},{8,9},{9,8},{10,11... | collective-permute-start | bytes 2654216 | tf_op jit(solution)/shard_map/ppermute | solution.py:29
  960.9 62.6 %collective-permute-start.104 = (bf16[4,72,640]{2,1,0:T(8,128)(2,1)S(1)}, bf16[4,72,640]{2,1,0:T(8,128)(2,1)}, u32[]{:S(2)}, u32[]{:S(2)}) collective-permute-start(bf16[4,72,640]{2,1,0:T(8,128)(2,1)S(1)} %dynamic-slice_bitcast_fusion.13), channel_id=1, source_target_pairs={{0,2},{2,0},{4,6},{6,4},{8,10},{10,8},{12,14},{14,12},{1,3},{3,1},... | collective-permute-start | bytes 1105928 | tf_op jit(solution)/shard_map/ppermute | solution.py:29
  967.9 55.6 %collective-permute-start.102 = (bf16[4,72,1152]{2,1,0:T(8,128)(2,1)}, bf16[4,72,1152]{2,1,0:T(8,128)(2,1)}, u32[]{:S(2)}, u32[]{:S(2)}) collective-permute-start(bf16[4,72,1152]{2,1,0:T(8,128)(2,1)} %split.78), channel_id=1, source_target_pairs={{0,1},{1,0},{2,3},{3,2},{4,5},{5,4},{6,7},{7,6},{8,9},{9,8},{10,11... | collective-permute-start | bytes 1990664 | tf_op jit(solution)/shard_map/ppermute | solution.py:29
  975.8 47.8 %collective-permute-start.101 = (bf16[4,72,1152]{2,1,0:T(8,128)(2,1)}, bf16[4,72,1152]{2,1,0:T(8,128)(2,1)}, u32[]{:S(2)}, u32[]{:S(2)}) collective-permute-start(bf16[4,72,1152]{2,1,0:T(8,128)(2,1)} %dynamic-slice_bitcast_fusion.8), channel_id=1, source_target_pairs={{0,2},{2,0},{4,6},{6,4},{8,10},{10,8},{12,14},{14,12},{1,3},{3,1},... | collective-permute-start | bytes 1990664 | tf_op jit(solution)/shard_map/ppermute | solution.py:29
  1034.5 61.6 %collective-permute-start.115 = (bf16[576,4608]{1,0:T(8,128)(2,1)}, bf16[576,4608]{1,0:T(8,128)(2,1)}, u32[]{:S(2)}, u32[]{:S(2)}) collective-permute-start(bf16[576,4608]{1,0:T(8,128)(2,1)} %convolution_convert_fusion), channel_id=1, source_target_pairs={{0,16},{16,0},{1,17},{17,1},{2,18},{18,2},{3,19},{19,3},{4,20},{20... | collective-permute-start | bytes 15925256 | tf_op jit(solution)/shard_map/ppermute | solution.py:29
  1045.0 52.2 %collective-permute-start.114 = (bf16[576,4608]{1,0:T(8,128)(2,1)}, bf16[576,4608]{1,0:T(8,128)(2,1)}, u32[]{:S(2)}, u32[]{:S(2)}) collective-permute-start(bf16[576,4608]{1,0:T(8,128)(2,1)} %convolution_convert_fusion.1), channel_id=1, source_target_pairs={{0,16},{16,0},{1,17},{17,1},{2,18},{18,2},{3,19},{19,3},{4,20},{20... | collective-permute-start | bytes 15925256 | tf_op jit(solution)/shard_map/ppermute | solution.py:29
  1110.0 113.8 %collective-permute-start.125 = (bf16[4,72,2304]{2,1,0:T(8,128)(2,1)}, bf16[4,72,2304]{2,1,0:T(8,128)(2,1)}, u32[]{:S(2)}, u32[]{:S(2)}) collective-permute-start(bf16[4,72,2304]{2,1,0:T(8,128)(2,1)} %dynamic-slice_bitcast_fusion), channel_id=1, source_target_pairs={{0,2},{2,0},{4,6},{6,4},{8,10},{10,8},{12,14},{14,12},{1,3},{3,1},... | collective-permute-start | bytes 3981320 | tf_op jit(solution)/shard_map/ppermute | solution.py:29
  1110.7 113.2 %collective-permute-start.124 = (bf16[576,1152]{1,0:T(8,128)(2,1)}, bf16[576,1152]{1,0:T(8,128)(2,1)}, u32[]{:S(2)}, u32[]{:S(2)}) collective-permute-start(bf16[576,1152]{1,0:T(8,128)(2,1)} %get-tuple-element.460), channel_id=1, source_target_pairs={{0,1},{1,0},{2,3},{3,2},{4,5},{5,4},{6,7},{7,6},{8,9},{9,8},{10,11... | collective-permute-start | bytes 3981320 | tf_op jit(solution)/shard_map/ppermute | solution.py:29
  1135.7 88.2 %collective-permute-start.123 = (bf16[4,72,2304]{2,1,0:T(8,128)(2,1)}, bf16[4,72,2304]{2,1,0:T(8,128)(2,1)}, u32[]{:S(2)}, u32[]{:S(2)}) collective-permute-start(bf16[4,72,2304]{2,1,0:T(8,128)(2,1)} %dynamic-slice_bitcast_fusion.1), channel_id=1, source_target_pairs={{0,2},{2,0},{4,6},{6,4},{8,10},{10,8},{12,14},{14,12},{1,3},{3,1},... | collective-permute-start | bytes 3981320 | tf_op jit(solution)/shard_map/ppermute | solution.py:29
  1141.7 82.2 %collective-permute-start.122 = (bf16[576,1152]{1,0:T(8,128)(2,1)}, bf16[576,1152]{1,0:T(8,128)(2,1)}, u32[]{:S(2)}, u32[]{:S(2)}) collective-permute-start(bf16[576,1152]{1,0:T(8,128)(2,1)} %get-tuple-element.463), channel_id=1, source_target_pairs={{0,1},{1,0},{2,3},{3,2},{4,5},{5,4},{6,7},{7,6},{8,9},{9,8},{10,11... | collective-permute-start | bytes 3981320 | tf_op jit(solution)/shard_map/ppermute | solution.py:29
  1143.3 56.6 %collective-permute-start.119 = (bf16[72,1728]{1,0:T(8,128)(2,1)}, bf16[72,1728]{1,0:T(8,128)(2,1)}, u32[]{:S(2)}, u32[]{:S(2)}) collective-permute-start(bf16[72,1728]{1,0:T(8,128)(2,1)} %get-tuple-element.600), channel_id=1, source_target_pairs={{0,4},{2,6},{4,0},{6,2},{8,12},{10,14},{12,8},{14,10},{1,5},{3,7},... | collective-permute-start | bytes 746504 | tf_op jit(solution)/shard_map/ppermute | solution.py:29
  1223.9 85.3 %collective-permute-start.148 = (bf16[576,1152]{1,0:T(8,128)(2,1)}, bf16[576,1152]{1,0:T(8,128)(2,1)}, u32[]{:S(2)}, u32[]{:S(2)}) collective-permute-start(bf16[576,1152]{1,0:T(8,128)(2,1)} %convolution_convert_fusion.4), channel_id=1, source_target_pairs={{0,16},{16,0},{1,17},{17,1},{2,18},{18,2},{3,19},{19,3},{4,20},{20... | collective-permute-start | bytes 3981320 | tf_op jit(solution)/shard_map/ppermute | solution.py:29
  1232.8 100.0 %collective-permute-start.147 = (bf16[576,1728]{1,0:T(8,128)(2,1)}, bf16[576,1728]{1,0:T(8,128)(2,1)}, u32[]{:S(2)}, u32[]{:S(2)}) collective-permute-start(bf16[576,1728]{1,0:T(8,128)(2,1)} %convolution_convert_fusion.6), channel_id=1, source_target_pairs={{0,16},{16,0},{1,17},{17,1},{2,18},{18,2},{3,19},{19,3},{4,20},{20... | collective-permute-start | bytes 5971976 | tf_op jit(solution)/shard_map/ppermute | solution.py:29
  1236.7 96.1 %collective-permute-start.146 = (bf16[576,1728]{1,0:T(8,128)(2,1)}, bf16[576,1728]{1,0:T(8,128)(2,1)}, u32[]{:S(2)}, u32[]{:S(2)}) collective-permute-start(bf16[576,1728]{1,0:T(8,128)(2,1)} %convolution_convert_fusion.7), channel_id=1, source_target_pairs={{0,16},{16,0},{1,17},{17,1},{2,18},{18,2},{3,19},{19,3},{4,20},{20... | collective-permute-start | bytes 5971976 | tf_op jit(solution)/shard_map/ppermute | solution.py:29
  1240.1 71.0 %collective-permute-start.145 = (bf16[4,72,1152]{2,1,0:T(8,128)(2,1)}, bf16[4,72,1152]{2,1,0:T(8,128)(2,1)}, u32[]{:S(2)}, u32[]{:S(2)}) collective-permute-start(bf16[4,72,1152]{2,1,0:T(8,128)(2,1)} %split.85), channel_id=1, source_target_pairs={{0,1},{1,0},{2,3},{3,2},{4,5},{5,4},{6,7},{7,6},{8,9},{9,8},{10,11... | collective-permute-start | bytes 1990664 | tf_op jit(solution)/shard_map/ppermute | solution.py:29
  1357.9 45.3 %collective-permute-start.158 = (bf16[4,72,640]{2,1,0:T(8,128)(2,1)S(1)}, bf16[4,72,640]{2,1,0:T(8,128)(2,1)S(1)}, u32[]{:S(2)}, u32[]{:S(2)}) collective-permute-start(bf16[4,72,640]{2,1,0:T(8,128)(2,1)S(1)} %dynamic-slice_bitcast_fusion.12), channel_id=1, source_target_pairs={{0,2},{2,0},{4,6},{6,4},{8,10},{10,8},{12,14},{14,12},{1,3},{3,1},... | collective-permute-start | bytes 1105928 | tf_op jit(solution)/shard_map/ppermute | solution.py:29
  (330 other events, 4135.1 us)

commit v4 on v3

--- a/solution.py
+++ b/solution.py
@@ -81,13 +81,22 @@
     def over_core(self, v):
         return swap_with(v, "dp", self.n_dp, 1)
 
-    def gather_weight(self, v):
+    def with_core(self, mine, layout):
+        return layout, mine + [self.over_core(v) for v in mine]
+
+    def line_gather(self, v):
+        return [swap_with(v, "ctx", self.n_ctx, 2 * k) for k in range(1, self.n_line)]
+
+    def line_stack(self, blocks):
+        return flip_to(jnp.stack(blocks), 0, self.n_line, self.line)
+
+
+    def gather_halves(self, v):
         others = range(1, self.n_tp)
-        got = [swap_with(v, "ctx", self.n_ctx, 2 * k) for k in range(1, self.n_line)]
-        got = yield got
+        got = yield self.line_gather(v)
         half = v.shape[1] // 2
         lines = [
-            flip_to(jnp.stack([b[:, cut] for b in [v] + got]), 0, self.n_line, self.line)
+            self.line_stack([b[:, cut] for b in [v] + got])
             for cut in (slice(0, half), slice(half, None))
         ]
         got = self.over_side(lines[0]), [self.over_tp(lines[1], r) for r in others]
@@ -96,10 +105,37 @@
         strips = jnp.stack([lines[1]] + tp_got)
         got = [self.over_tp(block, r) for r in others], self.over_side(strips)
         tp_got, side_got = yield got
-        first = [block] + tp_got
-        second = self.pair_stack(strips, side_got)
-        mine = first + [second]
-        return mine + [self.over_core(v) for v in mine]
+        mine = [block] + tp_got + [self.pair_stack(strips, side_got)]
+        layout = tuple(((r, None, half), (self.n_tp, r, half)) for r in range(self.n_tp))
+        return self.with_core(mine, layout)
+
+    def gather_sideways(self, v):
+        got = yield self.line_gather(v)
+        line = self.line_stack([v] + got)
+        got = yield [self.over_tp(line, r) for r in range(1, self.n_tp)]
+        strips = jnp.stack([line] + got)
+        got = yield self.over_side(strips)
+        mine = [self.pair_stack(strips, got)]
+        layout = tuple(((0, r, v.shape[1]),) for r in range(self.n_tp))
+        return self.with_core(mine, layout)
+
+    def gather_rest(self, block):
+        got = yield [self.over_tp(block, r) for r in range(1, self.n_tp)]
+        layout = tuple(((r, None, block.shape[1]),) for r in range(self.n_tp))
+        return self.with_core([block] + got, layout)
+
+    def scatter_far(self, left, rights):
+        others = range(1, self.n_tp)
+        half_width = left.shape[1] // 2
+        mine, theirs = left[:, :half_width], left[:, half_width:]
+        got = [self.over_core(dot(theirs, v, TN).astype(BF16)) for v in rights]
+        got = yield got
+        totals = [(dot(mine, v, TN) + g.astype(F32)).astype(BF16) for v, g in zip(rights, got)]
+        if len(totals) == 1:
+            totals = jnp.split(totals[0], self.n_tp, axis=1)
+        got = yield [self.over_tp(totals[r], r) for r in others]
+        total = (totals[0].astype(F32) + sum(v.astype(F32) for v in got)).astype(BF16)
+        return lax.psum_scatter(total, "ctx", scatter_dimension=0, tiled=True).astype(F32)
 
     def scatter_weight(self, left, rights):
         others = range(1, self.n_tp)
@@ -149,6 +185,15 @@
         self.pending = next(steps)
 
 
+def at_once(steps):
+    pending = next(steps)
+    while True:
+        try:
+            pending = steps.send(pending)
+        except StopIteration as stop:
+            return stop.value
+
+
 class Lanes:
     def __init__(self):
         self.tasks = []
@@ -308,66 +353,60 @@
     )(*xs, grad, lse)
 
 
-def weight_specs(pieces):
-    return [pl.BlockSpec(memory_space=pl.ANY)] * len(pieces)
-
-
 def weight_scratch(pieces):
-    strips = len(pieces) // 2 - 1
-    rows, half = pieces[0].shape
+    layout, arrays = pieces
+    columns = sum(part[2] for strip in layout for part in strip)
+    parts = max(len(strip) for strip in layout)
     return [
-        pltpu.VMEM((2 * rows, strips * 2 * half), BF16),
-        pltpu.SemaphoreType.DMA((2, strips, 2)),
+        pltpu.VMEM((2 * arrays[0].shape[-2], columns), BF16),
+        pltpu.SemaphoreType.DMA((2, len(layout), parts)),
     ]
 
 
-def weight_copies(refs, w_s, sems):
+def weight_copies(layout, refs, w_s, sems):
     count = len(refs) // 2
-    copies = [([], []) for _ in range(count - 1)]
+    rows = w_s.shape[0] // 2
+    copies = [[] for _ in layout]
     for group in range(2):
-        firsts, seconds = refs[group * count : group * count + count - 1], refs[group * count + count - 1]
-        for strip, first in enumerate(firsts):
-            rows, half = first.shape
-            for part, source in enumerate((first, seconds.at[strip])):
-                target = w_s.at[pl.ds(group * rows, rows), pl.ds((2 * strip + part) * half, half)]
-                copies[strip][part].append(
+        low = 0
+        for strip, parts in enumerate(layout):
+            for part, (place, entry, columns) in enumerate(parts):
+                source = refs[group * count + place]
+                if entry is not None:
+                    source = source.at[entry]
+                target = w_s.at[pl.ds(group * rows, rows), pl.ds(low, columns)]
+                low += columns
+                copies[strip].append(
                     pltpu.make_async_copy(source, target, sems.at[group, strip, part])
                 )
     return copies
 
 
-def start_copies(copies):
-    for strip in copies:
-        for part in strip:
-            for copy in part:
-                copy.start()
-
-
-def await_copies(parts):
+def await_copies(copies):
     @pl.when(pl.program_id(0) == 0)
     def _():
-        for part in parts:
-            for copy in part:
-                copy.wait()
-
-
-def turn_copies(parts, w_s, t_s):
+        for copy in copies:
+            copy.wait()
+
+
+def turn_copies(copies, w_s, t_s):
     @pl.when(pl.program_id(0) == 0)
     def _():
-        low = 0
-        for part in parts:
-            for copy in part:
+        size = w_s.shape[1] // len(copies) // 2
+        for strip, waits in enumerate(copies):
+            for copy in waits:
                 copy.wait()
-            size = w_s.shape[1] // len(parts)
-            t_s[low : low + size] = w_s[:, low : low + size].T
-            low += size
+            for low in (2 * strip * size, (2 * strip + 1) * size):
+                t_s[low : low + size] = w_s[:, low : low + size].T
 
 
 def begin_copies(*many):
     @pl.when(pl.program_id(0) == 0)
     def _():
         for copies in many:
-            start_copies(copies)
+            for strip in copies:
+                for copy in strip:
+                    copy.start()
 
 
 def row_normal(v):
@@ -423,8 +462,8 @@
         dv_s[:, low:high] = jnp.where(mask, dv, dv_s[:, low:high])
 
 
-def branch_kernel(strips, stride, x_ref, mod_ref, *refs):
-    count = 2 * (strips + 1)
+def branch_kernel(layout, count, stride, x_ref, mod_ref, *refs):
+    strips = len(layout)
     w_refs = refs[:count]
     h_ref, qkv_ref, lse_ref, o_ref, a_ref, y_ref, g_ref = refs[count : count + 7]
     w_s, sems, p_s, o_s, z_s = refs[count + 7 :]
@@ -433,7 +472,7 @@
     padded = o_s.shape[1]
     spare = padded - head_cols
     columns = w_s.shape[1] // strips
-    copies = weight_copies(w_refs, w_s, sems)
+    copies = weight_copies(layout, w_refs, w_s, sems)
     begin_copies(copies)
     x = x_ref[...].astype(F32)
     shift_a, scale_a, gate_a, shift_m, scale_m = [mod_ref[0, i : i + 1, :] for i in range(5)]
@@ -469,8 +508,10 @@
     g_ref[...] = (row_normal(y)[0] * (1.0 + scale_m) + shift_m).astype(BF16)
 
 
-def branch_back_kernel(strips, stride, x_ref, mod_ref, da_ref, dy_ref, qkv_ref, lse_ref, *refs):
-    count = 2 * (strips + 1)
+def branch_back_kernel(
+    layout, count, stride, x_ref, mod_ref, da_ref, dy_ref, qkv_ref, lse_ref, *refs
+):
+    strips = len(layout)
     w_refs = refs[:count]
     dx_ref, sums_ref = refs[count : count + 2]
     out_refs = refs[count + 2 : count + 2 + strips]
@@ -480,7 +521,7 @@
     padded = g_s.shape[1]
     spare = padded - head_cols
     columns = w_s.shape[1] // strips
-    copies = weight_copies(w_refs, w_s, sems)
+    copies = weight_copies(layout, w_refs, w_s, sems)
     begin_copies(copies)
     heads = head_cols // HEAD_DIM
     allowed = same_sequence(rows, stride) if stride > 1 else None
@@ -512,15 +553,16 @@
 GELU_B = 0.044715
 
 
-def up_kernel(strips, g_ref, *refs):
-    count = 2 * (strips + 1)
+def up_kernel(layout, count, g_ref, *refs):
+    strips = len(layout)
     z_ref, slope_ref, w_s, sems = refs[count:]
-    copies = weight_copies(refs[:count], w_s, sems)
+    copies = weight_copies(layout, refs[:count], w_s, sems)
     begin_copies(copies)
     half = w_s.shape[1] // (2 * strips)
     g = g_ref[...]
     for index in range(2 * strips):
-        await_copies([copies[index // 2][index % 2]])
+        if index % 2 == 0:
+            await_copies(copies[index // 2])
         low = index * half
         u = dot(g, w_s[:, low : low + half])
         square = u * u
@@ -532,26 +574,29 @@
         slope_ref[:, low : low + half] = slope.astype(BF16)
 
 
-def down_kernel(strips, z_ref, y_ref, mod_ref, *refs):
-    count = 2 * (strips + 1)
+def down_kernel(layout, count, z_ref, y_ref, mod_ref, *refs):
+    strips = len(layout)
     m_ref, x_ref, w_s, sems, t_s = refs[count:]
-    copies = weight_copies(refs[:count], w_s, sems)
+    copies = weight_copies(layout, refs[:count], w_s, sems)
     begin_copies(copies)
-    half = w_s.shape[1] // (2 * strips)
-    turn_copies([copies[i // 2][i % 2] for i in range(2 * strips)], w_s, t_s)
+    turn_copies(copies, w_s, t_s)
     total = dot(z_ref[...], t_s[...])
     m_ref[...] = total.astype(BF16)
     x_ref[...] = (y_ref[...] + mod_ref[0, 5:6, :] * total).astype(BF16)
 
 
-def mlp_back_kernel(strips, dx_ref, mod_ref, m_ref, slope_ref, y_ref, a_ref, *refs):
-    count = 2 * (strips + 1)
-    dm_ref, du_ref, dy_ref, da_ref, sums_ref, up_s, up_sems, down_s, down_sems, t_s = refs[2 * count :]
-    ups = weight_copies(refs[:count], up_s, up_sems)
-    downs = weight_copies(refs[count : 2 * count], down_s, down_sems)
+def mlp_back_kernel(
+    up_layout, ups_count, down_layout, count, dx_ref, mod_ref, m_ref, slope_ref, y_ref, a_ref, *refs
+):
+    strips = len(up_layout)
+    (dm_ref, du_ref, dy_ref, da_ref, sums_ref, up_s, up_sems, down_s, down_sems, t_s) = refs[
+        ups_count + count :
+    ]
+    ups = weight_copies(up_layout, refs[:ups_count], up_s, up_sems)
+    downs = weight_copies(down_layout, refs[ups_count : ups_count + count], down_s, down_sems)
     begin_copies(downs, ups)
     half = up_s.shape[1] // (2 * strips)
-    turn_copies([ups[i // 2][i % 2] for i in range(2 * strips)], up_s, t_s)
+    turn_copies(ups, up_s, t_s)
     scale_m, gate_m, share, gate_a = [mod_ref[0, i : i + 1, :] for i in (4, 5, 6, 2)]
     dx = dx_ref[...].astype(F32) * share
     sums_ref[...] = jnp.zeros(sums_ref.shape, F32)
@@ -561,7 +606,8 @@
     grad = jnp.zeros(y_ref.shape, F32)
     for index in range(2 * strips):
         low = index * half
-        await_copies([downs[index // 2][index % 2]])
+        if index % 2 == 0:
+            await_copies(downs[index // 2])
         dz = dot(dm, down_s[:, low : low + half])
         du = (dz * slope_ref[:, low : low + half].astype(F32)).astype(BF16)
         du_ref[:, low : low + half] = du
@@ -588,9 +634,9 @@
         else:
             operands.append(arrays[v])
             specs.append(row_block(rows, arrays[v].shape[1]))
-    for pieces in weights:
+    for _, pieces in weights:
         operands += pieces
-        specs += weight_specs(pieces)
+        specs += [pl.BlockSpec(memory_space=pl.ANY)] * len(pieces)
     out_specs = [row_block(rows, v.shape[1]) for v in outs]
     out_shape = list(outs)
     if sums is not None:
@@ -619,7 +665,7 @@
 
 def fused_branch(x, mods, pieces, clips, stride):
     count, width = x.shape
-    rows, strips = count // clips, len(pieces) // 2 - 1
+    rows, strips = count // clips, len(pieces[0])
     head_cols = width // strips
     padded = padded_to(head_cols)
     outs = [
@@ -637,7 +683,7 @@
         pltpu.VMEM((rows, padded), BF16),
     ]
     return block_call(
-        functools.partial(branch_kernel, strips, stride),
+        functools.partial(branch_kernel, pieces[0], len(pieces[1]), stride),
         clips, rows, [x], mods, [pieces], outs, None, scratch,
         12 * count * width * width, [0, None],
     )
@@ -645,7 +691,7 @@
 
 def fused_branch_back(x, mods, da, dy, qkv, lse, pieces, clips, stride):
     count, width = x.shape
-    rows, strips = count // clips, len(pieces) // 2 - 1
+    rows, strips = count // clips, len(pieces[0])
     head_cols = width // strips
     padded = padded_to(head_cols)
     outs = [shape_of(count, width)] + [shape_of(count, 3 * head_cols) for _ in range(strips)]
@@ -654,7 +700,7 @@
         pltpu.VMEM((rows, padded), BF16),
     ] + [pltpu.VMEM((rows, padded), F32)] * 3
     return block_call(
-        functools.partial(branch_back_kernel, strips, stride),
+        functools.partial(branch_back_kernel, pieces[0], len(pieces[1]), stride),
         clips, rows, [x, da, dy, qkv, lse], mods, [pieces], outs, 1, scratch,
         16 * count * width * width, [0, None, 1, 2, 3, 4],
     )
@@ -662,21 +708,21 @@
 
 def fused_up(g, mods, pieces, clips):
     count, width = g.shape
-    rows, strips = count // clips, len(pieces) // 2 - 1
-    units = strips * 2 * pieces[0].shape[1]
+    rows, strips = count // clips, len(pieces[0])
+    units = sum(part[2] for strip in pieces[0] for part in strip)
     outs = [shape_of(count, units), shape_of(count, units)]
     return block_call(
-        functools.partial(up_kernel, strips),
+        functools.partial(up_kernel, pieces[0], len(pieces[1])),
         clips, rows, [g], mods, [pieces], outs, None, [], 2 * count * width * units, [0],
     )
 
 
 def fused_down(z, y, mods, pieces, clips):
     count, width = y.shape
-    rows, strips = count // clips, len(pieces) // 2 - 1
+    rows, strips = count // clips, len(pieces[0])
     outs = [shape_of(count, width), shape_of(count, width)]
     return block_call(
-        functools.partial(down_kernel, strips),
+        functools.partial(down_kernel, pieces[0], len(pieces[1])),
         clips, rows, [z, y], mods, [pieces], outs, None, [pltpu.VMEM((z.shape[1], width), BF16)],
         2 * z.size * width, [0, 1, None],
     )
@@ -684,7 +730,7 @@
 
 def fused_mlp_back(dx, mods, m, slope, y, a, ups, downs, clips):
     count, width = y.shape
-    rows, strips = count // clips, len(ups) // 2 - 1
+    rows = count // clips
     outs = [
         shape_of(count, width),
         shape_of(*slope.shape),
@@ -692,7 +738,7 @@
         shape_of(count, width),
     ]
     return block_call(
-        functools.partial(mlp_back_kernel, strips),
+        functools.partial(mlp_back_kernel, ups[0], len(ups[1]), downs[0], len(downs[1])),
         clips, rows, [dx, m, slope, y, a], mods, [ups, downs], outs, 4,
         [pltpu.VMEM((slope.shape[1], width), BF16)],
         4 * slope.size * width, [0, None, 1, 2, 3, 4],
@@ -776,15 +822,25 @@
     cond_rows = lax.dynamic_slice_in_dim(cond_all, first_row, rows_here, axis=1)
     ada_low = w_ada.astype(BF16)
     shares = jnp.stack([dot(cond_rows, ada_low[level]) for level in range(LAYERS)], axis=1)
-    sums = shares[:clips] + swap_with(shares[clips:], "dp", n_dp, 1)
-    step = 1
-    while step < n_ctx:
-        sums = sums + swap_with(sums, "ctx", n_ctx, step)
-        step *= 2
-    strips = [sums] + [swap_with(sums, "tp", n_tp, r) for r in range(1, n_tp)]
-    strips = flip_to(jnp.stack(strips, axis=2), 2, n_tp, moves.tp)
-    mods = strips.reshape(clips, LAYERS, 6, width)
-    mods = [moves.halves(mods[:, level]) for level in range(LAYERS)]
+
+    def total_over_ctx(v):
+        got = yield [swap_with(v, "ctx", n_ctx, 2 * k) for k in range(1, n_ctx // 2)]
+        return v + sum(got)
+
+    def modulation_vectors():
+        sums = shares[:clips] + swap_with(shares[clips:], "dp", n_dp, 1)
+        sums = yield from total_over_ctx(sums)
+        pairs = [
+            [(c * n_tp + t, (c ^ dx) * n_tp + (t ^ r)) for c in range(n_ctx) for t in range(n_tp)]
+            for r in range(n_tp)
+            for dx in range(2)
+        ]
+        got = yield [lax.ppermute(sums, ("ctx", "tp"), entry) for entry in pairs[1:]]
+        got = [sums] + got
+        strips = [got[2 * r] + got[2 * r + 1] for r in range(n_tp)]
+        strips = flip_to(jnp.stack(strips, axis=2), 2, n_tp, moves.tp)
+        found = strips.reshape(clips, LAYERS, 6, width)
+        return [moves.halves(found[:, level]) for level in range(LAYERS)]
 
     def to_frames(v):
         v = v.reshape(clips, frames_here, n_ctx, piece, width)
@@ -865,21 +921,47 @@
         shards.append(w_up[level].astype(BF16))
         shards.append(w_down[level].T.astype(BF16))
     lanes = Lanes()
-    gathers = []
-
-    def tick(values=()):
-        rest, values = lanes.fence((shards[len(gathers) :], values))
-        if rest:
-            gathers.append(lanes.start(moves.gather_weight(rest[0])))
+    gathers = {}
+
+    shards, blocks = (
+        shards,
+        {
+            index: lax.all_gather(shards[index], "ctx", axis=0, tiled=True)
+            for index in range(1, len(shards), 2)
+        },
+    )
+
+    def set_out(index):
+        if index in blocks:
+            steps = moves.gather_rest(blocks[index])
+        elif index == 0:
+            steps = moves.gather_halves(shards[index])
+        else:
+            steps = moves.gather_sideways(shards[index])
+        gathers[index] = lanes.start(steps)
+
+    def tick(values=(), out=()):
+        held = {index: blocks.get(index, shards[index]) for index in out}
+        held, values = lanes.fence((held, values))
+        for index in out:
+            if index in blocks:
+                blocks[index] = held[index]
+            else:
+                shards[index] = held[index]
+            set_out(index)
         return values
 
     def whole(index):
-        pieces = gathers[index].result
-        count = len(pieces) // 2
+        layout, arrays = gathers[index].result
+        count = len(arrays) // 2
         groups = []
-        for group in (pieces[:count], pieces[count:]):
-            strips = [v for r in range(n_tp) for v in (group[r], group[-1][r])]
-            groups.append(jnp.concatenate(strips, axis=1))
+        for group in (arrays[:count], arrays[count:]):
+            parts = [
+                group[place] if entry is None else group[place][entry]
+                for strip in layout
+                for place, entry, _ in strip
+            ]
+            groups.append(jnp.concatenate(parts, axis=1))
         return jnp.concatenate(groups, axis=0)
 
     def attention_weights(index):
@@ -891,12 +973,14 @@
     def modulations(level):
         return [mods[level][:, i] for i in range(6)]
 
+    set_out(0)
     moved = lanes.start(to_frames(moves.halves(tokens)))
-    gathers.append(lanes.start(moves.gather_weight(shards[0])))
-    tick()
+    vectors_task = lanes.start(modulation_vectors())
+    tick(out=(2,))
     residual = moved.result
     tick()
-    tick()
+    tick(out=(1,))
+    mods = vectors_task.result
     fused = (
         whole_frames
         and head_cols % 32 == 0
@@ -910,7 +994,22 @@
     mod_grads = [None] * LAYERS
 
     def start_scatter(level, name, left, rights):
-        scatters[level, name] = lanes.start(moves.scatter_weight(left, rights))
+        far = level and name != "out"
+        steps = (moves.scatter_far if far else moves.scatter_weight)(left, rights)
+        scatters[level, name] = lanes.start(steps)
+
+    def mod_strip(grads):
+        parts = moves.halves(grads).reshape(clips, n_tp, -1)
+        parts = flip_to(parts, 1, n_tp, moves.tp)
+        got = yield [swap_with(parts[:, r], "tp", n_tp, r) for r in range(1, n_tp)]
+        strip = parts[:, 0] + sum(got)
+        strip = yield from total_over_ctx(strip)
+        got = yield swap_with(strip, "ctx", n_ctx, 1)
+        strip = strip + got
+        got = yield swap_with(strip, "dp", n_dp, 1)
+        return jnp.concatenate([strip, got], axis=0)
+
+    strips = {}
 
     def fused_passes(v):
         vectors, saved = [], []
@@ -923,9 +1022,9 @@
             stride = piece if level % 2 else 1
             joined = gathers[3 * level].result
             kept = fused_branch(v, vectors[level], joined, clips, stride)
-            normed, qkv, lse, result, branch, middle, normed_mlp = tick(kept)
+            normed, qkv, lse, result, branch, middle, normed_mlp = tick(kept, (4,) if level == 0 else ())
             up = gathers[3 * level + 1].result
-            act, slope = tick(fused_up(normed_mlp, vectors[level], up, clips))
+            act, slope = tick(fused_up(normed_mlp, vectors[level], up, clips), (3,) if level == 0 else ())
             down = gathers[3 * level + 2].result
             branch_mlp, after = fused_down(act, middle, vectors[level], down, clips)
             saved.append((v, normed, qkv, lse, result, branch, middle, normed_mlp))
@@ -933,9 +1032,9 @@
             v = after
             if level == 0:
                 moved = lanes.start(frames_to_clips(shaped(v)))
-                tick()
-                turned = lanes.start(here_to_clips(moves.halves(cotangent)))
-                tick()
+                tick(out=(5,))
+                late = tick(cotangent)
+                turned = lanes.start(here_to_clips(moves.halves(late)))
                 v = flat(moved.result)
         finished = lanes.start(clips_to_here(moves.halves(shaped(v))))
         grad = flat(turned.result)
@@ -947,6 +1046,7 @@
             )
             grad_branch, grad_pre, grad_middle, grad_out, sums = lanes.fence(back)
             start_scatter(level, "down", grad_branch, [act])
+            grad_out = lanes.fence(grad_out, (finished,))
             if level == 0:
                 start_scatter(level, "up", normed_mlp, [grad_pre])
                 grad_out = lanes.fence(grad_out)
@@ -959,9 +1059,10 @@
                 moved = lanes.start(clips_to_frames(shaped(grad)))
                 start_scatter(level, "up", normed_mlp, [grad_pre])
                 lanes.fence()
+                start_scatter(level, "qkv", normed, grad_qkv)
                 start_scatter(level, "out", grad_out, [result])
-                start_scatter(level, "qkv", normed, grad_qkv)
                 lanes.fence()
+                strips[level] = lanes.start(mod_strip(mod_grads[level]))
                 grad = flat(moved.result)
             else:
                 start_scatter(level, "qkv", normed, grad_qkv)
@@ -984,14 +1085,14 @@
                 saved = [entry[1] for entry in saved]
             else:
                 result, saved = attend(projected, rows, stride)
-            result, saved = tick((result, saved))
+            result, saved = tick((result, saved), (4,) if level == 0 else ())
             branch = shaped(dot(result, outs, NT))
             middle = residual + gate_a[:, None] * branch
             normed_mlp = flat(modulate(middle, shift_m, scale_m))
             up = whole(3 * level + 1)
             pre_act = dot(normed_mlp, up)
             act = gelu(pre_act).astype(BF16)
-            act, pre_act = tick((act, pre_act))
+            act, pre_act = tick((act, pre_act), (3,) if level == 0 else ())
             down = whole(3 * level + 2)
             branch_mlp = shaped(dot(act, down, NT))
             records.append(
@@ -1001,7 +1102,7 @@
             residual = middle + gate_m[:, None] * branch_mlp
             if spatial:
                 moved = lanes.start(frames_to_clips(residual.astype(BF16)))
-                tick()
+                tick(out=(5,))
                 turned = lanes.start(here_to_clips(moves.halves(cotangent)))
                 tick()
                 residual = moved.result.astype(F32)
@@ -1071,16 +1172,10 @@
     ada_grads = []
     cond_part = 0.0
     for level in range(LAYERS):
-        strips = moves.halves(mod_grads[level]).reshape(clips, n_tp, -1)
-        strips = flip_to(strips, 1, n_tp, moves.tp)
-        strip = strips[:, 0]
-        for r in range(1, n_tp):
-            strip = strip + swap_with(strips[:, r], "tp", n_tp, r)
-        step = 1
-        while step < n_ctx:
-            strip = strip + swap_with(strip, "ctx", n_ctx, step)
-            step *= 2
-        strip = jnp.concatenate([strip, swap_with(strip, "dp", n_dp, 1)], axis=0)
+        if level in strips:
+            strip = strips[level].result
+        else:
+            strip = at_once(mod_strip(mod_grads[level]))
         ada_grads.append(
             lax.dot_general(cond_rows.astype(F32), strip, TN, precision=HIGHEST)
         )

time: 1470 us -> 1390 us (0.946)
  waiting for transfers between devices: 444 us -> 409 us
  starting transfers between devices: 227 us -> 205 us
  other arithmetic: 127 us -> 112 us
    ppermute x8, waiting for transfers between devices: 48.9 us -> 17 us  [trade(): block = lax.ppermute(block, ('ctx', 'tp'), pairs)]
    ppermute x161 -> x115, starting transfers between devices: 216 us -> 192 us  [swap_with(): return lax.ppermute(v, axis_name, [(i, i ^ k) for i in range(n)])]
    ppermute x161 -> x115, waiting for transfers between devices: 395 us -> 380 us  [swap_with(): return lax.ppermute(v, axis_name, [(i, i ^ k) for i in range(n)])]
    unnamed x450 -> x304, local copies, waits for them, and re-layouts: 44.3 us -> 34.6 us
  transfers between devices with their start and end apart: 169 -> 132, of which waited for: 56 -> 41; matrix products, arithmetic and copies ran while one was open for 20% -> 21% of each run, Pallas kernels for 25% -> 26%
where the time goes in v4:
time: 1390 us; the launch traced here: 1380 us
  waiting for transfers between devices  409 us (29%)
  Pallas kernels  379 us (27%)
  starting transfers between devices  205 us (15%)
  matrix products  136 us (10%)
  local copies, waits for them, and re-layouts  123 us (9%)
  other arithmetic  112 us (8%)
  between operations  17.7 us (1%)
    ppermute x115, waiting for transfers between devices, swap_with(): return lax.ppermute(v, axis_name, [(i, i ^ k) for i in range(n)])  380 us
    pallas_call x10, Pallas kernels, block_call(): pl.pallas_call(kernel, grid=(clips,), in_specs=specs, out_specs=out_specs...  379 us
    ppermute x115, starting transfers between devices, swap_with(): return lax.ppermute(v, axis_name, [(i, i ^ k) for i in range(n)])  192 us
    dot_general x22, matrix products, dot(): return lax.dot_general(a, b, dims, preferred_element_type=F32)  132 us
    unnamed x304, local copies, waits for them, and re-layouts  34.6 us
  transfers between devices with their start and end apart: 132, of which 41 were waited for; matrix products, arithmetic and copies ran while one was open for 21% of the time, Pallas kernels for 26%

profile of v4, /device:TPU:0, one launch (start us, length us, event | category | flops | bytes accessed | tf_op | source)
XLA Modules:
  0.0 1381.1 jit_solution(2887948313012138834)
XLA Ops:
  51.2 4.6 collective-permute-done.6
  57.6 9.3 collective-permute-done.7
  66.9 6.7 collective-permute-start.8
  73.8 3.5 collective-permute-done.8
  95.6 8.7 collective-permute-done.14
  104.3 23.3 %collective-permute-done.15 = bf16[72,2304]{1,0:T(8,128)(2,1)S(1)} collective-permute-done((bf16[72,2304]{1,0:T(8,128)(2,1)S(1)}, bf16[72,2304]{1,0:T(8,128)(2,1)S(1)}, u32[]{:S(2)}, u32[]{:S(2)}) %collective-permute-start.15) | collective-permute-done | bytes 331808 | tf_op jit(solution)/shard_map/ppermute | solution.py:29
  135.0 42.3 %collective-permute-done.19 = bf16[4,72,2304]{2,1,0:T(8,128)(2,1)} collective-permute-done((bf16[4,72,2304]{2,1,0:T(8,128)(2,1)S(1)}, bf16[4,72,2304]{2,1,0:T(8,128)(2,1)}, u32[]{:S(2)}, u32[]{:S(2)}) %collective-permute-start.19) | collective-permute-done | bytes 1327136 | tf_op jit(solution)/shard_map/ppermute | solution.py:29
  193.0 39.9 %shard_map.152 = (bf16[1024,1152]{1,0:T(8,128)(2,1)}, bf16[1024,3840]{1,0:T(8,128)(2,1)}, f32[1024,128]{1,0:T(8,128)}, bf16[1024,1152]{1,0:T(8,128)(2,1)}, bf16[...) custom-call(bf16[1024,1152]{1,0:T(8,128)(2,1)} %bitcast.807, ...), custom_call_target="tpu_custom_call" | custom-call | flops 16307453952 | bytes 13123584 | tf_op jit(solution)/shard_map/pallas_call | solution.py:650
  232.9 15.2 %collective-permute-done.23 = bf16[2,4,72,2304]{3,2,1,0:T(8,128)(2,1)} collective-permute-done((bf16[2,4,72,2304]{3,2,1,0:T(8,128)(2,1)S(1)}, bf16[2,4,72,2304]{3,2,1,0:T(8,128)(2,1)}, u32[]{:S(2)}, u32[]{:S(2)}) %collective-permute-start.23) | collective-permute-done | bytes 2654240 | tf_op jit(solution)/shard_map/ppermute | solution.py:29
  255.6 12.7 collective-permute-start.27
  271.7 26.9 %shard_map.153 = (bf16[1024,4608]{1,0:T(8,128)(2,1)}, bf16[1024,4608]{1,0:T(8,128)(2,1)}) custom-call(bf16[1024,1152]{1,0:T(8,128)(2,1)} %get-tuple-element.221.g_ref, bf16[576,2304]{1,0:T(8,128)(2,1)} %bitcast.66.refs_0_, bf16[576,2304]{1,0:T(8,128)(2,1)} %collective-permute-done.24.refs_1_, bf16[576,2304]{1,0:T(8,128)(2,1)} %collective-permute-done.25.refs_2_, ...), custom_call_target="tpu_custom_call" | custom-call | flops 10871635968 | bytes 12976128 | tf_op jit(solution)/shard_map/pallas_call | solution.py:650
  305.5 22.0 %shard_map.154 = (bf16[1024,1152]{1,0:T(8,128)(2,1)}, bf16[1024,1152]{1,0:T(8,128)(2,1)}) custom-call(bf16[1024,4608]{1,0:T(8,128)(2,1)} %get-tuple-element.226.z_ref, f32[1024,1152]{1,0:T(8,128)} %get-tuple-element.227.y_ref, f32[4,8,1152]{2,1,0:T(8,128)} %concatenate.597.mod_ref, bf16[2,576,2304]{2,1,0:T(8,128)(2,1)} %bitcast.96.refs_0_.refs_4_, ...), custom_call_target="tpu_custom_call" | custom-call | flops 10871635968 | bytes 24920064 | tf_op jit(solution)/shard_map/pallas_call | solution.py:650
  334.3 5.3 all-gather.7.cloned.1.call-done.refs_0_.refs_2_
  339.7 65.7 %collective-permute-done.32.refs_1_ = bf16[576,2304]{1,0:T(8,128)(2,1)} collective-permute-done((bf16[576,2304]{1,0:T(8,128)(2,1)}, bf16[576,2304]{1,0:T(8,128)(2,1)}, u32[]{:S(2)}, u32[]{:S(2)}) %collective-permute-start.32) | collective-permute-done | bytes 2654240 | tf_op jit(solution)/shard_map/ppermute | solution.py:29
  405.3 10.8 collective-permute-done.33
  427.7 11.4 collective-permute-start.38
  444.2 34.2 %collective-permute-done.38 = bf16[4,4,1,16,1152]{4,3,1,0,2:T(8,128)(2,1)S(1)} collective-permute-done((bf16[4,4,1,16,1152]{4,3,1,0,2:T(8,128)(2,1)}, bf16[4,4,1,16,1152]{4,3,1,0,2:T(8,128)(2,1)S(1)}, u32[]{:S(2)}, u32[]{:S(2)}) %collective-permute-start.38) | collective-permute-done | bytes 589856 | tf_op jit(solution)/shard_map/ppermute | solution.py:29
  502.0 39.8 %shard_map.155 = (bf16[1024,1152]{1,0:T(8,128)(2,1)}, bf16[1024,3840]{1,0:T(8,128)(2,1)}, f32[1024,128]{1,0:T(8,128)}, bf16[1024,1152]{1,0:T(8,128)(2,1)}, bf16[...) custom-call(bf16[1024,1152]{1,0:T(8,128)(2,1)} %bitcast.809, ...), custom_call_target="tpu_custom_call" | custom-call | flops 16307453952 | bytes 13123584 | tf_op jit(solution)/shard_map/pallas_call | solution.py:650
  542.5 10.1 collective-permute-start.46
  554.2 26.6 %shard_map.156 = (bf16[1024,4608]{1,0:T(8,128)(2,1)}, bf16[1024,4608]{1,0:T(8,128)(2,1)}) custom-call(bf16[1024,1152]{1,0:T(8,128)(2,1)} %get-tuple-element.251.g_ref, bf16[2,576,2304]{2,1,0:T(8,128)(2,1)} %bitcast.154.refs_0_, bf16[2,576,2304]{2,1,0:T(8,128)(2,1)} %collective-permute-done.44.refs_1_), custom_call_target="tpu_custom_call" | custom-call | flops 10871635968 | bytes 12976128 | tf_op jit(solution)/shard_map/pallas_call | solution.py:650
  580.8 16.5 %collective-permute-done.46 = bf16[4,2,2,1,16,1152]{5,4,1,2,0,3:T(8,128)(2,1)S(1)} collective-permute-done((bf16[4,2,2,1,16,1152]{5,4,1,2,0,3:T(8,128)(2,1)S(1)}, bf16[4,2,2,1,16,1152]{5,4,1,2,0,3:T(8,128)(2,1)S(1)}, u32[]{:S(2)}, u32[]{:S(2)}) %collective-permute-start.46) | collective-permute-done | bytes 589856 | tf_op jit(solution)/shard_map/ppermute | solution.py:29
  597.3 22.4 %shard_map.157 = (bf16[1024,1152]{1,0:T(8,128)(2,1)}, bf16[1024,1152]{1,0:T(8,128)(2,1)}) custom-call(bf16[1024,4608]{1,0:T(8,128)(2,1)} %get-tuple-element.256.z_ref, f32[1024,1152]{1,0:T(8,128)} %get-tuple-element.257.y_ref, f32[4,8,1152]{2,1,0:T(8,128)} %pad_maximum_fusion.63.mod_ref, bf16[576,2304]{1,0:T(8,128)(2,1)} %all-gather.7.cloned.1.call-done.refs_0_.refs_2_, ...), custom_call_target="tpu_custom_call" | custom-call | flops 10871635968 | bytes 24920064 | tf_op jit(solution)/shard_map/pallas_call | solution.py:650
  627.9 44.4 %shard_map.158 = (bf16[1024,1152]{1,0:T(8,128)(2,1)}, bf16[1024,4608]{1,0:T(8,128)(2,1)}, f32[1024,1152]{1,0:T(8,128)}, bf16[1024,1152]{1,0:T(8,128)(2,1)}, f32[4,8,1152]{2,1,0:T(8,128)}) custom-call(bf16[1024,1152]{1,0:T(8,128)(2,1)} %bitcast.813, f32[4,8,1152]{2,1,0:T(8,128)} %pad_maximum_fusion.63.mod_ref, bf16[1024,1152]{1,0:T(8,128)(2,1)} %get-tuple-element.263.m_ref, ...), custom_call_target="tpu_custom_call" | custom-call | flops 21743271936 | bytes 42614784 | tf_op jit(solution)/shard_map/pallas_call | solution.py:650
  672.3 11.1 convolution_convert_fusion.3
  687.7 4.1 collective-permute-start.52
  691.8 10.3 convolution_convert_fusion.2
  702.2 7.8 add_convert_fusion.3
  714.1 56.0 %shard_map.159 = (bf16[1024,1152]{1,0:T(8,128)(2,1)}, f32[4,8,1152]{2,1,0:T(8,128)}, bf16[1024,1728]{1,0:T(8,128)(2,1)}, bf16[1024,1728]{1,0:T(8,128)(2,1)}) custom-call(bf16[1024,1152]{1,0:T(8,128)(2,1)} %bitcast.810, f32[4,8,1152]{2,1,0:T(8,128)} %pad_maximum_fusion.63.mod_ref, bf16[1024,1152]{1,0:T(8,128)(2,1)} %get-tuple-element.274.da_ref, ...), custom_call_target="tpu_custom_call" | custom-call | flops 21743271936 | bytes 28590080 | tf_op jit(solution)/shard_map/pallas_call | solution.py:650
  770.0 5.2 convolution_convert_fusion.5
  783.5 4.7 add_convert_fusion.4
  797.5 3.9 convolution_convert_fusion.8
  803.7 6.0 convolution_convert_fusion.9
  810.2 6.2 collective-permute-done.58
  816.4 8.1 add_convert_fusion.2
  831.9 14.9 %collective-permute-done.62 = bf16[4,4,1,16,1152]{4,3,1,0,2:T(8,128)(2,1)S(1)} collective-permute-done((bf16[4,4,1,16,1152]{4,3,1,0,2:T(8,128)(2,1)S(1)}, bf16[4,4,1,16,1152]{4,3,1,0,2:T(8,128)(2,1)S(1)}, u32[]{:S(2)}, u32[]{:S(2)}) %collective-permute-start.62) | collective-permute-done | bytes 589856 | tf_op jit(solution)/shard_map/ppermute | solution.py:29
  846.9 32.7 %collective-permute-start.60 = (bf16[4,4,1,16,1152]{4,3,1,0,2:T(8,128)(2,1)S(1)}, bf16[4,4,1,16,1152]{4,3,1,0,2:T(8,128)(2,1)S(1)}, u32[]{:S(2)}, u32[]{:S(2)}) collective-permute-start(bf16[4,4,1,16,1152]{4,3,1,0,2:T(8,128)(2,1)S(1)} %pad_maximum_fusion.58), channel_id=1, source_target_pairs={{0,4},{2,6},{4,0},{6,2},{8,12},{10,14},{12,8},{14,10},{1,5},{3,7},... | collective-permute-start | bytes 1769480 | tf_op jit(solution)/shard_map/ppermute | solution.py:29
  880.9 8.4 collective-permute-done.61
  891.0 9.1 collective-permute-done.60
  908.7 5.3 add_convert_fusion.10
  918.7 45.9 %shard_map.160 = (bf16[1024,1152]{1,0:T(8,128)(2,1)}, bf16[1024,4608]{1,0:T(8,128)(2,1)}, f32[1024,1152]{1,0:T(8,128)}, bf16[1024,1152]{1,0:T(8,128)(2,1)}, f32[4,8,1152]{2,1,0:T(8,128)}) custom-call(bf16[1024,1152]{1,0:T(8,128)(2,1)} %bitcast.812, f32[4,8,1152]{2,1,0:T(8,128)} %concatenate.597.mod_ref, bf16[1024,1152]{1,0:T(8,128)(2,1)} %get-tuple-element.299.m_ref, ...), custom_call_target="tpu_custom_call" | custom-call | flops 21743271936 | bytes 42614784 | tf_op jit(solution)/shard_map/pallas_call | solution.py:650
  964.7 11.0 convolution_convert_fusion.1
  979.5 4.5 add_convert_fusion.7
  989.3 8.0 convolution_convert_fusion
  1011.8 9.5 add_convert_fusion.1
  1035.4 32.2 %collective-permute-done.80 = f32[4,3456]{1,0:T(4,128)S(1)} collective-permute-done((f32[4,3456]{1,0:T(4,128)S(1)}, f32[4,3456]{1,0:T(4,128)S(1)}, u32[]{:S(2)}, u32[]{:S(2)}) %collective-permute-start.80) | collective-permute-done | bytes 55328 | tf_op jit(solution)/shard_map/ppermute | solution.py:29
  1070.6 6.5 reduce-scatter.4.cloned.1.call-done
  1079.3 9.6 add_convert_fusion
  1104.3 55.3 %shard_map.161 = (bf16[1024,1152]{1,0:T(8,128)(2,1)}, f32[4,8,1152]{2,1,0:T(8,128)}, bf16[1024,1728]{1,0:T(8,128)(2,1)}, bf16[1024,1728]{1,0:T(8,128)(2,1)}) custom-call(bf16[1024,1152]{1,0:T(8,128)(2,1)} %bitcast.808, f32[4,8,1152]{2,1,0:T(8,128)} %concatenate.597.mod_ref, bf16[1024,1152]{1,0:T(8,128)(2,1)} %get-tuple-element.324.da_ref, ...), custom_call_target="tpu_custom_call" | custom-call | flops 21743271936 | bytes 28590080 | tf_op jit(solution)/shard_map/pallas_call | solution.py:650
  1159.7 5.2 convolution_convert_fusion.4
  1167.4 6.3 convolution_convert_fusion.6
  1181.8 3.9 convolution_convert_fusion.7
  1191.6 4.1 collective-permute-done.92
  1232.2 15.5 %collective-permute-done.89 = bf16[4,1,128,1152]{3,2,0,1:T(8,128)(2,1)S(1)} collective-permute-done((bf16[4,1,128,1152]{3,2,0,1:T(8,128)(2,1)}, bf16[4,1,128,1152]{3,2,0,1:T(8,128)(2,1)S(1)}, u32[]{:S(2)}, u32[]{:S(2)}) %collective-permute-start.89) | collective-permute-done | bytes 1179680 | tf_op jit(solution)/shard_map/ppermute | solution.py:29
  1257.1 6.3 collective-permute-done.102
  1268.3 4.6 collective-permute-done.103
  1276.7 3.9 add_convert_fusion.8
  1283.4 3.9 add_convert_fusion.9
  1292.6 4.9 collective-permute-start.109
  1298.8 8.7 collective-permute-done.109
  1309.9 11.8 collective-permute-done.110
  1328.3 6.2 collective-permute-done.116
  1334.8 9.5 collective-permute-start.123
  1354.5 5.3 collective-permute-done.120
  1359.8 11.4 collective-permute-done.121
  (844 shorter events, 373.3 us)
Async XLA Ops:
  7.2 172.4 %all-gather.9.cloned.1.call-start = ((), (), s32[]{:S(2)}) async-start(), calls=%async_computation.8 | async-start | bytes 2985984 | tf_op jit(solution)/shard_map/all_gather | solution.py:929
  10.9 66.3 %collective-permute-start = (bf16[72,2304]{1,0:T(8,128)(2,1)}, bf16[72,2304]{1,0:T(8,128)(2,1)}, u32[]{:S(2)}, u32[]{:S(2)}) collective-permute-start(bf16[72,2304]{1,0:T(8,128)(2,1)} %concatenate.579), channel_id=1, source_target_pairs={{0,4},{2,6},{4,0},{6,2},{8,12},{10,14},{12,8},{14,10},{1,5},{3,7},... | collective-permute-start | bytes 995336 | tf_op jit(solution)/shard_map/ppermute | solution.py:29
  14.0 63.3 %collective-permute-start.1 = (bf16[72,2304]{1,0:T(8,128)(2,1)}, bf16[72,2304]{1,0:T(8,128)(2,1)}, u32[]{:S(2)}, u32[]{:S(2)}) collective-permute-start(bf16[72,2304]{1,0:T(8,128)(2,1)} %concatenate.579), channel_id=1, source_target_pairs={{0,8},{2,10},{4,12},{6,14},{8,0},{10,2},{12,4},{14,6},{1,9},{3,11}... | collective-permute-start | bytes 995336 | tf_op jit(solution)/shard_map/ppermute | solution.py:29
  16.5 60.7 %collective-permute-start.2 = (bf16[72,2304]{1,0:T(8,128)(2,1)}, bf16[72,2304]{1,0:T(8,128)(2,1)}, u32[]{:S(2)}, u32[]{:S(2)}) collective-permute-start(bf16[72,2304]{1,0:T(8,128)(2,1)} %concatenate.579), channel_id=1, source_target_pairs={{0,12},{2,14},{4,8},{6,10},{8,4},{10,6},{12,0},{14,2},{1,13},{3,15... | collective-permute-start | bytes 995336 | tf_op jit(solution)/shard_map/ppermute | solution.py:29
  19.0 279.6 %all-gather.5.cloned.1.call-start = ((), (), s32[]{:S(2)}) async-start(), calls=%async_computation.3 | async-start | bytes 2985984 | tf_op jit(solution)/shard_map/all_gather | solution.py:929
  47.1 292.6 %all-gather.7.cloned.1.call-start = ((), (), s32[]{:S(2)}) async-start(), calls=%async_computation.4 | async-start | bytes 2985984 | tf_op jit(solution)/shard_map/all_gather | solution.py:929
  84.8 42.8 %collective-permute-start.10 = (bf16[4,72,1152]{2,1,0:T(8,128)(2,1)S(1)}, bf16[4,72,1152]{2,1,0:T(8,128)(2,1)S(1)}, u32[]{:S(2)}, u32[]{:S(2)}) collective-permute-start(bf16[4,72,1152]{2,1,0:T(8,128)(2,1)S(1)} %fusion.55), channel_id=1, source_target_pairs={{0,1},{1,0},{2,3},{3,2},{4,5},{5,4},{6,7},{7,6},{8,9},{9,8},{10,11... | collective-permute-start | bytes 1990664 | tf_op jit(solution)/shard_map/ppermute | solution.py:29
  86.1 41.5 %collective-permute-start.9 = (bf16[4,72,1152]{2,1,0:T(8,128)(2,1)S(1)}, bf16[4,72,1152]{2,1,0:T(8,128)(2,1)S(1)}, u32[]{:S(2)}, u32[]{:S(2)}) collective-permute-start(bf16[4,72,1152]{2,1,0:T(8,128)(2,1)S(1)} %fusion.56), channel_id=1, source_target_pairs={{0,2},{2,0},{4,6},{6,4},{8,10},{10,8},{12,14},{14,12},{1,3},{3,1},... | collective-permute-start | bytes 1990664 | tf_op jit(solution)/shard_map/ppermute | solution.py:29
  129.1 50.5 %collective-permute-start.17 = (bf16[576,1152]{1,0:T(8,128)(2,1)}, bf16[576,1152]{1,0:T(8,128)(2,1)}, u32[]{:S(2)}, u32[]{:S(2)}) collective-permute-start(bf16[576,1152]{1,0:T(8,128)(2,1)} %bitcast.65.refs_0_), channel_id=1, source_target_pairs={{0,1},{1,0},{2,3},{3,2},{4,5},{5,4},{6,7},{7,6},{8,9},{9,8},{10,11... | collective-permute-start | bytes 3981320 | tf_op jit(solution)/shard_map/ppermute | solution.py:29
  130.4 61.4 %collective-permute-start.20 = (bf16[576,1152]{1,0:T(8,128)(2,1)}, bf16[576,1152]{1,0:T(8,128)(2,1)}, u32[]{:S(2)}, u32[]{:S(2)}) collective-permute-start(bf16[576,1152]{1,0:T(8,128)(2,1)} %bitcast.65.refs_0_), channel_id=1, source_target_pairs={{0,16},{16,0},{1,17},{17,1},{2,18},{18,2},{3,19},{19,3},{4,20},{20... | collective-permute-start | bytes 3981320 | tf_op jit(solution)/shard_map/ppermute | solution.py:29
  132.4 44.9 %collective-permute-start.19 = (bf16[4,72,2304]{2,1,0:T(8,128)(2,1)S(1)}, bf16[4,72,2304]{2,1,0:T(8,128)(2,1)}, u32[]{:S(2)}, u32[]{:S(2)}) collective-permute-start(bf16[4,72,2304]{2,1,0:T(8,128)(2,1)S(1)} %fusion.28), channel_id=1, source_target_pairs={{0,1},{1,0},{2,3},{3,2},{4,5},{5,4},{6,7},{7,6},{8,9},{9,8},{10,11... | collective-permute-start | bytes 3981320 | tf_op jit(solution)/shard_map/ppermute | solution.py:29
  133.3 45.2 %collective-permute-start.18 = (bf16[2,4,72,1152]{3,2,1,0:T(8,128)(2,1)S(1)}, bf16[2,4,72,1152]{3,2,1,0:T(8,128)(2,1)S(1)}, u32[]{:S(2)}, u32[]{:S(2)}) collective-permute-start(bf16[2,4,72,1152]{3,2,1,0:T(8,128)(2,1)S(1)} %pad_maximum_fusion.32), channel_id=1, source_target_pairs={{0,2},{2,0},{4,6},{6,4},{8,10},{10,8},{12,14},{14,12},{1,3},{3,1},... | collective-permute-start | bytes 3981320 | tf_op jit(solution)/shard_map/ppermute | solution.py:29
  187.9 60.1 %collective-permute-start.23 = (bf16[2,4,72,2304]{3,2,1,0:T(8,128)(2,1)S(1)}, bf16[2,4,72,2304]{3,2,1,0:T(8,128)(2,1)}, u32[]{:S(2)}, u32[]{:S(2)}) collective-permute-start(bf16[2,4,72,2304]{3,2,1,0:T(8,128)(2,1)S(1)} %pad_maximum_fusion.3), channel_id=1, source_target_pairs={{0,2},{2,0},{4,6},{6,4},{8,10},{10,8},{12,14},{14,12},{1,3},{3,1},... | collective-permute-start | bytes 7962632 | tf_op jit(solution)/shard_map/ppermute | solution.py:29
  188.6 60.0 %collective-permute-start.24 = (bf16[576,2304]{1,0:T(8,128)(2,1)}, bf16[576,2304]{1,0:T(8,128)(2,1)}, u32[]{:S(2)}, u32[]{:S(2)}) collective-permute-start(bf16[576,2304]{1,0:T(8,128)(2,1)} %bitcast.66.refs_0_), channel_id=1, source_target_pairs={{0,1},{1,0},{2,3},{3,2},{4,5},{5,4},{6,7},{7,6},{8,9},{9,8},{10,11... | collective-permute-start | bytes 7962632 | tf_op jit(solution)/shard_map/ppermute | solution.py:29
  191.9 78.3 %collective-permute-start.25 = (bf16[576,2304]{1,0:T(8,128)(2,1)}, bf16[576,2304]{1,0:T(8,128)(2,1)}, u32[]{:S(2)}, u32[]{:S(2)}) collective-permute-start(bf16[576,2304]{1,0:T(8,128)(2,1)} %bitcast.66.refs_0_), channel_id=1, source_target_pairs={{0,16},{16,0},{1,17},{17,1},{2,18},{18,2},{3,19},{19,3},{4,20},{20... | collective-permute-start | bytes 7962632 | tf_op jit(solution)/shard_map/ppermute | solution.py:29
  254.3 51.2 %collective-permute-start.30 = (bf16[2,576,2304]{2,1,0:T(8,128)(2,1)}, bf16[2,576,2304]{2,1,0:T(8,128)(2,1)}, u32[]{:S(2)}, u32[]{:S(2)}) collective-permute-start(bf16[2,576,2304]{2,1,0:T(8,128)(2,1)} %bitcast.96.refs_0_.refs_4_), channel_id=1, source_target_pairs={{0,16},{16,0},{1,17},{17,1},{2,18},{18,2},{3,19},{19,3},{4,20},{20... | collective-permute-start | bytes 15925256 | tf_op jit(solution)/shard_map/ppermute | solution.py:29
  254.8 752.2 %reduce-scatter.8.cloned.1.call-start = ((), (), s32[]{:S(2)}) async-start(), calls=%async_computation.7 | async-start | bytes 2985984 | tf_op jit(solution)/shard_map/reduce_scatter | solution.py:138
  255.6 43.1 %collective-permute-start.27 = (bf16[72,2304]{1,0:T(8,128)(2,1)S(1)}, bf16[72,2304]{1,0:T(8,128)(2,1)S(1)}, u32[]{:S(2)}, u32[]{:S(2)}) collective-permute-start(bf16[72,2304]{1,0:T(8,128)(2,1)S(1)} %copy-done.36), channel_id=1, source_target_pairs={{0,4},{2,6},{4,0},{6,2},{8,12},{10,14},{12,8},{14,10},{1,5},{3,7},... | collective-permute-start | bytes 995336 | tf_op jit(solution)/shard_map/ppermute | solution.py:29
  304.8 100.5 %collective-permute-start.32 = (bf16[576,2304]{1,0:T(8,128)(2,1)}, bf16[576,2304]{1,0:T(8,128)(2,1)}, u32[]{:S(2)}, u32[]{:S(2)}) collective-permute-start(bf16[576,2304]{1,0:T(8,128)(2,1)} %all-gather.5.cloned.1.call-done.refs_0_), channel_id=1, source_target_pairs={{0,1},{1,0},{2,3},{3,2},{4,5},{5,4},{6,7},{7,6},{8,9},{9,8},{10,11... | collective-permute-start | bytes 7962632 | tf_op jit(solution)/shard_map/ppermute | solution.py:29
  330.5 85.6 %collective-permute-start.33 = (bf16[4,4,1,16,1152]{4,3,1,0,2:T(8,128)(2,1)}, bf16[4,4,1,16,1152]{4,3,1,0,2:T(8,128)(2,1)}, u32[]{:S(2)}, u32[]{:S(2)}) collective-permute-start(bf16[4,4,1,16,1152]{4,3,1,0,2:T(8,128)(2,1)} %get-tuple-element.479), channel_id=1, source_target_pairs={{0,1},{1,0},{2,3},{3,2},{4,5},{5,4},{6,7},{7,6},{8,9},{9,8},{10,11... | collective-permute-start | bytes 1769480 | tf_op jit(solution)/shard_map/ppermute | solution.py:876
  331.9 84.2 %collective-permute-start.34 = (bf16[4,4,1,16,1152]{4,3,1,0,2:T(8,128)(2,1)}, bf16[4,4,1,16,1152]{4,3,1,0,2:T(8,128)(2,1)}, u32[]{:S(2)}, u32[]{:S(2)}) collective-permute-start(bf16[4,4,1,16,1152]{4,3,1,0,2:T(8,128)(2,1)} %get-tuple-element.478), channel_id=1, source_target_pairs={{0,2},{1,3},{2,0},{3,1},{4,6},{5,7},{6,4},{7,5},{8,10},{9,11},{10,... | collective-permute-start | bytes 1769480 | tf_op jit(solution)/shard_map/ppermute | solution.py:876
  331.9 84.2 %collective-permute-start.35 = (bf16[4,4,1,16,1152]{4,3,1,0,2:T(8,128)(2,1)}, bf16[4,4,1,16,1152]{4,3,1,0,2:T(8,128)(2,1)}, u32[]{:S(2)}, u32[]{:S(2)}) collective-permute-start(bf16[4,4,1,16,1152]{4,3,1,0,2:T(8,128)(2,1)} %get-tuple-element.477), channel_id=1, source_target_pairs={{0,3},{1,2},{2,1},{3,0},{4,7},{5,6},{6,5},{7,4},{8,11},{9,10},{10,... | collective-permute-start | bytes 1769480 | tf_op jit(solution)/shard_map/ppermute | solution.py:876
  419.1 59.8 %collective-permute-start.36 = (bf16[2,4,72,2304]{3,2,1,0:T(8,128)(2,1)}, bf16[2,4,72,2304]{3,2,1,0:T(8,128)(2,1)}, u32[]{:S(2)}, u32[]{:S(2)}) collective-permute-start(bf16[2,4,72,2304]{3,2,1,0:T(8,128)(2,1)} %pad_maximum_fusion.4), channel_id=1, source_target_pairs={{0,2},{2,0},{4,6},{6,4},{8,10},{10,8},{12,14},{14,12},{1,3},{3,1},... | collective-permute-start | bytes 7962632 | tf_op jit(solution)/shard_map/ppermute | solution.py:29
  419.1 59.8 %collective-permute-start.40 = (bf16[576,2304]{1,0:T(8,128)(2,1)}, bf16[576,2304]{1,0:T(8,128)(2,1)}, u32[]{:S(2)}, u32[]{:S(2)}) collective-permute-start(bf16[576,2304]{1,0:T(8,128)(2,1)} %all-gather.7.cloned.1.call-done.refs_0_.refs_2_), channel_id=1, source_target_pairs={{0,1},{1,0},{2,3},{3,2},{4,5},{5,4},{6,7},{7,6},{8,9},{9,8},{10,11... | collective-permute-start | bytes 7962632 | tf_op jit(solution)/shard_map/ppermute | solution.py:29
  427.7 50.6 %collective-permute-start.38 = (bf16[4,4,1,16,1152]{4,3,1,0,2:T(8,128)(2,1)}, bf16[4,4,1,16,1152]{4,3,1,0,2:T(8,128)(2,1)S(1)}, u32[]{:S(2)}, u32[]{:S(2)}) collective-permute-start(bf16[4,4,1,16,1152]{4,3,1,0,2:T(8,128)(2,1)} %pad_maximum_fusion.50), channel_id=1, source_target_pairs={{0,8},{2,10},{4,12},{6,14},{8,0},{10,2},{12,4},{14,6},{1,9},{3,11}... | collective-permute-start | bytes 1769480 | tf_op jit(solution)/shard_map/ppermute | solution.py:29
  444.1 57.5 %collective-permute-start.41 = (bf16[576,2304]{1,0:T(8,128)(2,1)}, bf16[576,2304]{1,0:T(8,128)(2,1)}, u32[]{:S(2)}, u32[]{:S(2)}) collective-permute-start(bf16[576,2304]{1,0:T(8,128)(2,1)} %all-gather.5.cloned.1.call-done.refs_0_), channel_id=1, source_target_pairs={{0,16},{16,0},{1,17},{17,1},{2,18},{18,2},{3,19},{19,3},{4,20},{20... | collective-permute-start | bytes 7962632 | tf_op jit(solution)/shard_map/ppermute | solution.py:29
  478.4 118.9 %collective-permute-start.48 = (bf16[576,2304]{1,0:T(8,128)(2,1)}, bf16[576,2304]{1,0:T(8,128)(2,1)}, u32[]{:S(2)}, u32[]{:S(2)}) collective-permute-start(bf16[576,2304]{1,0:T(8,128)(2,1)} %all-gather.7.cloned.1.call-done.refs_0_.refs_2_), channel_id=1, source_target_pairs={{0,16},{16,0},{1,17},{17,1},{2,18},{18,2},{3,19},{19,3},{4,20},{20... | collective-permute-start | bytes 7962632 | tf_op jit(solution)/shard_map/ppermute | solution.py:29
  493.6 59.9 %collective-permute-start.44 = (bf16[2,576,2304]{2,1,0:T(8,128)(2,1)}, bf16[2,576,2304]{2,1,0:T(8,128)(2,1)}, u32[]{:S(2)}, u32[]{:S(2)}) collective-permute-start(bf16[2,576,2304]{2,1,0:T(8,128)(2,1)} %bitcast.154.refs_0_), channel_id=1, source_target_pairs={{0,16},{16,0},{1,17},{17,1},{2,18},{18,2},{3,19},{19,3},{4,20},{20... | collective-permute-start | bytes 15925256 | tf_op jit(solution)/shard_map/ppermute | solution.py:29
  498.5 43.4 %collective-permute-start.43 = (bf16[4,4,2,1,16,1152]{5,4,1,2,0,3:T(8,128)(2,1)S(1)}, bf16[4,4,2,1,16,1152]{5,4,1,2,0,3:T(8,128)(2,1)S(1)}, u32[]{:S(2)}, u32[]{:S(2)}) collective-permute-start(bf16[4,4,2,1,16,1152]{5,4,1,2,0,3:T(8,128)(2,1)S(1)} %get-tuple-element.461), channel_id=1, source_target_pairs={{0,2},{1,3},{2,0},{3,1},{4,6},{5,7},{6,4},{7,5},{8,10},{9,11},{10,... | collective-permute-start | bytes 3538952 | tf_op jit(solution)/shard_map/ppermute | solution.py:876
  501.7 95.6 %collective-permute-start.49 = (bf16[576,2304]{1,0:T(8,128)(2,1)}, bf16[576,2304]{1,0:T(8,128)(2,1)}, u32[]{:S(2)}, u32[]{:S(2)}) collective-permute-start(bf16[576,2304]{1,0:T(8,128)(2,1)} %collective-permute-done.40.refs_1_.refs_3_), channel_id=1, source_target_pairs={{0,16},{16,0},{1,17},{17,1},{2,18},{18,2},{3,19},{19,3},{4,20},{20... | collective-permute-start | bytes 7962632 | tf_op jit(solution)/shard_map/ppermute | solution.py:29
  542.5 54.8 %collective-permute-start.46 = (bf16[4,2,2,1,16,1152]{5,4,1,2,0,3:T(8,128)(2,1)S(1)}, bf16[4,2,2,1,16,1152]{5,4,1,2,0,3:T(8,128)(2,1)S(1)}, u32[]{:S(2)}, u32[]{:S(2)}) collective-permute-start(bf16[4,2,2,1,16,1152]{5,4,1,2,0,3:T(8,128)(2,1)S(1)} %pad_maximum_fusion.53), channel_id=1, source_target_pairs={{0,8},{2,10},{4,12},{6,14},{8,0},{10,2},{12,4},{14,6},{1,9},{3,11}... | collective-permute-start | bytes 1769480 | tf_op jit(solution)/shard_map/ppermute | solution.py:29
  553.5 43.7 %collective-permute-start.45 = (bf16[4,2,2,1,16,1152]{5,4,1,2,0,3:T(8,128)(2,1)}, bf16[4,2,2,1,16,1152]{5,4,1,2,0,3:T(8,128)(2,1)S(1)}, u32[]{:S(2)}, u32[]{:S(2)}) collective-permute-start(bf16[4,2,2,1,16,1152]{5,4,1,2,0,3:T(8,128)(2,1)} %pad_maximum_fusion.52), channel_id=1, source_target_pairs={{0,4},{2,6},{4,0},{6,2},{8,12},{10,14},{12,8},{14,10},{1,5},{3,7},... | collective-permute-start | bytes 1769480 | tf_op jit(solution)/shard_map/ppermute | solution.py:29
  624.8 47.5 %collective-permute-start.50 = (bf16[4,4,2,1,16,1152]{5,4,2,1,0,3:T(8,128)(2,1)}, bf16[4,4,2,1,16,1152]{5,4,2,1,0,3:T(8,128)(2,1)S(1)}, u32[]{:S(2)}, u32[]{:S(2)}) collective-permute-start(bf16[4,4,2,1,16,1152]{5,4,2,1,0,3:T(8,128)(2,1)} %get-tuple-element.457), channel_id=1, source_target_pairs={{0,2},{1,3},{2,0},{3,1},{4,6},{5,7},{6,4},{7,5},{8,10},{9,11},{10,... | collective-permute-start | bytes 3538952 | tf_op jit(solution)/shard_map/ppermute | solution.py:876
  685.7 89.6 %collective-permute-start.54 = (bf16[4,2,2,1,16,1152]{5,4,2,1,0,3:T(8,128)(2,1)}, bf16[4,2,2,1,16,1152]{5,4,2,1,0,3:T(8,128)(2,1)}, u32[]{:S(2)}, u32[]{:S(2)}) collective-permute-start(bf16[4,2,2,1,16,1152]{5,4,2,1,0,3:T(8,128)(2,1)} %pad_maximum_fusion.57), channel_id=1, source_target_pairs={{0,12},{2,14},{4,8},{6,10},{8,4},{10,6},{12,0},{14,2},{1,13},{3,15... | collective-permute-start | bytes 1769480 | tf_op jit(solution)/shard_map/ppermute | solution.py:29
  686.9 88.6 %collective-permute-start.53 = (bf16[4,2,2,1,16,1152]{5,4,2,1,0,3:T(8,128)(2,1)}, bf16[4,2,2,1,16,1152]{5,4,2,1,0,3:T(8,128)(2,1)}, u32[]{:S(2)}, u32[]{:S(2)}) collective-permute-start(bf16[4,2,2,1,16,1152]{5,4,2,1,0,3:T(8,128)(2,1)} %pad_maximum_fusion.56), channel_id=1, source_target_pairs={{0,8},{2,10},{4,12},{6,14},{8,0},{10,2},{12,4},{14,6},{1,9},{3,11}... | collective-permute-start | bytes 1769480 | tf_op jit(solution)/shard_map/ppermute | solution.py:29
  687.7 87.7 %collective-permute-start.52 = (bf16[4,2,2,1,16,1152]{5,4,2,1,0,3:T(8,128)(2,1)}, bf16[4,2,2,1,16,1152]{5,4,2,1,0,3:T(8,128)(2,1)}, u32[]{:S(2)}, u32[]{:S(2)}) collective-permute-start(bf16[4,2,2,1,16,1152]{5,4,2,1,0,3:T(8,128)(2,1)} %pad_maximum_fusion.55), channel_id=1, source_target_pairs={{0,4},{2,6},{4,0},{6,2},{8,12},{10,14},{12,8},{14,10},{1,5},{3,7},... | collective-permute-start | bytes 1769480 | tf_op jit(solution)/shard_map/ppermute | solution.py:29
  702.2 107.5 %collective-permute-start.59 = (bf16[576,4608]{1,0:T(8,128)(2,1)}, bf16[576,4608]{1,0:T(8,128)(2,1)}, u32[]{:S(2)}, u32[]{:S(2)}) collective-permute-start(bf16[576,4608]{1,0:T(8,128)(2,1)} %convolution_convert_fusion.2), channel_id=1, source_target_pairs={{0,16},{16,0},{1,17},{17,1},{2,18},{18,2},{3,19},{19,3},{4,20},{20... | collective-permute-start | bytes 15925256 | tf_op jit(solution)/shard_map/ppermute | solution.py:29
  712.4 63.1 %collective-permute-start.55 = (bf16[576,2304]{1,0:T(8,128)(2,1)S(1)}, bf16[576,2304]{1,0:T(8,128)(2,1)}, u32[]{:S(2)}, u32[]{:S(2)}) collective-permute-start(bf16[576,2304]{1,0:T(8,128)(2,1)S(1)} %split.64), channel_id=1, source_target_pairs={{0,1},{1,0},{2,3},{3,2},{4,5},{5,4},{6,7},{7,6},{8,9},{9,8},{10,11... | collective-permute-start | bytes 7962632 | tf_op jit(solution)/shard_map/ppermute | solution.py:29
  775.2 55.4 %collective-permute-start.66 = (bf16[576,1152]{1,0:T(8,128)(2,1)}, bf16[576,1152]{1,0:T(8,128)(2,1)}, u32[]{:S(2)}, u32[]{:S(2)}) collective-permute-start(bf16[576,1152]{1,0:T(8,128)(2,1)} %convolution_convert_fusion.5), channel_id=1, source_target_pairs={{0,16},{16,0},{1,17},{17,1},{2,18},{18,2},{3,19},{19,3},{4,20},{20... | collective-permute-start | bytes 3981320 | tf_op jit(solution)/shard_map/ppermute | solution.py:29
  788.2 280.5 %reduce-scatter.6.cloned.1.call-start = ((), (), s32[]{:S(2)}) async-start(), calls=%async_computation.6 | async-start | bytes 2985984 | tf_op jit(solution)/shard_map/reduce_scatter | solution.py:138
  809.6 90.5 %collective-permute-start.65 = (bf16[576,1728]{1,0:T(8,128)(2,1)}, bf16[576,1728]{1,0:T(8,128)(2,1)}, u32[]{:S(2)}, u32[]{:S(2)}) collective-permute-start(bf16[576,1728]{1,0:T(8,128)(2,1)} %convolution_convert_fusion.8), channel_id=1, source_target_pairs={{0,16},{16,0},{1,17},{17,1},{2,18},{18,2},{3,19},{19,3},{4,20},{20... | collective-permute-start | bytes 5971976 | tf_op jit(solution)/shard_map/ppermute | solution.py:29
  809.7 90.5 %collective-permute-start.64 = (bf16[576,1728]{1,0:T(8,128)(2,1)}, bf16[576,1728]{1,0:T(8,128)(2,1)}, u32[]{:S(2)}, u32[]{:S(2)}) collective-permute-start(bf16[576,1728]{1,0:T(8,128)(2,1)} %convolution_convert_fusion.9), channel_id=1, source_target_pairs={{0,16},{16,0},{1,17},{17,1},{2,18},{18,2},{3,19},{19,3},{4,20},{20... | collective-permute-start | bytes 5971976 | tf_op jit(solution)/shard_map/ppermute | solution.py:29
  824.7 75.4 %collective-permute-start.63 = (bf16[576,2304]{1,0:T(8,128)(2,1)S(1)}, bf16[576,2304]{1,0:T(8,128)(2,1)S(1)}, u32[]{:S(2)}, u32[]{:S(2)}) collective-permute-start(bf16[576,2304]{1,0:T(8,128)(2,1)S(1)} %split.65), channel_id=1, source_target_pairs={{0,1},{1,0},{2,3},{3,2},{4,5},{5,4},{6,7},{7,6},{8,9},{9,8},{10,11... | collective-permute-start | bytes 7962632 | tf_op jit(solution)/shard_map/ppermute | solution.py:29
  830.7 58.7 %collective-permute-start.61 = (bf16[4,4,1,16,1152]{4,3,1,0,2:T(8,128)(2,1)S(1)}, bf16[4,4,1,16,1152]{4,3,1,0,2:T(8,128)(2,1)S(1)}, u32[]{:S(2)}, u32[]{:S(2)}) collective-permute-start(bf16[4,4,1,16,1152]{4,3,1,0,2:T(8,128)(2,1)S(1)} %pad_maximum_fusion.59), channel_id=1, source_target_pairs={{0,8},{2,10},{4,12},{6,14},{8,0},{10,2},{12,4},{14,6},{1,9},{3,11}... | collective-permute-start | bytes 1769480 | tf_op jit(solution)/shard_map/ppermute | solution.py:29
  846.9 53.2 %collective-permute-start.60 = (bf16[4,4,1,16,1152]{4,3,1,0,2:T(8,128)(2,1)S(1)}, bf16[4,4,1,16,1152]{4,3,1,0,2:T(8,128)(2,1)S(1)}, u32[]{:S(2)}, u32[]{:S(2)}) collective-permute-start(bf16[4,4,1,16,1152]{4,3,1,0,2:T(8,128)(2,1)S(1)} %pad_maximum_fusion.58), channel_id=1, source_target_pairs={{0,4},{2,6},{4,0},{6,2},{8,12},{10,14},{12,8},{14,10},{1,5},{3,7},... | collective-permute-start | bytes 1769480 | tf_op jit(solution)/shard_map/ppermute | solution.py:29
  889.3 75.3 %collective-permute-start.70 = (f32[4,3456]{1,0:T(4,128)}, f32[4,3456]{1,0:T(4,128)}, u32[]{:S(2)}, u32[]{:S(2)}) collective-permute-start(f32[4,3456]{1,0:T(4,128)} %bitcast.665), channel_id=1, source_target_pairs={{0,1},{1,0},{2,3},{3,2},{4,5},{5,4},{6,7},{7,6},{8,9},{9,8},{10,11... | collective-permute-start | bytes 165896 | tf_op jit(solution)/shard_map/ppermute | solution.py:29
  906.4 58.2 %collective-permute-start.69 = (bf16[4,72,640]{2,1,0:T(8,128)(2,1)}, bf16[4,72,640]{2,1,0:T(8,128)(2,1)}, u32[]{:S(2)}, u32[]{:S(2)}) collective-permute-start(bf16[4,72,640]{2,1,0:T(8,128)(2,1)} %dynamic-slice_bitcast_fusion.7), channel_id=1, source_target_pairs={{0,2},{2,0},{4,6},{6,4},{8,10},{10,8},{12,14},{14,12},{1,3},{3,1},... | collective-permute-start | bytes 1105928 | tf_op jit(solution)/shard_map/ppermute | solution.py:29
  907.1 57.5 %collective-permute-start.68 = (bf16[576,256]{1,0:T(8,128)(2,1)}, bf16[576,256]{1,0:T(8,128)(2,1)}, u32[]{:S(2)}, u32[]{:S(2)}) collective-permute-start(bf16[576,256]{1,0:T(8,128)(2,1)} %slice.974), channel_id=1, source_target_pairs={{0,1},{1,0},{2,3},{3,2},{4,5},{5,4},{6,7},{7,6},{8,9},{9,8},{10,11... | collective-permute-start | bytes 884744 | tf_op jit(solution)/shard_map/ppermute | solution.py:29
  913.9 50.7 %collective-permute-start.67 = (bf16[576,1728]{1,0:T(8,128)(2,1)}, bf16[576,1728]{1,0:T(8,128)(2,1)}, u32[]{:S(2)}, u32[]{:S(2)}) collective-permute-start(bf16[576,1728]{1,0:T(8,128)(2,1)} %add_convert_fusion.10), channel_id=1, source_target_pairs={{0,1},{1,0},{2,3},{3,2},{4,5},{5,4},{6,7},{7,6},{8,9},{9,8},{10,11... | collective-permute-start | bytes 5971976 | tf_op jit(solution)/shard_map/ppermute | solution.py:29
  918.7 158.4 %reduce-scatter.4.cloned.1.call-start = ((), (), s32[]{:S(2)}) async-start(), calls=%async_computation.5 | async-start | bytes 2322432 | tf_op jit(solution)/shard_map/reduce_scatter | solution.py:138
  1027.0 52.3 %collective-permute-start.82 = (bf16[4,72,2304]{2,1,0:T(8,128)(2,1)}, bf16[4,72,2304]{2,1,0:T(8,128)(2,1)}, u32[]{:S(2)}, u32[]{:S(2)}) collective-permute-start(bf16[4,72,2304]{2,1,0:T(8,128)(2,1)} %dynamic-slice_bitcast_fusion.1), channel_id=1, source_target_pairs={{0,2},{2,0},{4,6},{6,4},{8,10},{10,8},{12,14},{14,12},{1,3},{3,1},... | collective-permute-start | bytes 3981320 | tf_op jit(solution)/shard_map/ppermute | solution.py:29
  1028.5 50.8 %collective-permute-start.81 = (bf16[576,1152]{1,0:T(8,128)(2,1)}, bf16[576,1152]{1,0:T(8,128)(2,1)}, u32[]{:S(2)}, u32[]{:S(2)}) collective-permute-start(bf16[576,1152]{1,0:T(8,128)(2,1)} %get-tuple-element.417), channel_id=1, source_target_pairs={{0,1},{1,0},{2,3},{3,2},{4,5},{5,4},{6,7},{7,6},{8,9},{9,8},{10,11... | collective-permute-start | bytes 3981320 | tf_op jit(solution)/shard_map/ppermute | solution.py:29
  1032.6 46.6 %collective-permute-start.77 = (bf16[72,576]{1,0:T(8,128)(2,1)S(1)}, bf16[72,576]{1,0:T(8,128)(2,1)S(1)}, u32[]{:S(2)}, u32[]{:S(2)}) collective-permute-start(bf16[72,576]{1,0:T(8,128)(2,1)S(1)} %get-tuple-element.595), channel_id=1, source_target_pairs={{0,4},{2,6},{4,0},{6,2},{8,12},{10,14},{12,8},{14,10},{1,5},{3,7},... | collective-permute-start | bytes 248840 | tf_op jit(solution)/shard_map/ppermute | solution.py:29
  1032.7 46.6 %collective-permute-start.78 = (bf16[72,576]{1,0:T(8,128)(2,1)S(1)}, bf16[72,576]{1,0:T(8,128)(2,1)S(1)}, u32[]{:S(2)}, u32[]{:S(2)}) collective-permute-start(bf16[72,576]{1,0:T(8,128)(2,1)S(1)} %get-tuple-element.596), channel_id=1, source_target_pairs={{0,8},{2,10},{4,12},{6,14},{8,0},{10,2},{12,4},{14,6},{1,9},{3,11}... | collective-permute-start | bytes 248840 | tf_op jit(solution)/shard_map/ppermute | solution.py:29
  1093.1 72.5 %collective-permute-start.88 = (bf16[4,72,2304]{2,1,0:T(8,128)(2,1)}, bf16[4,72,2304]{2,1,0:T(8,128)(2,1)}, u32[]{:S(2)}, u32[]{:S(2)}) collective-permute-start(bf16[4,72,2304]{2,1,0:T(8,128)(2,1)} %dynamic-slice_bitcast_fusion), channel_id=1, source_target_pairs={{0,2},{2,0},{4,6},{6,4},{8,10},{10,8},{12,14},{14,12},{1,3},{3,1},... | collective-permute-start | bytes 3981320 | tf_op jit(solution)/shard_map/ppermute | solution.py:29
  1094.5 71.1 %collective-permute-start.87 = (bf16[576,1152]{1,0:T(8,128)(2,1)}, bf16[576,1152]{1,0:T(8,128)(2,1)}, u32[]{:S(2)}, u32[]{:S(2)}) collective-permute-start(bf16[576,1152]{1,0:T(8,128)(2,1)} %get-tuple-element.414), channel_id=1, source_target_pairs={{0,1},{1,0},{2,3},{3,2},{4,5},{5,4},{6,7},{7,6},{8,9},{9,8},{10,11... | collective-permute-start | bytes 3981320 | tf_op jit(solution)/shard_map/ppermute | solution.py:29
  1099.2 66.4 %collective-permute-start.86 = (bf16[4,72,1152]{2,1,0:T(8,128)(2,1)}, bf16[4,72,1152]{2,1,0:T(8,128)(2,1)}, u32[]{:S(2)}, u32[]{:S(2)}) collective-permute-start(bf16[4,72,1152]{2,1,0:T(8,128)(2,1)} %split.68), channel_id=1, source_target_pairs={{0,1},{1,0},{2,3},{3,2},{4,5},{5,4},{6,7},{7,6},{8,9},{9,8},{10,11... | collective-permute-start | bytes 1990664 | tf_op jit(solution)/shard_map/ppermute | solution.py:29
  1103.2 62.4 %collective-permute-start.85 = (bf16[4,72,1152]{2,1,0:T(8,128)(2,1)}, bf16[4,72,1152]{2,1,0:T(8,128)(2,1)}, u32[]{:S(2)}, u32[]{:S(2)}) collective-permute-start(bf16[4,72,1152]{2,1,0:T(8,128)(2,1)} %dynamic-slice_bitcast_fusion.4), channel_id=1, source_target_pairs={{0,2},{2,0},{4,6},{6,4},{8,10},{10,8},{12,14},{14,12},{1,3},{3,1},... | collective-permute-start | bytes 1990664 | tf_op jit(solution)/shard_map/ppermute | solution.py:29
  1104.3 60.8 %collective-permute-start.84 = (f32[4,3456]{1,0:T(4,128)S(1)}, f32[4,3456]{1,0:T(4,128)S(1)}, u32[]{:S(2)}, u32[]{:S(2)}) collective-permute-start(f32[4,3456]{1,0:T(4,128)S(1)} %add.325), channel_id=1, source_target_pairs={{0,16},{16,0},{1,17},{17,1},{2,18},{18,2},{3,19},{19,3},{4,20},{20... | collective-permute-start | bytes 165896 | tf_op jit(solution)/shard_map/ppermute | solution.py:29
  1165.1 90.0 %collective-permute-start.108 = (bf16[576,1152]{1,0:T(8,128)(2,1)}, bf16[576,1152]{1,0:T(8,128)(2,1)}, u32[]{:S(2)}, u32[]{:S(2)}) collective-permute-start(bf16[576,1152]{1,0:T(8,128)(2,1)} %convolution_convert_fusion.4), channel_id=1, source_target_pairs={{0,16},{16,0},{1,17},{17,1},{2,18},{18,2},{3,19},{19,3},{4,20},{20... | collective-permute-start | bytes 3981320 | tf_op jit(solution)/shard_map/ppermute | solution.py:29
  1173.7 99.3 %collective-permute-start.107 = (bf16[576,1728]{1,0:T(8,128)(2,1)}, bf16[576,1728]{1,0:T(8,128)(2,1)}, u32[]{:S(2)}, u32[]{:S(2)}) collective-permute-start(bf16[576,1728]{1,0:T(8,128)(2,1)} %convolution_convert_fusion.6), channel_id=1, source_target_pairs={{0,16},{16,0},{1,17},{17,1},{2,18},{18,2},{3,19},{19,3},{4,20},{20... | collective-permute-start | bytes 5971976 | tf_op jit(solution)/shard_map/ppermute | solution.py:29
  1191.6 81.3 %collective-permute-start.106 = (bf16[576,1728]{1,0:T(8,128)(2,1)}, bf16[576,1728]{1,0:T(8,128)(2,1)}, u32[]{:S(2)}, u32[]{:S(2)}) collective-permute-start(bf16[576,1728]{1,0:T(8,128)(2,1)} %convolution_convert_fusion.7), channel_id=1, source_target_pairs={{0,16},{16,0},{1,17},{17,1},{2,18},{18,2},{3,19},{19,3},{4,20},{20... | collective-permute-start | bytes 5971976 | tf_op jit(solution)/shard_map/ppermute | solution.py:29
  1214.1 42.5 %collective-permute-start.101 = (bf16[72,2304]{1,0:T(8,128)(2,1)}, bf16[72,2304]{1,0:T(8,128)(2,1)S(1)}, u32[]{:S(2)}, u32[]{:S(2)}) collective-permute-start(bf16[72,2304]{1,0:T(8,128)(2,1)} %get-tuple-element.500), channel_id=1, source_target_pairs={{0,4},{2,6},{4,0},{6,2},{8,12},{10,14},{12,8},{14,10},{1,5},{3,7},... | collective-permute-start | bytes 995336 | tf_op jit(solution)/shard_map/ppermute | solution.py:29
  1282.0 39.8 %collective-permute-start.115 = (bf16[4,72,640]{2,1,0:T(8,128)(2,1)S(1)}, bf16[4,72,640]{2,1,0:T(8,128)(2,1)S(1)}, u32[]{:S(2)}, u32[]{:S(2)}) collective-permute-start(bf16[4,72,640]{2,1,0:T(8,128)(2,1)S(1)} %dynamic-slice_bitcast_fusion.6), channel_id=1, source_target_pairs={{0,2},{2,0},{4,6},{6,4},{8,10},{10,8},{12,14},{14,12},{1,3},{3,1},... | collective-permute-start | bytes 1105928 | tf_op jit(solution)/shard_map/ppermute | solution.py:29
  (218 other events, 2597.6 us)
Sparse Core Ops, SparseCore 0:
  19.1 70.8 all-gather.8
  92.2 79.5 all-gather.4
  254.9 84.6 all-gather.6
  788.3 84.3 reduce-scatter.7
  918.8 70.2 reduce-scatter.5
  1004.0 73.0 reduce-scatter.3

commit v5 on v4

--- a/solution.py
+++ b/solution.py
@@ -109,16 +109,6 @@
         layout = tuple(((r, None, half), (self.n_tp, r, half)) for r in range(self.n_tp))
         return self.with_core(mine, layout)
 
-    def gather_sideways(self, v):
-        got = yield self.line_gather(v)
-        line = self.line_stack([v] + got)
-        got = yield [self.over_tp(line, r) for r in range(1, self.n_tp)]
-        strips = jnp.stack([line] + got)
-        got = yield self.over_side(strips)
-        mine = [self.pair_stack(strips, got)]
-        layout = tuple(((0, r, v.shape[1]),) for r in range(self.n_tp))
-        return self.with_core(mine, layout)
-
     def gather_rest(self, block):
         got = yield [self.over_tp(block, r) for r in range(1, self.n_tp)]
         layout = tuple(((r, None, block.shape[1]),) for r in range(self.n_tp))
@@ -135,7 +125,8 @@
             totals = jnp.split(totals[0], self.n_tp, axis=1)
         got = yield [self.over_tp(totals[r], r) for r in others]
         total = (totals[0].astype(F32) + sum(v.astype(F32) for v in got)).astype(BF16)
-        return lax.psum_scatter(total, "ctx", scatter_dimension=0, tiled=True).astype(F32)
+        shard = yield Rest(lax.psum_scatter(total, "ctx", scatter_dimension=0, tiled=True))
+        return shard.astype(F32)
 
     def scatter_weight(self, left, rights):
         others = range(1, self.n_tp)
@@ -179,10 +170,19 @@
         return own.astype(F32) + sum(v.astype(F32) for v in got)
 
 
+class Rest:
+    def __init__(self, value):
+        self.value = value
+
+
 class Task:
     def __init__(self, steps):
         self.steps, self.result = steps, None
-        self.pending = next(steps)
+        self.take(next(steps))
+
+    def take(self, pending):
+        self.resting = isinstance(pending, Rest)
+        self.pending = pending.value if self.resting else pending
 
 
 def at_once(steps):
@@ -203,13 +203,13 @@
         self.tasks.append(task)
         return task
 
-    def fence(self, values=(), but=()):
-        due = [t for t in self.tasks if t not in but]
+    def fence(self, values=(), but=(), last=False):
+        due = [t for t in self.tasks if t not in but and (last or not t.resting)]
         values, pending = lax.optimization_barrier((values, [t.pending for t in due]))
-        going = [t for t in self.tasks if t in but]
+        going = [t for t in self.tasks if t not in due]
         for task, done in zip(due, pending):
             try:
-                task.pending = task.steps.send(done)
+                task.take(task.steps.send(done))
                 going.append(task)
             except StopIteration as stop:
                 task.result = stop.value
@@ -923,31 +923,42 @@
     lanes = Lanes()
     gathers = {}
 
-    shards, blocks = (
-        shards,
-        {
-            index: lax.all_gather(shards[index], "ctx", axis=0, tiled=True)
-            for index in range(1, len(shards), 2)
-        },
-    )
+    blocks = {}
+
+    def gather_far(index):
+        blocks[index] = lax.all_gather(shards[index], "ctx", axis=0, tiled=True)
 
     def set_out(index):
         if index in blocks:
             steps = moves.gather_rest(blocks[index])
-        elif index == 0:
+        else:
             steps = moves.gather_halves(shards[index])
-        else:
-            steps = moves.gather_sideways(shards[index])
         gathers[index] = lanes.start(steps)
 
-    def tick(values=(), out=()):
-        held = {index: blocks.get(index, shards[index]) for index in out}
-        held, values = lanes.fence((held, values))
-        for index in out:
+    plan = [
+        ((2,), (), ()),
+        ((), (2,), ()),
+        ((1,), (), ()),
+        ((4,), (), (5,)),
+        ((3,), (), ()),
+        ((), (3,), ()),
+        ((5,), (), ()),
+        ((), (5,), ()),
+        ((), (), ()),
+    ]
+
+    def tick(values=()):
+        out, but, far = plan.pop(0)
+        held = {index: blocks.get(index, shards[index]) for index in out + far}
+        held, values = lanes.fence((held, values), [gathers[index] for index in but])
+        for index in out + far:
             if index in blocks:
                 blocks[index] = held[index]
             else:
                 shards[index] = held[index]
+        for index in far:
+            gather_far(index)
+        for index in out:
             set_out(index)
         return values
 
@@ -973,13 +984,15 @@
     def modulations(level):
         return [mods[level][:, i] for i in range(6)]
 
+    gather_far(1)
+    gather_far(3)
     set_out(0)
     moved = lanes.start(to_frames(moves.halves(tokens)))
     vectors_task = lanes.start(modulation_vectors())
-    tick(out=(2,))
+    tick()
     residual = moved.result
     tick()
-    tick(out=(1,))
+    tick()
     mods = vectors_task.result
     fused = (
         whole_frames
@@ -998,9 +1011,9 @@
         steps = (moves.scatter_far if far else moves.scatter_weight)(left, rights)
         scatters[level, name] = lanes.start(steps)
 
-    def mod_strip(grads):
-        parts = moves.halves(grads).reshape(clips, n_tp, -1)
-        parts = flip_to(parts, 1, n_tp, moves.tp)
+    def mod_strip():
+        parts = [moves.halves(v).reshape(clips, n_tp, -1) for v in mod_grads]
+        parts = flip_to(jnp.stack(parts, axis=2), 1, n_tp, moves.tp)
         got = yield [swap_with(parts[:, r], "tp", n_tp, r) for r in range(1, n_tp)]
         strip = parts[:, 0] + sum(got)
         strip = yield from total_over_ctx(strip)
@@ -1008,8 +1021,6 @@
         strip = strip + got
         got = yield swap_with(strip, "dp", n_dp, 1)
         return jnp.concatenate([strip, got], axis=0)
-
-    strips = {}
 
     def fused_passes(v):
         vectors, saved = [], []
@@ -1022,9 +1033,9 @@
             stride = piece if level % 2 else 1
             joined = gathers[3 * level].result
             kept = fused_branch(v, vectors[level], joined, clips, stride)
-            normed, qkv, lse, result, branch, middle, normed_mlp = tick(kept, (4,) if level == 0 else ())
+            normed, qkv, lse, result, branch, middle, normed_mlp = tick(kept)
             up = gathers[3 * level + 1].result
-            act, slope = tick(fused_up(normed_mlp, vectors[level], up, clips), (3,) if level == 0 else ())
+            act, slope = tick(fused_up(normed_mlp, vectors[level], up, clips))
             down = gathers[3 * level + 2].result
             branch_mlp, after = fused_down(act, middle, vectors[level], down, clips)
             saved.append((v, normed, qkv, lse, result, branch, middle, normed_mlp))
@@ -1032,7 +1043,7 @@
             v = after
             if level == 0:
                 moved = lanes.start(frames_to_clips(shaped(v)))
-                tick(out=(5,))
+                tick()
                 late = tick(cotangent)
                 turned = lanes.start(here_to_clips(moves.halves(late)))
                 v = flat(moved.result)
@@ -1046,23 +1057,23 @@
             )
             grad_branch, grad_pre, grad_middle, grad_out, sums = lanes.fence(back)
             start_scatter(level, "down", grad_branch, [act])
-            grad_out = lanes.fence(grad_out, (finished,))
+            late = tuple(scatters[level + 1, n] for n in ("qkv", "out")) if not level else (finished,)
+            grad_out = lanes.fence(grad_out, late)
             if level == 0:
                 start_scatter(level, "up", normed_mlp, [grad_pre])
-                grad_out = lanes.fence(grad_out)
+                grad_out = lanes.fence(grad_out, (scatters[level, "down"],))
             back = fused_branch_back(
                 v, vectors[level], grad_out, grad_middle, qkv, lse, joined, clips, stride
             )
-            grad, more, *grad_qkv = lanes.fence(back)
+            grad, more, *grad_qkv = lanes.fence(back, (scatters[level, "down"],) if level else ())
             mod_grads[level] = (sums + more)[:, :6]
             if level:
                 moved = lanes.start(clips_to_frames(shaped(grad)))
                 start_scatter(level, "up", normed_mlp, [grad_pre])
-                lanes.fence()
+                lanes.fence((), (scatters[level, "down"],))
                 start_scatter(level, "qkv", normed, grad_qkv)
                 start_scatter(level, "out", grad_out, [result])
                 lanes.fence()
-                strips[level] = lanes.start(mod_strip(mod_grads[level]))
                 grad = flat(moved.result)
             else:
                 start_scatter(level, "qkv", normed, grad_qkv)
@@ -1085,14 +1096,14 @@
                 saved = [entry[1] for entry in saved]
             else:
                 result, saved = attend(projected, rows, stride)
-            result, saved = tick((result, saved), (4,) if level == 0 else ())
+            result, saved = tick((result, saved))
             branch = shaped(dot(result, outs, NT))
             middle = residual + gate_a[:, None] * branch
             normed_mlp = flat(modulate(middle, shift_m, scale_m))
             up = whole(3 * level + 1)
             pre_act = dot(normed_mlp, up)
             act = gelu(pre_act).astype(BF16)
-            act, pre_act = tick((act, pre_act), (3,) if level == 0 else ())
+            act, pre_act = tick((act, pre_act))
             down = whole(3 * level + 2)
             branch_mlp = shaped(dot(act, down, NT))
             records.append(
@@ -1102,7 +1113,7 @@
             residual = middle + gate_m[:, None] * branch_mlp
             if spatial:
                 moved = lanes.start(frames_to_clips(residual.astype(BF16)))
-                tick(out=(5,))
+                tick()
                 turned = lanes.start(here_to_clips(moves.halves(cotangent)))
                 tick()
                 residual = moved.result.astype(F32)
@@ -1156,8 +1167,9 @@
     passes = fused_passes if fused else plain_passes
     finished, gradient = passes(residual)
     grad_tokens = from_frames(moves.halves(gradient.astype(BF16))).astype(F32)
+    lanes.fence()
     while lanes.tasks:
-        lanes.fence()
+        lanes.fence(last=True)
     output = finished.result
     grads = [
         (
@@ -1171,11 +1183,9 @@
 
     ada_grads = []
     cond_part = 0.0
+    both = at_once(mod_strip())
     for level in range(LAYERS):
-        if level in strips:
-            strip = strips[level].result
-        else:
-            strip = at_once(mod_strip(mod_grads[level]))
+        strip = both[:, level]
         ada_grads.append(
             lax.dot_general(cond_rows.astype(F32), strip, TN, precision=HIGHEST)
         )

time: 1390 us -> 1310 us (0.942)
  waiting for transfers between devices: 409 us -> 353 us
  starting transfers between devices: 205 us -> 175 us
    ppermute x115 -> x117, waiting for transfers between devices: 380 us -> 322 us  [swap_with(): return lax.ppermute(v, axis_name, [(i, i ^ k) for i in range(n)])]
    ppermute x115 -> x117, starting transfers between devices: 192 us -> 162 us  [swap_with(): return lax.ppermute(v, axis_name, [(i, i ^ k) for i in range(n)])]
    unnamed x304 -> x362, local copies, waits for them, and re-layouts: 34.6 us -> 45.4 us
  transfers between devices with their start and end apart: 132 -> 134, of which waited for: 41 -> 43; matrix products, arithmetic and copies ran while one was open for 21% -> 23% of each run, Pallas kernels for 26% -> 28%
where the time goes in v5:
time: 1310 us; the launch traced here: 1300 us
  Pallas kernels  380 us (29%)
  waiting for transfers between devices  353 us (27%)
  starting transfers between devices  175 us (13%)
  matrix products  132 us (10%)
  local copies, waits for them, and re-layouts  122 us (9%)
  other arithmetic  120 us (9%)
  between operations  17.8 us (1%)
    pallas_call x10, Pallas kernels, block_call(): pl.pallas_call(kernel, grid=(clips,), in_specs=specs, out_specs=out_specs...  380 us
    ppermute x117, waiting for transfers between devices, swap_with(): return lax.ppermute(v, axis_name, [(i, i ^ k) for i in range(n)])  322 us
    ppermute x117, starting transfers between devices, swap_with(): return lax.ppermute(v, axis_name, [(i, i ^ k) for i in range(n)])  162 us
    dot_general x22, matrix products, dot(): return lax.dot_general(a, b, dims, preferred_element_type=F32)  128 us
    unnamed x362, local copies, waits for them, and re-layouts  45.4 us
    ppermute x8, waiting for transfers between devices, trade(): block = lax.ppermute(block, ('ctx', 'tp'), pairs)  30.6 us
  transfers between devices with their start and end apart: 134, of which 43 were waited for; matrix products, arithmetic and copies ran while one was open for 23% of the time, Pallas kernels for 28%

profile of v5, /device:TPU:0, one launch (start us, length us, event | category | flops | bytes accessed | tf_op | source)
XLA Modules:
  0.0 1299.5 jit_solution(10283074260811739435)
XLA Ops:
  51.2 4.5 collective-permute-done.6
  57.6 9.4 collective-permute-done.7
  67.0 6.9 collective-permute-start.8
  107.1 20.0 %collective-permute-done.15 = bf16[72,2304]{1,0:T(8,128)(2,1)} collective-permute-done((bf16[72,2304]{1,0:T(8,128)(2,1)S(1)}, bf16[72,2304]{1,0:T(8,128)(2,1)}, u32[]{:S(2)}, u32[]{:S(2)}) %collective-permute-start.15) | collective-permute-done | bytes 331808 | tf_op jit(solution)/shard_map/ppermute | solution.py:29
  127.1 4.3 collective-permute-done.18
  143.7 3.7 collective-permute-done.20.refs_4_
  150.0 39.8 %shard_map.152 = (bf16[1024,1152]{1,0:T(8,128)(2,1)}, bf16[1024,3840]{1,0:T(8,128)(2,1)}, f32[1024,128]{1,0:T(8,128)}, bf16[1024,1152]{1,0:T(8,128)(2,1)}, bf16[...) custom-call(bf16[1024,1152]{1,0:T(8,128)(2,1)} %bitcast.877, ...), custom_call_target="tpu_custom_call" | custom-call | flops 16307453952 | bytes 13123584 | tf_op jit(solution)/shard_map/pallas_call | solution.py:650
  189.8 12.2 collective-permute-done.23
  208.9 5.8 collective-permute-start.29
  218.4 26.9 %shard_map.153 = (bf16[1024,4608]{1,0:T(8,128)(2,1)}, bf16[1024,4608]{1,0:T(8,128)(2,1)}) custom-call(bf16[1024,1152]{1,0:T(8,128)(2,1)} %get-tuple-element.222.g_ref, bf16[576,2304]{1,0:T(8,128)(2,1)} %bitcast.916, bf16[576,2304]{1,0:T(8,128)(2,1)} %collective-permute-done.24.refs_1_, bf16[576,2304]{1,0:T(8,128)(2,1)} %collective-permute-done.25.refs_2_, ...), custom_call_target="tpu_custom_call" | custom-call | flops 10871635968 | bytes 12976128 | tf_op jit(solution)/shard_map/pallas_call | solution.py:650
  258.6 22.0 %shard_map.154 = (bf16[1024,1152]{1,0:T(8,128)(2,1)}, bf16[1024,1152]{1,0:T(8,128)(2,1)}) custom-call(bf16[1024,4608]{1,0:T(8,128)(2,1)} %get-tuple-element.229.z_ref, f32[1024,1152]{1,0:T(8,128)} %get-tuple-element.230.y_ref, f32[4,8,1152]{2,1,0:T(8,128)} %concatenate.640.mod_ref, bf16[576,1152]{1,0:T(8,128)(2,1)} %bitcast.101.refs_0_.refs_4_, ...), custom_call_target="tpu_custom_call" | custom-call | flops 10871635968 | bytes 24920064 | tf_op jit(solution)/shard_map/pallas_call | solution.py:650
  288.6 10.2 collective-permute-done.37
  301.1 13.4 %collective-permute-done.39 = bf16[4,4,1,16,1152]{4,3,1,0,2:T(8,128)(2,1)S(1)} collective-permute-done((bf16[4,4,1,16,1152]{4,3,1,0,2:T(8,128)(2,1)S(1)}, bf16[4,4,1,16,1152]{4,3,1,0,2:T(8,128)(2,1)S(1)}, u32[]{:S(2)}, u32[]{:S(2)}) %collective-permute-start.39) | collective-permute-done | bytes 589856 | tf_op jit(solution)/shard_map/ppermute | solution.py:876
  322.9 3.6 collective-permute-start.45
  327.4 5.7 collective-permute-start.44
  334.1 34.3 %collective-permute-done.40.refs_1_ = bf16[576,2304]{1,0:T(8,128)(2,1)S(1)} collective-permute-done((bf16[576,2304]{1,0:T(8,128)(2,1)S(1)}, bf16[576,2304]{1,0:T(8,128)(2,1)S(1)}, u32[]{:S(2)}, u32[]{:S(2)}) %collective-permute-start.40) | collective-permute-done | bytes 2654240 | tf_op jit(solution)/shard_map/ppermute | solution.py:29
  369.8 10.4 collective-permute-start.43
  384.2 6.2 collective-permute-done.43
  390.4 5.3 collective-permute-done.41.refs_1_
  415.6 39.7 %shard_map.155 = (bf16[1024,1152]{1,0:T(8,128)(2,1)}, bf16[1024,3840]{1,0:T(8,128)(2,1)}, f32[1024,128]{1,0:T(8,128)}, bf16[1024,1152]{1,0:T(8,128)(2,1)}, bf16[...) custom-call(bf16[1024,1152]{1,0:T(8,128)(2,1)} %bitcast.879, ...), custom_call_target="tpu_custom_call" | custom-call | flops 16307453952 | bytes 13123584 | tf_op jit(solution)/shard_map/pallas_call | solution.py:650
  459.4 4.7 collective-permute-start.55
  464.1 6.6 collective-permute-start.54
  471.1 26.7 %shard_map.156 = (bf16[1024,4608]{1,0:T(8,128)(2,1)}, bf16[1024,4608]{1,0:T(8,128)(2,1)}) custom-call(bf16[1024,1152]{1,0:T(8,128)(2,1)} %get-tuple-element.256.g_ref, bf16[576,1152]{1,0:T(8,128)(2,1)} %bitcast.141.refs_0_, bf16[576,1152]{1,0:T(8,128)(2,1)} %collective-permute-done.41.refs_1_, bf16[2,576,1152]{2,1,0:T(8,128)(2,1)} %bitcast.871, ...), custom_call_target="tpu_custom_call" | custom-call | flops 10871635968 | bytes 12976128 | tf_op jit(solution)/shard_map/pallas_call | solution.py:650
  497.9 18.4 %collective-permute-done.54 = bf16[4,2,2,1,16,1152]{5,4,1,2,0,3:T(8,128)(2,1)} collective-permute-done((bf16[4,2,2,1,16,1152]{5,4,1,2,0,3:T(8,128)(2,1)}, bf16[4,2,2,1,16,1152]{5,4,1,2,0,3:T(8,128)(2,1)}, u32[]{:S(2)}, u32[]{:S(2)}) %collective-permute-start.54) | collective-permute-done | bytes 589856 | tf_op jit(solution)/shard_map/ppermute | solution.py:29
  521.6 22.0 %shard_map.157 = (bf16[1024,1152]{1,0:T(8,128)(2,1)}, bf16[1024,1152]{1,0:T(8,128)(2,1)}) custom-call(bf16[1024,4608]{1,0:T(8,128)(2,1)} %get-tuple-element.263.z_ref, f32[1024,1152]{1,0:T(8,128)} %get-tuple-element.264.y_ref, f32[4,8,1152]{2,1,0:T(8,128)} %pad_maximum_fusion.71.mod_ref, bf16[576,2304]{1,0:T(8,128)(2,1)} %all-gather.7.cloned.1.call-done.refs_0_.refs_6_, ...), custom_call_target="tpu_custom_call" | custom-call | flops 10871635968 | bytes 24920064 | tf_op jit(solution)/shard_map/pallas_call | solution.py:650
  549.1 45.4 %shard_map.158 = (bf16[1024,1152]{1,0:T(8,128)(2,1)}, bf16[1024,4608]{1,0:T(8,128)(2,1)}, f32[1024,1152]{1,0:T(8,128)}, bf16[1024,1152]{1,0:T(8,128)(2,1)}, f32[4,8,1152]{2,1,0:T(8,128)}) custom-call(bf16[1024,1152]{1,0:T(8,128)(2,1)} %bitcast.881, f32[4,8,1152]{2,1,0:T(8,128)} %pad_maximum_fusion.71.mod_ref, bf16[1024,1152]{1,0:T(8,128)(2,1)} %get-tuple-element.270.m_ref, ...), custom_call_target="tpu_custom_call" | custom-call | flops 21743271936 | bytes 42614784 | tf_op jit(solution)/shard_map/pallas_call | solution.py:650
  594.5 10.8 convolution_convert_fusion.3
  612.7 10.3 convolution_convert_fusion.2
  623.0 56.2 %shard_map.159 = (bf16[1024,1152]{1,0:T(8,128)(2,1)}, f32[4,8,1152]{2,1,0:T(8,128)}, bf16[1024,1728]{1,0:T(8,128)(2,1)}, bf16[1024,1728]{1,0:T(8,128)(2,1)}) custom-call(bf16[1024,1152]{1,0:T(8,128)(2,1)} %bitcast.880, f32[4,8,1152]{2,1,0:T(8,128)} %pad_maximum_fusion.71.mod_ref, bf16[1024,1152]{1,0:T(8,128)(2,1)} %get-tuple-element.281.da_ref, ...), custom_call_target="tpu_custom_call" | custom-call | flops 21743271936 | bytes 28590080 | tf_op jit(solution)/shard_map/pallas_call | solution.py:650
  679.3 6.0 convolution_convert_fusion.8
  691.1 9.1 add_convert_fusion.3
  706.9 3.9 convolution_convert_fusion.9
  711.5 4.7 collective-permute-done.65
  721.9 3.6 collective-permute-start.70
  726.5 8.2 add_convert_fusion.2
  735.7 4.4 collective-permute-done.70
  740.1 34.4 %collective-permute-done.69 = bf16[4,4,1,16,1152]{4,3,1,0,2:T(8,128)(2,1)S(1)} collective-permute-done((bf16[4,4,1,16,1152]{4,3,1,0,2:T(8,128)(2,1)}, bf16[4,4,1,16,1152]{4,3,1,0,2:T(8,128)(2,1)S(1)}, u32[]{:S(2)}, u32[]{:S(2)}) %collective-permute-start.69) | collective-permute-done | bytes 589856 | tf_op jit(solution)/shard_map/ppermute | solution.py:29
  781.1 7.5 collective-permute-done.68
  792.6 37.1 %collective-permute-done.71 = bf16[576,2304]{1,0:T(8,128)(2,1)S(1)} collective-permute-done((bf16[576,2304]{1,0:T(8,128)(2,1)S(1)}, bf16[576,2304]{1,0:T(8,128)(2,1)S(1)}, u32[]{:S(2)}, u32[]{:S(2)}) %collective-permute-start.71) | collective-permute-done | bytes 2654240 | tf_op jit(solution)/shard_map/ppermute | solution.py:29
  844.6 5.7 add_convert_fusion.10
  856.9 45.7 %shard_map.160 = (bf16[1024,1152]{1,0:T(8,128)(2,1)}, bf16[1024,4608]{1,0:T(8,128)(2,1)}, f32[1024,1152]{1,0:T(8,128)}, bf16[1024,1152]{1,0:T(8,128)(2,1)}, f32[4,8,1152]{2,1,0:T(8,128)}) custom-call(bf16[1024,1152]{1,0:T(8,128)(2,1)} %bitcast.883, f32[4,8,1152]{2,1,0:T(8,128)} %concatenate.640.mod_ref, bf16[1024,1152]{1,0:T(8,128)(2,1)} %get-tuple-element.306.m_ref, ...), custom_call_target="tpu_custom_call" | custom-call | flops 21743271936 | bytes 42614784 | tf_op jit(solution)/shard_map/pallas_call | solution.py:650
  902.6 11.2 convolution_convert_fusion
  914.0 10.3 convolution_convert_fusion.1
  942.8 3.5 add_convert_fusion.7
  949.0 9.6 add_convert_fusion
  969.4 7.8 add_convert_fusion.1
  985.6 55.7 %shard_map.161 = (bf16[1024,1152]{1,0:T(8,128)(2,1)}, f32[4,8,1152]{2,1,0:T(8,128)}, bf16[1024,1728]{1,0:T(8,128)(2,1)}, bf16[1024,1728]{1,0:T(8,128)(2,1)}) custom-call(bf16[1024,1152]{1,0:T(8,128)(2,1)} %bitcast.878, f32[4,8,1152]{2,1,0:T(8,128)} %concatenate.640.mod_ref, bf16[1024,1152]{1,0:T(8,128)(2,1)} %get-tuple-element.322.da_ref, ...), custom_call_target="tpu_custom_call" | custom-call | flops 21743271936 | bytes 28590080 | tf_op jit(solution)/shard_map/pallas_call | solution.py:650
  1042.0 5.3 convolution_convert_fusion.4
  1052.9 5.9 convolution_convert_fusion.6
  1072.1 3.9 convolution_convert_fusion.7
  1088.6 6.0 collective-permute-done.96
  1110.0 23.9 %collective-permute-done.89 = bf16[4,1,128,1152]{3,2,0,1:T(8,128)(2,1)S(1)} collective-permute-done((bf16[4,1,128,1152]{3,2,0,1:T(8,128)(2,1)}, bf16[4,1,128,1152]{3,2,0,1:T(8,128)(2,1)S(1)}, u32[]{:S(2)}, u32[]{:S(2)}) %collective-permute-start.89) | collective-permute-done | bytes 1179680 | tf_op jit(solution)/shard_map/ppermute | solution.py:29
  1141.7 10.1 collective-permute-done.103
  1153.3 8.8 collective-permute-done.101
  1166.7 4.1 add_convert_fusion.9
  1170.8 4.7 add_convert_fusion.6
  1191.7 3.6 collective-permute-done.111
  1195.3 8.7 collective-permute-done.112
  1204.0 14.8 %collective-permute-start.109 = (bf16[72,2304]{1,0:T(8,128)(2,1)}, bf16[72,2304]{1,0:T(8,128)(2,1)}, u32[]{:S(2)}, u32[]{:S(2)}) collective-permute-start(bf16[72,2304]{1,0:T(8,128)(2,1)} %get-tuple-element.505), channel_id=1, source_target_pairs={{0,8},{2,10},{4,12},{6,14},{8,0},{10,2},{12,4},{14,6},{1,9},{3,11}... | collective-permute-start | bytes 995336 | tf_op jit(solution)/shard_map/ppermute | solution.py:29
  1223.1 9.4 collective-permute-done.109
  1246.3 5.9 collective-permute-done.118
  1254.2 7.3 collective-permute-start.125
  1271.0 5.4 collective-permute-done.122
  1276.4 12.4 collective-permute-done.123
  (928 shorter events, 387.4 us)
Async XLA Ops:
  7.2 124.2 %all-gather.9.cloned.1.call-start = ((), (), s32[]{:S(2)}) async-start(), calls=%async_computation.8 | async-start | bytes 2985984 | tf_op jit(solution)/shard_map/all_gather | solution.py:929
  10.9 66.3 %collective-permute-start = (bf16[72,2304]{1,0:T(8,128)(2,1)}, bf16[72,2304]{1,0:T(8,128)(2,1)}, u32[]{:S(2)}, u32[]{:S(2)}) collective-permute-start(bf16[72,2304]{1,0:T(8,128)(2,1)} %concatenate.622), channel_id=1, source_target_pairs={{0,4},{2,6},{4,0},{6,2},{8,12},{10,14},{12,8},{14,10},{1,5},{3,7},... | collective-permute-start | bytes 995336 | tf_op jit(solution)/shard_map/ppermute | solution.py:29
  14.0 63.3 %collective-permute-start.1 = (bf16[72,2304]{1,0:T(8,128)(2,1)}, bf16[72,2304]{1,0:T(8,128)(2,1)}, u32[]{:S(2)}, u32[]{:S(2)}) collective-permute-start(bf16[72,2304]{1,0:T(8,128)(2,1)} %concatenate.622), channel_id=1, source_target_pairs={{0,8},{2,10},{4,12},{6,14},{8,0},{10,2},{12,4},{14,6},{1,9},{3,11}... | collective-permute-start | bytes 995336 | tf_op jit(solution)/shard_map/ppermute | solution.py:29
  16.6 60.7 %collective-permute-start.2 = (bf16[72,2304]{1,0:T(8,128)(2,1)}, bf16[72,2304]{1,0:T(8,128)(2,1)}, u32[]{:S(2)}, u32[]{:S(2)}) collective-permute-start(bf16[72,2304]{1,0:T(8,128)(2,1)} %concatenate.622), channel_id=1, source_target_pairs={{0,12},{2,14},{4,8},{6,10},{8,4},{10,6},{12,0},{14,2},{1,13},{3,15... | collective-permute-start | bytes 995336 | tf_op jit(solution)/shard_map/ppermute | solution.py:29
  19.0 226.4 %all-gather.5.cloned.1.call-start = ((), (), s32[]{:S(2)}) async-start(), calls=%async_computation.3 | async-start | bytes 2985984 | tf_op jit(solution)/shard_map/all_gather | solution.py:929
  43.2 34.0 %collective-permute-start.3 = (bf16[4,1,128,1152]{3,2,0,1:T(8,128)(2,1)}, bf16[4,1,128,1152]{3,2,0,1:T(8,128)(2,1)S(1)}, u32[]{:S(2)}, u32[]{:S(2)}) collective-permute-start(bf16[4,1,128,1152]{3,2,0,1:T(8,128)(2,1)} %get-tuple-element.485), channel_id=1, source_target_pairs={{0,1},{1,0},{2,3},{3,2},{4,5},{5,4},{6,7},{7,6},{8,9},{9,8},{10,11... | collective-permute-start | bytes 3538952 | tf_op jit(solution)/shard_map/ppermute | solution.py:29
  47.0 337.2 %all-gather.7.cloned.1.call-start = ((), (), s32[]{:S(2)}) async-start(), calls=%async_computation.4 | async-start | bytes 2985984 | tf_op jit(solution)/shard_map/all_gather | solution.py:929
  93.4 33.7 %collective-permute-start.15 = (bf16[72,2304]{1,0:T(8,128)(2,1)S(1)}, bf16[72,2304]{1,0:T(8,128)(2,1)}, u32[]{:S(2)}, u32[]{:S(2)}) collective-permute-start(bf16[72,2304]{1,0:T(8,128)(2,1)S(1)} %get-tuple-element.207), channel_id=1, source_target_pairs={{0,8},{2,10},{4,12},{6,14},{8,0},{10,2},{12,4},{14,6},{1,9},{3,11}... | collective-permute-start | bytes 995336 | tf_op jit(solution)/shard_map/ppermute | solution.py:29
  93.7 33.4 %collective-permute-start.16 = (bf16[72,2304]{1,0:T(8,128)(2,1)S(1)}, bf16[72,2304]{1,0:T(8,128)(2,1)}, u32[]{:S(2)}, u32[]{:S(2)}) collective-permute-start(bf16[72,2304]{1,0:T(8,128)(2,1)S(1)} %get-tuple-element.207), channel_id=1, source_target_pairs={{0,12},{2,14},{4,8},{6,10},{8,4},{10,6},{12,0},{14,2},{1,13},{3,15... | collective-permute-start | bytes 995336 | tf_op jit(solution)/shard_map/ppermute | solution.py:29
  100.3 31.1 %collective-permute-start.18 = (bf16[2,4,72,1152]{3,2,1,0:T(8,128)(2,1)}, bf16[2,4,72,1152]{3,2,1,0:T(8,128)(2,1)}, u32[]{:S(2)}, u32[]{:S(2)}) collective-permute-start(bf16[2,4,72,1152]{3,2,1,0:T(8,128)(2,1)} %pad_maximum_fusion.30), channel_id=1, source_target_pairs={{0,2},{2,0},{4,6},{6,4},{8,10},{10,8},{12,14},{14,12},{1,3},{3,1},... | collective-permute-start | bytes 3981320 | tf_op jit(solution)/shard_map/ppermute | solution.py:29
  107.1 35.6 %collective-permute-start.19 = (bf16[576,1152]{1,0:T(8,128)(2,1)}, bf16[576,1152]{1,0:T(8,128)(2,1)}, u32[]{:S(2)}, u32[]{:S(2)}) collective-permute-start(bf16[576,1152]{1,0:T(8,128)(2,1)} %bitcast.67.refs_0_), channel_id=1, source_target_pairs={{0,16},{16,0},{1,17},{17,1},{2,18},{18,2},{3,19},{19,3},{4,20},{20... | collective-permute-start | bytes 3981320 | tf_op jit(solution)/shard_map/ppermute | solution.py:29
  131.4 70.7 %collective-permute-start.24 = (bf16[576,2304]{1,0:T(8,128)(2,1)}, bf16[576,2304]{1,0:T(8,128)(2,1)}, u32[]{:S(2)}, u32[]{:S(2)}) collective-permute-start(bf16[576,2304]{1,0:T(8,128)(2,1)} %bitcast.914), channel_id=1, source_target_pairs={{0,1},{1,0},{2,3},{3,2},{4,5},{5,4},{6,7},{7,6},{8,9},{9,8},{10,11... | collective-permute-start | bytes 7962632 | tf_op jit(solution)/shard_map/ppermute | solution.py:29
  132.6 83.1 %collective-permute-start.25 = (bf16[576,2304]{1,0:T(8,128)(2,1)}, bf16[576,2304]{1,0:T(8,128)(2,1)}, u32[]{:S(2)}, u32[]{:S(2)}) collective-permute-start(bf16[576,2304]{1,0:T(8,128)(2,1)} %bitcast.915), channel_id=1, source_target_pairs={{0,16},{16,0},{1,17},{17,1},{2,18},{18,2},{3,19},{19,3},{4,20},{20... | collective-permute-start | bytes 7962632 | tf_op jit(solution)/shard_map/ppermute | solution.py:29
  142.7 59.3 %collective-permute-start.23 = (bf16[4,72,1152]{2,1,0:T(8,128)(2,1)}, bf16[4,72,1152]{2,1,0:T(8,128)(2,1)S(1)}, u32[]{:S(2)}, u32[]{:S(2)}) collective-permute-start(bf16[4,72,1152]{2,1,0:T(8,128)(2,1)} %fusion.55), channel_id=1, source_target_pairs={{0,1},{1,0},{2,3},{3,2},{4,5},{5,4},{6,7},{7,6},{8,9},{9,8},{10,11... | collective-permute-start | bytes 1990664 | tf_op jit(solution)/shard_map/ppermute | solution.py:29
  147.4 54.6 %collective-permute-start.22 = (bf16[4,72,1152]{2,1,0:T(8,128)(2,1)S(1)}, bf16[4,72,1152]{2,1,0:T(8,128)(2,1)S(1)}, u32[]{:S(2)}, u32[]{:S(2)}) collective-permute-start(bf16[4,72,1152]{2,1,0:T(8,128)(2,1)S(1)} %fusion.56), channel_id=1, source_target_pairs={{0,2},{2,0},{4,6},{6,4},{8,10},{10,8},{12,14},{14,12},{1,3},{3,1},... | collective-permute-start | bytes 1990664 | tf_op jit(solution)/shard_map/ppermute | solution.py:29
  205.4 42.3 %collective-permute-start.28 = (bf16[2,4,72,1152]{3,2,1,0:T(8,128)(2,1)}, bf16[2,4,72,1152]{3,2,1,0:T(8,128)(2,1)}, u32[]{:S(2)}, u32[]{:S(2)}) collective-permute-start(bf16[2,4,72,1152]{3,2,1,0:T(8,128)(2,1)} %pad_maximum_fusion.32), channel_id=1, source_target_pairs={{0,2},{2,0},{4,6},{6,4},{8,10},{10,8},{12,14},{14,12},{1,3},{3,1},... | collective-permute-start | bytes 3981320 | tf_op jit(solution)/shard_map/ppermute | solution.py:29
  208.7 39.1 %collective-permute-start.27 = (bf16[576,1152]{1,0:T(8,128)(2,1)}, bf16[576,1152]{1,0:T(8,128)(2,1)}, u32[]{:S(2)}, u32[]{:S(2)}) collective-permute-start(bf16[576,1152]{1,0:T(8,128)(2,1)} %bitcast.101.refs_0_.refs_4_), channel_id=1, source_target_pairs={{0,1},{1,0},{2,3},{3,2},{4,5},{5,4},{6,7},{7,6},{8,9},{9,8},{10,11... | collective-permute-start | bytes 3981320 | tf_op jit(solution)/shard_map/ppermute | solution.py:29
  208.9 36.4 %collective-permute-start.29 = (bf16[72,2304]{1,0:T(8,128)(2,1)S(1)}, bf16[72,2304]{1,0:T(8,128)(2,1)S(1)}, u32[]{:S(2)}, u32[]{:S(2)}) collective-permute-start(bf16[72,2304]{1,0:T(8,128)(2,1)S(1)} %copy-done.84), channel_id=1, source_target_pairs={{0,4},{2,6},{4,0},{6,2},{8,12},{10,14},{12,8},{14,10},{1,5},{3,7},... | collective-permute-start | bytes 995336 | tf_op jit(solution)/shard_map/ppermute | solution.py:29
  214.8 1008.2 %reduce-scatter.6.cloned.1.call-start = ((), (), s32[]{:S(2)}) async-start(), calls=%async_computation.6 | async-start | bytes 2985984 | tf_op jit(solution)/shard_map/reduce_scatter | solution.py:128
  215.6 32.1 %collective-permute-start.30 = (bf16[72,2304]{1,0:T(8,128)(2,1)S(1)}, bf16[72,2304]{1,0:T(8,128)(2,1)S(1)}, u32[]{:S(2)}, u32[]{:S(2)}) collective-permute-start(bf16[72,2304]{1,0:T(8,128)(2,1)S(1)} %copy-done.84), channel_id=1, source_target_pairs={{0,8},{2,10},{4,12},{6,14},{8,0},{10,2},{12,4},{14,6},{1,9},{3,11}... | collective-permute-start | bytes 995336 | tf_op jit(solution)/shard_map/ppermute | solution.py:29
  255.4 31.0 %collective-permute-start.36 = (bf16[4,72,1152]{2,1,0:T(8,128)(2,1)}, bf16[4,72,1152]{2,1,0:T(8,128)(2,1)}, u32[]{:S(2)}, u32[]{:S(2)}) collective-permute-start(bf16[4,72,1152]{2,1,0:T(8,128)(2,1)} %fusion.53), channel_id=1, source_target_pairs={{0,1},{1,0},{2,3},{3,2},{4,5},{5,4},{6,7},{7,6},{8,9},{9,8},{10,11... | collective-permute-start | bytes 1990664 | tf_op jit(solution)/shard_map/ppermute | solution.py:29
  257.0 31.6 %collective-permute-start.35 = (bf16[4,72,1152]{2,1,0:T(8,128)(2,1)}, bf16[4,72,1152]{2,1,0:T(8,128)(2,1)}, u32[]{:S(2)}, u32[]{:S(2)}) collective-permute-start(bf16[4,72,1152]{2,1,0:T(8,128)(2,1)} %fusion.54), channel_id=1, source_target_pairs={{0,2},{2,0},{4,6},{6,4},{8,10},{10,8},{12,14},{14,12},{1,3},{3,1},... | collective-permute-start | bytes 1990664 | tf_op jit(solution)/shard_map/ppermute | solution.py:29
  286.4 81.9 %collective-permute-start.40 = (bf16[576,2304]{1,0:T(8,128)(2,1)S(1)}, bf16[576,2304]{1,0:T(8,128)(2,1)S(1)}, u32[]{:S(2)}, u32[]{:S(2)}) collective-permute-start(bf16[576,2304]{1,0:T(8,128)(2,1)S(1)} %copy-done.155), channel_id=1, source_target_pairs={{0,1},{1,0},{2,3},{3,2},{4,5},{5,4},{6,7},{7,6},{8,9},{9,8},{10,11... | collective-permute-start | bytes 7962632 | tf_op jit(solution)/shard_map/ppermute | solution.py:29
  316.8 73.6 %collective-permute-start.42 = (bf16[2,4,72,1152]{3,2,1,0:T(8,128)(2,1)}, bf16[2,4,72,1152]{3,2,1,0:T(8,128)(2,1)}, u32[]{:S(2)}, u32[]{:S(2)}) collective-permute-start(bf16[2,4,72,1152]{3,2,1,0:T(8,128)(2,1)} %pad_maximum_fusion.34), channel_id=1, source_target_pairs={{0,2},{2,0},{4,6},{6,4},{8,10},{10,8},{12,14},{14,12},{1,3},{3,1},... | collective-permute-start | bytes 3981320 | tf_op jit(solution)/shard_map/ppermute | solution.py:29
  320.9 74.8 %collective-permute-start.41 = (bf16[576,1152]{1,0:T(8,128)(2,1)}, bf16[576,1152]{1,0:T(8,128)(2,1)}, u32[]{:S(2)}, u32[]{:S(2)}) collective-permute-start(bf16[576,1152]{1,0:T(8,128)(2,1)} %bitcast.141.refs_0_), channel_id=1, source_target_pairs={{0,1},{1,0},{2,3},{3,2},{4,5},{5,4},{6,7},{7,6},{8,9},{9,8},{10,11... | collective-permute-start | bytes 3981320 | tf_op jit(solution)/shard_map/ppermute | solution.py:29
  322.9 60.7 %collective-permute-start.45 = (bf16[4,4,1,16,1152]{4,3,1,0,2:T(8,128)(2,1)}, bf16[4,4,1,16,1152]{4,3,1,0,2:T(8,128)(2,1)}, u32[]{:S(2)}, u32[]{:S(2)}) collective-permute-start(bf16[4,4,1,16,1152]{4,3,1,0,2:T(8,128)(2,1)} %pad_maximum_fusion.59), channel_id=1, source_target_pairs={{0,12},{2,14},{4,8},{6,10},{8,4},{10,6},{12,0},{14,2},{1,13},{3,15... | collective-permute-start | bytes 1769480 | tf_op jit(solution)/shard_map/ppermute | solution.py:29
  327.4 56.3 %collective-permute-start.44 = (bf16[4,4,1,16,1152]{4,3,1,0,2:T(8,128)(2,1)}, bf16[4,4,1,16,1152]{4,3,1,0,2:T(8,128)(2,1)}, u32[]{:S(2)}, u32[]{:S(2)}) collective-permute-start(bf16[4,4,1,16,1152]{4,3,1,0,2:T(8,128)(2,1)} %pad_maximum_fusion.58), channel_id=1, source_target_pairs={{0,8},{2,10},{4,12},{6,14},{8,0},{10,2},{12,4},{14,6},{1,9},{3,11}... | collective-permute-start | bytes 1769480 | tf_op jit(solution)/shard_map/ppermute | solution.py:29
  383.7 75.7 %collective-permute-start.49 = (bf16[576,1152]{1,0:T(8,128)(2,1)}, bf16[576,1152]{1,0:T(8,128)(2,1)}, u32[]{:S(2)}, u32[]{:S(2)}) collective-permute-start(bf16[576,1152]{1,0:T(8,128)(2,1)} %bitcast.141.refs_0_), channel_id=1, source_target_pairs={{0,16},{16,0},{1,17},{17,1},{2,18},{18,2},{3,19},{19,3},{4,20},{20... | collective-permute-start | bytes 3981320 | tf_op jit(solution)/shard_map/ppermute | solution.py:29
  405.3 50.1 %collective-permute-start.48 = (bf16[4,4,2,1,16,1152]{5,4,1,2,0,3:T(8,128)(2,1)}, bf16[4,4,2,1,16,1152]{5,4,1,2,0,3:T(8,128)(2,1)}, u32[]{:S(2)}, u32[]{:S(2)}) collective-permute-start(bf16[4,4,2,1,16,1152]{5,4,1,2,0,3:T(8,128)(2,1)} %get-tuple-element.465), channel_id=1, source_target_pairs={{0,2},{1,3},{2,0},{3,1},{4,6},{5,7},{6,4},{7,5},{8,10},{9,11},{10,... | collective-permute-start | bytes 3538952 | tf_op jit(solution)/shard_map/ppermute | solution.py:876
  408.5 62.2 %collective-permute-start.51 = (bf16[2,576,1152]{2,1,0:T(8,128)(2,1)S(1)}, bf16[2,576,1152]{2,1,0:T(8,128)(2,1)}, u32[]{:S(2)}, u32[]{:S(2)}) collective-permute-start(bf16[2,576,1152]{2,1,0:T(8,128)(2,1)S(1)} %bitcast.870), channel_id=1, source_target_pairs={{0,16},{16,0},{1,17},{17,1},{2,18},{18,2},{3,19},{19,3},{4,20},{20... | collective-permute-start | bytes 7962632 | tf_op jit(solution)/shard_map/ppermute | solution.py:29
  412.7 51.4 %collective-permute-start.50 = (bf16[576,1152]{1,0:T(8,128)(2,1)}, bf16[576,1152]{1,0:T(8,128)(2,1)}, u32[]{:S(2)}, u32[]{:S(2)}) collective-permute-start(bf16[576,1152]{1,0:T(8,128)(2,1)} %collective-permute-done.41.refs_1_), channel_id=1, source_target_pairs={{0,16},{16,0},{1,17},{17,1},{2,18},{18,2},{3,19},{19,3},{4,20},{20... | collective-permute-start | bytes 3981320 | tf_op jit(solution)/shard_map/ppermute | solution.py:29
  414.5 83.4 %collective-permute-start.52 = (bf16[576,2304]{1,0:T(8,128)(2,1)}, bf16[576,2304]{1,0:T(8,128)(2,1)}, u32[]{:S(2)}, u32[]{:S(2)}) collective-permute-start(bf16[576,2304]{1,0:T(8,128)(2,1)} %all-gather.7.cloned.1.call-done.refs_0_.refs_6_), channel_id=1, source_target_pairs={{0,1},{1,0},{2,3},{3,2},{4,5},{5,4},{6,7},{7,6},{8,9},{9,8},{10,11... | collective-permute-start | bytes 7962632 | tf_op jit(solution)/shard_map/ppermute | solution.py:29
  455.3 64.2 %collective-permute-start.56 = (bf16[576,2304]{1,0:T(8,128)(2,1)}, bf16[576,2304]{1,0:T(8,128)(2,1)}, u32[]{:S(2)}, u32[]{:S(2)}) collective-permute-start(bf16[576,2304]{1,0:T(8,128)(2,1)} %all-gather.7.cloned.1.call-done.refs_0_.refs_6_), channel_id=1, source_target_pairs={{0,16},{16,0},{1,17},{17,1},{2,18},{18,2},{3,19},{19,3},{4,20},{20... | collective-permute-start | bytes 7962632 | tf_op jit(solution)/shard_map/ppermute | solution.py:29
  459.4 38.4 %collective-permute-start.55 = (bf16[4,2,2,1,16,1152]{5,4,1,2,0,3:T(8,128)(2,1)}, bf16[4,2,2,1,16,1152]{5,4,1,2,0,3:T(8,128)(2,1)S(1)}, u32[]{:S(2)}, u32[]{:S(2)}) collective-permute-start(bf16[4,2,2,1,16,1152]{5,4,1,2,0,3:T(8,128)(2,1)} %pad_maximum_fusion.62), channel_id=1, source_target_pairs={{0,12},{2,14},{4,8},{6,10},{8,4},{10,6},{12,0},{14,2},{1,13},{3,15... | collective-permute-start | bytes 1769480 | tf_op jit(solution)/shard_map/ppermute | solution.py:29
  464.1 52.2 %collective-permute-start.54 = (bf16[4,2,2,1,16,1152]{5,4,1,2,0,3:T(8,128)(2,1)}, bf16[4,2,2,1,16,1152]{5,4,1,2,0,3:T(8,128)(2,1)}, u32[]{:S(2)}, u32[]{:S(2)}) collective-permute-start(bf16[4,2,2,1,16,1152]{5,4,1,2,0,3:T(8,128)(2,1)} %pad_maximum_fusion.61), channel_id=1, source_target_pairs={{0,8},{2,10},{4,12},{6,14},{8,0},{10,2},{12,4},{14,6},{1,9},{3,11}... | collective-permute-start | bytes 1769480 | tf_op jit(solution)/shard_map/ppermute | solution.py:29
  470.7 45.6 %collective-permute-start.53 = (bf16[4,2,2,1,16,1152]{5,4,1,2,0,3:T(8,128)(2,1)}, bf16[4,2,2,1,16,1152]{5,4,1,2,0,3:T(8,128)(2,1)S(1)}, u32[]{:S(2)}, u32[]{:S(2)}) collective-permute-start(bf16[4,2,2,1,16,1152]{5,4,1,2,0,3:T(8,128)(2,1)} %pad_maximum_fusion.60), channel_id=1, source_target_pairs={{0,4},{2,6},{4,0},{6,2},{8,12},{10,14},{12,8},{14,10},{1,5},{3,7},... | collective-permute-start | bytes 1769480 | tf_op jit(solution)/shard_map/ppermute | solution.py:29
  548.6 45.9 %collective-permute-start.58 = (bf16[4,4,2,1,16,1152]{5,4,2,1,0,3:T(8,128)(2,1)}, bf16[4,4,2,1,16,1152]{5,4,2,1,0,3:T(8,128)(2,1)S(1)}, u32[]{:S(2)}, u32[]{:S(2)}) collective-permute-start(bf16[4,4,2,1,16,1152]{5,4,2,1,0,3:T(8,128)(2,1)} %get-tuple-element.461), channel_id=1, source_target_pairs={{0,2},{1,3},{2,0},{3,1},{4,6},{5,7},{6,4},{7,5},{8,10},{9,11},{10,... | collective-permute-start | bytes 3538952 | tf_op jit(solution)/shard_map/ppermute | solution.py:876
  606.5 72.7 %collective-permute-start.62 = (bf16[4,2,2,1,16,1152]{5,4,2,1,0,3:T(8,128)(2,1)}, bf16[4,2,2,1,16,1152]{5,4,2,1,0,3:T(8,128)(2,1)S(1)}, u32[]{:S(2)}, u32[]{:S(2)}) collective-permute-start(bf16[4,2,2,1,16,1152]{5,4,2,1,0,3:T(8,128)(2,1)} %pad_maximum_fusion.65), channel_id=1, source_target_pairs={{0,12},{2,14},{4,8},{6,10},{8,4},{10,6},{12,0},{14,2},{1,13},{3,15... | collective-permute-start | bytes 1769480 | tf_op jit(solution)/shard_map/ppermute | solution.py:29
  610.9 68.3 %collective-permute-start.61 = (bf16[4,2,2,1,16,1152]{5,4,2,1,0,3:T(8,128)(2,1)}, bf16[4,2,2,1,16,1152]{5,4,2,1,0,3:T(8,128)(2,1)S(1)}, u32[]{:S(2)}, u32[]{:S(2)}) collective-permute-start(bf16[4,2,2,1,16,1152]{5,4,2,1,0,3:T(8,128)(2,1)} %pad_maximum_fusion.64), channel_id=1, source_target_pairs={{0,8},{2,10},{4,12},{6,14},{8,0},{10,2},{12,4},{14,6},{1,9},{3,11}... | collective-permute-start | bytes 1769480 | tf_op jit(solution)/shard_map/ppermute | solution.py:29
  611.8 67.4 %collective-permute-start.60 = (bf16[4,2,2,1,16,1152]{5,4,2,1,0,3:T(8,128)(2,1)}, bf16[4,2,2,1,16,1152]{5,4,2,1,0,3:T(8,128)(2,1)}, u32[]{:S(2)}, u32[]{:S(2)}) collective-permute-start(bf16[4,2,2,1,16,1152]{5,4,2,1,0,3:T(8,128)(2,1)} %pad_maximum_fusion.63), channel_id=1, source_target_pairs={{0,4},{2,6},{4,0},{6,2},{8,12},{10,14},{12,8},{14,10},{1,5},{3,7},... | collective-permute-start | bytes 1769480 | tf_op jit(solution)/shard_map/ppermute | solution.py:29
  622.9 87.9 %collective-permute-start.66 = (bf16[576,4608]{1,0:T(8,128)(2,1)}, bf16[576,4608]{1,0:T(8,128)(2,1)}, u32[]{:S(2)}, u32[]{:S(2)}) collective-permute-start(bf16[576,4608]{1,0:T(8,128)(2,1)} %convolution_convert_fusion.2), channel_id=1, source_target_pairs={{0,16},{16,0},{1,17},{17,1},{2,18},{18,2},{3,19},{19,3},{4,20},{20... | collective-permute-start | bytes 15925256 | tf_op jit(solution)/shard_map/ppermute | solution.py:29
  685.3 107.3 %collective-permute-start.73 = (bf16[576,1728]{1,0:T(8,128)(2,1)}, bf16[576,1728]{1,0:T(8,128)(2,1)}, u32[]{:S(2)}, u32[]{:S(2)}) collective-permute-start(bf16[576,1728]{1,0:T(8,128)(2,1)} %convolution_convert_fusion.8), channel_id=1, source_target_pairs={{0,16},{16,0},{1,17},{17,1},{2,18},{18,2},{3,19},{19,3},{4,20},{20... | collective-permute-start | bytes 5971976 | tf_op jit(solution)/shard_map/ppermute | solution.py:29
  710.8 81.8 %collective-permute-start.67 = (bf16[576,2304]{1,0:T(8,128)(2,1)}, bf16[576,2304]{1,0:T(8,128)(2,1)S(1)}, u32[]{:S(2)}, u32[]{:S(2)}) collective-permute-start(bf16[576,2304]{1,0:T(8,128)(2,1)} %split.64), channel_id=1, source_target_pairs={{0,1},{1,0},{2,3},{3,2},{4,5},{5,4},{6,7},{7,6},{8,9},{9,8},{10,11... | collective-permute-start | bytes 7962632 | tf_op jit(solution)/shard_map/ppermute | solution.py:29
  726.4 48.1 %collective-permute-start.69 = (bf16[4,4,1,16,1152]{4,3,1,0,2:T(8,128)(2,1)}, bf16[4,4,1,16,1152]{4,3,1,0,2:T(8,128)(2,1)S(1)}, u32[]{:S(2)}, u32[]{:S(2)}) collective-permute-start(bf16[4,4,1,16,1152]{4,3,1,0,2:T(8,128)(2,1)} %pad_maximum_fusion.67), channel_id=1, source_target_pairs={{0,8},{2,10},{4,12},{6,14},{8,0},{10,2},{12,4},{14,6},{1,9},{3,11}... | collective-permute-start | bytes 1769480 | tf_op jit(solution)/shard_map/ppermute | solution.py:29
  734.9 94.8 %collective-permute-start.71 = (bf16[576,2304]{1,0:T(8,128)(2,1)S(1)}, bf16[576,2304]{1,0:T(8,128)(2,1)S(1)}, u32[]{:S(2)}, u32[]{:S(2)}) collective-permute-start(bf16[576,2304]{1,0:T(8,128)(2,1)S(1)} %split.65), channel_id=1, source_target_pairs={{0,1},{1,0},{2,3},{3,2},{4,5},{5,4},{6,7},{7,6},{8,9},{9,8},{10,11... | collective-permute-start | bytes 7962632 | tf_op jit(solution)/shard_map/ppermute | solution.py:29
  740.1 52.5 %collective-permute-start.72 = (bf16[576,1728]{1,0:T(8,128)(2,1)S(1)}, bf16[576,1728]{1,0:T(8,128)(2,1)S(1)}, u32[]{:S(2)}, u32[]{:S(2)}) collective-permute-start(bf16[576,1728]{1,0:T(8,128)(2,1)S(1)} %copy-done.159), channel_id=1, source_target_pairs={{0,16},{16,0},{1,17},{17,1},{2,18},{18,2},{3,19},{19,3},{4,20},{20... | collective-permute-start | bytes 5971976 | tf_op jit(solution)/shard_map/ppermute | solution.py:29
  831.9 391.1 %reduce-scatter.4.cloned.1.call-start = ((), (), s32[]{:S(2)}) async-start(), calls=%async_computation.5 | async-start | bytes 2985984 | tf_op jit(solution)/shard_map/reduce_scatter | solution.py:128
  842.6 60.0 %collective-permute-start.77 = (bf16[4,72,640]{2,1,0:T(8,128)(2,1)S(1)}, bf16[4,72,640]{2,1,0:T(8,128)(2,1)}, u32[]{:S(2)}, u32[]{:S(2)}) collective-permute-start(bf16[4,72,640]{2,1,0:T(8,128)(2,1)S(1)} %dynamic-slice_bitcast_fusion.7), channel_id=1, source_target_pairs={{0,2},{2,0},{4,6},{6,4},{8,10},{10,8},{12,14},{14,12},{1,3},{3,1},... | collective-permute-start | bytes 1105928 | tf_op jit(solution)/shard_map/ppermute | solution.py:29
  844.2 58.4 %collective-permute-start.76 = (bf16[576,256]{1,0:T(8,128)(2,1)}, bf16[576,256]{1,0:T(8,128)(2,1)}, u32[]{:S(2)}, u32[]{:S(2)}) collective-permute-start(bf16[576,256]{1,0:T(8,128)(2,1)} %slice.1070), channel_id=1, source_target_pairs={{0,1},{1,0},{2,3},{3,2},{4,5},{5,4},{6,7},{7,6},{8,9},{9,8},{10,11... | collective-permute-start | bytes 884744 | tf_op jit(solution)/shard_map/ppermute | solution.py:29
  850.3 52.3 %collective-permute-start.75 = (bf16[576,1728]{1,0:T(8,128)(2,1)}, bf16[576,1728]{1,0:T(8,128)(2,1)}, u32[]{:S(2)}, u32[]{:S(2)}) collective-permute-start(bf16[576,1728]{1,0:T(8,128)(2,1)} %add_convert_fusion.10), channel_id=1, source_target_pairs={{0,1},{1,0},{2,3},{3,2},{4,5},{5,4},{6,7},{7,6},{8,9},{9,8},{10,11... | collective-permute-start | bytes 5971976 | tf_op jit(solution)/shard_map/ppermute | solution.py:29
  856.8 366.2 %reduce-scatter.8.cloned.1.call-start = ((), (), s32[]{:S(2)}) async-start(), calls=%async_computation.7 | async-start | bytes 2322432 | tf_op jit(solution)/shard_map/reduce_scatter | solution.py:128
  913.9 35.2 %collective-permute-start.81 = (bf16[576,4608]{1,0:T(8,128)(2,1)}, bf16[576,4608]{1,0:T(8,128)(2,1)}, u32[]{:S(2)}, u32[]{:S(2)}) collective-permute-start(bf16[576,4608]{1,0:T(8,128)(2,1)} %convolution_convert_fusion), channel_id=1, source_target_pairs={{0,16},{16,0},{1,17},{17,1},{2,18},{18,2},{3,19},{19,3},{4,20},{20... | collective-permute-start | bytes 15925256 | tf_op jit(solution)/shard_map/ppermute | solution.py:29
  963.4 86.6 %collective-permute-start.88 = (bf16[4,72,2304]{2,1,0:T(8,128)(2,1)}, bf16[4,72,2304]{2,1,0:T(8,128)(2,1)}, u32[]{:S(2)}, u32[]{:S(2)}) collective-permute-start(bf16[4,72,2304]{2,1,0:T(8,128)(2,1)} %dynamic-slice_bitcast_fusion), channel_id=1, source_target_pairs={{0,2},{2,0},{4,6},{6,4},{8,10},{10,8},{12,14},{14,12},{1,3},{3,1},... | collective-permute-start | bytes 3981320 | tf_op jit(solution)/shard_map/ppermute | solution.py:29
  964.1 85.8 %collective-permute-start.87 = (bf16[576,1152]{1,0:T(8,128)(2,1)}, bf16[576,1152]{1,0:T(8,128)(2,1)}, u32[]{:S(2)}, u32[]{:S(2)}) collective-permute-start(bf16[576,1152]{1,0:T(8,128)(2,1)} %get-tuple-element.418), channel_id=1, source_target_pairs={{0,1},{1,0},{2,3},{3,2},{4,5},{5,4},{6,7},{7,6},{8,9},{9,8},{10,11... | collective-permute-start | bytes 3981320 | tf_op jit(solution)/shard_map/ppermute | solution.py:29
  966.7 74.6 %collective-permute-start.85 = (bf16[72,576]{1,0:T(8,128)(2,1)S(1)}, bf16[72,576]{1,0:T(8,128)(2,1)S(1)}, u32[]{:S(2)}, u32[]{:S(2)}) collective-permute-start(bf16[72,576]{1,0:T(8,128)(2,1)S(1)} %get-tuple-element.616), channel_id=1, source_target_pairs={{0,8},{2,10},{4,12},{6,14},{8,0},{10,2},{12,4},{14,6},{1,9},{3,11}... | collective-permute-start | bytes 248840 | tf_op jit(solution)/shard_map/ppermute | solution.py:29
  982.8 67.1 %collective-permute-start.83 = (bf16[4,72,2304]{2,1,0:T(8,128)(2,1)}, bf16[4,72,2304]{2,1,0:T(8,128)(2,1)}, u32[]{:S(2)}, u32[]{:S(2)}) collective-permute-start(bf16[4,72,2304]{2,1,0:T(8,128)(2,1)} %dynamic-slice_bitcast_fusion.1), channel_id=1, source_target_pairs={{0,2},{2,0},{4,6},{6,4},{8,10},{10,8},{12,14},{14,12},{1,3},{3,1},... | collective-permute-start | bytes 3981320 | tf_op jit(solution)/shard_map/ppermute | solution.py:29
  984.7 65.2 %collective-permute-start.82 = (bf16[576,1152]{1,0:T(8,128)(2,1)}, bf16[576,1152]{1,0:T(8,128)(2,1)}, u32[]{:S(2)}, u32[]{:S(2)}) collective-permute-start(bf16[576,1152]{1,0:T(8,128)(2,1)} %get-tuple-element.421), channel_id=1, source_target_pairs={{0,1},{1,0},{2,3},{3,2},{4,5},{5,4},{6,7},{7,6},{8,9},{9,8},{10,11... | collective-permute-start | bytes 3981320 | tf_op jit(solution)/shard_map/ppermute | solution.py:29
  1049.9 88.8 %collective-permute-start.107 = (bf16[576,1152]{1,0:T(8,128)(2,1)}, bf16[576,1152]{1,0:T(8,128)(2,1)}, u32[]{:S(2)}, u32[]{:S(2)}) collective-permute-start(bf16[576,1152]{1,0:T(8,128)(2,1)} %convolution_convert_fusion.4), channel_id=1, source_target_pairs={{0,16},{16,0},{1,17},{17,1},{2,18},{18,2},{3,19},{19,3},{4,20},{20... | collective-permute-start | bytes 3981320 | tf_op jit(solution)/shard_map/ppermute | solution.py:29
  1058.9 103.2 %collective-permute-start.106 = (bf16[576,1728]{1,0:T(8,128)(2,1)}, bf16[576,1728]{1,0:T(8,128)(2,1)}, u32[]{:S(2)}, u32[]{:S(2)}) collective-permute-start(bf16[576,1728]{1,0:T(8,128)(2,1)} %convolution_convert_fusion.6), channel_id=1, source_target_pairs={{0,16},{16,0},{1,17},{17,1},{2,18},{18,2},{3,19},{19,3},{4,20},{20... | collective-permute-start | bytes 5971976 | tf_op jit(solution)/shard_map/ppermute | solution.py:29
  1077.0 85.2 %collective-permute-start.105 = (bf16[576,1728]{1,0:T(8,128)(2,1)}, bf16[576,1728]{1,0:T(8,128)(2,1)}, u32[]{:S(2)}, u32[]{:S(2)}) collective-permute-start(bf16[576,1728]{1,0:T(8,128)(2,1)} %convolution_convert_fusion.7), channel_id=1, source_target_pairs={{0,16},{16,0},{1,17},{17,1},{2,18},{18,2},{3,19},{19,3},{4,20},{20... | collective-permute-start | bytes 5971976 | tf_op jit(solution)/shard_map/ppermute | solution.py:29
  1078.3 61.9 %collective-permute-start.104 = (bf16[4,72,1152]{2,1,0:T(8,128)(2,1)}, bf16[4,72,1152]{2,1,0:T(8,128)(2,1)}, u32[]{:S(2)}, u32[]{:S(2)}) collective-permute-start(bf16[4,72,1152]{2,1,0:T(8,128)(2,1)} %split.69), channel_id=1, source_target_pairs={{0,1},{1,0},{2,3},{3,2},{4,5},{5,4},{6,7},{7,6},{8,9},{9,8},{10,11... | collective-permute-start | bytes 1990664 | tf_op jit(solution)/shard_map/ppermute | solution.py:29
  1185.0 33.8 %collective-permute-start.108 = (bf16[72,2304]{1,0:T(8,128)(2,1)S(1)}, bf16[72,2304]{1,0:T(8,128)(2,1)S(1)}, u32[]{:S(2)}, u32[]{:S(2)}) collective-permute-start(bf16[72,2304]{1,0:T(8,128)(2,1)S(1)} %get-tuple-element.504), channel_id=1, source_target_pairs={{0,4},{2,6},{4,0},{6,2},{8,12},{10,14},{12,8},{14,10},{1,5},{3,7},... | collective-permute-start | bytes 995336 | tf_op jit(solution)/shard_map/ppermute | solution.py:29
  1190.6 41.9 %collective-permute-start.117 = (bf16[4,72,640]{2,1,0:T(8,128)(2,1)S(1)}, bf16[4,72,640]{2,1,0:T(8,128)(2,1)}, u32[]{:S(2)}, u32[]{:S(2)}) collective-permute-start(bf16[4,72,640]{2,1,0:T(8,128)(2,1)S(1)} %dynamic-slice_bitcast_fusion.6), channel_id=1, source_target_pairs={{0,2},{2,0},{4,6},{6,4},{8,10},{10,8},{12,14},{14,12},{1,3},{3,1},... | collective-permute-start | bytes 1105928 | tf_op jit(solution)/shard_map/ppermute | solution.py:29
  1195.3 37.2 %collective-permute-start.115 = (bf16[4,72,1920]{2,1,0:T(8,128)(2,1)}, bf16[4,72,1920]{2,1,0:T(8,128)(2,1)}, u32[]{:S(2)}, u32[]{:S(2)}) collective-permute-start(bf16[4,72,1920]{2,1,0:T(8,128)(2,1)} %dynamic-slice_bitcast_fusion.2), channel_id=1, source_target_pairs={{0,2},{2,0},{4,6},{6,4},{8,10},{10,8},{12,14},{14,12},{1,3},{3,1},... | collective-permute-start | bytes 3317768 | tf_op jit(solution)/shard_map/ppermute | solution.py:29
  (250 other events, 2526.6 us)
Sparse Core Ops, SparseCore 0:
  19.1 70.8 all-gather.8
  92.2 67.4 all-gather.4
  214.9 81.6 all-gather.6
  832.0 70.5 reduce-scatter.5
  906.6 73.5 reduce-scatter.3
  983.6 74.1 reduce-scatter.7

commit v6 on v5

--- a/solution.py
+++ b/solution.py
@@ -114,40 +114,57 @@
         layout = tuple(((r, None, block.shape[1]),) for r in range(self.n_tp))
         return self.with_core([block] + got, layout)
 
-    def scatter_far(self, left, rights):
-        others = range(1, self.n_tp)
-        half_width = left.shape[1] // 2
-        mine, theirs = left[:, :half_width], left[:, half_width:]
-        got = [self.over_core(dot(theirs, v, TN).astype(BF16)) for v in rights]
-        got = yield got
-        totals = [(dot(mine, v, TN) + g.astype(F32)).astype(BF16) for v, g in zip(rights, got)]
-        if len(totals) == 1:
-            totals = jnp.split(totals[0], self.n_tp, axis=1)
-        got = yield [self.over_tp(totals[r], r) for r in others]
+    def scatter_core(self, groups):
+        halves = [(v[:, : v.shape[1] // 2], v[:, v.shape[1] // 2 :]) for v, _ in groups]
+        got = yield [
+            [self.over_core(dot(theirs, v, TN).astype(BF16)) for v in rights]
+            for (_, theirs), (_, rights) in zip(halves, groups)
+        ]
+        found = []
+        for (mine, _), (_, rights), came in zip(halves, groups, got):
+            totals = [
+                (dot(mine, v, TN) + g.astype(F32)).astype(BF16) for v, g in zip(rights, came)
+            ]
+            if len(totals) == 1:
+                totals = jnp.split(totals[0], self.n_tp, axis=1)
+            found.append(totals)
+        return found
+
+    def scatter_far(self, groups):
+        found = yield from self.scatter_core(groups)
+        totals = [
+            jnp.concatenate([v[r] for v in found], axis=1) if len(found) > 1 else found[0][r]
+            for r in range(self.n_tp)
+        ]
+        got = yield [self.over_tp(totals[r], r) for r in range(1, self.n_tp)]
         total = (totals[0].astype(F32) + sum(v.astype(F32) for v in got)).astype(BF16)
         shard = yield Rest(lax.psum_scatter(total, "ctx", scatter_dimension=0, tiled=True))
         return shard.astype(F32)
 
-    def scatter_weight(self, left, rights):
+    def scatter_weight(self, groups):
         others = range(1, self.n_tp)
-        half_width = left.shape[1] // 2
-        mine, theirs = left[:, :half_width], left[:, half_width:]
-        got = [self.over_core(dot(theirs, v, TN).astype(BF16)) for v in rights]
-        got = yield got
-        totals = [(dot(mine, v, TN) + g.astype(F32)).astype(BF16) for v, g in zip(rights, got)]
-        if len(totals) == 1:
-            totals = jnp.split(totals[0], self.n_tp, axis=1)
-        columns = totals[0].shape[1]
-        half = max(columns // 2 // LANES, 1) * LANES
-        firsts = [v[:, :half] for v in totals]
-        seconds = jnp.concatenate([v[:, half:] for v in totals], axis=1)
-        got = (
-            [self.over_tp(firsts[r], r) for r in others],
-            self.over_side(self.of_side(seconds, 1 - self.side)),
-        )
+        found = yield from self.scatter_core(groups)
+        sizes = [v[0].shape[1] for v in found]
+        half = max(sum(sizes) // 2 // LANES, 1) * LANES
+        firsts, seconds = [[] for _ in range(self.n_tp)], []
+        for r in range(self.n_tp):
+            low = 0
+            for v, size in zip(found, sizes):
+                cut = min(max(half - low, 0), size)
+                if cut:
+                    firsts[r].append(v[r][:, :cut])
+                if cut < size:
+                    seconds.append(v[r][:, cut:])
+                low += size
+        firsts = [jnp.concatenate(v, axis=1) if len(v) > 1 else v[0] for v in firsts]
+
+        def of_side(side):
+            return jnp.concatenate([self.of_side(v, side) for v in seconds], axis=-1)
+
+        got = [self.over_tp(firsts[r], r) for r in others], self.over_side(of_side(1 - self.side))
         tp_got, side_got = yield got
         first = (firsts[0].astype(F32) + sum(v.astype(F32) for v in tp_got)).astype(BF16)
-        second = self.of_side(seconds, self.side).astype(F32) + side_got.astype(F32)
+        second = of_side(self.side).astype(F32) + side_got.astype(F32)
         second = jnp.split(second.astype(BF16), self.n_tp, axis=-1)
         got = (
             self.over_side(self.of_side(first, 1 - self.side)),
@@ -829,6 +846,7 @@
 
     def modulation_vectors():
         sums = shares[:clips] + swap_with(shares[clips:], "dp", n_dp, 1)
+        sums = yield sums
         sums = yield from total_over_ctx(sums)
         pairs = [
             [(c * n_tp + t, (c ^ dx) * n_tp + (t ^ r)) for c in range(n_ctx) for t in range(n_tp)]
@@ -854,11 +872,13 @@
         return jnp.stack([v[:, 0]] + got, axis=2).reshape(clips, -1, width)
 
     def from_frames(v):
+        got = ()
         if spread_tp > 1:
             v = v.reshape(clips, groups, spread_tp, patches_here, width)
-            blocks = [v[:, :, 0]]
-            blocks += [swap_with(v[:, :, r], "tp", n_tp, r) for r in range(1, spread_tp)]
-            v = flip_to(jnp.stack(blocks, axis=1), 1, spread_tp, moves.tp)
+            got = [swap_with(v[:, :, r], "tp", n_tp, r) for r in range(1, spread_tp)]
+        got = yield got
+        if spread_tp > 1:
+            v = flip_to(jnp.stack([v[:, :, 0]] + got, axis=1), 1, spread_tp, moves.tp)
         v = v.reshape(clips, frames_here, n_ctx, piece, width)
         v = flip_to(v, 2, n_ctx, moves.ctx)
         return v.reshape(clips, frames_here, patches_here, width)
@@ -941,16 +961,16 @@
         ((1,), (), ()),
         ((4,), (), (5,)),
         ((3,), (), ()),
-        ((), (3,), ()),
+        ((), (3, 4), ()),
         ((5,), (), ()),
         ((), (5,), ()),
         ((), (), ()),
     ]
 
-    def tick(values=()):
+    def tick(values=(), waiting=()):
         out, but, far = plan.pop(0)
         held = {index: blocks.get(index, shards[index]) for index in out + far}
-        held, values = lanes.fence((held, values), [gathers[index] for index in but])
+        held, values = lanes.fence((held, values), [gathers[index] for index in but] + list(waiting))
         for index in out + far:
             if index in blocks:
                 blocks[index] = held[index]
@@ -1006,10 +1026,18 @@
     scatters = {}
     mod_grads = [None] * LAYERS
 
-    def start_scatter(level, name, left, rights):
-        far = level and name != "out"
-        steps = (moves.scatter_far if far else moves.scatter_weight)(left, rights)
-        scatters[level, name] = lanes.start(steps)
+    def start_scatter(level, names, *groups):
+        steps = (moves.scatter_far if level else moves.scatter_weight)(groups)
+        scatters[level, names] = lanes.start(steps)
+        return scatters[level, names]
+
+    def scattered(level, name):
+        for (at, names), task in scatters.items():
+            if at == level and name in names:
+                columns = {"qkv": 3 * head_cols, "out": head_cols}
+                units = w_up.shape[2]
+                low = sum(columns.get(n, units) for n in names[: names.index(name)])
+                return task.result[:, low : low + columns.get(name, units)]
 
     def mod_strip():
         parts = [moves.halves(v).reshape(clips, n_tp, -1) for v in mod_grads]
@@ -1035,7 +1063,8 @@
             kept = fused_branch(v, vectors[level], joined, clips, stride)
             normed, qkv, lse, result, branch, middle, normed_mlp = tick(kept)
             up = gathers[3 * level + 1].result
-            act, slope = tick(fused_up(normed_mlp, vectors[level], up, clips))
+            waiting = (turned,) if level else ()
+            act, slope = tick(fused_up(normed_mlp, vectors[level], up, clips), waiting)
             down = gathers[3 * level + 2].result
             branch_mlp, after = fused_down(act, middle, vectors[level], down, clips)
             saved.append((v, normed, qkv, lse, result, branch, middle, normed_mlp))
@@ -1047,6 +1076,7 @@
                 late = tick(cotangent)
                 turned = lanes.start(here_to_clips(moves.halves(late)))
                 v = flat(moved.result)
+        v = lanes.fence(v)
         finished = lanes.start(clips_to_here(moves.halves(shaped(v))))
         grad = flat(turned.result)
         for level in reversed(range(LAYERS)):
@@ -1056,28 +1086,29 @@
                 grad, vectors[level], branch_mlp, slope, middle, branch, up, down, clips
             )
             grad_branch, grad_pre, grad_middle, grad_out, sums = lanes.fence(back)
-            start_scatter(level, "down", grad_branch, [act])
-            late = tuple(scatters[level + 1, n] for n in ("qkv", "out")) if not level else (finished,)
-            grad_out = lanes.fence(grad_out, late)
-            if level == 0:
-                start_scatter(level, "up", normed_mlp, [grad_pre])
-                grad_out = lanes.fence(grad_out, (scatters[level, "down"],))
+            if level:
+                waiting = start_scatter(level, ("down",), (grad_branch, [act]))
+                grad_out = lanes.fence(grad_out, (finished,))
+            else:
+                start_scatter(
+                    level, ("down", "up"), (grad_branch, [act]), (normed_mlp, [grad_pre])
+                )
+                grad_out = lanes.fence(grad_out, (scatters[1, ("qkv", "out")],))
             back = fused_branch_back(
                 v, vectors[level], grad_out, grad_middle, qkv, lse, joined, clips, stride
             )
-            grad, more, *grad_qkv = lanes.fence(back, (scatters[level, "down"],) if level else ())
+            grad, more, *grad_qkv = lanes.fence(back, (waiting,) if level else ())
             mod_grads[level] = (sums + more)[:, :6]
+            joint = (normed, grad_qkv), (grad_out, [result])
             if level:
                 moved = lanes.start(clips_to_frames(shaped(grad)))
-                start_scatter(level, "up", normed_mlp, [grad_pre])
-                lanes.fence((), (scatters[level, "down"],))
-                start_scatter(level, "qkv", normed, grad_qkv)
-                start_scatter(level, "out", grad_out, [result])
-                lanes.fence()
+                task = start_scatter(level, ("up",), (normed_mlp, [grad_pre]))
+                lanes.fence((), (waiting,))
+                start_scatter(level, ("qkv", "out"), *joint)
+                lanes.fence((), (task,))
                 grad = flat(moved.result)
             else:
-                start_scatter(level, "qkv", normed, grad_qkv)
-                start_scatter(level, "out", grad_out, [result])
+                start_scatter(level, ("qkv", "out"), *joint)
         return finished, shaped(grad)
 
     def plain_passes(residual):
@@ -1129,17 +1160,17 @@
             gate_m_grad = jnp.sum(gradient * branch_mlp, axis=1)
             low_grad = flat((gradient * gate_m[:, None]).astype(BF16))
             grad_pre = gelu_slope(pre_act, dot(low_grad, down)).astype(BF16)
-            start_scatter(level, "down", low_grad, [act])
+            start_scatter(level, ("down",), (low_grad, [act]))
             grad_pre = lanes.fence(grad_pre)
             grad_normed = shaped(dot(grad_pre, up, NT))
-            start_scatter(level, "up", normed_mlp, [grad_pre])
+            start_scatter(level, ("up",), (normed_mlp, [grad_pre]))
             grad_normed = lanes.fence(grad_normed)
             added, shift_m_grad, scale_m_grad = modulate_back(grad_normed, middle, scale_m)
             gradient = gradient + added
             gate_a_grad = jnp.sum(gradient * branch, axis=1)
             low_grad = flat((gradient * gate_a[:, None]).astype(BF16))
             grad_heads = dot(low_grad, outs).astype(BF16)
-            start_scatter(level, "out", low_grad, [result])
+            start_scatter(level, ("out",), (low_grad, [result]))
             grad_heads = lanes.fence(grad_heads)
             if spatial and not whole_frames:
                 grad_qkv = [
@@ -1149,7 +1180,7 @@
             else:
                 grad_qkv = attend_back(projected, grad_heads, saved, rows, stride)
             grad_qkv = lanes.fence(grad_qkv)
-            start_scatter(level, "qkv", normed, grad_qkv)
+            start_scatter(level, ("qkv",), (normed, grad_qkv))
             grad_normed = shaped(sum(dot(v, w, NT) for v, w in zip(grad_qkv, qkvs)))
             added, shift_a_grad, scale_a_grad = modulate_back(grad_normed, residual, scale_a)
             gradient = gradient + added
@@ -1166,24 +1197,28 @@
 
     passes = fused_passes if fused else plain_passes
     finished, gradient = passes(residual)
-    grad_tokens = from_frames(moves.halves(gradient.astype(BF16))).astype(F32)
+    mod_grads, gradient = lanes.fence((mod_grads, gradient))
+    hanging = [scatters[key] for key in scatters if key == (0, ("down", "up"))]
+    both = at_once(mod_strip())
+    lanes.fence((), hanging)
     lanes.fence()
+    moved = lanes.start(from_frames(moves.halves(gradient.astype(BF16))))
     while lanes.tasks:
         lanes.fence(last=True)
+    grad_tokens = moved.result.astype(F32)
     output = finished.result
     grads = [
         (
-            scatters[level, "qkv"].result.reshape(rows_here, 3, head_cols).transpose(1, 0, 2),
-            scatters[level, "out"].result.T,
-            scatters[level, "up"].result,
-            scatters[level, "down"].result.T,
+            scattered(level, "qkv").reshape(rows_here, 3, head_cols).transpose(1, 0, 2),
+            scattered(level, "out").T,
+            scattered(level, "up"),
+            scattered(level, "down").T,
         )
         for level in range(LAYERS)
     ]
 
     ada_grads = []
     cond_part = 0.0
-    both = at_once(mod_strip())
     for level in range(LAYERS):
         strip = both[:, level]
         ada_grads.append(

time: 1310 us -> 1340 us (1.023)
  waiting for transfers between devices: 353 us -> 410 us
  starting transfers between devices: 175 us -> 137 us
  local copies, waits for them, and re-layouts: 122 us -> 137 us
    ppermute x117 -> x96, waiting for transfers between devices: 322 us -> 380 us  [swap_with(): return lax.ppermute(v, axis_name, [(i, i ^ k) for i in range(n)])]
    ppermute x117 -> x96, starting transfers between devices: 162 us -> 122 us  [swap_with(): return lax.ppermute(v, axis_name, [(i, i ^ k) for i in range(n)])]
    unnamed x362 -> x343, local copies, waits for them, and re-layouts: 45.4 us -> 38.9 us
  transfers between devices with their start and end apart: 134 -> 113, of which waited for: 43 -> 39; matrix products, arithmetic and copies ran while one was open for 23% -> 22% of each run, Pallas kernels for 28% -> 29%
where the time goes in v6:
time: 1340 us; the launch traced here: 1330 us
  waiting for transfers between devices  410 us (31%)
  Pallas kernels  380 us (28%)
  local copies, waits for them, and re-layouts  137 us (10%)
  starting transfers between devices  137 us (10%)
  matrix products  134 us (10%)
  other arithmetic  116 us (9%)
  between operations  17.7 us (1%)
    pallas_call x10, Pallas kernels, block_call(): pl.pallas_call(kernel, grid=(clips,), in_specs=specs, out_specs=out_specs...  380 us
    ppermute x96, waiting for transfers between devices, swap_with(): return lax.ppermute(v, axis_name, [(i, i ^ k) for i in range(n)])  380 us
    dot_general x22, matrix products, dot(): return lax.dot_general(a, b, dims, preferred_element_type=F32)  132 us
    ppermute x96, starting transfers between devices, swap_with(): return lax.ppermute(v, axis_name, [(i, i ^ k) for i in range(n)])  122 us
    unnamed x343, local copies, waits for them, and re-layouts  38.9 us
  transfers between devices with their start and end apart: 113, of which 39 were waited for; matrix products, arithmetic and copies ran while one was open for 22% of the time, Pallas kernels for 29%

profile of v6, /device:TPU:0, one launch (start us, length us, event | category | flops | bytes accessed | tf_op | source)
XLA Modules:
  0.0 1331.9 jit_solution(15474805430248005051)
XLA Ops:
  47.8 18.4 %collective-permute-done.3 = bf16[4,1,128,1152]{3,2,0,1:T(8,128)(2,1)} collective-permute-done((bf16[4,1,128,1152]{3,2,0,1:T(8,128)(2,1)}, bf16[4,1,128,1152]{3,2,0,1:T(8,128)(2,1)}, u32[]{:S(2)}, u32[]{:S(2)}) %collective-permute-start.3) | collective-permute-done | bytes 1179680 | tf_op jit(solution)/shard_map/ppermute | solution.py:29
  81.3 3.7 collective-permute-start.10
  86.9 3.6 collective-permute-done.10
  93.9 3.7 collective-permute-done.9
  107.3 7.1 collective-permute-done.11
  116.2 10.4 collective-permute-done.12
  134.6 4.0 collective-permute-done.17
  157.5 39.8 %shard_map.152 = (bf16[1024,1152]{1,0:T(8,128)(2,1)}, bf16[1024,3840]{1,0:T(8,128)(2,1)}, f32[1024,128]{1,0:T(8,128)}, bf16[1024,1152]{1,0:T(8,128)(2,1)}, bf16[...) custom-call(bf16[1024,1152]{1,0:T(8,128)(2,1)} %bitcast.819, ...), custom_call_target="tpu_custom_call" | custom-call | flops 16307453952 | bytes 13123584 | tf_op jit(solution)/shard_map/pallas_call | solution.py:667
  197.3 14.3 %collective-permute-done.23 = bf16[4,72,1152]{2,1,0:T(8,128)(2,1)S(1)} collective-permute-done((bf16[4,72,1152]{2,1,0:T(8,128)(2,1)}, bf16[4,72,1152]{2,1,0:T(8,128)(2,1)S(1)}, u32[]{:S(2)}, u32[]{:S(2)}) %collective-permute-start.23) | collective-permute-done | bytes 663584 | tf_op jit(solution)/shard_map/ppermute | solution.py:29
  225.1 27.0 %shard_map.153 = (bf16[1024,4608]{1,0:T(8,128)(2,1)}, bf16[1024,4608]{1,0:T(8,128)(2,1)}) custom-call(bf16[1024,1152]{1,0:T(8,128)(2,1)} %get-tuple-element.207.g_ref, bf16[576,2304]{1,0:T(8,128)(2,1)} %bitcast.859, bf16[576,2304]{1,0:T(8,128)(2,1)} %collective-permute-done.24.refs_1_, bf16[576,2304]{1,0:T(8,128)(2,1)} %collective-permute-done.25.refs_2_, ...), custom_call_target="tpu_custom_call" | custom-call | flops 10871635968 | bytes 12976128 | tf_op jit(solution)/shard_map/pallas_call | solution.py:667
  265.4 22.1 %shard_map.154 = (bf16[1024,1152]{1,0:T(8,128)(2,1)}, bf16[1024,1152]{1,0:T(8,128)(2,1)}) custom-call(bf16[1024,4608]{1,0:T(8,128)(2,1)} %get-tuple-element.214.z_ref, f32[1024,1152]{1,0:T(8,128)} %get-tuple-element.215.y_ref, f32[4,8,1152]{2,1,0:T(8,128)} %concatenate.622.mod_ref, bf16[576,1152]{1,0:T(8,128)(2,1)} %bitcast.100.refs_0_.refs_4_, ...), custom_call_target="tpu_custom_call" | custom-call | flops 10871635968 | bytes 24920064 | tf_op jit(solution)/shard_map/pallas_call | solution.py:667
  296.1 8.4 collective-permute-done.35
  307.4 13.2 collective-permute-done.37
  321.8 3.7 collective-permute-start.43
  326.5 9.0 collective-permute-start.42
  338.6 36.6 %collective-permute-done.40.refs_1_ = bf16[576,2304]{1,0:T(8,128)(2,1)} collective-permute-done((bf16[576,2304]{1,0:T(8,128)(2,1)}, bf16[576,2304]{1,0:T(8,128)(2,1)}, u32[]{:S(2)}, u32[]{:S(2)}) %collective-permute-start.40) | collective-permute-done | bytes 2654240 | tf_op jit(solution)/shard_map/ppermute | solution.py:29
  395.1 39.8 %shard_map.155 = (bf16[1024,1152]{1,0:T(8,128)(2,1)}, bf16[1024,3840]{1,0:T(8,128)(2,1)}, f32[1024,128]{1,0:T(8,128)}, bf16[1024,1152]{1,0:T(8,128)(2,1)}, bf16[...) custom-call(bf16[1024,1152]{1,0:T(8,128)(2,1)} %bitcast.821, ...), custom_call_target="tpu_custom_call" | custom-call | flops 16307453952 | bytes 13123584 | tf_op jit(solution)/shard_map/pallas_call | solution.py:667
  434.9 7.2 collective-permute-done.47
  447.7 7.2 collective-permute-done.49.refs_3_
  456.0 26.7 %shard_map.156 = (bf16[1024,4608]{1,0:T(8,128)(2,1)}, bf16[1024,4608]{1,0:T(8,128)(2,1)}) custom-call(bf16[1024,1152]{1,0:T(8,128)(2,1)} %get-tuple-element.241.g_ref, bf16[576,1152]{1,0:T(8,128)(2,1)} %bitcast.147.refs_0_, bf16[576,1152]{1,0:T(8,128)(2,1)} %collective-permute-done.46.refs_1_, bf16[2,576,1152]{2,1,0:T(8,128)(2,1)} %bitcast.813, ...), custom_call_target="tpu_custom_call" | custom-call | flops 10871635968 | bytes 12976128 | tf_op jit(solution)/shard_map/pallas_call | solution.py:667
  482.7 23.5 %collective-permute-done.52.refs_1_.refs_7_ = bf16[576,2304]{1,0:T(8,128)(2,1)} collective-permute-done((bf16[576,2304]{1,0:T(8,128)(2,1)}, bf16[576,2304]{1,0:T(8,128)(2,1)}, u32[]{:S(2)}, u32[]{:S(2)}) %collective-permute-start.52) | collective-permute-done | bytes 2654240 | tf_op jit(solution)/shard_map/ppermute | solution.py:29
  507.7 4.0 collective-permute-start.57
  511.8 8.6 collective-permute-start.56
  521.6 22.0 %shard_map.157 = (bf16[1024,1152]{1,0:T(8,128)(2,1)}, bf16[1024,1152]{1,0:T(8,128)(2,1)}) custom-call(bf16[1024,4608]{1,0:T(8,128)(2,1)} %get-tuple-element.247.z_ref, f32[1024,1152]{1,0:T(8,128)} %get-tuple-element.248.y_ref, f32[4,8,1152]{2,1,0:T(8,128)} %pad_maximum_fusion.66.mod_ref, bf16[576,2304]{1,0:T(8,128)(2,1)} %all-gather.7.cloned.1.call-done.refs_0_.refs_6_, ...), custom_call_target="tpu_custom_call" | custom-call | flops 10871635968 | bytes 24920064 | tf_op jit(solution)/shard_map/pallas_call | solution.py:667
  543.6 20.0 %collective-permute-done.56 = bf16[4,2,2,1,16,1152]{5,4,1,2,0,3:T(8,128)(2,1)S(1)} collective-permute-done((bf16[4,2,2,1,16,1152]{5,4,1,2,0,3:T(8,128)(2,1)S(1)}, bf16[4,2,2,1,16,1152]{5,4,1,2,0,3:T(8,128)(2,1)S(1)}, u32[]{:S(2)}, u32[]{:S(2)}) %collective-permute-start.56) | collective-permute-done | bytes 589856 | tf_op jit(solution)/shard_map/ppermute | solution.py:29
  572.5 45.2 %shard_map.158 = (bf16[1024,1152]{1,0:T(8,128)(2,1)}, bf16[1024,4608]{1,0:T(8,128)(2,1)}, f32[1024,1152]{1,0:T(8,128)}, bf16[1024,1152]{1,0:T(8,128)(2,1)}, f32[4,8,1152]{2,1,0:T(8,128)}) custom-call(bf16[1024,1152]{1,0:T(8,128)(2,1)} %bitcast.824, f32[4,8,1152]{2,1,0:T(8,128)} %pad_maximum_fusion.66.mod_ref, bf16[1024,1152]{1,0:T(8,128)(2,1)} %get-tuple-element.256.m_ref, ...), custom_call_target="tpu_custom_call" | custom-call | flops 21743271936 | bytes 42614784 | tf_op jit(solution)/shard_map/pallas_call | solution.py:667
  617.7 10.9 convolution_convert_fusion.3
  635.9 10.3 convolution_convert_fusion.2
  646.3 56.1 %shard_map.159 = (bf16[1024,1152]{1,0:T(8,128)(2,1)}, f32[4,8,1152]{2,1,0:T(8,128)}, bf16[1024,1728]{1,0:T(8,128)(2,1)}, bf16[1024,1728]{1,0:T(8,128)(2,1)}) custom-call(bf16[1024,1152]{1,0:T(8,128)(2,1)} %bitcast.822, f32[4,8,1152]{2,1,0:T(8,128)} %pad_maximum_fusion.66.mod_ref, bf16[1024,1152]{1,0:T(8,128)(2,1)} %get-tuple-element.267.da_ref, ...), custom_call_target="tpu_custom_call" | custom-call | flops 21743271936 | bytes 28590080 | tf_op jit(solution)/shard_map/pallas_call | solution.py:667
  702.5 6.1 convolution_convert_fusion.8
  724.5 8.0 add_convert_fusion.3
  738.1 3.9 convolution_convert_fusion.9
  755.3 11.1 collective-permute-done.70
  766.3 35.0 %collective-permute-done.69 = bf16[4,4,1,16,1152]{4,3,1,0,2:T(8,128)(2,1)S(1)} collective-permute-done((bf16[4,4,1,16,1152]{4,3,1,0,2:T(8,128)(2,1)S(1)}, bf16[4,4,1,16,1152]{4,3,1,0,2:T(8,128)(2,1)S(1)}, u32[]{:S(2)}, u32[]{:S(2)}) %collective-permute-start.69) | collective-permute-done | bytes 589856 | tf_op jit(solution)/shard_map/ppermute | solution.py:29
  802.2 7.8 add_convert_fusion.2
  816.5 4.7 add_convert_fusion.12
  832.5 45.6 %shard_map.160 = (bf16[1024,1152]{1,0:T(8,128)(2,1)}, bf16[1024,4608]{1,0:T(8,128)(2,1)}, f32[1024,1152]{1,0:T(8,128)}, bf16[1024,1152]{1,0:T(8,128)(2,1)}, f32[4,8,1152]{2,1,0:T(8,128)}) custom-call(bf16[1024,1152]{1,0:T(8,128)(2,1)} %bitcast.825, f32[4,8,1152]{2,1,0:T(8,128)} %concatenate.622.mod_ref, bf16[1024,1152]{1,0:T(8,128)(2,1)} %get-tuple-element.291.m_ref, ...), custom_call_target="tpu_custom_call" | custom-call | flops 21743271936 | bytes 42614784 | tf_op jit(solution)/shard_map/pallas_call | solution.py:667
  878.1 53.2 %collective-permute-done.75 = bf16[576,2304]{1,0:T(8,128)(2,1)} collective-permute-done((bf16[576,2304]{1,0:T(8,128)(2,1)}, bf16[576,2304]{1,0:T(8,128)(2,1)}, u32[]{:S(2)}, u32[]{:S(2)}) %collective-permute-start.75) | collective-permute-done | bytes 2654240 | tf_op jit(solution)/shard_map/ppermute | solution.py:29
  931.3 10.9 convolution_convert_fusion
  942.3 10.4 convolution_convert_fusion.1
  960.3 3.9 add_convert_fusion.6
  964.2 5.6 add_convert_fusion.11
  969.8 9.5 add_convert_fusion
  985.0 7.9 add_convert_fusion.1
  996.3 4.2 add_convert_fusion.4
  1000.6 5.2 convolution_convert_fusion.4
  1005.8 55.9 %shard_map.161 = (bf16[1024,1152]{1,0:T(8,128)(2,1)}, f32[4,8,1152]{2,1,0:T(8,128)}, bf16[1024,1728]{1,0:T(8,128)(2,1)}, bf16[1024,1728]{1,0:T(8,128)(2,1)}) custom-call(bf16[1024,1152]{1,0:T(8,128)(2,1)} %bitcast.820, f32[4,8,1152]{2,1,0:T(8,128)} %concatenate.622.mod_ref, bf16[1024,1152]{1,0:T(8,128)(2,1)} %get-tuple-element.306.da_ref, ...), custom_call_target="tpu_custom_call" | custom-call | flops 21743271936 | bytes 28590080 | tf_op jit(solution)/shard_map/pallas_call | solution.py:667
  1061.7 6.5 convolution_convert_fusion.6
  1068.6 3.9 convolution_convert_fusion.7
  1083.6 3.9 add_convert_fusion.5
  1088.5 19.8 %collective-permute-done.81 = bf16[4,72,2304]{2,1,0:T(8,128)(2,1)} collective-permute-done((bf16[4,72,2304]{2,1,0:T(8,128)(2,1)}, bf16[4,72,2304]{2,1,0:T(8,128)(2,1)}, u32[]{:S(2)}, u32[]{:S(2)}) %collective-permute-start.81) | collective-permute-done | bytes 1327136 | tf_op jit(solution)/shard_map/ppermute | solution.py:29
  1108.3 13.7 %collective-permute-done.80 = bf16[4,72,2304]{2,1,0:T(8,128)(2,1)} collective-permute-done((bf16[4,72,2304]{2,1,0:T(8,128)(2,1)}, bf16[4,72,2304]{2,1,0:T(8,128)(2,1)}, u32[]{:S(2)}, u32[]{:S(2)}) %collective-permute-start.80) | collective-permute-done | bytes 1327136 | tf_op jit(solution)/shard_map/ppermute | solution.py:29
  1122.0 5.5 add_convert_fusion.9
  1131.9 3.8 fusion.1
  1137.5 4.1 add_convert_fusion.10
  1160.5 4.4 collective-permute-done.97
  1164.9 7.9 collective-permute-done.98
  1175.5 14.4 %collective-permute-done.100 = f32[4,2,3456]{2,0,1:T(4,128)S(1)} collective-permute-done((f32[4,2,3456]{2,0,1:T(4,128)S(1)}, f32[4,2,3456]{2,0,1:T(4,128)S(1)}, u32[]{:S(2)}, u32[]{:S(2)}) %collective-permute-start.100) | collective-permute-done | bytes 110624 | tf_op jit(solution)/shard_map/ppermute | solution.py:29
  1210.3 23.6 %collective-permute-done.105 = f32[4,2,2,72]{3,0,1,2:T(4,128)S(1)} collective-permute-done((f32[4,2,2,72]{3,0,1,2:T(4,128)S(1)}, f32[4,2,2,72]{3,0,1,2:T(4,128)S(1)}, u32[]{:S(2)}, u32[]{:S(2)}) %collective-permute-start.105) | collective-permute-done | bytes 4640 | tf_op jit(solution)/shard_map/ppermute | solution.py:29
  1249.6 7.3 collective-permute-done.89
  1256.9 5.6 collective-permute-done.91
  1264.6 8.7 collective-permute-start.92
  1278.7 6.4 collective-permute-done.95
  1286.6 12.9 collective-permute-done.93
  (855 shorter events, 366.5 us)
Async XLA Ops:
  7.2 132.5 %all-gather.9.cloned.1.call-start = ((), (), s32[]{:S(2)}) async-start(), calls=%async_computation.8 | async-start | bytes 2985984 | tf_op jit(solution)/shard_map/all_gather | solution.py:949
  11.1 36.7 %collective-permute-start = (bf16[72,2304]{1,0:T(8,128)(2,1)}, bf16[72,2304]{1,0:T(8,128)(2,1)}, u32[]{:S(2)}, u32[]{:S(2)}) collective-permute-start(bf16[72,2304]{1,0:T(8,128)(2,1)} %concatenate.602), channel_id=1, source_target_pairs={{0,4},{2,6},{4,0},{6,2},{8,12},{10,14},{12,8},{14,10},{1,5},{3,7},... | collective-permute-start | bytes 995336 | tf_op jit(solution)/shard_map/ppermute | solution.py:29
  14.1 33.7 %collective-permute-start.1 = (bf16[72,2304]{1,0:T(8,128)(2,1)}, bf16[72,2304]{1,0:T(8,128)(2,1)}, u32[]{:S(2)}, u32[]{:S(2)}) collective-permute-start(bf16[72,2304]{1,0:T(8,128)(2,1)} %concatenate.602), channel_id=1, source_target_pairs={{0,8},{2,10},{4,12},{6,14},{8,0},{10,2},{12,4},{14,6},{1,9},{3,11}... | collective-permute-start | bytes 995336 | tf_op jit(solution)/shard_map/ppermute | solution.py:29
  16.7 31.1 %collective-permute-start.2 = (bf16[72,2304]{1,0:T(8,128)(2,1)}, bf16[72,2304]{1,0:T(8,128)(2,1)}, u32[]{:S(2)}, u32[]{:S(2)}) collective-permute-start(bf16[72,2304]{1,0:T(8,128)(2,1)} %concatenate.602), channel_id=1, source_target_pairs={{0,12},{2,14},{4,8},{6,10},{8,4},{10,6},{12,0},{14,2},{1,13},{3,15... | collective-permute-start | bytes 995336 | tf_op jit(solution)/shard_map/ppermute | solution.py:29
  41.6 210.6 %all-gather.5.cloned.1.call-start = ((), (), s32[]{:S(2)}) async-start(), calls=%async_computation.3 | async-start | bytes 2985984 | tf_op jit(solution)/shard_map/all_gather | solution.py:949
  78.6 260.0 %all-gather.7.cloned.1.call-start = ((), (), s32[]{:S(2)}) async-start(), calls=%async_computation.4 | async-start | bytes 2985984 | tf_op jit(solution)/shard_map/all_gather | solution.py:949
  93.4 33.2 %collective-permute-start.12 = (bf16[72,2304]{1,0:T(8,128)(2,1)}, bf16[72,2304]{1,0:T(8,128)(2,1)S(1)}, u32[]{:S(2)}, u32[]{:S(2)}) collective-permute-start(bf16[72,2304]{1,0:T(8,128)(2,1)} %get-tuple-element.188), channel_id=1, source_target_pairs={{0,8},{2,10},{4,12},{6,14},{8,0},{10,2},{12,4},{14,6},{1,9},{3,11}... | collective-permute-start | bytes 995336 | tf_op jit(solution)/shard_map/ppermute | solution.py:29
  97.6 29.2 %collective-permute-start.13 = (bf16[72,2304]{1,0:T(8,128)(2,1)}, bf16[72,2304]{1,0:T(8,128)(2,1)S(1)}, u32[]{:S(2)}, u32[]{:S(2)}) collective-permute-start(bf16[72,2304]{1,0:T(8,128)(2,1)} %get-tuple-element.188), channel_id=1, source_target_pairs={{0,12},{2,14},{4,8},{6,10},{8,4},{10,6},{12,0},{14,2},{1,13},{3,15... | collective-permute-start | bytes 995336 | tf_op jit(solution)/shard_map/ppermute | solution.py:29
  100.9 37.7 %collective-permute-start.15 = (bf16[2,4,72,1152]{3,2,1,0:T(8,128)(2,1)S(1)}, bf16[2,4,72,1152]{3,2,1,0:T(8,128)(2,1)S(1)}, u32[]{:S(2)}, u32[]{:S(2)}) collective-permute-start(bf16[2,4,72,1152]{3,2,1,0:T(8,128)(2,1)S(1)} %pad_maximum_fusion.27), channel_id=1, source_target_pairs={{0,2},{2,0},{4,6},{6,4},{8,10},{10,8},{12,14},{14,12},{1,3},{3,1},... | collective-permute-start | bytes 3981320 | tf_op jit(solution)/shard_map/ppermute | solution.py:29
  103.8 35.9 %collective-permute-start.14 = (bf16[576,1152]{1,0:T(8,128)(2,1)}, bf16[576,1152]{1,0:T(8,128)(2,1)}, u32[]{:S(2)}, u32[]{:S(2)}) collective-permute-start(bf16[576,1152]{1,0:T(8,128)(2,1)} %bitcast.61.refs_0_), channel_id=1, source_target_pairs={{0,1},{1,0},{2,3},{3,2},{4,5},{5,4},{6,7},{7,6},{8,9},{9,8},{10,11... | collective-permute-start | bytes 3981320 | tf_op jit(solution)/shard_map/ppermute | solution.py:29
  139.7 71.9 %collective-permute-start.24 = (bf16[576,2304]{1,0:T(8,128)(2,1)}, bf16[576,2304]{1,0:T(8,128)(2,1)}, u32[]{:S(2)}, u32[]{:S(2)}) collective-permute-start(bf16[576,2304]{1,0:T(8,128)(2,1)} %bitcast.857), channel_id=1, source_target_pairs={{0,1},{1,0},{2,3},{3,2},{4,5},{5,4},{6,7},{7,6},{8,9},{9,8},{10,11... | collective-permute-start | bytes 7962632 | tf_op jit(solution)/shard_map/ppermute | solution.py:29
  141.4 79.7 %collective-permute-start.25 = (bf16[576,2304]{1,0:T(8,128)(2,1)}, bf16[576,2304]{1,0:T(8,128)(2,1)}, u32[]{:S(2)}, u32[]{:S(2)}) collective-permute-start(bf16[576,2304]{1,0:T(8,128)(2,1)} %bitcast.858), channel_id=1, source_target_pairs={{0,16},{16,0},{1,17},{17,1},{2,18},{18,2},{3,19},{19,3},{4,20},{20... | collective-permute-start | bytes 7962632 | tf_op jit(solution)/shard_map/ppermute | solution.py:29
  154.7 56.9 %collective-permute-start.23 = (bf16[4,72,1152]{2,1,0:T(8,128)(2,1)}, bf16[4,72,1152]{2,1,0:T(8,128)(2,1)S(1)}, u32[]{:S(2)}, u32[]{:S(2)}) collective-permute-start(bf16[4,72,1152]{2,1,0:T(8,128)(2,1)} %fusion.55), channel_id=1, source_target_pairs={{0,1},{1,0},{2,3},{3,2},{4,5},{5,4},{6,7},{7,6},{8,9},{9,8},{10,11... | collective-permute-start | bytes 1990664 | tf_op jit(solution)/shard_map/ppermute | solution.py:29
  156.0 55.6 %collective-permute-start.22 = (bf16[4,72,1152]{2,1,0:T(8,128)(2,1)S(1)}, bf16[4,72,1152]{2,1,0:T(8,128)(2,1)S(1)}, u32[]{:S(2)}, u32[]{:S(2)}) collective-permute-start(bf16[4,72,1152]{2,1,0:T(8,128)(2,1)S(1)} %fusion.56), channel_id=1, source_target_pairs={{0,2},{2,0},{4,6},{6,4},{8,10},{10,8},{12,14},{14,12},{1,3},{3,1},... | collective-permute-start | bytes 1990664 | tf_op jit(solution)/shard_map/ppermute | solution.py:29
  215.0 37.9 %collective-permute-start.28 = (bf16[2,4,72,1152]{3,2,1,0:T(8,128)(2,1)S(1)}, bf16[2,4,72,1152]{3,2,1,0:T(8,128)(2,1)}, u32[]{:S(2)}, u32[]{:S(2)}) collective-permute-start(bf16[2,4,72,1152]{3,2,1,0:T(8,128)(2,1)S(1)} %pad_maximum_fusion.29), channel_id=1, source_target_pairs={{0,2},{2,0},{4,6},{6,4},{8,10},{10,8},{12,14},{14,12},{1,3},{3,1},... | collective-permute-start | bytes 3981320 | tf_op jit(solution)/shard_map/ppermute | solution.py:29
  218.3 34.6 %collective-permute-start.27 = (bf16[576,1152]{1,0:T(8,128)(2,1)}, bf16[576,1152]{1,0:T(8,128)(2,1)}, u32[]{:S(2)}, u32[]{:S(2)}) collective-permute-start(bf16[576,1152]{1,0:T(8,128)(2,1)} %bitcast.100.refs_0_.refs_4_), channel_id=1, source_target_pairs={{0,1},{1,0},{2,3},{3,2},{4,5},{5,4},{6,7},{7,6},{8,9},{9,8},{10,11... | collective-permute-start | bytes 3981320 | tf_op jit(solution)/shard_map/ppermute | solution.py:29
  219.9 32.2 %collective-permute-start.29 = (bf16[72,2304]{1,0:T(8,128)(2,1)S(1)}, bf16[72,2304]{1,0:T(8,128)(2,1)}, u32[]{:S(2)}, u32[]{:S(2)}) collective-permute-start(bf16[72,2304]{1,0:T(8,128)(2,1)S(1)} %copy-done.87), channel_id=1, source_target_pairs={{0,4},{2,6},{4,0},{6,2},{8,12},{10,14},{12,8},{14,10},{1,5},{3,7},... | collective-permute-start | bytes 995336 | tf_op jit(solution)/shard_map/ppermute | solution.py:29
  220.4 1058.3 %reduce-scatter.4.cloned.1.call-start = ((), (), s32[]{:S(2)}) async-start(), calls=%async_computation.5 | async-start | bytes 2985984 | tf_op jit(solution)/shard_map/reduce_scatter | solution.py:141
  221.2 31.8 %collective-permute-start.30 = (bf16[72,2304]{1,0:T(8,128)(2,1)S(1)}, bf16[72,2304]{1,0:T(8,128)(2,1)}, u32[]{:S(2)}, u32[]{:S(2)}) collective-permute-start(bf16[72,2304]{1,0:T(8,128)(2,1)S(1)} %copy-done.87), channel_id=1, source_target_pairs={{0,8},{2,10},{4,12},{6,14},{8,0},{10,2},{12,4},{14,6},{1,9},{3,11}... | collective-permute-start | bytes 995336 | tf_op jit(solution)/shard_map/ppermute | solution.py:29
  224.4 28.6 %collective-permute-start.31 = (bf16[72,2304]{1,0:T(8,128)(2,1)S(1)}, bf16[72,2304]{1,0:T(8,128)(2,1)}, u32[]{:S(2)}, u32[]{:S(2)}) collective-permute-start(bf16[72,2304]{1,0:T(8,128)(2,1)S(1)} %copy-done.87), channel_id=1, source_target_pairs={{0,12},{2,14},{4,8},{6,10},{8,4},{10,6},{12,0},{14,2},{1,13},{3,15... | collective-permute-start | bytes 995336 | tf_op jit(solution)/shard_map/ppermute | solution.py:29
  262.7 73.6 %collective-permute-start.39 = (bf16[4,72,1152]{2,1,0:T(8,128)(2,1)}, bf16[4,72,1152]{2,1,0:T(8,128)(2,1)}, u32[]{:S(2)}, u32[]{:S(2)}) collective-permute-start(bf16[4,72,1152]{2,1,0:T(8,128)(2,1)} %fusion.53), channel_id=1, source_target_pairs={{0,1},{1,0},{2,3},{3,2},{4,5},{5,4},{6,7},{7,6},{8,9},{9,8},{10,11... | collective-permute-start | bytes 1990664 | tf_op jit(solution)/shard_map/ppermute | solution.py:29
  294.0 43.7 %collective-permute-start.38 = (bf16[4,72,1152]{2,1,0:T(8,128)(2,1)S(1)}, bf16[4,72,1152]{2,1,0:T(8,128)(2,1)S(1)}, u32[]{:S(2)}, u32[]{:S(2)}) collective-permute-start(bf16[4,72,1152]{2,1,0:T(8,128)(2,1)S(1)} %fusion.54), channel_id=1, source_target_pairs={{0,2},{2,0},{4,6},{6,4},{8,10},{10,8},{12,14},{14,12},{1,3},{3,1},... | collective-permute-start | bytes 1990664 | tf_op jit(solution)/shard_map/ppermute | solution.py:29
  304.6 70.6 %collective-permute-start.40 = (bf16[576,2304]{1,0:T(8,128)(2,1)}, bf16[576,2304]{1,0:T(8,128)(2,1)}, u32[]{:S(2)}, u32[]{:S(2)}) collective-permute-start(bf16[576,2304]{1,0:T(8,128)(2,1)} %all-gather.5.cloned.1.call-done.refs_0_), channel_id=1, source_target_pairs={{0,1},{1,0},{2,3},{3,2},{4,5},{5,4},{6,7},{7,6},{8,9},{9,8},{10,11... | collective-permute-start | bytes 7962632 | tf_op jit(solution)/shard_map/ppermute | solution.py:29
  321.8 53.4 %collective-permute-start.43 = (bf16[4,4,1,16,1152]{4,3,1,0,2:T(8,128)(2,1)}, bf16[4,4,1,16,1152]{4,3,1,0,2:T(8,128)(2,1)}, u32[]{:S(2)}, u32[]{:S(2)}) collective-permute-start(bf16[4,4,1,16,1152]{4,3,1,0,2:T(8,128)(2,1)} %pad_maximum_fusion.54), channel_id=1, source_target_pairs={{0,12},{2,14},{4,8},{6,10},{8,4},{10,6},{12,0},{14,2},{1,13},{3,15... | collective-permute-start | bytes 1769480 | tf_op jit(solution)/shard_map/ppermute | solution.py:29
  326.5 48.7 %collective-permute-start.42 = (bf16[4,4,1,16,1152]{4,3,1,0,2:T(8,128)(2,1)}, bf16[4,4,1,16,1152]{4,3,1,0,2:T(8,128)(2,1)}, u32[]{:S(2)}, u32[]{:S(2)}) collective-permute-start(bf16[4,4,1,16,1152]{4,3,1,0,2:T(8,128)(2,1)} %pad_maximum_fusion.53), channel_id=1, source_target_pairs={{0,8},{2,10},{4,12},{6,14},{8,0},{10,2},{12,4},{14,6},{1,9},{3,11}... | collective-permute-start | bytes 1769480 | tf_op jit(solution)/shard_map/ppermute | solution.py:29
  336.4 38.8 %collective-permute-start.41 = (bf16[4,4,1,16,1152]{4,3,1,0,2:T(8,128)(2,1)}, bf16[4,4,1,16,1152]{4,3,1,0,2:T(8,128)(2,1)}, u32[]{:S(2)}, u32[]{:S(2)}) collective-permute-start(bf16[4,4,1,16,1152]{4,3,1,0,2:T(8,128)(2,1)} %pad_maximum_fusion.52), channel_id=1, source_target_pairs={{0,4},{2,6},{4,0},{6,2},{8,12},{10,14},{12,8},{14,10},{1,5},{3,7},... | collective-permute-start | bytes 1769480 | tf_op jit(solution)/shard_map/ppermute | solution.py:29
  338.6 56.5 %collective-permute-start.44 = (bf16[576,2304]{1,0:T(8,128)(2,1)}, bf16[576,2304]{1,0:T(8,128)(2,1)}, u32[]{:S(2)}, u32[]{:S(2)}) collective-permute-start(bf16[576,2304]{1,0:T(8,128)(2,1)} %all-gather.5.cloned.1.call-done.refs_0_), channel_id=1, source_target_pairs={{0,16},{16,0},{1,17},{17,1},{2,18},{18,2},{3,19},{19,3},{4,20},{20... | collective-permute-start | bytes 7962632 | tf_op jit(solution)/shard_map/ppermute | solution.py:29
  385.0 49.9 %collective-permute-start.48 = (bf16[4,4,2,1,16,1152]{5,4,1,2,0,3:T(8,128)(2,1)}, bf16[4,4,2,1,16,1152]{5,4,1,2,0,3:T(8,128)(2,1)}, u32[]{:S(2)}, u32[]{:S(2)}) collective-permute-start(bf16[4,4,2,1,16,1152]{5,4,1,2,0,3:T(8,128)(2,1)} %get-tuple-element.439), channel_id=1, source_target_pairs={{0,2},{1,3},{2,0},{3,1},{4,6},{5,7},{6,4},{7,5},{8,10},{9,11},{10,... | collective-permute-start | bytes 3538952 | tf_op jit(solution)/shard_map/ppermute | solution.py:896
  389.1 53.1 %collective-permute-start.47 = (bf16[2,4,72,1152]{3,2,1,0:T(8,128)(2,1)}, bf16[2,4,72,1152]{3,2,1,0:T(8,128)(2,1)}, u32[]{:S(2)}, u32[]{:S(2)}) collective-permute-start(bf16[2,4,72,1152]{3,2,1,0:T(8,128)(2,1)} %pad_maximum_fusion.31), channel_id=1, source_target_pairs={{0,2},{2,0},{4,6},{6,4},{8,10},{10,8},{12,14},{14,12},{1,3},{3,1},... | collective-permute-start | bytes 3981320 | tf_op jit(solution)/shard_map/ppermute | solution.py:29
  390.9 51.2 %collective-permute-start.46 = (bf16[576,1152]{1,0:T(8,128)(2,1)}, bf16[576,1152]{1,0:T(8,128)(2,1)}, u32[]{:S(2)}, u32[]{:S(2)}) collective-permute-start(bf16[576,1152]{1,0:T(8,128)(2,1)} %bitcast.147.refs_0_), channel_id=1, source_target_pairs={{0,1},{1,0},{2,3},{3,2},{4,5},{5,4},{6,7},{7,6},{8,9},{9,8},{10,11... | collective-permute-start | bytes 3981320 | tf_op jit(solution)/shard_map/ppermute | solution.py:29
  445.9 60.3 %collective-permute-start.52 = (bf16[576,2304]{1,0:T(8,128)(2,1)}, bf16[576,2304]{1,0:T(8,128)(2,1)}, u32[]{:S(2)}, u32[]{:S(2)}) collective-permute-start(bf16[576,2304]{1,0:T(8,128)(2,1)} %all-gather.7.cloned.1.call-done.refs_0_.refs_6_), channel_id=1, source_target_pairs={{0,1},{1,0},{2,3},{3,2},{4,5},{5,4},{6,7},{7,6},{8,9},{9,8},{10,11... | collective-permute-start | bytes 7962632 | tf_op jit(solution)/shard_map/ppermute | solution.py:29
  447.4 74.2 %collective-permute-start.53 = (bf16[576,2304]{1,0:T(8,128)(2,1)}, bf16[576,2304]{1,0:T(8,128)(2,1)}, u32[]{:S(2)}, u32[]{:S(2)}) collective-permute-start(bf16[576,2304]{1,0:T(8,128)(2,1)} %all-gather.7.cloned.1.call-done.refs_0_.refs_6_), channel_id=1, source_target_pairs={{0,16},{16,0},{1,17},{17,1},{2,18},{18,2},{3,19},{19,3},{4,20},{20... | collective-permute-start | bytes 7962632 | tf_op jit(solution)/shard_map/ppermute | solution.py:29
  507.7 35.9 %collective-permute-start.57 = (bf16[4,2,2,1,16,1152]{5,4,1,2,0,3:T(8,128)(2,1)S(1)}, bf16[4,2,2,1,16,1152]{5,4,1,2,0,3:T(8,128)(2,1)S(1)}, u32[]{:S(2)}, u32[]{:S(2)}) collective-permute-start(bf16[4,2,2,1,16,1152]{5,4,1,2,0,3:T(8,128)(2,1)S(1)} %pad_maximum_fusion.57), channel_id=1, source_target_pairs={{0,12},{2,14},{4,8},{6,10},{8,4},{10,6},{12,0},{14,2},{1,13},{3,15... | collective-permute-start | bytes 1769480 | tf_op jit(solution)/shard_map/ppermute | solution.py:29
  511.8 51.9 %collective-permute-start.56 = (bf16[4,2,2,1,16,1152]{5,4,1,2,0,3:T(8,128)(2,1)S(1)}, bf16[4,2,2,1,16,1152]{5,4,1,2,0,3:T(8,128)(2,1)S(1)}, u32[]{:S(2)}, u32[]{:S(2)}) collective-permute-start(bf16[4,2,2,1,16,1152]{5,4,1,2,0,3:T(8,128)(2,1)S(1)} %pad_maximum_fusion.56), channel_id=1, source_target_pairs={{0,8},{2,10},{4,12},{6,14},{8,0},{10,2},{12,4},{14,6},{1,9},{3,11}... | collective-permute-start | bytes 1769480 | tf_op jit(solution)/shard_map/ppermute | solution.py:29
  521.4 42.3 %collective-permute-start.55 = (bf16[4,2,2,1,16,1152]{5,4,1,2,0,3:T(8,128)(2,1)}, bf16[4,2,2,1,16,1152]{5,4,1,2,0,3:T(8,128)(2,1)S(1)}, u32[]{:S(2)}, u32[]{:S(2)}) collective-permute-start(bf16[4,2,2,1,16,1152]{5,4,1,2,0,3:T(8,128)(2,1)} %pad_maximum_fusion.55), channel_id=1, source_target_pairs={{0,4},{2,6},{4,0},{6,2},{8,12},{10,14},{12,8},{14,10},{1,5},{3,7},... | collective-permute-start | bytes 1769480 | tf_op jit(solution)/shard_map/ppermute | solution.py:29
  569.1 48.6 %collective-permute-start.58 = (bf16[4,4,2,1,16,1152]{5,4,2,1,0,3:T(8,128)(2,1)}, bf16[4,4,2,1,16,1152]{5,4,2,1,0,3:T(8,128)(2,1)S(1)}, u32[]{:S(2)}, u32[]{:S(2)}) collective-permute-start(bf16[4,4,2,1,16,1152]{5,4,2,1,0,3:T(8,128)(2,1)} %get-tuple-element.435), channel_id=1, source_target_pairs={{0,2},{1,3},{2,0},{3,1},{4,6},{5,7},{6,4},{7,5},{8,10},{9,11},{10,... | collective-permute-start | bytes 3538952 | tf_op jit(solution)/shard_map/ppermute | solution.py:896
  629.8 72.7 %collective-permute-start.62 = (bf16[4,2,2,1,16,1152]{5,4,2,1,0,3:T(8,128)(2,1)}, bf16[4,2,2,1,16,1152]{5,4,2,1,0,3:T(8,128)(2,1)S(1)}, u32[]{:S(2)}, u32[]{:S(2)}) collective-permute-start(bf16[4,2,2,1,16,1152]{5,4,2,1,0,3:T(8,128)(2,1)} %pad_maximum_fusion.60), channel_id=1, source_target_pairs={{0,12},{2,14},{4,8},{6,10},{8,4},{10,6},{12,0},{14,2},{1,13},{3,15... | collective-permute-start | bytes 1769480 | tf_op jit(solution)/shard_map/ppermute | solution.py:29
  633.1 69.3 %collective-permute-start.61 = (bf16[4,2,2,1,16,1152]{5,4,2,1,0,3:T(8,128)(2,1)}, bf16[4,2,2,1,16,1152]{5,4,2,1,0,3:T(8,128)(2,1)S(1)}, u32[]{:S(2)}, u32[]{:S(2)}) collective-permute-start(bf16[4,2,2,1,16,1152]{5,4,2,1,0,3:T(8,128)(2,1)} %pad_maximum_fusion.59), channel_id=1, source_target_pairs={{0,8},{2,10},{4,12},{6,14},{8,0},{10,2},{12,4},{14,6},{1,9},{3,11}... | collective-permute-start | bytes 1769480 | tf_op jit(solution)/shard_map/ppermute | solution.py:29
  634.0 68.4 %collective-permute-start.60 = (bf16[4,2,2,1,16,1152]{5,4,2,1,0,3:T(8,128)(2,1)}, bf16[4,2,2,1,16,1152]{5,4,2,1,0,3:T(8,128)(2,1)}, u32[]{:S(2)}, u32[]{:S(2)}) collective-permute-start(bf16[4,2,2,1,16,1152]{5,4,2,1,0,3:T(8,128)(2,1)} %pad_maximum_fusion.58), channel_id=1, source_target_pairs={{0,4},{2,6},{4,0},{6,2},{8,12},{10,14},{12,8},{14,10},{1,5},{3,7},... | collective-permute-start | bytes 1769480 | tf_op jit(solution)/shard_map/ppermute | solution.py:29
  646.2 95.8 %collective-permute-start.66 = (bf16[576,4608]{1,0:T(8,128)(2,1)}, bf16[576,4608]{1,0:T(8,128)(2,1)}, u32[]{:S(2)}, u32[]{:S(2)}) collective-permute-start(bf16[576,4608]{1,0:T(8,128)(2,1)} %convolution_convert_fusion.2), channel_id=1, source_target_pairs={{0,16},{16,0},{1,17},{17,1},{2,18},{18,2},{3,19},{19,3},{4,20},{20... | collective-permute-start | bytes 15925256 | tf_op jit(solution)/shard_map/ppermute | solution.py:29
  708.6 107.9 %collective-permute-start.72 = (bf16[576,1728]{1,0:T(8,128)(2,1)}, bf16[576,1728]{1,0:T(8,128)(2,1)}, u32[]{:S(2)}, u32[]{:S(2)}) collective-permute-start(bf16[576,1728]{1,0:T(8,128)(2,1)} %convolution_convert_fusion.8), channel_id=1, source_target_pairs={{0,16},{16,0},{1,17},{17,1},{2,18},{18,2},{3,19},{19,3},{4,20},{20... | collective-permute-start | bytes 5971976 | tf_op jit(solution)/shard_map/ppermute | solution.py:29
  710.4 31.6 %collective-permute-start.63 = (bf16[4,4,1,16,1152]{4,3,1,0,2:T(8,128)(2,1)}, bf16[4,4,1,16,1152]{4,3,1,0,2:T(8,128)(2,1)}, u32[]{:S(2)}, u32[]{:S(2)}) collective-permute-start(bf16[4,4,1,16,1152]{4,3,1,0,2:T(8,128)(2,1)} %get-tuple-element.422), channel_id=1, source_target_pairs={{0,1},{1,0},{2,3},{3,2},{4,5},{5,4},{6,7},{7,6},{8,9},{9,8},{10,11... | collective-permute-start | bytes 1769480 | tf_op jit(solution)/shard_map/ppermute | solution.py:896
  711.4 31.7 %collective-permute-start.64 = (bf16[4,4,1,16,1152]{4,3,1,0,2:T(8,128)(2,1)}, bf16[4,4,1,16,1152]{4,3,1,0,2:T(8,128)(2,1)}, u32[]{:S(2)}, u32[]{:S(2)}) collective-permute-start(bf16[4,4,1,16,1152]{4,3,1,0,2:T(8,128)(2,1)} %get-tuple-element.421), channel_id=1, source_target_pairs={{0,2},{1,3},{2,0},{3,1},{4,6},{5,7},{6,4},{7,5},{8,10},{9,11},{10,... | collective-permute-start | bytes 1769480 | tf_op jit(solution)/shard_map/ppermute | solution.py:896
  712.5 30.6 %collective-permute-start.65 = (bf16[4,4,1,16,1152]{4,3,1,0,2:T(8,128)(2,1)S(1)}, bf16[4,4,1,16,1152]{4,3,1,0,2:T(8,128)(2,1)}, u32[]{:S(2)}, u32[]{:S(2)}) collective-permute-start(bf16[4,4,1,16,1152]{4,3,1,0,2:T(8,128)(2,1)S(1)} %get-tuple-element.423), channel_id=1, source_target_pairs={{0,3},{1,2},{2,1},{3,0},{4,7},{5,6},{6,5},{7,4},{8,11},{9,10},{10,... | collective-permute-start | bytes 1769480 | tf_op jit(solution)/shard_map/ppermute | solution.py:896
  742.0 74.5 %collective-permute-start.71 = (bf16[576,1728]{1,0:T(8,128)(2,1)}, bf16[576,1728]{1,0:T(8,128)(2,1)S(1)}, u32[]{:S(2)}, u32[]{:S(2)}) collective-permute-start(bf16[576,1728]{1,0:T(8,128)(2,1)} %convolution_convert_fusion.9), channel_id=1, source_target_pairs={{0,16},{16,0},{1,17},{17,1},{2,18},{18,2},{3,19},{19,3},{4,20},{20... | collective-permute-start | bytes 5971976 | tf_op jit(solution)/shard_map/ppermute | solution.py:29
  742.0 74.5 %collective-permute-start.67 = (bf16[576,2304]{1,0:T(8,128)(2,1)}, bf16[576,2304]{1,0:T(8,128)(2,1)}, u32[]{:S(2)}, u32[]{:S(2)}) collective-permute-start(bf16[576,2304]{1,0:T(8,128)(2,1)} %split.64), channel_id=1, source_target_pairs={{0,1},{1,0},{2,3},{3,2},{4,5},{5,4},{6,7},{7,6},{8,9},{9,8},{10,11... | collective-permute-start | bytes 7962632 | tf_op jit(solution)/shard_map/ppermute | solution.py:29
  751.1 50.3 %collective-permute-start.69 = (bf16[4,4,1,16,1152]{4,3,1,0,2:T(8,128)(2,1)S(1)}, bf16[4,4,1,16,1152]{4,3,1,0,2:T(8,128)(2,1)S(1)}, u32[]{:S(2)}, u32[]{:S(2)}) collective-permute-start(bf16[4,4,1,16,1152]{4,3,1,0,2:T(8,128)(2,1)S(1)} %pad_maximum_fusion.62), channel_id=1, source_target_pairs={{0,8},{2,10},{4,12},{6,14},{8,0},{10,2},{12,4},{14,6},{1,9},{3,11}... | collective-permute-start | bytes 1769480 | tf_op jit(solution)/shard_map/ppermute | solution.py:29
  766.3 50.1 %collective-permute-start.73 = (bf16[576,1152]{1,0:T(8,128)(2,1)}, bf16[576,1152]{1,0:T(8,128)(2,1)}, u32[]{:S(2)}, u32[]{:S(2)}) collective-permute-start(bf16[576,1152]{1,0:T(8,128)(2,1)} %convolution_convert_fusion.5), channel_id=1, source_target_pairs={{0,16},{16,0},{1,17},{17,1},{2,18},{18,2},{3,19},{19,3},{4,20},{20... | collective-permute-start | bytes 3981320 | tf_op jit(solution)/shard_map/ppermute | solution.py:29
  816.3 61.8 %collective-permute-start.74 = (bf16[576,2304]{1,0:T(8,128)(2,1)}, bf16[576,2304]{1,0:T(8,128)(2,1)}, u32[]{:S(2)}, u32[]{:S(2)}) collective-permute-start(bf16[576,2304]{1,0:T(8,128)(2,1)} %split.65), channel_id=1, source_target_pairs={{0,1},{1,0},{2,3},{3,2},{4,5},{5,4},{6,7},{7,6},{8,9},{9,8},{10,11... | collective-permute-start | bytes 7962632 | tf_op jit(solution)/shard_map/ppermute | solution.py:29
  827.5 103.8 %collective-permute-start.75 = (bf16[576,2304]{1,0:T(8,128)(2,1)}, bf16[576,2304]{1,0:T(8,128)(2,1)}, u32[]{:S(2)}, u32[]{:S(2)}) collective-permute-start(bf16[576,2304]{1,0:T(8,128)(2,1)} %pad_maximum_fusion.3), channel_id=1, source_target_pairs={{0,1},{1,0},{2,3},{3,2},{4,5},{5,4},{6,7},{7,6},{8,9},{9,8},{10,11... | collective-permute-start | bytes 7962632 | tf_op jit(solution)/shard_map/ppermute | solution.py:29
  964.1 314.5 %reduce-scatter.8.cloned.1.call-start = ((), (), s32[]{:S(2)}) async-start(), calls=%async_computation.7 | async-start | bytes 2985984 | tf_op jit(solution)/shard_map/reduce_scatter | solution.py:141
  981.8 79.9 %collective-permute-start.79 = (bf16[4,72,4608]{2,1,0:T(8,128)(2,1)}, bf16[4,72,4608]{2,1,0:T(8,128)(2,1)}, u32[]{:S(2)}, u32[]{:S(2)}) collective-permute-start(bf16[4,72,4608]{2,1,0:T(8,128)(2,1)} %pad_maximum_fusion.4), channel_id=1, source_target_pairs={{0,2},{2,0},{4,6},{6,4},{8,10},{10,8},{12,14},{14,12},{1,3},{3,1},... | collective-permute-start | bytes 7962632 | tf_op jit(solution)/shard_map/ppermute | solution.py:29
  996.0 65.7 %collective-permute-start.78 = (bf16[576,2304]{1,0:T(8,128)(2,1)}, bf16[576,2304]{1,0:T(8,128)(2,1)}, u32[]{:S(2)}, u32[]{:S(2)}) collective-permute-start(bf16[576,2304]{1,0:T(8,128)(2,1)} %split.67), channel_id=1, source_target_pairs={{0,1},{1,0},{2,3},{3,2},{4,5},{5,4},{6,7},{7,6},{8,9},{9,8},{10,11... | collective-permute-start | bytes 7962632 | tf_op jit(solution)/shard_map/ppermute | solution.py:29
  1000.6 278.1 %reduce-scatter.6.cloned.1.call-start = ((), (), s32[]{:S(2)}) async-start(), calls=%async_computation.6 | async-start | bytes 2985984 | tf_op jit(solution)/shard_map/reduce_scatter | solution.py:141
  1005.8 82.7 %collective-permute-start.84 = (bf16[576,1152]{1,0:T(8,128)(2,1)}, bf16[576,1152]{1,0:T(8,128)(2,1)}, u32[]{:S(2)}, u32[]{:S(2)}) collective-permute-start(bf16[576,1152]{1,0:T(8,128)(2,1)} %convolution_convert_fusion.4), channel_id=1, source_target_pairs={{0,16},{16,0},{1,17},{17,1},{2,18},{18,2},{3,19},{19,3},{4,20},{20... | collective-permute-start | bytes 3981320 | tf_op jit(solution)/shard_map/ppermute | solution.py:29
  1068.2 53.8 %collective-permute-start.83 = (bf16[576,1728]{1,0:T(8,128)(2,1)}, bf16[576,1728]{1,0:T(8,128)(2,1)}, u32[]{:S(2)}, u32[]{:S(2)}) collective-permute-start(bf16[576,1728]{1,0:T(8,128)(2,1)} %convolution_convert_fusion.6), channel_id=1, source_target_pairs={{0,16},{16,0},{1,17},{17,1},{2,18},{18,2},{3,19},{19,3},{4,20},{20... | collective-permute-start | bytes 5971976 | tf_op jit(solution)/shard_map/ppermute | solution.py:29
  1072.5 49.4 %collective-permute-start.82 = (bf16[576,1728]{1,0:T(8,128)(2,1)}, bf16[576,1728]{1,0:T(8,128)(2,1)}, u32[]{:S(2)}, u32[]{:S(2)}) collective-permute-start(bf16[576,1728]{1,0:T(8,128)(2,1)} %convolution_convert_fusion.7), channel_id=1, source_target_pairs={{0,16},{16,0},{1,17},{17,1},{2,18},{18,2},{3,19},{19,3},{4,20},{20... | collective-permute-start | bytes 5971976 | tf_op jit(solution)/shard_map/ppermute | solution.py:29
  1076.4 31.8 %collective-permute-start.81 = (bf16[4,72,2304]{2,1,0:T(8,128)(2,1)}, bf16[4,72,2304]{2,1,0:T(8,128)(2,1)}, u32[]{:S(2)}, u32[]{:S(2)}) collective-permute-start(bf16[4,72,2304]{2,1,0:T(8,128)(2,1)} %split.71), channel_id=1, source_target_pairs={{0,1},{1,0},{2,3},{3,2},{4,5},{5,4},{6,7},{7,6},{8,9},{9,8},{10,11... | collective-permute-start | bytes 3981320 | tf_op jit(solution)/shard_map/ppermute | solution.py:29
  1081.8 40.2 %collective-permute-start.80 = (bf16[4,72,2304]{2,1,0:T(8,128)(2,1)}, bf16[4,72,2304]{2,1,0:T(8,128)(2,1)}, u32[]{:S(2)}, u32[]{:S(2)}) collective-permute-start(bf16[4,72,2304]{2,1,0:T(8,128)(2,1)} %dynamic-slice_bitcast_fusion.2), channel_id=1, source_target_pairs={{0,2},{2,0},{4,6},{6,4},{8,10},{10,8},{12,14},{14,12},{1,3},{3,1},... | collective-permute-start | bytes 3981320 | tf_op jit(solution)/shard_map/ppermute | solution.py:29
  1147.4 94.9 %collective-permute-start.86 = (bf16[4,72,2304]{2,1,0:T(8,128)(2,1)}, bf16[4,72,2304]{2,1,0:T(8,128)(2,1)}, u32[]{:S(2)}, u32[]{:S(2)}) collective-permute-start(bf16[4,72,2304]{2,1,0:T(8,128)(2,1)} %concatenate.696), channel_id=1, source_target_pairs={{0,2},{2,0},{4,6},{6,4},{8,10},{10,8},{12,14},{14,12},{1,3},{3,1},... | collective-permute-start | bytes 3981320 | tf_op jit(solution)/shard_map/ppermute | solution.py:29
  1148.9 93.4 %collective-permute-start.85 = (bf16[576,1152]{1,0:T(8,128)(2,1)}, bf16[576,1152]{1,0:T(8,128)(2,1)}, u32[]{:S(2)}, u32[]{:S(2)}) collective-permute-start(bf16[576,1152]{1,0:T(8,128)(2,1)} %slice.1020), channel_id=1, source_target_pairs={{0,1},{1,0},{2,3},{3,2},{4,5},{5,4},{6,7},{7,6},{8,9},{9,8},{10,11... | collective-permute-start | bytes 3981320 | tf_op jit(solution)/shard_map/ppermute | solution.py:29
  1191.3 57.5 %collective-permute-start.87 = (bf16[72,4608]{1,0:T(8,128)(2,1)}, bf16[72,4608]{1,0:T(8,128)(2,1)}, u32[]{:S(2)}, u32[]{:S(2)}) collective-permute-start(bf16[72,4608]{1,0:T(8,128)(2,1)} %get-tuple-element.389), channel_id=1, source_target_pairs={{0,4},{2,6},{4,0},{6,2},{8,12},{10,14},{12,8},{14,10},{1,5},{3,7},... | collective-permute-start | bytes 1990664 | tf_op jit(solution)/shard_map/ppermute | solution.py:29
  1193.8 55.7 %collective-permute-start.88 = (bf16[72,4608]{1,0:T(8,128)(2,1)}, bf16[72,4608]{1,0:T(8,128)(2,1)}, u32[]{:S(2)}, u32[]{:S(2)}) collective-permute-start(bf16[72,4608]{1,0:T(8,128)(2,1)} %get-tuple-element.390), channel_id=1, source_target_pairs={{0,8},{2,10},{4,12},{6,14},{8,0},{10,2},{12,4},{14,6},{1,9},{3,11}... | collective-permute-start | bytes 1990664 | tf_op jit(solution)/shard_map/ppermute | solution.py:29
  1248.8 36.3 %collective-permute-start.95 = (bf16[4,1,128,1152]{3,2,0,1:T(8,128)(2,1)}, bf16[4,1,128,1152]{3,2,0,1:T(8,128)(2,1)S(1)}, u32[]{:S(2)}, u32[]{:S(2)}) collective-permute-start(bf16[4,1,128,1152]{3,2,0,1:T(8,128)(2,1)} %get-tuple-element.415), channel_id=1, source_target_pairs={{0,1},{1,0},{2,3},{3,2},{4,5},{5,4},{6,7},{7,6},{8,9},{9,8},{10,11... | collective-permute-start | bytes 3538952 | tf_op jit(solution)/shard_map/ppermute | solution.py:29
  (219 other events, 2062.2 us)
Sparse Core Ops, SparseCore 0:
  41.7 84.2 all-gather.8
  128.2 65.6 all-gather.4
  220.5 71.8 all-gather.6
  964.3 82.5 reduce-scatter.3
  1050.8 79.3 reduce-scatter.7
  1133.6 103.7 reduce-scatter.5

commit v7 on v6

--- a/solution.py
+++ b/solution.py
@@ -220,8 +220,8 @@
         self.tasks.append(task)
         return task
 
-    def fence(self, values=(), but=(), last=False):
-        due = [t for t in self.tasks if t not in but and (last or not t.resting)]
+    def fence(self, values=(), but=(), also=(), last=False):
+        due = [t for t in self.tasks if t not in but and (last or not t.resting or t in also)]
         values, pending = lax.optimization_barrier((values, [t.pending for t in due]))
         going = [t for t in self.tasks if t not in due]
         for task, done in zip(due, pending):
@@ -959,18 +959,18 @@
         ((2,), (), ()),
         ((), (2,), ()),
         ((1,), (), ()),
-        ((4,), (), (5,)),
+        ((), (), (4, 5)),
         ((3,), (), ()),
-        ((), (3, 4), ()),
-        ((5,), (), ()),
+        ((4,), (3,), ()),
+        ((5,), (4,), ()),
         ((), (5,), ()),
         ((), (), ()),
     ]
 
-    def tick(values=(), waiting=()):
+    def tick(values=()):
         out, but, far = plan.pop(0)
         held = {index: blocks.get(index, shards[index]) for index in out + far}
-        held, values = lanes.fence((held, values), [gathers[index] for index in but] + list(waiting))
+        held, values = lanes.fence((held, values), [gathers[index] for index in but])
         for index in out + far:
             if index in blocks:
                 blocks[index] = held[index]
@@ -1027,7 +1027,8 @@
     mod_grads = [None] * LAYERS
 
     def start_scatter(level, names, *groups):
-        steps = (moves.scatter_far if level else moves.scatter_weight)(groups)
+        far = level and len(groups) == 1
+        steps = (moves.scatter_far if far else moves.scatter_weight)(groups)
         scatters[level, names] = lanes.start(steps)
         return scatters[level, names]
 
@@ -1042,9 +1043,9 @@
     def mod_strip():
         parts = [moves.halves(v).reshape(clips, n_tp, -1) for v in mod_grads]
         parts = flip_to(jnp.stack(parts, axis=2), 1, n_tp, moves.tp)
+        parts = yield from total_over_ctx(parts)
         got = yield [swap_with(parts[:, r], "tp", n_tp, r) for r in range(1, n_tp)]
         strip = parts[:, 0] + sum(got)
-        strip = yield from total_over_ctx(strip)
         got = yield swap_with(strip, "ctx", n_ctx, 1)
         strip = strip + got
         got = yield swap_with(strip, "dp", n_dp, 1)
@@ -1061,10 +1062,12 @@
             stride = piece if level % 2 else 1
             joined = gathers[3 * level].result
             kept = fused_branch(v, vectors[level], joined, clips, stride)
-            normed, qkv, lse, result, branch, middle, normed_mlp = tick(kept)
+            kept, late = tick((kept, cotangent))
+            normed, qkv, lse, result, branch, middle, normed_mlp = kept
+            if level == 0:
+                turned = lanes.start(here_to_clips(moves.halves(late)))
             up = gathers[3 * level + 1].result
-            waiting = (turned,) if level else ()
-            act, slope = tick(fused_up(normed_mlp, vectors[level], up, clips), waiting)
+            act, slope = tick(fused_up(normed_mlp, vectors[level], up, clips))
             down = gathers[3 * level + 2].result
             branch_mlp, after = fused_down(act, middle, vectors[level], down, clips)
             saved.append((v, normed, qkv, lse, result, branch, middle, normed_mlp))
@@ -1073,10 +1076,8 @@
             if level == 0:
                 moved = lanes.start(frames_to_clips(shaped(v)))
                 tick()
-                late = tick(cotangent)
-                turned = lanes.start(here_to_clips(moves.halves(late)))
+                tick()
                 v = flat(moved.result)
-        v = lanes.fence(v)
         finished = lanes.start(clips_to_here(moves.halves(shaped(v))))
         grad = flat(turned.result)
         for level in reversed(range(LAYERS)):
@@ -1085,27 +1086,28 @@
             back = fused_mlp_back(
                 grad, vectors[level], branch_mlp, slope, middle, branch, up, down, clips
             )
-            grad_branch, grad_pre, grad_middle, grad_out, sums = lanes.fence(back)
+            late = () if level else (second, third)
+            grad_branch, grad_pre, grad_middle, grad_out, sums = lanes.fence(back, late)
             if level:
-                waiting = start_scatter(level, ("down",), (grad_branch, [act]))
+                first = start_scatter(level, ("down",), (grad_branch, [act]))
                 grad_out = lanes.fence(grad_out, (finished,))
             else:
                 start_scatter(
                     level, ("down", "up"), (grad_branch, [act]), (normed_mlp, [grad_pre])
                 )
-                grad_out = lanes.fence(grad_out, (scatters[1, ("qkv", "out")],))
+                grad_out = lanes.fence(grad_out)
             back = fused_branch_back(
                 v, vectors[level], grad_out, grad_middle, qkv, lse, joined, clips, stride
             )
-            grad, more, *grad_qkv = lanes.fence(back, (waiting,) if level else ())
+            grad, more, *grad_qkv = lanes.fence(back, (first,) if level else ())
             mod_grads[level] = (sums + more)[:, :6]
             joint = (normed, grad_qkv), (grad_out, [result])
             if level:
                 moved = lanes.start(clips_to_frames(shaped(grad)))
-                task = start_scatter(level, ("up",), (normed_mlp, [grad_pre]))
-                lanes.fence((), (waiting,))
-                start_scatter(level, ("qkv", "out"), *joint)
-                lanes.fence((), (task,))
+                second = start_scatter(level, ("up",), (normed_mlp, [grad_pre]))
+                lanes.fence((), (first,))
+                third = start_scatter(level, ("qkv", "out"), *joint)
+                lanes.fence((), (second,))
                 grad = flat(moved.result)
             else:
                 start_scatter(level, ("qkv", "out"), *joint)
@@ -1197,14 +1199,17 @@
 
     passes = fused_passes if fused else plain_passes
     finished, gradient = passes(residual)
-    mod_grads, gradient = lanes.fence((mod_grads, gradient))
     hanging = [scatters[key] for key in scatters if key == (0, ("down", "up"))]
-    both = at_once(mod_strip())
-    lanes.fence((), hanging)
-    lanes.fence()
+    first = [scatters[key] for key in scatters if key == (1, ("down",))]
+    second = [scatters[key] for key in scatters if key == (1, ("up",))]
+    both = lanes.start(mod_strip())
+    gradient = lanes.fence(gradient, (), first)
+    gradient = lanes.fence(gradient, hanging)
+    gradient = lanes.fence(gradient, (), second)
     moved = lanes.start(from_frames(moves.halves(gradient.astype(BF16))))
     while lanes.tasks:
         lanes.fence(last=True)
+    both = both.result
     grad_tokens = moved.result.astype(F32)
     output = finished.result
     grads = [
@@ -1227,19 +1232,19 @@
         cond_part = cond_part + lax.dot_general(
             strip, ada_low[level].astype(F32), NT, precision=HIGHEST
         )
-    step = 1
-    while step < n_tp:
-        cond_part = cond_part + swap_with(cond_part, "tp", n_tp, step)
-        step *= 2
-    cond_grad = jnp.stack(
-        [cond_part[:clips], swap_with(cond_part[clips:], "dp", n_dp, 1)], axis=1
-    )[:, :, None]
-    step = 1
-    while step < n_ctx:
-        cond_grad = jnp.concatenate(
-            [cond_grad, swap_with(cond_grad, "ctx", n_ctx, step)], axis=2
+    over_tp = [swap_with(cond_part[:clips], "tp", n_tp, r) for r in range(1, n_tp)]
+    over_both = [
+        lax.ppermute(
+            cond_part[clips:],
+            ("dp", "tp"),
+            [(d * n_tp + t, (1 - d) * n_tp + (t ^ r)) for d in range(n_dp) for t in range(n_tp)],
         )
-        step *= 2
+        for r in range(n_tp)
+    ]
+    cond_grad = jnp.stack([cond_part[:clips] + sum(over_tp), sum(over_both)], axis=1)[:, :, None]
+    cond_grad = jnp.concatenate([cond_grad, swap_with(cond_grad, "ctx", n_ctx, 1)], axis=2)
+    blocks = [cond_grad] + [swap_with(cond_grad, "ctx", n_ctx, 2 * k) for k in range(1, n_ctx // 2)]
+    cond_grad = jnp.concatenate(blocks, axis=2)
     cond_grad = flip_to(cond_grad, 2, n_ctx, moves.ctx).reshape(clips, width)
     cond_grad = moves.halves(cond_grad)
     grad_condition = jax.vjp(jax.nn.silu, cond_full)[1](cond_grad)[0]

time: 1340 us -> 1370 us (1.022)
  local copies, waits for them, and re-layouts: 137 us -> 152 us
  waiting for transfers between devices: 410 us -> 424 us
    all_gather x3 -> x4, waiting for transfers between devices: 0.02 us -> 26 us  [gather_far(): blocks[index] = lax.all_gather(shards[index], 'ctx', axis=0, tiled=True)]
    ppermute x96 -> x95, waiting for transfers between devices: 380 us -> 358 us  [swap_with(): return lax.ppermute(v, axis_name, [(i, i ^ k) for i in range(n)])]
    ppermute x96 -> x95, starting transfers between devices: 122 us -> 119 us  [swap_with(): return lax.ppermute(v, axis_name, [(i, i ^ k) for i in range(n)])]
    unnamed x343 -> x348, local copies, waits for them, and re-layouts: 38.9 us -> 37.1 us
  transfers between devices with their start and end apart: 113 -> 114, of which waited for: 39 -> 41; matrix products, arithmetic and copies ran while one was open for 22% -> 24% of each run, Pallas kernels for 29% -> 23%
where the time goes in v7:
time: 1370 us; the launch traced here: 1360 us
  waiting for transfers between devices  424 us (31%)
  Pallas kernels  380 us (28%)
  local copies, waits for them, and re-layouts  152 us (11%)
  starting transfers between devices  136 us (10%)
  matrix products  131 us (10%)
  other arithmetic  120 us (9%)
  between operations  17.6 us (1%)
    pallas_call x10, Pallas kernels, block_call(): pl.pallas_call(kernel, grid=(clips,), in_specs=specs, out_specs=out_specs...  380 us
    ppermute x95, waiting for transfers between devices, swap_with(): return lax.ppermute(v, axis_name, [(i, i ^ k) for i in range(n)])  358 us
    dot_general x22, matrix products, dot(): return lax.dot_general(a, b, dims, preferred_element_type=F32)  126 us
    ppermute x95, starting transfers between devices, swap_with(): return lax.ppermute(v, axis_name, [(i, i ^ k) for i in range(n)])  119 us
    unnamed x348, local copies, waits for them, and re-layouts  37.1 us
    ppermute x8, waiting for transfers between devices, trade(): block = lax.ppermute(block, ('ctx', 'tp'), pairs)  30.7 us
  transfers between devices with their start and end apart: 114, of which 41 were waited for; matrix products, arithmetic and copies ran while one was open for 24% of the time, Pallas kernels for 23%

profile of v7, /device:TPU:0, one launch (start us, length us, event | category | flops | bytes accessed | tf_op | source)
XLA Modules:
  0.0 1360.7 jit_solution(7655851724689123127)
XLA Ops:
  47.7 18.4 %collective-permute-done.3 = bf16[4,1,128,1152]{3,2,0,1:T(8,128)(2,1)} collective-permute-done((bf16[4,1,128,1152]{3,2,0,1:T(8,128)(2,1)}, bf16[4,1,128,1152]{3,2,0,1:T(8,128)(2,1)}, u32[]{:S(2)}, u32[]{:S(2)}) %collective-permute-start.3) | collective-permute-done | bytes 1179680 | tf_op jit(solution)/shard_map/ppermute | solution.py:29
  77.8 3.6 collective-permute-start.10
  83.5 4.7 collective-permute-done.10
  88.2 3.9 collective-permute-start.11
  93.2 3.6 collective-permute-done.9
  109.4 3.7 collective-permute-done.11
  115.0 10.3 collective-permute-done.12
  131.8 3.9 collective-permute-done.16
  135.7 4.2 collective-permute-done.17
  159.3 40.4 %shard_map.152 = (bf16[1024,1152]{1,0:T(8,128)(2,1)}, bf16[1024,3840]{1,0:T(8,128)(2,1)}, f32[1024,128]{1,0:T(8,128)}, bf16[1024,1152]{1,0:T(8,128)(2,1)}, bf16[...) custom-call(bf16[1024,1152]{1,0:T(8,128)(2,1)} %bitcast.757, ...), custom_call_target="tpu_custom_call" | custom-call | flops 16307453952 | bytes 13123584 | tf_op jit(solution)/shard_map/pallas_call | solution.py:667
  199.7 13.2 collective-permute-done.23
  243.9 26.3 %shard_map.153 = (bf16[1024,4608]{1,0:T(8,128)(2,1)}, bf16[1024,4608]{1,0:T(8,128)(2,1)}) custom-call(bf16[1024,1152]{1,0:T(8,128)(2,1)} %get-tuple-element.207.g_ref, bf16[576,2304]{1,0:T(8,128)(2,1)} %bitcast.793, bf16[576,2304]{1,0:T(8,128)(2,1)} %collective-permute-done.24.refs_1_, bf16[576,2304]{1,0:T(8,128)(2,1)} %collective-permute-done.25.refs_2_, ...), custom_call_target="tpu_custom_call" | custom-call | flops 10871635968 | bytes 12976128 | tf_op jit(solution)/shard_map/pallas_call | solution.py:667
  270.3 30.7 %collective-permute-done.29 = bf16[4,4,2,1,16,1152]{5,4,1,2,0,3:T(8,128)(2,1)S(1)} collective-permute-done((bf16[4,4,2,1,16,1152]{5,4,1,2,0,3:T(8,128)(2,1)}, bf16[4,4,2,1,16,1152]{5,4,1,2,0,3:T(8,128)(2,1)S(1)}, u32[]{:S(2)}, u32[]{:S(2)}) %collective-permute-start.29) | collective-permute-done | bytes 1179680 | tf_op jit(solution)/shard_map/ppermute | solution.py:896
  314.3 22.3 %shard_map.154 = (bf16[1024,1152]{1,0:T(8,128)(2,1)}, bf16[1024,1152]{1,0:T(8,128)(2,1)}) custom-call(bf16[1024,4608]{1,0:T(8,128)(2,1)} %get-tuple-element.214.z_ref, f32[1024,1152]{1,0:T(8,128)} %get-tuple-element.215.y_ref, f32[4,8,1152]{2,1,0:T(8,128)} %concatenate.559.mod_ref, bf16[576,1152]{1,0:T(8,128)(2,1)} %bitcast.100.refs_0_.refs_4_, ...), custom_call_target="tpu_custom_call" | custom-call | flops 10871635968 | bytes 24920064 | tf_op jit(solution)/shard_map/pallas_call | solution.py:667
  343.7 41.6 %collective-permute-done.34 = bf16[4,2,2,1,16,1152]{5,4,1,2,0,3:T(8,128)(2,1)S(1)} collective-permute-done((bf16[4,2,2,1,16,1152]{5,4,1,2,0,3:T(8,128)(2,1)}, bf16[4,2,2,1,16,1152]{5,4,1,2,0,3:T(8,128)(2,1)S(1)}, u32[]{:S(2)}, u32[]{:S(2)}) %collective-permute-start.34) | collective-permute-done | bytes 589856 | tf_op jit(solution)/shard_map/ppermute | solution.py:29
  392.0 5.1 collective-permute-start.42
  399.5 26.0 %all-gather.10.cloned.1.call-done.refs_0_.refs_4_ = bf16[576,2304]{1,0:T(8,128)(2,1)} async-done(((bf16[72,2304]{1,0:T(8,128)(2,1)}), bf16[576,2304]{1,0:T(8,128)(2,1)}) %all-gather.10.cloned.1.call-update) | async-done | bytes 2654224 | tf_op jit(solution)/shard_map/all_gather | solution.py:949
  425.6 18.9 %collective-permute-done.39.refs_1_ = bf16[576,2304]{1,0:T(8,128)(2,1)} collective-permute-done((bf16[576,2304]{1,0:T(8,128)(2,1)}, bf16[576,2304]{1,0:T(8,128)(2,1)}, u32[]{:S(2)}, u32[]{:S(2)}) %collective-permute-start.39) | collective-permute-done | bytes 2654240 | tf_op jit(solution)/shard_map/ppermute | solution.py:29
  453.2 39.8 %shard_map.155 = (bf16[1024,1152]{1,0:T(8,128)(2,1)}, bf16[1024,3840]{1,0:T(8,128)(2,1)}, f32[1024,128]{1,0:T(8,128)}, bf16[1024,1152]{1,0:T(8,128)(2,1)}, bf16[...) custom-call(bf16[1024,1152]{1,0:T(8,128)(2,1)} %bitcast.759, ...), custom_call_target="tpu_custom_call" | custom-call | flops 16307453952 | bytes 13123584 | tf_op jit(solution)/shard_map/pallas_call | solution.py:667
  493.0 14.9 %collective-permute-done.45.refs_1_ = bf16[576,2304]{1,0:T(8,128)(2,1)} collective-permute-done((bf16[576,2304]{1,0:T(8,128)(2,1)}, bf16[576,2304]{1,0:T(8,128)(2,1)}, u32[]{:S(2)}, u32[]{:S(2)}) %collective-permute-start.45) | collective-permute-done | bytes 2654240 | tf_op jit(solution)/shard_map/ppermute | solution.py:29
  508.5 4.7 collective-permute-done.47.refs_3_
  513.2 26.8 %shard_map.156 = (bf16[1024,4608]{1,0:T(8,128)(2,1)}, bf16[1024,4608]{1,0:T(8,128)(2,1)}) custom-call(bf16[1024,1152]{1,0:T(8,128)(2,1)} %get-tuple-element.238.g_ref, bf16[576,2304]{1,0:T(8,128)(2,1)} %all-gather.8.cloned.1.call-done.refs_0_, bf16[576,2304]{1,0:T(8,128)(2,1)} %collective-permute-done.45.refs_1_, ...), custom_call_target="tpu_custom_call" | custom-call | flops 10871635968 | bytes 12976128 | tf_op jit(solution)/shard_map/pallas_call | solution.py:667
  539.9 28.2 %collective-permute-done.48.refs_1_.refs_5_ = bf16[576,2304]{1,0:T(8,128)(2,1)} collective-permute-done((bf16[576,2304]{1,0:T(8,128)(2,1)}, bf16[576,2304]{1,0:T(8,128)(2,1)}, u32[]{:S(2)}, u32[]{:S(2)}) %collective-permute-start.48) | collective-permute-done | bytes 2654240 | tf_op jit(solution)/shard_map/ppermute | solution.py:29
  573.5 21.8 %shard_map.157 = (bf16[1024,1152]{1,0:T(8,128)(2,1)}, bf16[1024,1152]{1,0:T(8,128)(2,1)}) custom-call(bf16[1024,4608]{1,0:T(8,128)(2,1)} %get-tuple-element.243.z_ref, f32[1024,1152]{1,0:T(8,128)} %get-tuple-element.244.y_ref, f32[4,8,1152]{2,1,0:T(8,128)} %pad_maximum_fusion.56.mod_ref, bf16[576,2304]{1,0:T(8,128)(2,1)} %all-gather.10.cloned.1.call-done.refs_0_.refs_4_, ...), custom_call_target="tpu_custom_call" | custom-call | flops 10871635968 | bytes 24920064 | tf_op jit(solution)/shard_map/pallas_call | solution.py:667
  600.8 45.3 %shard_map.158 = (bf16[1024,1152]{1,0:T(8,128)(2,1)}, bf16[1024,4608]{1,0:T(8,128)(2,1)}, f32[1024,1152]{1,0:T(8,128)}, bf16[1024,1152]{1,0:T(8,128)(2,1)}, f32[4,8,1152]{2,1,0:T(8,128)}) custom-call(bf16[1024,1152]{1,0:T(8,128)(2,1)} %bitcast.761, f32[4,8,1152]{2,1,0:T(8,128)} %pad_maximum_fusion.56.mod_ref, bf16[1024,1152]{1,0:T(8,128)(2,1)} %get-tuple-element.250.m_ref, ...), custom_call_target="tpu_custom_call" | custom-call | flops 21743271936 | bytes 42614784 | tf_op jit(solution)/shard_map/pallas_call | solution.py:667
  646.1 11.1 convolution_convert_fusion.3
  663.2 10.3 convolution_convert_fusion.2
  673.6 55.5 %shard_map.159 = (bf16[1024,1152]{1,0:T(8,128)(2,1)}, f32[4,8,1152]{2,1,0:T(8,128)}, bf16[1024,1728]{1,0:T(8,128)(2,1)}, bf16[1024,1728]{1,0:T(8,128)(2,1)}) custom-call(bf16[1024,1152]{1,0:T(8,128)(2,1)} %bitcast.760, f32[4,8,1152]{2,1,0:T(8,128)} %pad_maximum_fusion.56.mod_ref, bf16[1024,1152]{1,0:T(8,128)(2,1)} %get-tuple-element.261.da_ref, ...), custom_call_target="tpu_custom_call" | custom-call | flops 21743271936 | bytes 28590080 | tf_op jit(solution)/shard_map/pallas_call | solution.py:667
  743.8 3.8 convolution_convert_fusion.8
  748.8 8.2 add_convert_fusion.3
  761.9 5.1 convolution_convert_fusion.9
  775.6 15.5 %collective-permute-done.63 = bf16[4,4,1,16,1152]{4,3,1,0,2:T(8,128)(2,1)S(1)} collective-permute-done((bf16[4,4,1,16,1152]{4,3,1,0,2:T(8,128)(2,1)S(1)}, bf16[4,4,1,16,1152]{4,3,1,0,2:T(8,128)(2,1)S(1)}, u32[]{:S(2)}, u32[]{:S(2)}) %collective-permute-start.63) | collective-permute-done | bytes 589856 | tf_op jit(solution)/shard_map/ppermute | solution.py:29
  791.1 10.8 collective-permute-start.62
  804.7 22.7 %collective-permute-done.62 = bf16[4,4,1,16,1152]{4,3,1,0,2:T(8,128)(2,1)S(1)} collective-permute-done((bf16[4,4,1,16,1152]{4,3,1,0,2:T(8,128)(2,1)S(1)}, bf16[4,4,1,16,1152]{4,3,1,0,2:T(8,128)(2,1)S(1)}, u32[]{:S(2)}, u32[]{:S(2)}) %collective-permute-start.62) | collective-permute-done | bytes 589856 | tf_op jit(solution)/shard_map/ppermute | solution.py:29
  831.0 10.8 collective-permute-done.61
  844.8 45.6 %shard_map.160 = (bf16[1024,1152]{1,0:T(8,128)(2,1)}, bf16[1024,4608]{1,0:T(8,128)(2,1)}, f32[1024,1152]{1,0:T(8,128)}, bf16[1024,1152]{1,0:T(8,128)(2,1)}, f32[4,8,1152]{2,1,0:T(8,128)}) custom-call(bf16[1024,1152]{1,0:T(8,128)(2,1)} %bitcast.763, f32[4,8,1152]{2,1,0:T(8,128)} %concatenate.559.mod_ref, bf16[1024,1152]{1,0:T(8,128)(2,1)} %get-tuple-element.285.m_ref, ...), custom_call_target="tpu_custom_call" | custom-call | flops 21743271936 | bytes 42614784 | tf_op jit(solution)/shard_map/pallas_call | solution.py:667
  890.5 10.9 convolution_convert_fusion
  901.5 10.4 convolution_convert_fusion.1
  912.4 8.0 add_convert_fusion.2
  925.8 4.0 add_convert_fusion.11
  933.0 4.1 add_convert_fusion.10
  937.2 3.8 fusion
  945.0 3.5 concatenate.614
  953.2 4.7 add_convert_fusion.7
  962.4 22.7 %collective-permute-done.67 = bf16[576,2304]{1,0:T(8,128)(2,1)} collective-permute-done((bf16[576,2304]{1,0:T(8,128)(2,1)}, bf16[576,2304]{1,0:T(8,128)(2,1)}, u32[]{:S(2)}, u32[]{:S(2)}) %collective-permute-start.67) | collective-permute-done | bytes 2654240 | tf_op jit(solution)/shard_map/ppermute | solution.py:29
  985.2 27.4 %collective-permute-done.68 = bf16[576,1152]{1,0:T(8,128)(2,1)} collective-permute-done((bf16[576,1152]{1,0:T(8,128)(2,1)}, bf16[576,1152]{1,0:T(8,128)(2,1)}, u32[]{:S(2)}, u32[]{:S(2)}) %collective-permute-start.68) | collective-permute-done | bytes 1327136 | tf_op jit(solution)/shard_map/ppermute | solution.py:29
  1012.6 9.7 add_convert_fusion
  1028.8 7.8 add_convert_fusion.1
  1050.1 55.8 %shard_map.161 = (bf16[1024,1152]{1,0:T(8,128)(2,1)}, f32[4,8,1152]{2,1,0:T(8,128)}, bf16[1024,1728]{1,0:T(8,128)(2,1)}, bf16[1024,1728]{1,0:T(8,128)(2,1)}) custom-call(bf16[1024,1152]{1,0:T(8,128)(2,1)} %bitcast.758, f32[4,8,1152]{2,1,0:T(8,128)} %concatenate.559.mod_ref, bf16[1024,1152]{1,0:T(8,128)(2,1)} %get-tuple-element.295.da_ref, ...), custom_call_target="tpu_custom_call" | custom-call | flops 21743271936 | bytes 28590080 | tf_op jit(solution)/shard_map/pallas_call | solution.py:667
  1105.9 6.9 collective-permute-done.73
  1119.2 5.9 convolution_convert_fusion.6
  1125.1 3.9 convolution_convert_fusion.7
  1149.1 11.7 collective-permute-done.77
  1163.4 4.0 add_convert_fusion.4
  1167.4 4.1 collective-permute-done.78
  1174.1 5.0 add_convert_fusion.9
  1188.6 4.1 add_convert_fusion.8
  1195.9 3.8 concatenate.624
  1219.4 19.2 %collective-permute-done.88 = bf16[4,72,2304]{2,1,0:T(8,128)(2,1)} collective-permute-done((bf16[4,72,2304]{2,1,0:T(8,128)(2,1)}, bf16[4,72,2304]{2,1,0:T(8,128)(2,1)}, u32[]{:S(2)}, u32[]{:S(2)}) %collective-permute-start.88) | collective-permute-done | bytes 1327136 | tf_op jit(solution)/shard_map/ppermute | solution.py:29
  1250.9 16.8 %collective-permute-done.91 = bf16[72,4608]{1,0:T(8,128)(2,1)} collective-permute-done((bf16[72,4608]{1,0:T(8,128)(2,1)}, bf16[72,4608]{1,0:T(8,128)(2,1)}, u32[]{:S(2)}, u32[]{:S(2)}) %collective-permute-start.91) | collective-permute-done | bytes 663584 | tf_op jit(solution)/shard_map/ppermute | solution.py:29
  1276.8 9.0 collective-permute-start.96
  1293.6 7.4 collective-permute-done.96
  1300.9 10.7 collective-permute-done.97
  1338.6 6.9 collective-permute-start.105
  (857 shorter events, 389.1 us)
Async XLA Ops:
  7.2 133.8 %all-gather.12.cloned.1.call-start = ((), (), s32[]{:S(2)}) async-start(), calls=%async_computation.7 | async-start | bytes 2985984 | tf_op jit(solution)/shard_map/all_gather | solution.py:949
  11.0 36.6 %collective-permute-start = (bf16[72,2304]{1,0:T(8,128)(2,1)}, bf16[72,2304]{1,0:T(8,128)(2,1)}, u32[]{:S(2)}, u32[]{:S(2)}) collective-permute-start(bf16[72,2304]{1,0:T(8,128)(2,1)} %concatenate.539), channel_id=1, source_target_pairs={{0,4},{2,6},{4,0},{6,2},{8,12},{10,14},{12,8},{14,10},{1,5},{3,7},... | collective-permute-start | bytes 995336 | tf_op jit(solution)/shard_map/ppermute | solution.py:29
  14.1 33.6 %collective-permute-start.1 = (bf16[72,2304]{1,0:T(8,128)(2,1)}, bf16[72,2304]{1,0:T(8,128)(2,1)}, u32[]{:S(2)}, u32[]{:S(2)}) collective-permute-start(bf16[72,2304]{1,0:T(8,128)(2,1)} %concatenate.539), channel_id=1, source_target_pairs={{0,8},{2,10},{4,12},{6,14},{8,0},{10,2},{12,4},{14,6},{1,9},{3,11}... | collective-permute-start | bytes 995336 | tf_op jit(solution)/shard_map/ppermute | solution.py:29
  41.5 228.8 %all-gather.6.cloned.1.call-start = ((), (), s32[]{:S(2)}) async-start(), calls=%async_computation.2 | async-start | bytes 2985984 | tf_op jit(solution)/shard_map/all_gather | solution.py:949
  76.2 311.2 %all-gather.8.cloned.1.call-start = ((), (), s32[]{:S(2)}) async-start(), calls=%async_computation.3 | async-start | bytes 2985984 | tf_op jit(solution)/shard_map/all_gather | solution.py:949
  92.1 33.2 %collective-permute-start.12 = (bf16[72,2304]{1,0:T(8,128)(2,1)}, bf16[72,2304]{1,0:T(8,128)(2,1)S(1)}, u32[]{:S(2)}, u32[]{:S(2)}) collective-permute-start(bf16[72,2304]{1,0:T(8,128)(2,1)} %get-tuple-element.188), channel_id=1, source_target_pairs={{0,8},{2,10},{4,12},{6,14},{8,0},{10,2},{12,4},{14,6},{1,9},{3,11}... | collective-permute-start | bytes 995336 | tf_op jit(solution)/shard_map/ppermute | solution.py:29
  102.0 37.9 %collective-permute-start.15 = (bf16[2,4,72,1152]{3,2,1,0:T(8,128)(2,1)S(1)}, bf16[2,4,72,1152]{3,2,1,0:T(8,128)(2,1)S(1)}, u32[]{:S(2)}, u32[]{:S(2)}) collective-permute-start(bf16[2,4,72,1152]{3,2,1,0:T(8,128)(2,1)S(1)} %pad_maximum_fusion.25), channel_id=1, source_target_pairs={{0,2},{2,0},{4,6},{6,4},{8,10},{10,8},{12,14},{14,12},{1,3},{3,1},... | collective-permute-start | bytes 3981320 | tf_op jit(solution)/shard_map/ppermute | solution.py:29
  105.1 35.9 %collective-permute-start.14 = (bf16[576,1152]{1,0:T(8,128)(2,1)}, bf16[576,1152]{1,0:T(8,128)(2,1)}, u32[]{:S(2)}, u32[]{:S(2)}) collective-permute-start(bf16[576,1152]{1,0:T(8,128)(2,1)} %bitcast.61.refs_0_), channel_id=1, source_target_pairs={{0,1},{1,0},{2,3},{3,2},{4,5},{5,4},{6,7},{7,6},{8,9},{9,8},{10,11... | collective-permute-start | bytes 3981320 | tf_op jit(solution)/shard_map/ppermute | solution.py:29
  141.0 72.0 %collective-permute-start.24 = (bf16[576,2304]{1,0:T(8,128)(2,1)}, bf16[576,2304]{1,0:T(8,128)(2,1)}, u32[]{:S(2)}, u32[]{:S(2)}) collective-permute-start(bf16[576,2304]{1,0:T(8,128)(2,1)} %bitcast.791), channel_id=1, source_target_pairs={{0,1},{1,0},{2,3},{3,2},{4,5},{5,4},{6,7},{7,6},{8,9},{9,8},{10,11... | collective-permute-start | bytes 7962632 | tf_op jit(solution)/shard_map/ppermute | solution.py:29
  142.7 101.3 %collective-permute-start.25 = (bf16[576,2304]{1,0:T(8,128)(2,1)}, bf16[576,2304]{1,0:T(8,128)(2,1)}, u32[]{:S(2)}, u32[]{:S(2)}) collective-permute-start(bf16[576,2304]{1,0:T(8,128)(2,1)} %bitcast.792), channel_id=1, source_target_pairs={{0,16},{16,0},{1,17},{17,1},{2,18},{18,2},{3,19},{19,3},{4,20},{20... | collective-permute-start | bytes 7962632 | tf_op jit(solution)/shard_map/ppermute | solution.py:29
  157.2 55.7 %collective-permute-start.23 = (bf16[4,72,1152]{2,1,0:T(8,128)(2,1)}, bf16[4,72,1152]{2,1,0:T(8,128)(2,1)}, u32[]{:S(2)}, u32[]{:S(2)}) collective-permute-start(bf16[4,72,1152]{2,1,0:T(8,128)(2,1)} %fusion.53), channel_id=1, source_target_pairs={{0,1},{1,0},{2,3},{3,2},{4,5},{5,4},{6,7},{7,6},{8,9},{9,8},{10,11... | collective-permute-start | bytes 1990664 | tf_op jit(solution)/shard_map/ppermute | solution.py:29
  157.7 55.3 %collective-permute-start.22 = (bf16[4,72,1152]{2,1,0:T(8,128)(2,1)}, bf16[4,72,1152]{2,1,0:T(8,128)(2,1)}, u32[]{:S(2)}, u32[]{:S(2)}) collective-permute-start(bf16[4,72,1152]{2,1,0:T(8,128)(2,1)} %fusion.54), channel_id=1, source_target_pairs={{0,2},{2,0},{4,6},{6,4},{8,10},{10,8},{12,14},{14,12},{1,3},{3,1},... | collective-permute-start | bytes 1990664 | tf_op jit(solution)/shard_map/ppermute | solution.py:29
  229.6 71.4 %collective-permute-start.28 = (bf16[2,4,72,1152]{3,2,1,0:T(8,128)(2,1)}, bf16[2,4,72,1152]{3,2,1,0:T(8,128)(2,1)}, u32[]{:S(2)}, u32[]{:S(2)}) collective-permute-start(bf16[2,4,72,1152]{3,2,1,0:T(8,128)(2,1)} %pad_maximum_fusion.27), channel_id=1, source_target_pairs={{0,2},{2,0},{4,6},{6,4},{8,10},{10,8},{12,14},{14,12},{1,3},{3,1},... | collective-permute-start | bytes 3981320 | tf_op jit(solution)/shard_map/ppermute | solution.py:29
  234.1 66.9 %collective-permute-start.27 = (bf16[576,1152]{1,0:T(8,128)(2,1)}, bf16[576,1152]{1,0:T(8,128)(2,1)}, u32[]{:S(2)}, u32[]{:S(2)}) collective-permute-start(bf16[576,1152]{1,0:T(8,128)(2,1)} %bitcast.100.refs_0_.refs_4_), channel_id=1, source_target_pairs={{0,1},{1,0},{2,3},{3,2},{4,5},{5,4},{6,7},{7,6},{8,9},{9,8},{10,11... | collective-permute-start | bytes 3981320 | tf_op jit(solution)/shard_map/ppermute | solution.py:29
  235.6 189.9 %all-gather.10.cloned.1.call-start = ((), (), s32[]{:S(2)}) async-start(), calls=%async_computation.4 | async-start | bytes 2985984 | tf_op jit(solution)/shard_map/all_gather | solution.py:949
  241.9 59.1 %collective-permute-start.29 = (bf16[4,4,2,1,16,1152]{5,4,1,2,0,3:T(8,128)(2,1)}, bf16[4,4,2,1,16,1152]{5,4,1,2,0,3:T(8,128)(2,1)S(1)}, u32[]{:S(2)}, u32[]{:S(2)}) collective-permute-start(bf16[4,4,2,1,16,1152]{5,4,1,2,0,3:T(8,128)(2,1)} %get-tuple-element.441), channel_id=1, source_target_pairs={{0,2},{1,3},{2,0},{3,1},{4,6},{5,7},{6,4},{7,5},{8,10},{9,11},{10,... | collective-permute-start | bytes 3538952 | tf_op jit(solution)/shard_map/ppermute | solution.py:896
  305.9 861.6 %reduce-scatter.3.cloned.1.call-start = ((), (), s32[]{:S(2)}) async-start(), calls=%async_computation.5 | async-start | bytes 2985984 | tf_op jit(solution)/shard_map/reduce_scatter | solution.py:141
  307.5 35.2 %collective-permute-start.35 = (bf16[4,2,2,1,16,1152]{5,4,1,2,0,3:T(8,128)(2,1)}, bf16[4,2,2,1,16,1152]{5,4,1,2,0,3:T(8,128)(2,1)S(1)}, u32[]{:S(2)}, u32[]{:S(2)}) collective-permute-start(bf16[4,2,2,1,16,1152]{5,4,1,2,0,3:T(8,128)(2,1)} %pad_maximum_fusion.44), channel_id=1, source_target_pairs={{0,12},{2,14},{4,8},{6,10},{8,4},{10,6},{12,0},{14,2},{1,13},{3,15... | collective-permute-start | bytes 1769480 | tf_op jit(solution)/shard_map/ppermute | solution.py:29
  311.7 73.7 %collective-permute-start.34 = (bf16[4,2,2,1,16,1152]{5,4,1,2,0,3:T(8,128)(2,1)}, bf16[4,2,2,1,16,1152]{5,4,1,2,0,3:T(8,128)(2,1)S(1)}, u32[]{:S(2)}, u32[]{:S(2)}) collective-permute-start(bf16[4,2,2,1,16,1152]{5,4,1,2,0,3:T(8,128)(2,1)} %pad_maximum_fusion.43), channel_id=1, source_target_pairs={{0,8},{2,10},{4,12},{6,14},{8,0},{10,2},{12,4},{14,6},{1,9},{3,11}... | collective-permute-start | bytes 1769480 | tf_op jit(solution)/shard_map/ppermute | solution.py:29
  312.5 74.8 %collective-permute-start.33 = (bf16[4,2,2,1,16,1152]{5,4,1,2,0,3:T(8,128)(2,1)}, bf16[4,2,2,1,16,1152]{5,4,1,2,0,3:T(8,128)(2,1)S(1)}, u32[]{:S(2)}, u32[]{:S(2)}) collective-permute-start(bf16[4,2,2,1,16,1152]{5,4,1,2,0,3:T(8,128)(2,1)} %pad_maximum_fusion.42), channel_id=1, source_target_pairs={{0,4},{2,6},{4,0},{6,2},{8,12},{10,14},{12,8},{14,10},{1,5},{3,7},... | collective-permute-start | bytes 1769480 | tf_op jit(solution)/shard_map/ppermute | solution.py:29
  339.5 47.9 %collective-permute-start.36 = (bf16[4,4,1,16,1152]{4,3,1,0,2:T(8,128)(2,1)}, bf16[4,4,1,16,1152]{4,3,1,0,2:T(8,128)(2,1)}, u32[]{:S(2)}, u32[]{:S(2)}) collective-permute-start(bf16[4,4,1,16,1152]{4,3,1,0,2:T(8,128)(2,1)} %get-tuple-element.438), channel_id=1, source_target_pairs={{0,1},{1,0},{2,3},{3,2},{4,5},{5,4},{6,7},{7,6},{8,9},{9,8},{10,11... | collective-permute-start | bytes 1769480 | tf_op jit(solution)/shard_map/ppermute | solution.py:896
  341.2 46.2 %collective-permute-start.37 = (bf16[4,4,1,16,1152]{4,3,1,0,2:T(8,128)(2,1)}, bf16[4,4,1,16,1152]{4,3,1,0,2:T(8,128)(2,1)}, u32[]{:S(2)}, u32[]{:S(2)}) collective-permute-start(bf16[4,4,1,16,1152]{4,3,1,0,2:T(8,128)(2,1)} %get-tuple-element.437), channel_id=1, source_target_pairs={{0,2},{1,3},{2,0},{3,1},{4,6},{5,7},{6,4},{7,5},{8,10},{9,11},{10,... | collective-permute-start | bytes 1769480 | tf_op jit(solution)/shard_map/ppermute | solution.py:896
  342.7 44.7 %collective-permute-start.38 = (bf16[4,4,1,16,1152]{4,3,1,0,2:T(8,128)(2,1)S(1)}, bf16[4,4,1,16,1152]{4,3,1,0,2:T(8,128)(2,1)}, u32[]{:S(2)}, u32[]{:S(2)}) collective-permute-start(bf16[4,4,1,16,1152]{4,3,1,0,2:T(8,128)(2,1)S(1)} %get-tuple-element.439), channel_id=1, source_target_pairs={{0,3},{1,2},{2,1},{3,0},{4,7},{5,6},{6,5},{7,4},{8,11},{9,10},{10,... | collective-permute-start | bytes 1769480 | tf_op jit(solution)/shard_map/ppermute | solution.py:896
  385.4 59.1 %collective-permute-start.39 = (bf16[576,2304]{1,0:T(8,128)(2,1)}, bf16[576,2304]{1,0:T(8,128)(2,1)}, u32[]{:S(2)}, u32[]{:S(2)}) collective-permute-start(bf16[576,2304]{1,0:T(8,128)(2,1)} %all-gather.6.cloned.1.call-done.refs_0_), channel_id=1, source_target_pairs={{0,1},{1,0},{2,3},{3,2},{4,5},{5,4},{6,7},{7,6},{8,9},{9,8},{10,11... | collective-permute-start | bytes 7962632 | tf_op jit(solution)/shard_map/ppermute | solution.py:29
  392.0 52.5 %collective-permute-start.42 = (bf16[4,4,1,16,1152]{4,3,1,0,2:T(8,128)(2,1)}, bf16[4,4,1,16,1152]{4,3,1,0,2:T(8,128)(2,1)S(1)}, u32[]{:S(2)}, u32[]{:S(2)}) collective-permute-start(bf16[4,4,1,16,1152]{4,3,1,0,2:T(8,128)(2,1)} %pad_maximum_fusion.47), channel_id=1, source_target_pairs={{0,12},{2,14},{4,8},{6,10},{8,4},{10,6},{12,0},{14,2},{1,13},{3,15... | collective-permute-start | bytes 1769480 | tf_op jit(solution)/shard_map/ppermute | solution.py:29
  398.0 49.5 %collective-permute-start.41 = (bf16[4,4,1,16,1152]{4,3,1,0,2:T(8,128)(2,1)}, bf16[4,4,1,16,1152]{4,3,1,0,2:T(8,128)(2,1)}, u32[]{:S(2)}, u32[]{:S(2)}) collective-permute-start(bf16[4,4,1,16,1152]{4,3,1,0,2:T(8,128)(2,1)} %pad_maximum_fusion.46), channel_id=1, source_target_pairs={{0,8},{2,10},{4,12},{6,14},{8,0},{10,2},{12,4},{14,6},{1,9},{3,11}... | collective-permute-start | bytes 1769480 | tf_op jit(solution)/shard_map/ppermute | solution.py:29
  399.0 48.6 %collective-permute-start.40 = (bf16[4,4,1,16,1152]{4,3,1,0,2:T(8,128)(2,1)}, bf16[4,4,1,16,1152]{4,3,1,0,2:T(8,128)(2,1)}, u32[]{:S(2)}, u32[]{:S(2)}) collective-permute-start(bf16[4,4,1,16,1152]{4,3,1,0,2:T(8,128)(2,1)} %pad_maximum_fusion.45), channel_id=1, source_target_pairs={{0,4},{2,6},{4,0},{6,2},{8,12},{10,14},{12,8},{14,10},{1,5},{3,7},... | collective-permute-start | bytes 1769480 | tf_op jit(solution)/shard_map/ppermute | solution.py:29
  399.5 53.6 %collective-permute-start.43 = (bf16[576,2304]{1,0:T(8,128)(2,1)}, bf16[576,2304]{1,0:T(8,128)(2,1)}, u32[]{:S(2)}, u32[]{:S(2)}) collective-permute-start(bf16[576,2304]{1,0:T(8,128)(2,1)} %all-gather.6.cloned.1.call-done.refs_0_), channel_id=1, source_target_pairs={{0,16},{16,0},{1,17},{17,1},{2,18},{18,2},{3,19},{19,3},{4,20},{20... | collective-permute-start | bytes 7962632 | tf_op jit(solution)/shard_map/ppermute | solution.py:29
  447.6 60.3 %collective-permute-start.45 = (bf16[576,2304]{1,0:T(8,128)(2,1)}, bf16[576,2304]{1,0:T(8,128)(2,1)}, u32[]{:S(2)}, u32[]{:S(2)}) collective-permute-start(bf16[576,2304]{1,0:T(8,128)(2,1)} %all-gather.8.cloned.1.call-done.refs_0_), channel_id=1, source_target_pairs={{0,1},{1,0},{2,3},{3,2},{4,5},{5,4},{6,7},{7,6},{8,9},{9,8},{10,11... | collective-permute-start | bytes 7962632 | tf_op jit(solution)/shard_map/ppermute | solution.py:29
  449.8 58.6 %collective-permute-start.46 = (bf16[576,2304]{1,0:T(8,128)(2,1)}, bf16[576,2304]{1,0:T(8,128)(2,1)}, u32[]{:S(2)}, u32[]{:S(2)}) collective-permute-start(bf16[576,2304]{1,0:T(8,128)(2,1)} %all-gather.8.cloned.1.call-done.refs_0_), channel_id=1, source_target_pairs={{0,16},{16,0},{1,17},{17,1},{2,18},{18,2},{3,19},{19,3},{4,20},{20... | collective-permute-start | bytes 7962632 | tf_op jit(solution)/shard_map/ppermute | solution.py:29
  507.9 60.3 %collective-permute-start.48 = (bf16[576,2304]{1,0:T(8,128)(2,1)}, bf16[576,2304]{1,0:T(8,128)(2,1)}, u32[]{:S(2)}, u32[]{:S(2)}) collective-permute-start(bf16[576,2304]{1,0:T(8,128)(2,1)} %all-gather.10.cloned.1.call-done.refs_0_.refs_4_), channel_id=1, source_target_pairs={{0,1},{1,0},{2,3},{3,2},{4,5},{5,4},{6,7},{7,6},{8,9},{9,8},{10,11... | collective-permute-start | bytes 7962632 | tf_op jit(solution)/shard_map/ppermute | solution.py:29
  508.2 62.1 %collective-permute-start.49 = (bf16[576,2304]{1,0:T(8,128)(2,1)}, bf16[576,2304]{1,0:T(8,128)(2,1)}, u32[]{:S(2)}, u32[]{:S(2)}) collective-permute-start(bf16[576,2304]{1,0:T(8,128)(2,1)} %all-gather.10.cloned.1.call-done.refs_0_.refs_4_), channel_id=1, source_target_pairs={{0,16},{16,0},{1,17},{17,1},{2,18},{18,2},{3,19},{19,3},{4,20},{20... | collective-permute-start | bytes 7962632 | tf_op jit(solution)/shard_map/ppermute | solution.py:29
  599.3 46.8 %collective-permute-start.51 = (bf16[4,4,2,1,16,1152]{5,4,2,1,0,3:T(8,128)(2,1)S(1)}, bf16[4,4,2,1,16,1152]{5,4,2,1,0,3:T(8,128)(2,1)S(1)}, u32[]{:S(2)}, u32[]{:S(2)}) collective-permute-start(bf16[4,4,2,1,16,1152]{5,4,2,1,0,3:T(8,128)(2,1)S(1)} %get-tuple-element.433), channel_id=1, source_target_pairs={{0,2},{1,3},{2,0},{3,1},{4,6},{5,7},{6,4},{7,5},{8,10},{9,11},{10,... | collective-permute-start | bytes 3538952 | tf_op jit(solution)/shard_map/ppermute | solution.py:896
  657.6 71.4 %collective-permute-start.55 = (bf16[4,2,2,1,16,1152]{5,4,2,1,0,3:T(8,128)(2,1)S(1)}, bf16[4,2,2,1,16,1152]{5,4,2,1,0,3:T(8,128)(2,1)S(1)}, u32[]{:S(2)}, u32[]{:S(2)}) collective-permute-start(bf16[4,2,2,1,16,1152]{5,4,2,1,0,3:T(8,128)(2,1)S(1)} %pad_maximum_fusion.50), channel_id=1, source_target_pairs={{0,12},{2,14},{4,8},{6,10},{8,4},{10,6},{12,0},{14,2},{1,13},{3,15... | collective-permute-start | bytes 1769480 | tf_op jit(solution)/shard_map/ppermute | solution.py:29
  658.9 70.2 %collective-permute-start.54 = (bf16[4,2,2,1,16,1152]{5,4,2,1,0,3:T(8,128)(2,1)S(1)}, bf16[4,2,2,1,16,1152]{5,4,2,1,0,3:T(8,128)(2,1)S(1)}, u32[]{:S(2)}, u32[]{:S(2)}) collective-permute-start(bf16[4,2,2,1,16,1152]{5,4,2,1,0,3:T(8,128)(2,1)S(1)} %pad_maximum_fusion.49), channel_id=1, source_target_pairs={{0,8},{2,10},{4,12},{6,14},{8,0},{10,2},{12,4},{14,6},{1,9},{3,11}... | collective-permute-start | bytes 1769480 | tf_op jit(solution)/shard_map/ppermute | solution.py:29
  659.9 69.2 %collective-permute-start.53 = (bf16[4,2,2,1,16,1152]{5,4,2,1,0,3:T(8,128)(2,1)}, bf16[4,2,2,1,16,1152]{5,4,2,1,0,3:T(8,128)(2,1)S(1)}, u32[]{:S(2)}, u32[]{:S(2)}) collective-permute-start(bf16[4,2,2,1,16,1152]{5,4,2,1,0,3:T(8,128)(2,1)} %pad_maximum_fusion.48), channel_id=1, source_target_pairs={{0,4},{2,6},{4,0},{6,2},{8,12},{10,14},{12,8},{14,10},{1,5},{3,7},... | collective-permute-start | bytes 1769480 | tf_op jit(solution)/shard_map/ppermute | solution.py:29
  673.5 93.5 %collective-permute-start.59 = (bf16[576,4608]{1,0:T(8,128)(2,1)}, bf16[576,4608]{1,0:T(8,128)(2,1)}, u32[]{:S(2)}, u32[]{:S(2)}) collective-permute-start(bf16[576,4608]{1,0:T(8,128)(2,1)} %convolution_convert_fusion.2), channel_id=1, source_target_pairs={{0,16},{16,0},{1,17},{17,1},{2,18},{18,2},{3,19},{19,3},{4,20},{20... | collective-permute-start | bytes 15925256 | tf_op jit(solution)/shard_map/ppermute | solution.py:29
  731.9 35.6 %collective-permute-start.56 = (bf16[4,4,1,16,1152]{4,3,1,0,2:T(8,128)(2,1)}, bf16[4,4,1,16,1152]{4,3,1,0,2:T(8,128)(2,1)}, u32[]{:S(2)}, u32[]{:S(2)}) collective-permute-start(bf16[4,4,1,16,1152]{4,3,1,0,2:T(8,128)(2,1)} %get-tuple-element.420), channel_id=1, source_target_pairs={{0,1},{1,0},{2,3},{3,2},{4,5},{5,4},{6,7},{7,6},{8,9},{9,8},{10,11... | collective-permute-start | bytes 1769480 | tf_op jit(solution)/shard_map/ppermute | solution.py:896
  732.5 35.1 %collective-permute-start.57 = (bf16[4,4,1,16,1152]{4,3,1,0,2:T(8,128)(2,1)S(1)}, bf16[4,4,1,16,1152]{4,3,1,0,2:T(8,128)(2,1)}, u32[]{:S(2)}, u32[]{:S(2)}) collective-permute-start(bf16[4,4,1,16,1152]{4,3,1,0,2:T(8,128)(2,1)S(1)} %get-tuple-element.419), channel_id=1, source_target_pairs={{0,2},{1,3},{2,0},{3,1},{4,6},{5,7},{6,4},{7,5},{8,10},{9,11},{10,... | collective-permute-start | bytes 1769480 | tf_op jit(solution)/shard_map/ppermute | solution.py:896
  732.9 35.2 %collective-permute-start.58 = (bf16[4,4,1,16,1152]{4,3,1,0,2:T(8,128)(2,1)S(1)}, bf16[4,4,1,16,1152]{4,3,1,0,2:T(8,128)(2,1)}, u32[]{:S(2)}, u32[]{:S(2)}) collective-permute-start(bf16[4,4,1,16,1152]{4,3,1,0,2:T(8,128)(2,1)S(1)} %get-tuple-element.421), channel_id=1, source_target_pairs={{0,3},{1,2},{2,1},{3,0},{4,7},{5,6},{6,5},{7,4},{8,11},{9,10},{10,... | collective-permute-start | bytes 1769480 | tf_op jit(solution)/shard_map/ppermute | solution.py:896
  738.6 103.1 %collective-permute-start.66 = (bf16[576,1152]{1,0:T(8,128)(2,1)}, bf16[576,1152]{1,0:T(8,128)(2,1)}, u32[]{:S(2)}, u32[]{:S(2)}) collective-permute-start(bf16[576,1152]{1,0:T(8,128)(2,1)} %convolution_convert_fusion.5), channel_id=1, source_target_pairs={{0,16},{16,0},{1,17},{17,1},{2,18},{18,2},{3,19},{19,3},{4,20},{20... | collective-permute-start | bytes 3981320 | tf_op jit(solution)/shard_map/ppermute | solution.py:29
  767.0 74.8 %collective-permute-start.65 = (bf16[576,1728]{1,0:T(8,128)(2,1)}, bf16[576,1728]{1,0:T(8,128)(2,1)}, u32[]{:S(2)}, u32[]{:S(2)}) collective-permute-start(bf16[576,1728]{1,0:T(8,128)(2,1)} %convolution_convert_fusion.8), channel_id=1, source_target_pairs={{0,16},{16,0},{1,17},{17,1},{2,18},{18,2},{3,19},{19,3},{4,20},{20... | collective-permute-start | bytes 5971976 | tf_op jit(solution)/shard_map/ppermute | solution.py:29
  767.5 74.3 %collective-permute-start.64 = (bf16[576,1728]{1,0:T(8,128)(2,1)}, bf16[576,1728]{1,0:T(8,128)(2,1)}, u32[]{:S(2)}, u32[]{:S(2)}) collective-permute-start(bf16[576,1728]{1,0:T(8,128)(2,1)} %convolution_convert_fusion.9), channel_id=1, source_target_pairs={{0,16},{16,0},{1,17},{17,1},{2,18},{18,2},{3,19},{19,3},{4,20},{20... | collective-permute-start | bytes 5971976 | tf_op jit(solution)/shard_map/ppermute | solution.py:29
  767.6 74.2 %collective-permute-start.60 = (bf16[576,2304]{1,0:T(8,128)(2,1)}, bf16[576,2304]{1,0:T(8,128)(2,1)}, u32[]{:S(2)}, u32[]{:S(2)}) collective-permute-start(bf16[576,2304]{1,0:T(8,128)(2,1)} %split.72), channel_id=1, source_target_pairs={{0,1},{1,0},{2,3},{3,2},{4,5},{5,4},{6,7},{7,6},{8,9},{9,8},{10,11... | collective-permute-start | bytes 7962632 | tf_op jit(solution)/shard_map/ppermute | solution.py:29
  791.1 36.3 %collective-permute-start.62 = (bf16[4,4,1,16,1152]{4,3,1,0,2:T(8,128)(2,1)S(1)}, bf16[4,4,1,16,1152]{4,3,1,0,2:T(8,128)(2,1)S(1)}, u32[]{:S(2)}, u32[]{:S(2)}) collective-permute-start(bf16[4,4,1,16,1152]{4,3,1,0,2:T(8,128)(2,1)S(1)} %pad_maximum_fusion.52), channel_id=1, source_target_pairs={{0,8},{2,10},{4,12},{6,14},{8,0},{10,2},{12,4},{14,6},{1,9},{3,11}... | collective-permute-start | bytes 1769480 | tf_op jit(solution)/shard_map/ppermute | solution.py:29
  901.4 111.2 %collective-permute-start.71 = (bf16[576,4608]{1,0:T(8,128)(2,1)}, bf16[576,4608]{1,0:T(8,128)(2,1)}, u32[]{:S(2)}, u32[]{:S(2)}) collective-permute-start(bf16[576,4608]{1,0:T(8,128)(2,1)} %convolution_convert_fusion), channel_id=1, source_target_pairs={{0,16},{16,0},{1,17},{17,1},{2,18},{18,2},{3,19},{19,3},{4,20},{20... | collective-permute-start | bytes 15925256 | tf_op jit(solution)/shard_map/ppermute | solution.py:29
  911.9 100.7 %collective-permute-start.70 = (bf16[576,4608]{1,0:T(8,128)(2,1)}, bf16[576,4608]{1,0:T(8,128)(2,1)}, u32[]{:S(2)}, u32[]{:S(2)}) collective-permute-start(bf16[576,4608]{1,0:T(8,128)(2,1)} %convolution_convert_fusion.1), channel_id=1, source_target_pairs={{0,16},{16,0},{1,17},{17,1},{2,18},{18,2},{3,19},{19,3},{4,20},{20... | collective-permute-start | bytes 15925256 | tf_op jit(solution)/shard_map/ppermute | solution.py:29
  924.3 60.7 %collective-permute-start.67 = (bf16[576,2304]{1,0:T(8,128)(2,1)}, bf16[576,2304]{1,0:T(8,128)(2,1)}, u32[]{:S(2)}, u32[]{:S(2)}) collective-permute-start(bf16[576,2304]{1,0:T(8,128)(2,1)} %split.73), channel_id=1, source_target_pairs={{0,1},{1,0},{2,3},{3,2},{4,5},{5,4},{6,7},{7,6},{8,9},{9,8},{10,11... | collective-permute-start | bytes 7962632 | tf_op jit(solution)/shard_map/ppermute | solution.py:29
  948.5 36.7 %collective-permute-start.69 = (bf16[4,72,2304]{2,1,0:T(8,128)(2,1)}, bf16[4,72,2304]{2,1,0:T(8,128)(2,1)}, u32[]{:S(2)}, u32[]{:S(2)}) collective-permute-start(bf16[4,72,2304]{2,1,0:T(8,128)(2,1)} %concatenate.614), channel_id=1, source_target_pairs={{0,2},{2,0},{4,6},{6,4},{8,10},{10,8},{12,14},{14,12},{1,3},{3,1},... | collective-permute-start | bytes 3981320 | tf_op jit(solution)/shard_map/ppermute | solution.py:29
  949.2 63.4 %collective-permute-start.68 = (bf16[576,1152]{1,0:T(8,128)(2,1)}, bf16[576,1152]{1,0:T(8,128)(2,1)}, u32[]{:S(2)}, u32[]{:S(2)}) collective-permute-start(bf16[576,1152]{1,0:T(8,128)(2,1)} %slice.964), channel_id=1, source_target_pairs={{0,1},{1,0},{2,3},{3,2},{4,5},{5,4},{6,7},{7,6},{8,9},{9,8},{10,11... | collective-permute-start | bytes 3981320 | tf_op jit(solution)/shard_map/ppermute | solution.py:29
  957.9 311.3 %reduce-scatter.5.cloned.1.call-start = ((), (), s32[]{:S(2)}) async-start(), calls=%async_computation.6 | async-start | bytes 2985984 | tf_op jit(solution)/shard_map/reduce_scatter | solution.py:141
  1026.9 85.9 %collective-permute-start.75 = (bf16[4,72,4608]{2,1,0:T(8,128)(2,1)}, bf16[4,72,4608]{2,1,0:T(8,128)(2,1)}, u32[]{:S(2)}, u32[]{:S(2)}) collective-permute-start(bf16[4,72,4608]{2,1,0:T(8,128)(2,1)} %pad_maximum_fusion.2), channel_id=1, source_target_pairs={{0,2},{2,0},{4,6},{6,4},{8,10},{10,8},{12,14},{14,12},{1,3},{3,1},... | collective-permute-start | bytes 7962632 | tf_op jit(solution)/shard_map/ppermute | solution.py:29
  1039.8 73.0 %collective-permute-start.74 = (bf16[576,2304]{1,0:T(8,128)(2,1)}, bf16[576,2304]{1,0:T(8,128)(2,1)}, u32[]{:S(2)}, u32[]{:S(2)}) collective-permute-start(bf16[576,2304]{1,0:T(8,128)(2,1)} %split.77), channel_id=1, source_target_pairs={{0,1},{1,0},{2,3},{3,2},{4,5},{5,4},{6,7},{7,6},{8,9},{9,8},{10,11... | collective-permute-start | bytes 7962632 | tf_op jit(solution)/shard_map/ppermute | solution.py:29
  1043.9 68.9 %collective-permute-start.73 = (bf16[4,72,1152]{2,1,0:T(8,128)(2,1)}, bf16[4,72,1152]{2,1,0:T(8,128)(2,1)}, u32[]{:S(2)}, u32[]{:S(2)}) collective-permute-start(bf16[4,72,1152]{2,1,0:T(8,128)(2,1)} %split.76), channel_id=1, source_target_pairs={{0,1},{1,0},{2,3},{3,2},{4,5},{5,4},{6,7},{7,6},{8,9},{9,8},{10,11... | collective-permute-start | bytes 1990664 | tf_op jit(solution)/shard_map/ppermute | solution.py:29
  1046.6 66.2 %collective-permute-start.72 = (bf16[4,72,1152]{2,1,0:T(8,128)(2,1)S(1)}, bf16[4,72,1152]{2,1,0:T(8,128)(2,1)}, u32[]{:S(2)}, u32[]{:S(2)}) collective-permute-start(bf16[4,72,1152]{2,1,0:T(8,128)(2,1)S(1)} %dynamic-slice_bitcast_fusion.6), channel_id=1, source_target_pairs={{0,2},{2,0},{4,6},{6,4},{8,10},{10,8},{12,14},{14,12},{1,3},{3,1},... | collective-permute-start | bytes 1990664 | tf_op jit(solution)/shard_map/ppermute | solution.py:29
  1050.1 90.8 %collective-permute-start.83 = (bf16[576,1152]{1,0:T(8,128)(2,1)}, bf16[576,1152]{1,0:T(8,128)(2,1)}, u32[]{:S(2)}, u32[]{:S(2)}) collective-permute-start(bf16[576,1152]{1,0:T(8,128)(2,1)} %convolution_convert_fusion.4), channel_id=1, source_target_pairs={{0,16},{16,0},{1,17},{17,1},{2,18},{18,2},{3,19},{19,3},{4,20},{20... | collective-permute-start | bytes 3981320 | tf_op jit(solution)/shard_map/ppermute | solution.py:29
  1140.9 33.2 %collective-permute-start.82 = (bf16[576,1728]{1,0:T(8,128)(2,1)}, bf16[576,1728]{1,0:T(8,128)(2,1)}, u32[]{:S(2)}, u32[]{:S(2)}) collective-permute-start(bf16[576,1728]{1,0:T(8,128)(2,1)} %convolution_convert_fusion.6), channel_id=1, source_target_pairs={{0,16},{16,0},{1,17},{17,1},{2,18},{18,2},{3,19},{19,3},{4,20},{20... | collective-permute-start | bytes 5971976 | tf_op jit(solution)/shard_map/ppermute | solution.py:29
  1182.4 35.5 %collective-permute-start.89 = (f32[4,2,3456]{2,0,1:T(4,128)S(1)}, f32[4,2,3456]{2,0,1:T(4,128)S(1)}, u32[]{:S(2)}, u32[]{:S(2)}) collective-permute-start(f32[4,2,3456]{2,0,1:T(4,128)S(1)} %bitcast.785), channel_id=1, source_target_pairs={{0,1},{1,0},{2,3},{3,2},{4,5},{5,4},{6,7},{7,6},{8,9},{9,8},{10,11... | collective-permute-start | bytes 331784 | tf_op jit(solution)/shard_map/ppermute | solution.py:29
  1199.7 38.9 %collective-permute-start.88 = (bf16[4,72,2304]{2,1,0:T(8,128)(2,1)}, bf16[4,72,2304]{2,1,0:T(8,128)(2,1)}, u32[]{:S(2)}, u32[]{:S(2)}) collective-permute-start(bf16[4,72,2304]{2,1,0:T(8,128)(2,1)} %concatenate.624), channel_id=1, source_target_pairs={{0,2},{2,0},{4,6},{6,4},{8,10},{10,8},{12,14},{14,12},{1,3},{3,1},... | collective-permute-start | bytes 3981320 | tf_op jit(solution)/shard_map/ppermute | solution.py:29
  1200.2 38.4 %collective-permute-start.87 = (bf16[576,1152]{1,0:T(8,128)(2,1)}, bf16[576,1152]{1,0:T(8,128)(2,1)}, u32[]{:S(2)}, u32[]{:S(2)}) collective-permute-start(bf16[576,1152]{1,0:T(8,128)(2,1)} %slice.976), channel_id=1, source_target_pairs={{0,1},{1,0},{2,3},{3,2},{4,5},{5,4},{6,7},{7,6},{8,9},{9,8},{10,11... | collective-permute-start | bytes 3981320 | tf_op jit(solution)/shard_map/ppermute | solution.py:29
  1206.8 40.9 %collective-permute-start.90 = (bf16[72,4608]{1,0:T(8,128)(2,1)}, bf16[72,4608]{1,0:T(8,128)(2,1)}, u32[]{:S(2)}, u32[]{:S(2)}) collective-permute-start(bf16[72,4608]{1,0:T(8,128)(2,1)} %get-tuple-element.389), channel_id=1, source_target_pairs={{0,4},{2,6},{4,0},{6,2},{8,12},{10,14},{12,8},{14,10},{1,5},{3,7},... | collective-permute-start | bytes 1990664 | tf_op jit(solution)/shard_map/ppermute | solution.py:29
  1209.8 57.8 %collective-permute-start.91 = (bf16[72,4608]{1,0:T(8,128)(2,1)}, bf16[72,4608]{1,0:T(8,128)(2,1)}, u32[]{:S(2)}, u32[]{:S(2)}) collective-permute-start(bf16[72,4608]{1,0:T(8,128)(2,1)} %get-tuple-element.390), channel_id=1, source_target_pairs={{0,8},{2,10},{4,12},{6,14},{8,0},{10,2},{12,4},{14,6},{1,9},{3,11}... | collective-permute-start | bytes 1990664 | tf_op jit(solution)/shard_map/ppermute | solution.py:29
  1217.9 49.8 %collective-permute-start.92 = (bf16[72,4608]{1,0:T(8,128)(2,1)}, bf16[72,4608]{1,0:T(8,128)(2,1)}, u32[]{:S(2)}, u32[]{:S(2)}) collective-permute-start(bf16[72,4608]{1,0:T(8,128)(2,1)} %get-tuple-element.388), channel_id=1, source_target_pairs={{0,12},{2,14},{4,8},{6,10},{8,4},{10,6},{12,0},{14,2},{1,13},{3,15... | collective-permute-start | bytes 1990664 | tf_op jit(solution)/shard_map/ppermute | solution.py:29
  1271.5 40.1 %collective-permute-start.100 = (bf16[4,1,128,1152]{3,2,0,1:T(8,128)(2,1)S(1)}, bf16[4,1,128,1152]{3,2,0,1:T(8,128)(2,1)S(1)}, u32[]{:S(2)}, u32[]{:S(2)}) collective-permute-start(bf16[4,1,128,1152]{3,2,0,1:T(8,128)(2,1)S(1)} %get-tuple-element.413), channel_id=1, source_target_pairs={{0,1},{1,0},{2,3},{3,2},{4,5},{5,4},{6,7},{7,6},{8,9},{9,8},{10,11... | collective-permute-start | bytes 3538952 | tf_op jit(solution)/shard_map/ppermute | solution.py:29
  (224 other events, 2068.1 us)
Sparse Core Ops, SparseCore 0:
  41.7 85.1 all-gather.11
  129.0 63.6 all-gather.5
  235.7 71.5 all-gather.7
  309.4 116.1 all-gather.9
  958.0 72.9 reduce-scatter.2
  1167.5 101.6 reduce-scatter.4

commit v8 on v7

--- a/solution.py
+++ b/solution.py
@@ -671,7 +671,9 @@
         out_specs=out_specs,
         out_shape=out_shape,
         scratch_shapes=held + scratch,
-        cost_estimate=pl.CostEstimate(flops=flops, bytes_accessed=moved, transcendentals=0),
+        cost_estimate=pl.CostEstimate(
+            flops=flops // 32, bytes_accessed=moved // 32, transcendentals=0
+        ),
         compiler_params=pltpu.CompilerParams(vmem_limit_bytes=60 * 1024 * 1024),
     )(*operands)
 
@@ -846,7 +848,6 @@
 
     def modulation_vectors():
         sums = shares[:clips] + swap_with(shares[clips:], "dp", n_dp, 1)
-        sums = yield sums
         sums = yield from total_over_ctx(sums)
         pairs = [
             [(c * n_tp + t, (c ^ dx) * n_tp + (t ^ r)) for c in range(n_ctx) for t in range(n_tp)]
@@ -959,10 +960,10 @@
         ((2,), (), ()),
         ((), (2,), ()),
         ((1,), (), ()),
-        ((), (), (4, 5)),
+        ((4,), (), (5,)),
         ((3,), (), ()),
-        ((4,), (3,), ()),
-        ((5,), (4,), ()),
+        ((), (3,), ()),
+        ((5,), (), ()),
         ((), (5,), ()),
         ((), (), ()),
     ]
@@ -1062,10 +1063,7 @@
             stride = piece if level % 2 else 1
             joined = gathers[3 * level].result
             kept = fused_branch(v, vectors[level], joined, clips, stride)
-            kept, late = tick((kept, cotangent))
-            normed, qkv, lse, result, branch, middle, normed_mlp = kept
-            if level == 0:
-                turned = lanes.start(here_to_clips(moves.halves(late)))
+            normed, qkv, lse, result, branch, middle, normed_mlp = tick(kept)
             up = gathers[3 * level + 1].result
             act, slope = tick(fused_up(normed_mlp, vectors[level], up, clips))
             down = gathers[3 * level + 2].result
@@ -1076,7 +1074,8 @@
             if level == 0:
                 moved = lanes.start(frames_to_clips(shaped(v)))
                 tick()
-                tick()
+                late = tick(cotangent)
+                turned = lanes.start(here_to_clips(moves.halves(late)))
                 v = flat(moved.result)
         finished = lanes.start(clips_to_here(moves.halves(shaped(v))))
         grad = flat(turned.result)

time: 1370 us -> 1350 us (0.985)
  waiting for transfers between devices: 424 us -> 358 us
  starting transfers between devices: 136 us -> 159 us
    all_gather x4 -> x3, waiting for transfers between devices: 26 us -> 0.04 us  [gather_far(): blocks[index] = lax.all_gather(shards[index], 'ctx', axis=0, tiled=True)]
    ppermute x95 -> x102, starting transfers between devices: 119 us -> 144 us  [swap_with(): return lax.ppermute(v, axis_name, [(i, i ^ k) for i in range(n)])]
    ppermute x95 -> x102, waiting for transfers between devices: 358 us -> 333 us  [swap_with(): return lax.ppermute(v, axis_name, [(i, i ^ k) for i in range(n)])]
    unnamed x348 -> x404, local copies, waits for them, and re-layouts: 37.1 us -> 41.9 us
  transfers between devices with their start and end apart: 114 -> 120, of which waited for: 41 -> 34; matrix products, arithmetic and copies ran while one was open for 24% -> 25% of each run, Pallas kernels for 23% -> 23%
where the time goes in v8:
time: 1350 us; the launch traced here: 1340 us
  Pallas kernels  380 us (28%)
  waiting for transfers between devices  358 us (27%)
  local copies, waits for them, and re-layouts  160 us (12%)
  starting transfers between devices  159 us (12%)
  matrix products  135 us (10%)
  other arithmetic  131 us (10%)
  between operations  17.7 us (1%)
    pallas_call x10, Pallas kernels, block_call(): pl.pallas_call(kernel, grid=(clips,), in_specs=specs, out_specs=out_specs...  380 us
    ppermute x102, waiting for transfers between devices, swap_with(): return lax.ppermute(v, axis_name, [(i, i ^ k) for i in range(n)])  333 us
    ppermute x102, starting transfers between devices, swap_with(): return lax.ppermute(v, axis_name, [(i, i ^ k) for i in range(n)])  144 us
    dot_general x22, matrix products, dot(): return lax.dot_general(a, b, dims, preferred_element_type=F32)  129 us
    unnamed x404, local copies, waits for them, and re-layouts  41.9 us
  transfers between devices with their start and end apart: 120, of which 34 were waited for; matrix products, arithmetic and copies ran while one was open for 25% of the time, Pallas kernels for 23%

profile of v8, /device:TPU:0, one launch (start us, length us, event | category | flops | bytes accessed | tf_op | source)
XLA Modules:
  0.0 1340.2 jit_solution(3161341163722044903)
XLA Ops:
  50.8 4.8 collective-permute-done.6
  57.4 14.3 %collective-permute-done.7 = f32[4,2,3456]{2,0,1:T(4,128)S(1)} collective-permute-done((f32[4,2,3456]{2,0,1:T(4,128)}, f32[4,2,3456]{2,0,1:T(4,128)S(1)}, u32[]{:S(2)}, u32[]{:S(2)}) %collective-permute-start.7) | collective-permute-done | bytes 110624 | tf_op jit(solution)/shard_map/ppermute | solution.py:29
  75.0 5.1 collective-permute-done.8
  114.7 18.4 %collective-permute-done.15 = bf16[72,2304]{1,0:T(8,128)(2,1)} collective-permute-done((bf16[72,2304]{1,0:T(8,128)(2,1)}, bf16[72,2304]{1,0:T(8,128)(2,1)}, u32[]{:S(2)}, u32[]{:S(2)}) %collective-permute-start.15) | collective-permute-done | bytes 331808 | tf_op jit(solution)/shard_map/ppermute | solution.py:29
  156.1 40.1 %shard_map.152 = (bf16[1024,1152]{1,0:T(8,128)(2,1)}, bf16[1024,3840]{1,0:T(8,128)(2,1)}, f32[1024,128]{1,0:T(8,128)}, bf16[1024,1152]{1,0:T(8,128)(2,1)}, bf16[...) custom-call(bf16[1024,1152]{1,0:T(8,128)(2,1)} %bitcast.749, ...), custom_call_target="tpu_custom_call" | custom-call | flops 509607936 | bytes 410112 | tf_op jit(solution)/shard_map/pallas_call | solution.py:667
  196.2 18.4 %collective-permute-done.24.refs_1_ = bf16[576,2304]{1,0:T(8,128)(2,1)} collective-permute-done((bf16[576,2304]{1,0:T(8,128)(2,1)}, bf16[576,2304]{1,0:T(8,128)(2,1)}, u32[]{:S(2)}, u32[]{:S(2)}) %collective-permute-start.24) | collective-permute-done | bytes 2654240 | tf_op jit(solution)/shard_map/ppermute | solution.py:29
  227.8 26.7 %shard_map.153 = (bf16[1024,4608]{1,0:T(8,128)(2,1)}, bf16[1024,4608]{1,0:T(8,128)(2,1)}) custom-call(bf16[1024,1152]{1,0:T(8,128)(2,1)} %get-tuple-element.210.g_ref, bf16[576,2304]{1,0:T(8,128)(2,1)} %bitcast.67.refs_0_, bf16[576,2304]{1,0:T(8,128)(2,1)} %collective-permute-done.24.refs_1_, bf16[576,2304]{1,0:T(8,128)(2,1)} %collective-permute-done.25.refs_2_, ...), custom_call_target="tpu_custom_call" | custom-call | flops 339738624 | bytes 405504 | tf_op jit(solution)/shard_map/pallas_call | solution.py:667
  271.3 22.0 %shard_map.154 = (bf16[1024,1152]{1,0:T(8,128)(2,1)}, bf16[1024,1152]{1,0:T(8,128)(2,1)}) custom-call(bf16[1024,4608]{1,0:T(8,128)(2,1)} %get-tuple-element.217.z_ref, f32[1024,1152]{1,0:T(8,128)} %get-tuple-element.218.y_ref, f32[4,8,1152]{2,1,0:T(8,128)} %concatenate.620.mod_ref, bf16[576,1152]{1,0:T(8,128)(2,1)} %bitcast.783, ...), custom_call_target="tpu_custom_call" | custom-call | flops 339738624 | bytes 778752 | tf_op jit(solution)/shard_map/pallas_call | solution.py:667
  300.5 11.2 collective-permute-done.37
  312.9 12.5 collective-permute-done.39
  332.7 3.6 collective-permute-start.45
  337.2 9.3 collective-permute-start.44
  347.5 33.7 %collective-permute-done.40.refs_1_ = bf16[576,2304]{1,0:T(8,128)(2,1)S(1)} collective-permute-done((bf16[576,2304]{1,0:T(8,128)(2,1)S(1)}, bf16[576,2304]{1,0:T(8,128)(2,1)S(1)}, u32[]{:S(2)}, u32[]{:S(2)}) %collective-permute-start.40) | collective-permute-done | bytes 2654240 | tf_op jit(solution)/shard_map/ppermute | solution.py:29
  382.7 11.7 collective-permute-start.43
  398.0 8.2 collective-permute-done.43
  430.5 39.9 %shard_map.155 = (bf16[1024,1152]{1,0:T(8,128)(2,1)}, bf16[1024,3840]{1,0:T(8,128)(2,1)}, f32[1024,128]{1,0:T(8,128)}, bf16[1024,1152]{1,0:T(8,128)(2,1)}, bf16[...) custom-call(bf16[1024,1152]{1,0:T(8,128)(2,1)} %bitcast.751, ...), custom_call_target="tpu_custom_call" | custom-call | flops 509607936 | bytes 410112 | tf_op jit(solution)/shard_map/pallas_call | solution.py:667
  473.5 3.3 collective-permute-start.55
  478.6 10.0 collective-permute-start.54
  488.7 26.5 %shard_map.156 = (bf16[1024,4608]{1,0:T(8,128)(2,1)}, bf16[1024,4608]{1,0:T(8,128)(2,1)}) custom-call(bf16[1024,1152]{1,0:T(8,128)(2,1)} %get-tuple-element.244.g_ref, bf16[576,1152]{1,0:T(8,128)(2,1)} %bitcast.779, bf16[576,1152]{1,0:T(8,128)(2,1)} %collective-permute-done.41.refs_1_, bf16[2,576,1152]{2,1,0:T(8,128)(2,1)} %bitcast.741, ...), custom_call_target="tpu_custom_call" | custom-call | flops 339738624 | bytes 405504 | tf_op jit(solution)/shard_map/pallas_call | solution.py:667
  515.2 13.7 %collective-permute-done.54 = bf16[4,2,2,1,16,1152]{5,4,1,2,0,3:T(8,128)(2,1)S(1)} collective-permute-done((bf16[4,2,2,1,16,1152]{5,4,1,2,0,3:T(8,128)(2,1)}, bf16[4,2,2,1,16,1152]{5,4,1,2,0,3:T(8,128)(2,1)S(1)}, u32[]{:S(2)}, u32[]{:S(2)}) %collective-permute-start.54) | collective-permute-done | bytes 589856 | tf_op jit(solution)/shard_map/ppermute | solution.py:29
  529.1 5.2 collective-permute-done.57.refs_3_.refs_9_
  534.3 22.1 %shard_map.157 = (bf16[1024,1152]{1,0:T(8,128)(2,1)}, bf16[1024,1152]{1,0:T(8,128)(2,1)}) custom-call(bf16[1024,4608]{1,0:T(8,128)(2,1)} %get-tuple-element.251.z_ref, f32[1024,1152]{1,0:T(8,128)} %get-tuple-element.252.y_ref, f32[4,8,1152]{2,1,0:T(8,128)} %pad_maximum_fusion.65.mod_ref, bf16[576,2304]{1,0:T(8,128)(2,1)} %all-gather.7.cloned.1.call-done.refs_0_.refs_6_, ...), custom_call_target="tpu_custom_call" | custom-call | flops 339738624 | bytes 778752 | tf_op jit(solution)/shard_map/pallas_call | solution.py:667
  566.0 45.2 %shard_map.158 = (bf16[1024,1152]{1,0:T(8,128)(2,1)}, bf16[1024,4608]{1,0:T(8,128)(2,1)}, f32[1024,1152]{1,0:T(8,128)}, bf16[1024,1152]{1,0:T(8,128)(2,1)}, f32[4,8,1152]{2,1,0:T(8,128)}) custom-call(bf16[1024,1152]{1,0:T(8,128)(2,1)} %bitcast.797, f32[4,8,1152]{2,1,0:T(8,128)} %pad_maximum_fusion.65.mod_ref, bf16[1024,1152]{1,0:T(8,128)(2,1)} %get-tuple-element.258.m_ref, ...), custom_call_target="tpu_custom_call" | custom-call | flops 679477248 | bytes 1331712 | tf_op jit(solution)/shard_map/pallas_call | solution.py:667
  611.2 11.1 convolution_convert_fusion.3
  623.4 3.5 collective-permute-start.62
  629.6 10.4 convolution_convert_fusion.2
  640.0 55.9 %shard_map.159 = (bf16[1024,1152]{1,0:T(8,128)(2,1)}, f32[4,8,1152]{2,1,0:T(8,128)}, bf16[1024,1728]{1,0:T(8,128)(2,1)}, bf16[1024,1728]{1,0:T(8,128)(2,1)}) custom-call(bf16[1024,1152]{1,0:T(8,128)(2,1)} %bitcast.752, f32[4,8,1152]{2,1,0:T(8,128)} %pad_maximum_fusion.65.mod_ref, bf16[1024,1152]{1,0:T(8,128)(2,1)} %get-tuple-element.269.da_ref, ...), custom_call_target="tpu_custom_call" | custom-call | flops 679477248 | bytes 893440 | tf_op jit(solution)/shard_map/pallas_call | solution.py:667
  701.5 3.9 convolution_convert_fusion.8
  716.0 8.2 add_convert_fusion.3
  729.8 3.9 convolution_convert_fusion.9
  747.6 11.5 collective-permute-done.70
  760.2 34.2 %collective-permute-done.69 = bf16[4,4,1,16,1152]{4,3,1,0,2:T(8,128)(2,1)} collective-permute-done((bf16[4,4,1,16,1152]{4,3,1,0,2:T(8,128)(2,1)S(1)}, bf16[4,4,1,16,1152]{4,3,1,0,2:T(8,128)(2,1)}, u32[]{:S(2)}, u32[]{:S(2)}) %collective-permute-start.69) | collective-permute-done | bytes 589856 | tf_op jit(solution)/shard_map/ppermute | solution.py:29
  800.0 8.8 collective-permute-done.68
  812.3 45.5 %shard_map.160 = (bf16[1024,1152]{1,0:T(8,128)(2,1)}, bf16[1024,4608]{1,0:T(8,128)(2,1)}, f32[1024,1152]{1,0:T(8,128)}, bf16[1024,1152]{1,0:T(8,128)(2,1)}, f32[4,8,1152]{2,1,0:T(8,128)}) custom-call(bf16[1024,1152]{1,0:T(8,128)(2,1)} %bitcast.798, f32[4,8,1152]{2,1,0:T(8,128)} %concatenate.620.mod_ref, bf16[1024,1152]{1,0:T(8,128)(2,1)} %get-tuple-element.293.m_ref, ...), custom_call_target="tpu_custom_call" | custom-call | flops 679477248 | bytes 1331712 | tf_op jit(solution)/shard_map/pallas_call | solution.py:667
  857.8 11.2 convolution_convert_fusion
  869.1 10.4 convolution_convert_fusion.1
  880.0 8.0 add_convert_fusion.2
  893.2 4.0 add_convert_fusion.10
  897.2 4.8 add_convert_fusion.11
  902.0 3.8 fusion
  911.0 3.6 concatenate.691
  922.9 29.7 %collective-permute-done.74 = bf16[576,2304]{1,0:T(8,128)(2,1)} collective-permute-done((bf16[576,2304]{1,0:T(8,128)(2,1)}, bf16[576,2304]{1,0:T(8,128)(2,1)}, u32[]{:S(2)}, u32[]{:S(2)}) %collective-permute-start.74) | collective-permute-done | bytes 2654240 | tf_op jit(solution)/shard_map/ppermute | solution.py:29
  952.6 27.5 %collective-permute-done.75 = bf16[576,1152]{1,0:T(8,128)(2,1)} collective-permute-done((bf16[576,1152]{1,0:T(8,128)(2,1)}, bf16[576,1152]{1,0:T(8,128)(2,1)}, u32[]{:S(2)}, u32[]{:S(2)}) %collective-permute-start.75) | collective-permute-done | bytes 1327136 | tf_op jit(solution)/shard_map/ppermute | solution.py:29
  980.1 9.6 add_convert_fusion
  996.3 7.9 add_convert_fusion.1
  1016.2 4.0 add_convert_fusion.7
  1020.2 5.2 convolution_convert_fusion.4
  1025.5 56.0 %shard_map.161 = (bf16[1024,1152]{1,0:T(8,128)(2,1)}, f32[4,8,1152]{2,1,0:T(8,128)}, bf16[1024,1728]{1,0:T(8,128)(2,1)}, bf16[1024,1728]{1,0:T(8,128)(2,1)}) custom-call(bf16[1024,1152]{1,0:T(8,128)(2,1)} %bitcast.750, f32[4,8,1152]{2,1,0:T(8,128)} %concatenate.620.mod_ref, bf16[1024,1152]{1,0:T(8,128)(2,1)} %get-tuple-element.303.da_ref, ...), custom_call_target="tpu_custom_call" | custom-call | flops 679477248 | bytes 893440 | tf_op jit(solution)/shard_map/pallas_call | solution.py:667
  1088.2 5.9 convolution_convert_fusion.6
  1094.0 4.0 convolution_convert_fusion.7
  1113.2 6.9 collective-permute-done.83
  1123.3 13.5 %collective-permute-done.84 = bf16[72,2304]{1,0:T(8,128)(2,1)S(1)} collective-permute-done((bf16[72,2304]{1,0:T(8,128)(2,1)S(1)}, bf16[72,2304]{1,0:T(8,128)(2,1)S(1)}, u32[]{:S(2)}, u32[]{:S(2)}) %collective-permute-start.84) | collective-permute-done | bytes 331808 | tf_op jit(solution)/shard_map/ppermute | solution.py:29
  1139.1 4.0 add_convert_fusion.4
  1143.1 5.6 collective-permute-done.85
  1148.7 5.1 add_convert_fusion.9
  1164.2 4.0 add_convert_fusion.8
  1171.4 3.8 concatenate.701
  1182.7 8.3 collective-permute-start.97
  1199.0 15.6 %collective-permute-done.95 = bf16[4,72,2304]{2,1,0:T(8,128)(2,1)} collective-permute-done((bf16[4,72,2304]{2,1,0:T(8,128)(2,1)}, bf16[4,72,2304]{2,1,0:T(8,128)(2,1)}, u32[]{:S(2)}, u32[]{:S(2)}) %collective-permute-start.95) | collective-permute-done | bytes 1327136 | tf_op jit(solution)/shard_map/ppermute | solution.py:29
  1227.0 22.1 %collective-permute-done.98 = bf16[72,4608]{1,0:T(8,128)(2,1)} collective-permute-done((bf16[72,4608]{1,0:T(8,128)(2,1)}, bf16[72,4608]{1,0:T(8,128)(2,1)}, u32[]{:S(2)}, u32[]{:S(2)}) %collective-permute-start.98) | collective-permute-done | bytes 663584 | tf_op jit(solution)/shard_map/ppermute | solution.py:29
  1256.2 8.6 collective-permute-start.103
  1272.5 7.2 collective-permute-done.103
  1279.7 10.9 collective-permute-done.104
  1318.9 7.0 collective-permute-start.112
  (948 shorter events, 401.6 us)
Async XLA Ops:
  7.2 127.4 %all-gather.9.cloned.1.call-start = ((), (), s32[]{:S(2)}) async-start(), calls=%async_computation.6 | async-start | bytes 2985984 | tf_op jit(solution)/shard_map/all_gather | solution.py:950
  10.9 69.2 %collective-permute-start = (bf16[72,2304]{1,0:T(8,128)(2,1)}, bf16[72,2304]{1,0:T(8,128)(2,1)}, u32[]{:S(2)}, u32[]{:S(2)}) collective-permute-start(bf16[72,2304]{1,0:T(8,128)(2,1)} %concatenate.602), channel_id=1, source_target_pairs={{0,4},{2,6},{4,0},{6,2},{8,12},{10,14},{12,8},{14,10},{1,5},{3,7},... | collective-permute-start | bytes 995336 | tf_op jit(solution)/shard_map/ppermute | solution.py:29
  14.0 66.2 %collective-permute-start.1 = (bf16[72,2304]{1,0:T(8,128)(2,1)}, bf16[72,2304]{1,0:T(8,128)(2,1)}, u32[]{:S(2)}, u32[]{:S(2)}) collective-permute-start(bf16[72,2304]{1,0:T(8,128)(2,1)} %concatenate.602), channel_id=1, source_target_pairs={{0,8},{2,10},{4,12},{6,14},{8,0},{10,2},{12,4},{14,6},{1,9},{3,11}... | collective-permute-start | bytes 995336 | tf_op jit(solution)/shard_map/ppermute | solution.py:29
  16.5 63.6 %collective-permute-start.2 = (bf16[72,2304]{1,0:T(8,128)(2,1)}, bf16[72,2304]{1,0:T(8,128)(2,1)}, u32[]{:S(2)}, u32[]{:S(2)}) collective-permute-start(bf16[72,2304]{1,0:T(8,128)(2,1)} %concatenate.602), channel_id=1, source_target_pairs={{0,12},{2,14},{4,8},{6,10},{8,4},{10,6},{12,0},{14,2},{1,13},{3,15... | collective-permute-start | bytes 995336 | tf_op jit(solution)/shard_map/ppermute | solution.py:29
  19.0 235.6 %all-gather.5.cloned.1.call-start = ((), (), s32[]{:S(2)}) async-start(), calls=%async_computation.2 | async-start | bytes 2985984 | tf_op jit(solution)/shard_map/all_gather | solution.py:950
  42.1 38.0 %collective-permute-start.3 = (bf16[4,1,128,1152]{3,2,0,1:T(8,128)(2,1)}, bf16[4,1,128,1152]{3,2,0,1:T(8,128)(2,1)}, u32[]{:S(2)}, u32[]{:S(2)}) collective-permute-start(bf16[4,1,128,1152]{3,2,0,1:T(8,128)(2,1)} %slice_bitcast_fusion.5), channel_id=1, source_target_pairs={{0,1},{1,0},{2,3},{3,2},{4,5},{5,4},{6,7},{7,6},{8,9},{9,8},{10,11... | collective-permute-start | bytes 3538952 | tf_op jit(solution)/shard_map/ppermute | solution.py:29
  45.8 352.2 %all-gather.7.cloned.1.call-start = ((), (), s32[]{:S(2)}) async-start(), calls=%async_computation.3 | async-start | bytes 2985984 | tf_op jit(solution)/shard_map/all_gather | solution.py:950
  96.8 36.3 %collective-permute-start.15 = (bf16[72,2304]{1,0:T(8,128)(2,1)}, bf16[72,2304]{1,0:T(8,128)(2,1)}, u32[]{:S(2)}, u32[]{:S(2)}) collective-permute-start(bf16[72,2304]{1,0:T(8,128)(2,1)} %get-tuple-element.195), channel_id=1, source_target_pairs={{0,8},{2,10},{4,12},{6,14},{8,0},{10,2},{12,4},{14,6},{1,9},{3,11}... | collective-permute-start | bytes 995336 | tf_op jit(solution)/shard_map/ppermute | solution.py:29
  114.7 35.6 %collective-permute-start.19 = (bf16[576,1152]{1,0:T(8,128)(2,1)S(1)}, bf16[576,1152]{1,0:T(8,128)(2,1)}, u32[]{:S(2)}, u32[]{:S(2)}) collective-permute-start(bf16[576,1152]{1,0:T(8,128)(2,1)S(1)} %bitcast.774), channel_id=1, source_target_pairs={{0,16},{16,0},{1,17},{17,1},{2,18},{18,2},{3,19},{19,3},{4,20},{20... | collective-permute-start | bytes 3981320 | tf_op jit(solution)/shard_map/ppermute | solution.py:29
  143.5 52.7 %collective-permute-start.23 = (bf16[4,72,1152]{2,1,0:T(8,128)(2,1)}, bf16[4,72,1152]{2,1,0:T(8,128)(2,1)}, u32[]{:S(2)}, u32[]{:S(2)}) collective-permute-start(bf16[4,72,1152]{2,1,0:T(8,128)(2,1)} %fusion.56), channel_id=1, source_target_pairs={{0,1},{1,0},{2,3},{3,2},{4,5},{5,4},{6,7},{7,6},{8,9},{9,8},{10,11... | collective-permute-start | bytes 1990664 | tf_op jit(solution)/shard_map/ppermute | solution.py:29
  146.6 67.9 %collective-permute-start.24 = (bf16[576,2304]{1,0:T(8,128)(2,1)}, bf16[576,2304]{1,0:T(8,128)(2,1)}, u32[]{:S(2)}, u32[]{:S(2)}) collective-permute-start(bf16[576,2304]{1,0:T(8,128)(2,1)} %bitcast.67.refs_0_), channel_id=1, source_target_pairs={{0,1},{1,0},{2,3},{3,2},{4,5},{5,4},{6,7},{7,6},{8,9},{9,8},{10,11... | collective-permute-start | bytes 7962632 | tf_op jit(solution)/shard_map/ppermute | solution.py:29
  150.3 45.9 %collective-permute-start.22 = (bf16[4,72,1152]{2,1,0:T(8,128)(2,1)}, bf16[4,72,1152]{2,1,0:T(8,128)(2,1)S(1)}, u32[]{:S(2)}, u32[]{:S(2)}) collective-permute-start(bf16[4,72,1152]{2,1,0:T(8,128)(2,1)} %fusion.57), channel_id=1, source_target_pairs={{0,2},{2,0},{4,6},{6,4},{8,10},{10,8},{12,14},{14,12},{1,3},{3,1},... | collective-permute-start | bytes 1990664 | tf_op jit(solution)/shard_map/ppermute | solution.py:29
  153.5 69.7 %collective-permute-start.25 = (bf16[576,2304]{1,0:T(8,128)(2,1)}, bf16[576,2304]{1,0:T(8,128)(2,1)}, u32[]{:S(2)}, u32[]{:S(2)}) collective-permute-start(bf16[576,2304]{1,0:T(8,128)(2,1)} %bitcast.67.refs_0_), channel_id=1, source_target_pairs={{0,16},{16,0},{1,17},{17,1},{2,18},{18,2},{3,19},{19,3},{4,20},{20... | collective-permute-start | bytes 7962632 | tf_op jit(solution)/shard_map/ppermute | solution.py:29
  217.1 37.6 %collective-permute-start.28 = (bf16[2,4,72,1152]{3,2,1,0:T(8,128)(2,1)}, bf16[2,4,72,1152]{3,2,1,0:T(8,128)(2,1)}, u32[]{:S(2)}, u32[]{:S(2)}) collective-permute-start(bf16[2,4,72,1152]{3,2,1,0:T(8,128)(2,1)} %pad_maximum_fusion.28), channel_id=1, source_target_pairs={{0,2},{2,0},{4,6},{6,4},{8,10},{10,8},{12,14},{14,12},{1,3},{3,1},... | collective-permute-start | bytes 3981320 | tf_op jit(solution)/shard_map/ppermute | solution.py:29
  218.9 35.7 %collective-permute-start.27 = (bf16[576,1152]{1,0:T(8,128)(2,1)S(1)}, bf16[576,1152]{1,0:T(8,128)(2,1)S(1)}, u32[]{:S(2)}, u32[]{:S(2)}) collective-permute-start(bf16[576,1152]{1,0:T(8,128)(2,1)S(1)} %bitcast.781), channel_id=1, source_target_pairs={{0,1},{1,0},{2,3},{3,2},{4,5},{5,4},{6,7},{7,6},{8,9},{9,8},{10,11... | collective-permute-start | bytes 3981320 | tf_op jit(solution)/shard_map/ppermute | solution.py:29
  223.1 919.9 %reduce-scatter.3.cloned.1.call-start = ((), (), s32[]{:S(2)}) async-start(), calls=%async_computation.4 | async-start | bytes 2985984 | tf_op jit(solution)/shard_map/reduce_scatter | solution.py:141
  299.2 82.0 %collective-permute-start.40 = (bf16[576,2304]{1,0:T(8,128)(2,1)S(1)}, bf16[576,2304]{1,0:T(8,128)(2,1)S(1)}, u32[]{:S(2)}, u32[]{:S(2)}) collective-permute-start(bf16[576,2304]{1,0:T(8,128)(2,1)S(1)} %copy-done.24), channel_id=1, source_target_pairs={{0,1},{1,0},{2,3},{3,2},{4,5},{5,4},{6,7},{7,6},{8,9},{9,8},{10,11... | collective-permute-start | bytes 7962632 | tf_op jit(solution)/shard_map/ppermute | solution.py:29
  327.6 78.6 %collective-permute-start.42 = (bf16[2,4,72,1152]{3,2,1,0:T(8,128)(2,1)}, bf16[2,4,72,1152]{3,2,1,0:T(8,128)(2,1)}, u32[]{:S(2)}, u32[]{:S(2)}) collective-permute-start(bf16[2,4,72,1152]{3,2,1,0:T(8,128)(2,1)} %pad_maximum_fusion.30), channel_id=1, source_target_pairs={{0,2},{2,0},{4,6},{6,4},{8,10},{10,8},{12,14},{14,12},{1,3},{3,1},... | collective-permute-start | bytes 3981320 | tf_op jit(solution)/shard_map/ppermute | solution.py:29
  329.9 78.3 %collective-permute-start.41 = (bf16[576,1152]{1,0:T(8,128)(2,1)S(1)}, bf16[576,1152]{1,0:T(8,128)(2,1)}, u32[]{:S(2)}, u32[]{:S(2)}) collective-permute-start(bf16[576,1152]{1,0:T(8,128)(2,1)S(1)} %bitcast.777), channel_id=1, source_target_pairs={{0,1},{1,0},{2,3},{3,2},{4,5},{5,4},{6,7},{7,6},{8,9},{9,8},{10,11... | collective-permute-start | bytes 3981320 | tf_op jit(solution)/shard_map/ppermute | solution.py:29
  332.7 65.3 %collective-permute-start.45 = (bf16[4,4,1,16,1152]{4,3,1,0,2:T(8,128)(2,1)}, bf16[4,4,1,16,1152]{4,3,1,0,2:T(8,128)(2,1)S(1)}, u32[]{:S(2)}, u32[]{:S(2)}) collective-permute-start(bf16[4,4,1,16,1152]{4,3,1,0,2:T(8,128)(2,1)} %pad_maximum_fusion.53), channel_id=1, source_target_pairs={{0,12},{2,14},{4,8},{6,10},{8,4},{10,6},{12,0},{14,2},{1,13},{3,15... | collective-permute-start | bytes 1769480 | tf_op jit(solution)/shard_map/ppermute | solution.py:29
  337.2 60.8 %collective-permute-start.44 = (bf16[4,4,1,16,1152]{4,3,1,0,2:T(8,128)(2,1)}, bf16[4,4,1,16,1152]{4,3,1,0,2:T(8,128)(2,1)S(1)}, u32[]{:S(2)}, u32[]{:S(2)}) collective-permute-start(bf16[4,4,1,16,1152]{4,3,1,0,2:T(8,128)(2,1)} %pad_maximum_fusion.52), channel_id=1, source_target_pairs={{0,8},{2,10},{4,12},{6,14},{8,0},{10,2},{12,4},{14,6},{1,9},{3,11}... | collective-permute-start | bytes 1769480 | tf_op jit(solution)/shard_map/ppermute | solution.py:29
  421.4 49.0 %collective-permute-start.48 = (bf16[4,4,2,1,16,1152]{5,4,1,2,0,3:T(8,128)(2,1)}, bf16[4,4,2,1,16,1152]{5,4,1,2,0,3:T(8,128)(2,1)}, u32[]{:S(2)}, u32[]{:S(2)}) collective-permute-start(bf16[4,4,2,1,16,1152]{5,4,1,2,0,3:T(8,128)(2,1)} %get-tuple-element.447), channel_id=1, source_target_pairs={{0,2},{1,3},{2,0},{3,1},{4,6},{5,7},{6,4},{7,5},{8,10},{9,11},{10,... | collective-permute-start | bytes 3538952 | tf_op jit(solution)/shard_map/ppermute | solution.py:897
  424.9 63.8 %collective-permute-start.51 = (bf16[2,576,1152]{2,1,0:T(8,128)(2,1)S(1)}, bf16[2,576,1152]{2,1,0:T(8,128)(2,1)}, u32[]{:S(2)}, u32[]{:S(2)}) collective-permute-start(bf16[2,576,1152]{2,1,0:T(8,128)(2,1)S(1)} %bitcast.740), channel_id=1, source_target_pairs={{0,16},{16,0},{1,17},{17,1},{2,18},{18,2},{3,19},{19,3},{4,20},{20... | collective-permute-start | bytes 7962632 | tf_op jit(solution)/shard_map/ppermute | solution.py:29
  425.2 90.0 %collective-permute-start.52 = (bf16[576,2304]{1,0:T(8,128)(2,1)}, bf16[576,2304]{1,0:T(8,128)(2,1)}, u32[]{:S(2)}, u32[]{:S(2)}) collective-permute-start(bf16[576,2304]{1,0:T(8,128)(2,1)} %all-gather.7.cloned.1.call-done.refs_0_.refs_6_), channel_id=1, source_target_pairs={{0,1},{1,0},{2,3},{3,2},{4,5},{5,4},{6,7},{7,6},{8,9},{9,8},{10,11... | collective-permute-start | bytes 7962632 | tf_op jit(solution)/shard_map/ppermute | solution.py:29
  426.6 52.0 %collective-permute-start.49 = (bf16[576,1152]{1,0:T(8,128)(2,1)S(1)}, bf16[576,1152]{1,0:T(8,128)(2,1)}, u32[]{:S(2)}, u32[]{:S(2)}) collective-permute-start(bf16[576,1152]{1,0:T(8,128)(2,1)S(1)} %bitcast.778), channel_id=1, source_target_pairs={{0,16},{16,0},{1,17},{17,1},{2,18},{18,2},{3,19},{19,3},{4,20},{20... | collective-permute-start | bytes 3981320 | tf_op jit(solution)/shard_map/ppermute | solution.py:29
  426.6 62.0 %collective-permute-start.50 = (bf16[576,1152]{1,0:T(8,128)(2,1)}, bf16[576,1152]{1,0:T(8,128)(2,1)}, u32[]{:S(2)}, u32[]{:S(2)}) collective-permute-start(bf16[576,1152]{1,0:T(8,128)(2,1)} %collective-permute-done.41.refs_1_), channel_id=1, source_target_pairs={{0,16},{16,0},{1,17},{17,1},{2,18},{18,2},{3,19},{19,3},{4,20},{20... | collective-permute-start | bytes 3981320 | tf_op jit(solution)/shard_map/ppermute | solution.py:29
  473.5 41.7 %collective-permute-start.55 = (bf16[4,2,2,1,16,1152]{5,4,1,2,0,3:T(8,128)(2,1)}, bf16[4,2,2,1,16,1152]{5,4,1,2,0,3:T(8,128)(2,1)}, u32[]{:S(2)}, u32[]{:S(2)}) collective-permute-start(bf16[4,2,2,1,16,1152]{5,4,1,2,0,3:T(8,128)(2,1)} %pad_maximum_fusion.56), channel_id=1, source_target_pairs={{0,12},{2,14},{4,8},{6,10},{8,4},{10,6},{12,0},{14,2},{1,13},{3,15... | collective-permute-start | bytes 1769480 | tf_op jit(solution)/shard_map/ppermute | solution.py:29
  478.6 50.4 %collective-permute-start.54 = (bf16[4,2,2,1,16,1152]{5,4,1,2,0,3:T(8,128)(2,1)}, bf16[4,2,2,1,16,1152]{5,4,1,2,0,3:T(8,128)(2,1)S(1)}, u32[]{:S(2)}, u32[]{:S(2)}) collective-permute-start(bf16[4,2,2,1,16,1152]{5,4,1,2,0,3:T(8,128)(2,1)} %pad_maximum_fusion.55), channel_id=1, source_target_pairs={{0,8},{2,10},{4,12},{6,14},{8,0},{10,2},{12,4},{14,6},{1,9},{3,11}... | collective-permute-start | bytes 1769480 | tf_op jit(solution)/shard_map/ppermute | solution.py:29
  488.6 40.4 %collective-permute-start.53 = (bf16[4,2,2,1,16,1152]{5,4,1,2,0,3:T(8,128)(2,1)}, bf16[4,2,2,1,16,1152]{5,4,1,2,0,3:T(8,128)(2,1)S(1)}, u32[]{:S(2)}, u32[]{:S(2)}) collective-permute-start(bf16[4,2,2,1,16,1152]{5,4,1,2,0,3:T(8,128)(2,1)} %pad_maximum_fusion.54), channel_id=1, source_target_pairs={{0,4},{2,6},{4,0},{6,2},{8,12},{10,14},{12,8},{14,10},{1,5},{3,7},... | collective-permute-start | bytes 1769480 | tf_op jit(solution)/shard_map/ppermute | solution.py:29
  488.7 40.4 %collective-permute-start.56 = (bf16[576,2304]{1,0:T(8,128)(2,1)}, bf16[576,2304]{1,0:T(8,128)(2,1)S(1)}, u32[]{:S(2)}, u32[]{:S(2)}) collective-permute-start(bf16[576,2304]{1,0:T(8,128)(2,1)} %all-gather.7.cloned.1.call-done.refs_0_.refs_6_), channel_id=1, source_target_pairs={{0,16},{16,0},{1,17},{17,1},{2,18},{18,2},{3,19},{19,3},{4,20},{20... | collective-permute-start | bytes 7962632 | tf_op jit(solution)/shard_map/ppermute | solution.py:29
  561.4 49.8 %collective-permute-start.58 = (bf16[4,4,2,1,16,1152]{5,4,2,1,0,3:T(8,128)(2,1)}, bf16[4,4,2,1,16,1152]{5,4,2,1,0,3:T(8,128)(2,1)S(1)}, u32[]{:S(2)}, u32[]{:S(2)}) collective-permute-start(bf16[4,4,2,1,16,1152]{5,4,2,1,0,3:T(8,128)(2,1)} %get-tuple-element.443), channel_id=1, source_target_pairs={{0,2},{1,3},{2,0},{3,1},{4,6},{5,7},{6,4},{7,5},{8,10},{9,11},{10,... | collective-permute-start | bytes 3538952 | tf_op jit(solution)/shard_map/ppermute | solution.py:897
  623.4 72.5 %collective-permute-start.62 = (bf16[4,2,2,1,16,1152]{5,4,2,1,0,3:T(8,128)(2,1)}, bf16[4,2,2,1,16,1152]{5,4,2,1,0,3:T(8,128)(2,1)S(1)}, u32[]{:S(2)}, u32[]{:S(2)}) collective-permute-start(bf16[4,2,2,1,16,1152]{5,4,2,1,0,3:T(8,128)(2,1)} %pad_maximum_fusion.59), channel_id=1, source_target_pairs={{0,12},{2,14},{4,8},{6,10},{8,4},{10,6},{12,0},{14,2},{1,13},{3,15... | collective-permute-start | bytes 1769480 | tf_op jit(solution)/shard_map/ppermute | solution.py:29
  627.8 68.1 %collective-permute-start.61 = (bf16[4,2,2,1,16,1152]{5,4,2,1,0,3:T(8,128)(2,1)}, bf16[4,2,2,1,16,1152]{5,4,2,1,0,3:T(8,128)(2,1)S(1)}, u32[]{:S(2)}, u32[]{:S(2)}) collective-permute-start(bf16[4,2,2,1,16,1152]{5,4,2,1,0,3:T(8,128)(2,1)} %pad_maximum_fusion.58), channel_id=1, source_target_pairs={{0,8},{2,10},{4,12},{6,14},{8,0},{10,2},{12,4},{14,6},{1,9},{3,11}... | collective-permute-start | bytes 1769480 | tf_op jit(solution)/shard_map/ppermute | solution.py:29
  628.7 67.3 %collective-permute-start.60 = (bf16[4,2,2,1,16,1152]{5,4,2,1,0,3:T(8,128)(2,1)}, bf16[4,2,2,1,16,1152]{5,4,2,1,0,3:T(8,128)(2,1)}, u32[]{:S(2)}, u32[]{:S(2)}) collective-permute-start(bf16[4,2,2,1,16,1152]{5,4,2,1,0,3:T(8,128)(2,1)} %pad_maximum_fusion.57), channel_id=1, source_target_pairs={{0,4},{2,6},{4,0},{6,2},{8,12},{10,14},{12,8},{14,10},{1,5},{3,7},... | collective-permute-start | bytes 1769480 | tf_op jit(solution)/shard_map/ppermute | solution.py:29
  639.9 93.8 %collective-permute-start.66 = (bf16[576,4608]{1,0:T(8,128)(2,1)}, bf16[576,4608]{1,0:T(8,128)(2,1)}, u32[]{:S(2)}, u32[]{:S(2)}) collective-permute-start(bf16[576,4608]{1,0:T(8,128)(2,1)} %convolution_convert_fusion.2), channel_id=1, source_target_pairs={{0,16},{16,0},{1,17},{17,1},{2,18},{18,2},{3,19},{19,3},{4,20},{20... | collective-permute-start | bytes 15925256 | tf_op jit(solution)/shard_map/ppermute | solution.py:29
  697.9 36.3 %collective-permute-start.63 = (bf16[4,4,1,16,1152]{4,3,1,0,2:T(8,128)(2,1)S(1)}, bf16[4,4,1,16,1152]{4,3,1,0,2:T(8,128)(2,1)}, u32[]{:S(2)}, u32[]{:S(2)}) collective-permute-start(bf16[4,4,1,16,1152]{4,3,1,0,2:T(8,128)(2,1)S(1)} %get-tuple-element.430), channel_id=1, source_target_pairs={{0,1},{1,0},{2,3},{3,2},{4,5},{5,4},{6,7},{7,6},{8,9},{9,8},{10,11... | collective-permute-start | bytes 1769480 | tf_op jit(solution)/shard_map/ppermute | solution.py:897
  699.0 36.3 %collective-permute-start.64 = (bf16[4,4,1,16,1152]{4,3,1,0,2:T(8,128)(2,1)S(1)}, bf16[4,4,1,16,1152]{4,3,1,0,2:T(8,128)(2,1)}, u32[]{:S(2)}, u32[]{:S(2)}) collective-permute-start(bf16[4,4,1,16,1152]{4,3,1,0,2:T(8,128)(2,1)S(1)} %get-tuple-element.429), channel_id=1, source_target_pairs={{0,2},{1,3},{2,0},{3,1},{4,6},{5,7},{6,4},{7,5},{8,10},{9,11},{10,... | collective-permute-start | bytes 1769480 | tf_op jit(solution)/shard_map/ppermute | solution.py:897
  705.4 103.4 %collective-permute-start.72 = (bf16[576,1728]{1,0:T(8,128)(2,1)}, bf16[576,1728]{1,0:T(8,128)(2,1)}, u32[]{:S(2)}, u32[]{:S(2)}) collective-permute-start(bf16[576,1728]{1,0:T(8,128)(2,1)} %convolution_convert_fusion.8), channel_id=1, source_target_pairs={{0,16},{16,0},{1,17},{17,1},{2,18},{18,2},{3,19},{19,3},{4,20},{20... | collective-permute-start | bytes 5971976 | tf_op jit(solution)/shard_map/ppermute | solution.py:29
  733.7 75.1 %collective-permute-start.71 = (bf16[576,1728]{1,0:T(8,128)(2,1)}, bf16[576,1728]{1,0:T(8,128)(2,1)}, u32[]{:S(2)}, u32[]{:S(2)}) collective-permute-start(bf16[576,1728]{1,0:T(8,128)(2,1)} %convolution_convert_fusion.9), channel_id=1, source_target_pairs={{0,16},{16,0},{1,17},{17,1},{2,18},{18,2},{3,19},{19,3},{4,20},{20... | collective-permute-start | bytes 5971976 | tf_op jit(solution)/shard_map/ppermute | solution.py:29
  734.3 74.6 %collective-permute-start.67 = (bf16[576,2304]{1,0:T(8,128)(2,1)}, bf16[576,2304]{1,0:T(8,128)(2,1)}, u32[]{:S(2)}, u32[]{:S(2)}) collective-permute-start(bf16[576,2304]{1,0:T(8,128)(2,1)} %split.72), channel_id=1, source_target_pairs={{0,1},{1,0},{2,3},{3,2},{4,5},{5,4},{6,7},{7,6},{8,9},{9,8},{10,11... | collective-permute-start | bytes 7962632 | tf_op jit(solution)/shard_map/ppermute | solution.py:29
  744.4 50.0 %collective-permute-start.69 = (bf16[4,4,1,16,1152]{4,3,1,0,2:T(8,128)(2,1)S(1)}, bf16[4,4,1,16,1152]{4,3,1,0,2:T(8,128)(2,1)}, u32[]{:S(2)}, u32[]{:S(2)}) collective-permute-start(bf16[4,4,1,16,1152]{4,3,1,0,2:T(8,128)(2,1)S(1)} %pad_maximum_fusion.61), channel_id=1, source_target_pairs={{0,8},{2,10},{4,12},{6,14},{8,0},{10,2},{12,4},{14,6},{1,9},{3,11}... | collective-permute-start | bytes 1769480 | tf_op jit(solution)/shard_map/ppermute | solution.py:29
  759.2 49.7 %collective-permute-start.73 = (bf16[576,1152]{1,0:T(8,128)(2,1)}, bf16[576,1152]{1,0:T(8,128)(2,1)}, u32[]{:S(2)}, u32[]{:S(2)}) collective-permute-start(bf16[576,1152]{1,0:T(8,128)(2,1)} %convolution_convert_fusion.5), channel_id=1, source_target_pairs={{0,16},{16,0},{1,17},{17,1},{2,18},{18,2},{3,19},{19,3},{4,20},{20... | collective-permute-start | bytes 3981320 | tf_op jit(solution)/shard_map/ppermute | solution.py:29
  869.0 111.1 %collective-permute-start.78 = (bf16[576,4608]{1,0:T(8,128)(2,1)}, bf16[576,4608]{1,0:T(8,128)(2,1)}, u32[]{:S(2)}, u32[]{:S(2)}) collective-permute-start(bf16[576,4608]{1,0:T(8,128)(2,1)} %convolution_convert_fusion), channel_id=1, source_target_pairs={{0,16},{16,0},{1,17},{17,1},{2,18},{18,2},{3,19},{19,3},{4,20},{20... | collective-permute-start | bytes 15925256 | tf_op jit(solution)/shard_map/ppermute | solution.py:29
  879.5 100.7 %collective-permute-start.77 = (bf16[576,4608]{1,0:T(8,128)(2,1)}, bf16[576,4608]{1,0:T(8,128)(2,1)}, u32[]{:S(2)}, u32[]{:S(2)}) collective-permute-start(bf16[576,4608]{1,0:T(8,128)(2,1)} %convolution_convert_fusion.1), channel_id=1, source_target_pairs={{0,16},{16,0},{1,17},{17,1},{2,18},{18,2},{3,19},{19,3},{4,20},{20... | collective-permute-start | bytes 15925256 | tf_op jit(solution)/shard_map/ppermute | solution.py:29
  891.9 60.7 %collective-permute-start.74 = (bf16[576,2304]{1,0:T(8,128)(2,1)}, bf16[576,2304]{1,0:T(8,128)(2,1)}, u32[]{:S(2)}, u32[]{:S(2)}) collective-permute-start(bf16[576,2304]{1,0:T(8,128)(2,1)} %split.73), channel_id=1, source_target_pairs={{0,1},{1,0},{2,3},{3,2},{4,5},{5,4},{6,7},{7,6},{8,9},{9,8},{10,11... | collective-permute-start | bytes 7962632 | tf_op jit(solution)/shard_map/ppermute | solution.py:29
  914.6 38.0 %collective-permute-start.76 = (bf16[4,72,2304]{2,1,0:T(8,128)(2,1)}, bf16[4,72,2304]{2,1,0:T(8,128)(2,1)}, u32[]{:S(2)}, u32[]{:S(2)}) collective-permute-start(bf16[4,72,2304]{2,1,0:T(8,128)(2,1)} %concatenate.691), channel_id=1, source_target_pairs={{0,2},{2,0},{4,6},{6,4},{8,10},{10,8},{12,14},{14,12},{1,3},{3,1},... | collective-permute-start | bytes 3981320 | tf_op jit(solution)/shard_map/ppermute | solution.py:29
  915.0 65.2 %collective-permute-start.75 = (bf16[576,1152]{1,0:T(8,128)(2,1)}, bf16[576,1152]{1,0:T(8,128)(2,1)}, u32[]{:S(2)}, u32[]{:S(2)}) collective-permute-start(bf16[576,1152]{1,0:T(8,128)(2,1)} %slice.1036), channel_id=1, source_target_pairs={{0,1},{1,0},{2,3},{3,2},{4,5},{5,4},{6,7},{7,6},{8,9},{9,8},{10,11... | collective-permute-start | bytes 3981320 | tf_op jit(solution)/shard_map/ppermute | solution.py:29
  994.4 87.4 %collective-permute-start.82 = (bf16[4,72,4608]{2,1,0:T(8,128)(2,1)}, bf16[4,72,4608]{2,1,0:T(8,128)(2,1)}, u32[]{:S(2)}, u32[]{:S(2)}) collective-permute-start(bf16[4,72,4608]{2,1,0:T(8,128)(2,1)} %pad_maximum_fusion.3), channel_id=1, source_target_pairs={{0,2},{2,0},{4,6},{6,4},{8,10},{10,8},{12,14},{14,12},{1,3},{3,1},... | collective-permute-start | bytes 7962632 | tf_op jit(solution)/shard_map/ppermute | solution.py:29
  1008.2 73.6 %collective-permute-start.81 = (bf16[576,2304]{1,0:T(8,128)(2,1)}, bf16[576,2304]{1,0:T(8,128)(2,1)}, u32[]{:S(2)}, u32[]{:S(2)}) collective-permute-start(bf16[576,2304]{1,0:T(8,128)(2,1)} %split.77), channel_id=1, source_target_pairs={{0,1},{1,0},{2,3},{3,2},{4,5},{5,4},{6,7},{7,6},{8,9},{9,8},{10,11... | collective-permute-start | bytes 7962632 | tf_op jit(solution)/shard_map/ppermute | solution.py:29
  1012.1 69.4 %collective-permute-start.80 = (bf16[4,72,1152]{2,1,0:T(8,128)(2,1)}, bf16[4,72,1152]{2,1,0:T(8,128)(2,1)}, u32[]{:S(2)}, u32[]{:S(2)}) collective-permute-start(bf16[4,72,1152]{2,1,0:T(8,128)(2,1)} %split.76), channel_id=1, source_target_pairs={{0,1},{1,0},{2,3},{3,2},{4,5},{5,4},{6,7},{7,6},{8,9},{9,8},{10,11... | collective-permute-start | bytes 1990664 | tf_op jit(solution)/shard_map/ppermute | solution.py:29
  1015.8 66.0 %collective-permute-start.79 = (bf16[4,72,1152]{2,1,0:T(8,128)(2,1)S(1)}, bf16[4,72,1152]{2,1,0:T(8,128)(2,1)}, u32[]{:S(2)}, u32[]{:S(2)}) collective-permute-start(bf16[4,72,1152]{2,1,0:T(8,128)(2,1)S(1)} %dynamic-slice_bitcast_fusion.6), channel_id=1, source_target_pairs={{0,2},{2,0},{4,6},{6,4},{8,10},{10,8},{12,14},{14,12},{1,3},{3,1},... | collective-permute-start | bytes 1990664 | tf_op jit(solution)/shard_map/ppermute | solution.py:29
  1020.2 229.0 %reduce-scatter.5.cloned.1.call-start = ((), (), s32[]{:S(2)}) async-start(), calls=%async_computation.5 | async-start | bytes 2985984 | tf_op jit(solution)/shard_map/reduce_scatter | solution.py:141
  1025.4 84.5 %collective-permute-start.90 = (bf16[576,1152]{1,0:T(8,128)(2,1)}, bf16[576,1152]{1,0:T(8,128)(2,1)}, u32[]{:S(2)}, u32[]{:S(2)}) collective-permute-start(bf16[576,1152]{1,0:T(8,128)(2,1)} %convolution_convert_fusion.4), channel_id=1, source_target_pairs={{0,16},{16,0},{1,17},{17,1},{2,18},{18,2},{3,19},{19,3},{4,20},{20... | collective-permute-start | bytes 3981320 | tf_op jit(solution)/shard_map/ppermute | solution.py:29
  1110.0 38.7 %collective-permute-start.89 = (bf16[576,1728]{1,0:T(8,128)(2,1)}, bf16[576,1728]{1,0:T(8,128)(2,1)}, u32[]{:S(2)}, u32[]{:S(2)}) collective-permute-start(bf16[576,1728]{1,0:T(8,128)(2,1)} %convolution_convert_fusion.6), channel_id=1, source_target_pairs={{0,16},{16,0},{1,17},{17,1},{2,18},{18,2},{3,19},{19,3},{4,20},{20... | collective-permute-start | bytes 5971976 | tf_op jit(solution)/shard_map/ppermute | solution.py:29
  1110.0 38.7 %collective-permute-start.88 = (bf16[576,1728]{1,0:T(8,128)(2,1)}, bf16[576,1728]{1,0:T(8,128)(2,1)}, u32[]{:S(2)}, u32[]{:S(2)}) collective-permute-start(bf16[576,1728]{1,0:T(8,128)(2,1)} %convolution_convert_fusion.7), channel_id=1, source_target_pairs={{0,16},{16,0},{1,17},{17,1},{2,18},{18,2},{3,19},{19,3},{4,20},{20... | collective-permute-start | bytes 5971976 | tf_op jit(solution)/shard_map/ppermute | solution.py:29
  1110.5 38.2 %collective-permute-start.87 = (bf16[4,72,2304]{2,1,0:T(8,128)(2,1)}, bf16[4,72,2304]{2,1,0:T(8,128)(2,1)}, u32[]{:S(2)}, u32[]{:S(2)}) collective-permute-start(bf16[4,72,2304]{2,1,0:T(8,128)(2,1)} %split.83), channel_id=1, source_target_pairs={{0,1},{1,0},{2,3},{3,2},{4,5},{5,4},{6,7},{7,6},{8,9},{9,8},{10,11... | collective-permute-start | bytes 3981320 | tf_op jit(solution)/shard_map/ppermute | solution.py:29
  1111.9 36.8 %collective-permute-start.86 = (bf16[4,72,2304]{2,1,0:T(8,128)(2,1)}, bf16[4,72,2304]{2,1,0:T(8,128)(2,1)}, u32[]{:S(2)}, u32[]{:S(2)}) collective-permute-start(bf16[4,72,2304]{2,1,0:T(8,128)(2,1)} %dynamic-slice_bitcast_fusion.2), channel_id=1, source_target_pairs={{0,2},{2,0},{4,6},{6,4},{8,10},{10,8},{12,14},{14,12},{1,3},{3,1},... | collective-permute-start | bytes 3981320 | tf_op jit(solution)/shard_map/ppermute | solution.py:29
  1157.0 39.6 %collective-permute-start.96 = (f32[4,2,3456]{2,0,1:T(4,128)S(1)}, f32[4,2,3456]{2,0,1:T(4,128)S(1)}, u32[]{:S(2)}, u32[]{:S(2)}) collective-permute-start(f32[4,2,3456]{2,0,1:T(4,128)S(1)} %bitcast.873), channel_id=1, source_target_pairs={{0,1},{1,0},{2,3},{3,2},{4,5},{5,4},{6,7},{7,6},{8,9},{9,8},{10,11... | collective-permute-start | bytes 331784 | tf_op jit(solution)/shard_map/ppermute | solution.py:29
  1175.2 39.4 %collective-permute-start.95 = (bf16[4,72,2304]{2,1,0:T(8,128)(2,1)}, bf16[4,72,2304]{2,1,0:T(8,128)(2,1)}, u32[]{:S(2)}, u32[]{:S(2)}) collective-permute-start(bf16[4,72,2304]{2,1,0:T(8,128)(2,1)} %concatenate.701), channel_id=1, source_target_pairs={{0,2},{2,0},{4,6},{6,4},{8,10},{10,8},{12,14},{14,12},{1,3},{3,1},... | collective-permute-start | bytes 3981320 | tf_op jit(solution)/shard_map/ppermute | solution.py:29
  1176.5 38.1 %collective-permute-start.94 = (bf16[576,1152]{1,0:T(8,128)(2,1)}, bf16[576,1152]{1,0:T(8,128)(2,1)}, u32[]{:S(2)}, u32[]{:S(2)}) collective-permute-start(bf16[576,1152]{1,0:T(8,128)(2,1)} %slice.1048), channel_id=1, source_target_pairs={{0,1},{1,0},{2,3},{3,2},{4,5},{5,4},{6,7},{7,6},{8,9},{9,8},{10,11... | collective-permute-start | bytes 3981320 | tf_op jit(solution)/shard_map/ppermute | solution.py:29
  1182.7 41.3 %collective-permute-start.97 = (bf16[72,4608]{1,0:T(8,128)(2,1)}, bf16[72,4608]{1,0:T(8,128)(2,1)}, u32[]{:S(2)}, u32[]{:S(2)}) collective-permute-start(bf16[72,4608]{1,0:T(8,128)(2,1)} %get-tuple-element.397), channel_id=1, source_target_pairs={{0,4},{2,6},{4,0},{6,2},{8,12},{10,14},{12,8},{14,10},{1,5},{3,7},... | collective-permute-start | bytes 1990664 | tf_op jit(solution)/shard_map/ppermute | solution.py:29
  1191.0 58.2 %collective-permute-start.98 = (bf16[72,4608]{1,0:T(8,128)(2,1)}, bf16[72,4608]{1,0:T(8,128)(2,1)}, u32[]{:S(2)}, u32[]{:S(2)}) collective-permute-start(bf16[72,4608]{1,0:T(8,128)(2,1)} %get-tuple-element.398), channel_id=1, source_target_pairs={{0,8},{2,10},{4,12},{6,14},{8,0},{10,2},{12,4},{14,6},{1,9},{3,11}... | collective-permute-start | bytes 1990664 | tf_op jit(solution)/shard_map/ppermute | solution.py:29
  1196.6 52.6 %collective-permute-start.99 = (bf16[72,4608]{1,0:T(8,128)(2,1)}, bf16[72,4608]{1,0:T(8,128)(2,1)}, u32[]{:S(2)}, u32[]{:S(2)}) collective-permute-start(bf16[72,4608]{1,0:T(8,128)(2,1)} %get-tuple-element.396), channel_id=1, source_target_pairs={{0,12},{2,14},{4,8},{6,10},{8,4},{10,6},{12,0},{14,2},{1,13},{3,15... | collective-permute-start | bytes 1990664 | tf_op jit(solution)/shard_map/ppermute | solution.py:29
  1251.5 39.1 %collective-permute-start.107 = (bf16[4,1,128,1152]{3,2,0,1:T(8,128)(2,1)S(1)}, bf16[4,1,128,1152]{3,2,0,1:T(8,128)(2,1)S(1)}, u32[]{:S(2)}, u32[]{:S(2)}) collective-permute-start(bf16[4,1,128,1152]{3,2,0,1:T(8,128)(2,1)S(1)} %get-tuple-element.423), channel_id=1, source_target_pairs={{0,1},{1,0},{2,3},{3,2},{4,5},{5,4},{6,7},{7,6},{8,9},{9,8},{10,11... | collective-permute-start | bytes 3538952 | tf_op jit(solution)/shard_map/ppermute | solution.py:29
  (258 other events, 3003.7 us)
Sparse Core Ops, SparseCore 0:
  19.1 71.6 all-gather.8
  93.0 69.9 all-gather.4
  223.2 82.0 all-gather.6
  1020.3 96.4 reduce-scatter.2
  1143.2 103.8 reduce-scatter.4

commit v9 on v8

--- a/solution.py
+++ b/solution.py
@@ -1085,8 +1085,7 @@
             back = fused_mlp_back(
                 grad, vectors[level], branch_mlp, slope, middle, branch, up, down, clips
             )
-            late = () if level else (second, third)
-            grad_branch, grad_pre, grad_middle, grad_out, sums = lanes.fence(back, late)
+            grad_branch, grad_pre, grad_middle, grad_out, sums = lanes.fence(back)
             if level:
                 first = start_scatter(level, ("down",), (grad_branch, [act]))
                 grad_out = lanes.fence(grad_out, (finished,))
@@ -1098,15 +1097,15 @@
             back = fused_branch_back(
                 v, vectors[level], grad_out, grad_middle, qkv, lse, joined, clips, stride
             )
-            grad, more, *grad_qkv = lanes.fence(back, (first,) if level else ())
+            grad, more, *grad_qkv = lanes.fence(back)
             mod_grads[level] = (sums + more)[:, :6]
             joint = (normed, grad_qkv), (grad_out, [result])
             if level:
                 moved = lanes.start(clips_to_frames(shaped(grad)))
                 second = start_scatter(level, ("up",), (normed_mlp, [grad_pre]))
-                lanes.fence((), (first,))
+                lanes.fence()
                 third = start_scatter(level, ("qkv", "out"), *joint)
-                lanes.fence((), (second,))
+                lanes.fence()
                 grad = flat(moved.result)
             else:
                 start_scatter(level, ("qkv", "out"), *joint)

time: 1350 us -> 1330 us (0.985)
  waiting for transfers between devices: 358 us -> 300 us
  starting transfers between devices: 159 us -> 206 us
    ppermute x102, waiting for transfers between devices: 333 us -> 260 us  [swap_with(): return lax.ppermute(v, axis_name, [(i, i ^ k) for i in range(n)])]
    ppermute x102, starting transfers between devices: 144 us -> 191 us  [swap_with(): return lax.ppermute(v, axis_name, [(i, i ^ k) for i in range(n)])]
    ppermute x8, waiting for transfers between devices: 24.9 us -> 40 us  [trade(): block = lax.ppermute(block, ('ctx', 'tp'), pairs)]
    unnamed x404 -> x392, local copies, waits for them, and re-layouts: 41.9 us -> 44.3 us
  transfers between devices with their start and end apart: 120 -> 120, of which waited for: 34 -> 34; matrix products, arithmetic and copies ran while one was open for 25% -> 26% of each run, Pallas kernels for 23% -> 27%
where the time goes in v9:
time: 1330 us
  Pallas kernels  380 us (29%)
  waiting for transfers between devices  300 us (23%)
  starting transfers between devices  206 us (15%)
  local copies, waits for them, and re-layouts  161 us (12%)
  matrix products  138 us (10%)
  other arithmetic  123 us (9%)
  between operations  17.7 us (1%)
    pallas_call x10, Pallas kernels, block_call(): pl.pallas_call(kernel, grid=(clips,), in_specs=specs, out_specs=out_specs...  380 us
    ppermute x102, waiting for transfers between devices, swap_with(): return lax.ppermute(v, axis_name, [(i, i ^ k) for i in range(n)])  260 us
    ppermute x102, starting transfers between devices, swap_with(): return lax.ppermute(v, axis_name, [(i, i ^ k) for i in range(n)])  191 us
    dot_general x22, matrix products, dot(): return lax.dot_general(a, b, dims, preferred_element_type=F32)  132 us
    unnamed x392, local copies, waits for them, and re-layouts  44.3 us
    ppermute x8, waiting for transfers between devices, trade(): block = lax.ppermute(block, ('ctx', 'tp'), pairs)  40 us
  transfers between devices with their start and end apart: 120, of which 34 were waited for; matrix products, arithmetic and copies ran while one was open for 26% of the time, Pallas kernels for 27%

profile of v9, /device:TPU:0, one launch (start us, length us, event | category | flops | bytes accessed | tf_op | source)
XLA Modules:
  0.0 1325.4 jit_solution(13860079301239610968)
XLA Ops:
  50.2 4.7 collective-permute-done.6
  56.7 5.2 collective-permute-done.7
  62.0 6.9 collective-permute-start.8
  69.2 5.3 collective-permute-done.8
  88.6 4.3 collective-permute-start.14
  107.8 20.6 %collective-permute-done.15 = bf16[72,2304]{1,0:T(8,128)(2,1)} collective-permute-done((bf16[72,2304]{1,0:T(8,128)(2,1)}, bf16[72,2304]{1,0:T(8,128)(2,1)}, u32[]{:S(2)}, u32[]{:S(2)}) %collective-permute-start.15) | collective-permute-done | bytes 331808 | tf_op jit(solution)/shard_map/ppermute | solution.py:29
  150.5 39.9 %shard_map.152 = (bf16[1024,1152]{1,0:T(8,128)(2,1)}, bf16[1024,3840]{1,0:T(8,128)(2,1)}, f32[1024,128]{1,0:T(8,128)}, bf16[1024,1152]{1,0:T(8,128)(2,1)}, bf16[...) custom-call(bf16[1024,1152]{1,0:T(8,128)(2,1)} %bitcast.745, ...), custom_call_target="tpu_custom_call" | custom-call | flops 509607936 | bytes 410112 | tf_op jit(solution)/shard_map/pallas_call | solution.py:667
  190.5 17.4 %collective-permute-done.24.refs_1_ = bf16[576,2304]{1,0:T(8,128)(2,1)} collective-permute-done((bf16[576,2304]{1,0:T(8,128)(2,1)}, bf16[576,2304]{1,0:T(8,128)(2,1)}, u32[]{:S(2)}, u32[]{:S(2)}) %collective-permute-start.24) | collective-permute-done | bytes 2654240 | tf_op jit(solution)/shard_map/ppermute | solution.py:29
  215.9 4.6 collective-permute-start.29
  225.1 26.9 %shard_map.153 = (bf16[1024,4608]{1,0:T(8,128)(2,1)}, bf16[1024,4608]{1,0:T(8,128)(2,1)}) custom-call(bf16[1024,1152]{1,0:T(8,128)(2,1)} %get-tuple-element.215.g_ref, bf16[576,2304]{1,0:T(8,128)(2,1)} %bitcast.67.refs_0_, bf16[576,2304]{1,0:T(8,128)(2,1)} %collective-permute-done.24.refs_1_, bf16[576,2304]{1,0:T(8,128)(2,1)} %collective-permute-done.25.refs_2_, ...), custom_call_target="tpu_custom_call" | custom-call | flops 339738624 | bytes 405504 | tf_op jit(solution)/shard_map/pallas_call | solution.py:667
  262.6 22.2 %shard_map.154 = (bf16[1024,1152]{1,0:T(8,128)(2,1)}, bf16[1024,1152]{1,0:T(8,128)(2,1)}) custom-call(bf16[1024,4608]{1,0:T(8,128)(2,1)} %get-tuple-element.222.z_ref, f32[1024,1152]{1,0:T(8,128)} %get-tuple-element.223.y_ref, f32[4,8,1152]{2,1,0:T(8,128)} %concatenate.620.mod_ref, bf16[576,1152]{1,0:T(8,128)(2,1)} %bitcast.781, ...), custom_call_target="tpu_custom_call" | custom-call | flops 339738624 | bytes 778752 | tf_op jit(solution)/shard_map/pallas_call | solution.py:667
  291.0 11.9 collective-permute-done.37
  303.7 13.3 %collective-permute-done.39 = bf16[4,4,1,16,1152]{4,3,1,0,2:T(8,128)(2,1)S(1)} collective-permute-done((bf16[4,4,1,16,1152]{4,3,1,0,2:T(8,128)(2,1)S(1)}, bf16[4,4,1,16,1152]{4,3,1,0,2:T(8,128)(2,1)S(1)}, u32[]{:S(2)}, u32[]{:S(2)}) %collective-permute-start.39) | collective-permute-done | bytes 589856 | tf_op jit(solution)/shard_map/ppermute | solution.py:897
  328.9 9.0 collective-permute-start.44
  338.8 33.6 %collective-permute-done.40.refs_1_ = bf16[576,2304]{1,0:T(8,128)(2,1)S(1)} collective-permute-done((bf16[576,2304]{1,0:T(8,128)(2,1)S(1)}, bf16[576,2304]{1,0:T(8,128)(2,1)S(1)}, u32[]{:S(2)}, u32[]{:S(2)}) %collective-permute-start.40) | collective-permute-done | bytes 2654240 | tf_op jit(solution)/shard_map/ppermute | solution.py:29
  373.9 10.9 collective-permute-start.43
  388.6 8.9 collective-permute-done.43
  423.4 39.8 %shard_map.155 = (bf16[1024,1152]{1,0:T(8,128)(2,1)}, bf16[1024,3840]{1,0:T(8,128)(2,1)}, f32[1024,128]{1,0:T(8,128)}, bf16[1024,1152]{1,0:T(8,128)(2,1)}, bf16[...) custom-call(bf16[1024,1152]{1,0:T(8,128)(2,1)} %bitcast.747, ...), custom_call_target="tpu_custom_call" | custom-call | flops 509607936 | bytes 410112 | tf_op jit(solution)/shard_map/pallas_call | solution.py:667
  471.1 9.1 collective-permute-start.54
  480.8 26.8 %shard_map.156 = (bf16[1024,4608]{1,0:T(8,128)(2,1)}, bf16[1024,4608]{1,0:T(8,128)(2,1)}) custom-call(bf16[1024,1152]{1,0:T(8,128)(2,1)} %get-tuple-element.249.g_ref, bf16[576,1152]{1,0:T(8,128)(2,1)} %bitcast.777, bf16[576,1152]{1,0:T(8,128)(2,1)} %collective-permute-done.41.refs_1_, bf16[2,576,1152]{2,1,0:T(8,128)(2,1)} %bitcast.737, ...), custom_call_target="tpu_custom_call" | custom-call | flops 339738624 | bytes 405504 | tf_op jit(solution)/shard_map/pallas_call | solution.py:667
  507.6 13.9 %collective-permute-done.54 = bf16[4,2,2,1,16,1152]{5,4,1,2,0,3:T(8,128)(2,1)S(1)} collective-permute-done((bf16[4,2,2,1,16,1152]{5,4,1,2,0,3:T(8,128)(2,1)}, bf16[4,2,2,1,16,1152]{5,4,1,2,0,3:T(8,128)(2,1)S(1)}, u32[]{:S(2)}, u32[]{:S(2)}) %collective-permute-start.54) | collective-permute-done | bytes 589856 | tf_op jit(solution)/shard_map/ppermute | solution.py:29
  521.7 5.2 collective-permute-done.57.refs_3_.refs_9_
  526.9 22.0 %shard_map.157 = (bf16[1024,1152]{1,0:T(8,128)(2,1)}, bf16[1024,1152]{1,0:T(8,128)(2,1)}) custom-call(bf16[1024,4608]{1,0:T(8,128)(2,1)} %get-tuple-element.256.z_ref, f32[1024,1152]{1,0:T(8,128)} %get-tuple-element.257.y_ref, f32[4,8,1152]{2,1,0:T(8,128)} %pad_maximum_fusion.65.mod_ref, bf16[576,2304]{1,0:T(8,128)(2,1)} %all-gather.7.cloned.1.call-done.refs_0_.refs_6_, ...), custom_call_target="tpu_custom_call" | custom-call | flops 339738624 | bytes 778752 | tf_op jit(solution)/shard_map/pallas_call | solution.py:667
  557.2 45.3 %shard_map.158 = (bf16[1024,1152]{1,0:T(8,128)(2,1)}, bf16[1024,4608]{1,0:T(8,128)(2,1)}, f32[1024,1152]{1,0:T(8,128)}, bf16[1024,1152]{1,0:T(8,128)(2,1)}, f32[4,8,1152]{2,1,0:T(8,128)}) custom-call(bf16[1024,1152]{1,0:T(8,128)(2,1)} %bitcast.795, f32[4,8,1152]{2,1,0:T(8,128)} %pad_maximum_fusion.65.mod_ref, bf16[1024,1152]{1,0:T(8,128)(2,1)} %get-tuple-element.263.m_ref, ...), custom_call_target="tpu_custom_call" | custom-call | flops 679477248 | bytes 1331712 | tf_op jit(solution)/shard_map/pallas_call | solution.py:667
  603.5 10.8 convolution_convert_fusion.3
  614.6 8.8 collective-permute-done.59
  623.5 9.1 add_convert_fusion.3
  637.1 8.0 convolution_convert_fusion.2
  652.4 55.9 %shard_map.159 = (bf16[1024,1152]{1,0:T(8,128)(2,1)}, f32[4,8,1152]{2,1,0:T(8,128)}, bf16[1024,1728]{1,0:T(8,128)(2,1)}, bf16[1024,1728]{1,0:T(8,128)(2,1)}) custom-call(bf16[1024,1152]{1,0:T(8,128)(2,1)} %bitcast.748, f32[4,8,1152]{2,1,0:T(8,128)} %pad_maximum_fusion.65.mod_ref, bf16[1024,1152]{1,0:T(8,128)(2,1)} %get-tuple-element.274.da_ref, ...), custom_call_target="tpu_custom_call" | custom-call | flops 679477248 | bytes 893440 | tf_op jit(solution)/shard_map/pallas_call | solution.py:667
  708.3 5.2 convolution_convert_fusion.5
  722.5 4.7 add_convert_fusion.7
  728.0 6.7 convolution_convert_fusion.8
  739.1 13.9 %collective-permute-done.66 = bf16[4,4,1,16,1152]{4,3,1,0,2:T(8,128)(2,1)} collective-permute-done((bf16[4,4,1,16,1152]{4,3,1,0,2:T(8,128)(2,1)}, bf16[4,4,1,16,1152]{4,3,1,0,2:T(8,128)(2,1)}, u32[]{:S(2)}, u32[]{:S(2)}) %collective-permute-start.66) | collective-permute-done | bytes 589856 | tf_op jit(solution)/shard_map/ppermute | solution.py:897
  753.0 8.1 add_convert_fusion.2
  770.5 4.3 collective-permute-start.70
  778.2 13.8 %collective-permute-done.70 = bf16[4,4,1,16,1152]{4,3,1,0,2:T(8,128)(2,1)S(1)} collective-permute-done((bf16[4,4,1,16,1152]{4,3,1,0,2:T(8,128)(2,1)S(1)}, bf16[4,4,1,16,1152]{4,3,1,0,2:T(8,128)(2,1)S(1)}, u32[]{:S(2)}, u32[]{:S(2)}) %collective-permute-start.70) | collective-permute-done | bytes 589856 | tf_op jit(solution)/shard_map/ppermute | solution.py:29
  792.1 30.5 %collective-permute-start.68 = (bf16[4,4,1,16,1152]{4,3,1,0,2:T(8,128)(2,1)S(1)}, bf16[4,4,1,16,1152]{4,3,1,0,2:T(8,128)(2,1)S(1)}, u32[]{:S(2)}, u32[]{:S(2)}) collective-permute-start(bf16[4,4,1,16,1152]{4,3,1,0,2:T(8,128)(2,1)S(1)} %pad_maximum_fusion.60), channel_id=1, source_target_pairs={{0,4},{2,6},{4,0},{6,2},{8,12},{10,14},{12,8},{14,10},{1,5},{3,7},... | collective-permute-start | bytes 1769480 | tf_op jit(solution)/shard_map/ppermute | solution.py:29
  823.9 8.7 collective-permute-done.69
  832.6 11.1 collective-permute-done.68
  843.8 5.1 add_convert_fusion.11
  857.3 3.9 add_convert_fusion.10
  864.8 4.1 concatenate.691
  878.3 45.2 %shard_map.160 = (bf16[1024,1152]{1,0:T(8,128)(2,1)}, bf16[1024,4608]{1,0:T(8,128)(2,1)}, f32[1024,1152]{1,0:T(8,128)}, bf16[1024,1152]{1,0:T(8,128)(2,1)}, f32[4,8,1152]{2,1,0:T(8,128)}) custom-call(bf16[1024,1152]{1,0:T(8,128)(2,1)} %bitcast.796, f32[4,8,1152]{2,1,0:T(8,128)} %concatenate.620.mod_ref, bf16[1024,1152]{1,0:T(8,128)(2,1)} %get-tuple-element.299.m_ref, ...), custom_call_target="tpu_custom_call" | custom-call | flops 679477248 | bytes 1331712 | tf_op jit(solution)/shard_map/pallas_call | solution.py:667
  923.6 10.8 convolution_convert_fusion
  934.4 10.4 convolution_convert_fusion.1
  962.3 10.9 collective-permute-done.78
  977.5 9.3 add_convert_fusion
  995.9 8.2 add_convert_fusion.1
  1018.1 55.7 %shard_map.161 = (bf16[1024,1152]{1,0:T(8,128)(2,1)}, f32[4,8,1152]{2,1,0:T(8,128)}, bf16[1024,1728]{1,0:T(8,128)(2,1)}, bf16[1024,1728]{1,0:T(8,128)(2,1)}) custom-call(bf16[1024,1152]{1,0:T(8,128)(2,1)} %bitcast.746, f32[4,8,1152]{2,1,0:T(8,128)} %concatenate.620.mod_ref, bf16[1024,1152]{1,0:T(8,128)(2,1)} %get-tuple-element.315.da_ref, ...), custom_call_target="tpu_custom_call" | custom-call | flops 679477248 | bytes 893440 | tf_op jit(solution)/shard_map/pallas_call | solution.py:667
  1073.9 4.8 convolution_convert_fusion.4
  1081.5 6.0 convolution_convert_fusion.6
  1087.9 3.9 convolution_convert_fusion.7
  1111.7 15.3 %collective-permute-done.92 = f32[4,2,2,3456]{3,1,0,2:T(2,128)} collective-permute-done((f32[4,2,2,3456]{3,1,0,2:T(2,128)}, f32[4,2,2,3456]{3,1,0,2:T(2,128)}, u32[]{:S(2)}, u32[]{:S(2)}) %collective-permute-start.92) | collective-permute-done | bytes 221216 | tf_op jit(solution)/shard_map/ppermute | solution.py:29
  1127.0 7.0 collective-permute-start.93
  1135.7 6.2 collective-permute-done.93
  1142.0 5.7 add_convert_fusion.9
  1157.9 4.0 add_convert_fusion.8
  1176.8 6.3 collective-permute-start.97
  1186.5 15.7 %collective-permute-done.95 = bf16[4,72,2304]{2,1,0:T(8,128)(2,1)} collective-permute-done((bf16[4,72,2304]{2,1,0:T(8,128)(2,1)}, bf16[4,72,2304]{2,1,0:T(8,128)(2,1)}, u32[]{:S(2)}, u32[]{:S(2)}) %collective-permute-start.95) | collective-permute-done | bytes 1327136 | tf_op jit(solution)/shard_map/ppermute | solution.py:29
  1213.9 17.9 %collective-permute-done.98 = bf16[72,4608]{1,0:T(8,128)(2,1)} collective-permute-done((bf16[72,4608]{1,0:T(8,128)(2,1)}, bf16[72,4608]{1,0:T(8,128)(2,1)}, u32[]{:S(2)}, u32[]{:S(2)}) %collective-permute-start.98) | collective-permute-done | bytes 663584 | tf_op jit(solution)/shard_map/ppermute | solution.py:29
  1238.3 12.3 collective-permute-start.103
  1258.1 6.7 collective-permute-done.103
  1264.8 11.6 collective-permute-done.104
  1304.7 7.0 collective-permute-start.112
  (933 shorter events, 405.7 us)
Async XLA Ops:
  7.2 122.5 %all-gather.9.cloned.1.call-start = ((), (), s32[]{:S(2)}) async-start(), calls=%async_computation.6 | async-start | bytes 2985984 | tf_op jit(solution)/shard_map/all_gather | solution.py:950
  10.9 63.5 %collective-permute-start = (bf16[72,2304]{1,0:T(8,128)(2,1)}, bf16[72,2304]{1,0:T(8,128)(2,1)}, u32[]{:S(2)}, u32[]{:S(2)}) collective-permute-start(bf16[72,2304]{1,0:T(8,128)(2,1)} %concatenate.602), channel_id=1, source_target_pairs={{0,4},{2,6},{4,0},{6,2},{8,12},{10,14},{12,8},{14,10},{1,5},{3,7},... | collective-permute-start | bytes 995336 | tf_op jit(solution)/shard_map/ppermute | solution.py:29
  13.9 60.5 %collective-permute-start.1 = (bf16[72,2304]{1,0:T(8,128)(2,1)}, bf16[72,2304]{1,0:T(8,128)(2,1)}, u32[]{:S(2)}, u32[]{:S(2)}) collective-permute-start(bf16[72,2304]{1,0:T(8,128)(2,1)} %concatenate.602), channel_id=1, source_target_pairs={{0,8},{2,10},{4,12},{6,14},{8,0},{10,2},{12,4},{14,6},{1,9},{3,11}... | collective-permute-start | bytes 995336 | tf_op jit(solution)/shard_map/ppermute | solution.py:29
  16.5 57.9 %collective-permute-start.2 = (bf16[72,2304]{1,0:T(8,128)(2,1)}, bf16[72,2304]{1,0:T(8,128)(2,1)}, u32[]{:S(2)}, u32[]{:S(2)}) collective-permute-start(bf16[72,2304]{1,0:T(8,128)(2,1)} %concatenate.602), channel_id=1, source_target_pairs={{0,12},{2,14},{4,8},{6,10},{8,4},{10,6},{12,0},{14,2},{1,13},{3,15... | collective-permute-start | bytes 995336 | tf_op jit(solution)/shard_map/ppermute | solution.py:29
  19.0 233.2 %all-gather.5.cloned.1.call-start = ((), (), s32[]{:S(2)}) async-start(), calls=%async_computation.2 | async-start | bytes 2985984 | tf_op jit(solution)/shard_map/all_gather | solution.py:950
  42.1 32.3 %collective-permute-start.3 = (bf16[4,1,128,1152]{3,2,0,1:T(8,128)(2,1)}, bf16[4,1,128,1152]{3,2,0,1:T(8,128)(2,1)}, u32[]{:S(2)}, u32[]{:S(2)}) collective-permute-start(bf16[4,1,128,1152]{3,2,0,1:T(8,128)(2,1)} %slice_bitcast_fusion.5), channel_id=1, source_target_pairs={{0,1},{1,0},{2,3},{3,2},{4,5},{5,4},{6,7},{7,6},{8,9},{9,8},{10,11... | collective-permute-start | bytes 3538952 | tf_op jit(solution)/shard_map/ppermute | solution.py:29
  45.8 342.7 %all-gather.7.cloned.1.call-start = ((), (), s32[]{:S(2)}) async-start(), calls=%async_computation.3 | async-start | bytes 2985984 | tf_op jit(solution)/shard_map/all_gather | solution.py:950
  93.0 35.5 %collective-permute-start.15 = (bf16[72,2304]{1,0:T(8,128)(2,1)}, bf16[72,2304]{1,0:T(8,128)(2,1)}, u32[]{:S(2)}, u32[]{:S(2)}) collective-permute-start(bf16[72,2304]{1,0:T(8,128)(2,1)} %get-tuple-element.200), channel_id=1, source_target_pairs={{0,8},{2,10},{4,12},{6,14},{8,0},{10,2},{12,4},{14,6},{1,9},{3,11}... | collective-permute-start | bytes 995336 | tf_op jit(solution)/shard_map/ppermute | solution.py:29
  94.1 34.4 %collective-permute-start.16 = (bf16[72,2304]{1,0:T(8,128)(2,1)}, bf16[72,2304]{1,0:T(8,128)(2,1)}, u32[]{:S(2)}, u32[]{:S(2)}) collective-permute-start(bf16[72,2304]{1,0:T(8,128)(2,1)} %get-tuple-element.200), channel_id=1, source_target_pairs={{0,12},{2,14},{4,8},{6,10},{8,4},{10,6},{12,0},{14,2},{1,13},{3,15... | collective-permute-start | bytes 995336 | tf_op jit(solution)/shard_map/ppermute | solution.py:29
  107.8 36.2 %collective-permute-start.19 = (bf16[576,1152]{1,0:T(8,128)(2,1)S(1)}, bf16[576,1152]{1,0:T(8,128)(2,1)}, u32[]{:S(2)}, u32[]{:S(2)}) collective-permute-start(bf16[576,1152]{1,0:T(8,128)(2,1)S(1)} %bitcast.772), channel_id=1, source_target_pairs={{0,16},{16,0},{1,17},{17,1},{2,18},{18,2},{3,19},{19,3},{4,20},{20... | collective-permute-start | bytes 3981320 | tf_op jit(solution)/shard_map/ppermute | solution.py:29
  136.8 53.6 %collective-permute-start.23 = (bf16[4,72,1152]{2,1,0:T(8,128)(2,1)}, bf16[4,72,1152]{2,1,0:T(8,128)(2,1)}, u32[]{:S(2)}, u32[]{:S(2)}) collective-permute-start(bf16[4,72,1152]{2,1,0:T(8,128)(2,1)} %fusion.56), channel_id=1, source_target_pairs={{0,1},{1,0},{2,3},{3,2},{4,5},{5,4},{6,7},{7,6},{8,9},{9,8},{10,11... | collective-permute-start | bytes 1990664 | tf_op jit(solution)/shard_map/ppermute | solution.py:29
  141.2 66.7 %collective-permute-start.24 = (bf16[576,2304]{1,0:T(8,128)(2,1)}, bf16[576,2304]{1,0:T(8,128)(2,1)}, u32[]{:S(2)}, u32[]{:S(2)}) collective-permute-start(bf16[576,2304]{1,0:T(8,128)(2,1)} %bitcast.67.refs_0_), channel_id=1, source_target_pairs={{0,1},{1,0},{2,3},{3,2},{4,5},{5,4},{6,7},{7,6},{8,9},{9,8},{10,11... | collective-permute-start | bytes 7962632 | tf_op jit(solution)/shard_map/ppermute | solution.py:29
  144.0 46.5 %collective-permute-start.22 = (bf16[4,72,1152]{2,1,0:T(8,128)(2,1)S(1)}, bf16[4,72,1152]{2,1,0:T(8,128)(2,1)}, u32[]{:S(2)}, u32[]{:S(2)}) collective-permute-start(bf16[4,72,1152]{2,1,0:T(8,128)(2,1)S(1)} %fusion.57), channel_id=1, source_target_pairs={{0,2},{2,0},{4,6},{6,4},{8,10},{10,8},{12,14},{14,12},{1,3},{3,1},... | collective-permute-start | bytes 1990664 | tf_op jit(solution)/shard_map/ppermute | solution.py:29
  148.0 72.5 %collective-permute-start.25 = (bf16[576,2304]{1,0:T(8,128)(2,1)}, bf16[576,2304]{1,0:T(8,128)(2,1)}, u32[]{:S(2)}, u32[]{:S(2)}) collective-permute-start(bf16[576,2304]{1,0:T(8,128)(2,1)} %bitcast.67.refs_0_), channel_id=1, source_target_pairs={{0,16},{16,0},{1,17},{17,1},{2,18},{18,2},{3,19},{19,3},{4,20},{20... | collective-permute-start | bytes 7962632 | tf_op jit(solution)/shard_map/ppermute | solution.py:29
  210.4 41.7 %collective-permute-start.28 = (bf16[2,4,72,1152]{3,2,1,0:T(8,128)(2,1)}, bf16[2,4,72,1152]{3,2,1,0:T(8,128)(2,1)}, u32[]{:S(2)}, u32[]{:S(2)}) collective-permute-start(bf16[2,4,72,1152]{3,2,1,0:T(8,128)(2,1)} %pad_maximum_fusion.28), channel_id=1, source_target_pairs={{0,2},{2,0},{4,6},{6,4},{8,10},{10,8},{12,14},{14,12},{1,3},{3,1},... | collective-permute-start | bytes 3981320 | tf_op jit(solution)/shard_map/ppermute | solution.py:29
  213.4 38.8 %collective-permute-start.27 = (bf16[576,1152]{1,0:T(8,128)(2,1)S(1)}, bf16[576,1152]{1,0:T(8,128)(2,1)}, u32[]{:S(2)}, u32[]{:S(2)}) collective-permute-start(bf16[576,1152]{1,0:T(8,128)(2,1)S(1)} %bitcast.779), channel_id=1, source_target_pairs={{0,1},{1,0},{2,3},{3,2},{4,5},{5,4},{6,7},{7,6},{8,9},{9,8},{10,11... | collective-permute-start | bytes 3981320 | tf_op jit(solution)/shard_map/ppermute | solution.py:29
  215.9 36.1 %collective-permute-start.29 = (bf16[72,2304]{1,0:T(8,128)(2,1)}, bf16[72,2304]{1,0:T(8,128)(2,1)S(1)}, u32[]{:S(2)}, u32[]{:S(2)}) collective-permute-start(bf16[72,2304]{1,0:T(8,128)(2,1)} %get-tuple-element.221), channel_id=1, source_target_pairs={{0,4},{2,6},{4,0},{6,2},{8,12},{10,14},{12,8},{14,10},{1,5},{3,7},... | collective-permute-start | bytes 995336 | tf_op jit(solution)/shard_map/ppermute | solution.py:29
  220.5 915.2 %reduce-scatter.3.cloned.1.call-start = ((), (), s32[]{:S(2)}) async-start(), calls=%async_computation.4 | async-start | bytes 2985984 | tf_op jit(solution)/shard_map/reduce_scatter | solution.py:141
  258.2 32.3 %collective-permute-start.36 = (bf16[4,72,1152]{2,1,0:T(8,128)(2,1)}, bf16[4,72,1152]{2,1,0:T(8,128)(2,1)}, u32[]{:S(2)}, u32[]{:S(2)}) collective-permute-start(bf16[4,72,1152]{2,1,0:T(8,128)(2,1)} %fusion.54), channel_id=1, source_target_pairs={{0,1},{1,0},{2,3},{3,2},{4,5},{5,4},{6,7},{7,6},{8,9},{9,8},{10,11... | collective-permute-start | bytes 1990664 | tf_op jit(solution)/shard_map/ppermute | solution.py:29
  290.5 81.9 %collective-permute-start.40 = (bf16[576,2304]{1,0:T(8,128)(2,1)S(1)}, bf16[576,2304]{1,0:T(8,128)(2,1)S(1)}, u32[]{:S(2)}, u32[]{:S(2)}) collective-permute-start(bf16[576,2304]{1,0:T(8,128)(2,1)S(1)} %copy-done.25), channel_id=1, source_target_pairs={{0,1},{1,0},{2,3},{3,2},{4,5},{5,4},{6,7},{7,6},{8,9},{9,8},{10,11... | collective-permute-start | bytes 7962632 | tf_op jit(solution)/shard_map/ppermute | solution.py:29
  319.3 78.1 %collective-permute-start.42 = (bf16[2,4,72,1152]{3,2,1,0:T(8,128)(2,1)}, bf16[2,4,72,1152]{3,2,1,0:T(8,128)(2,1)}, u32[]{:S(2)}, u32[]{:S(2)}) collective-permute-start(bf16[2,4,72,1152]{3,2,1,0:T(8,128)(2,1)} %pad_maximum_fusion.30), channel_id=1, source_target_pairs={{0,2},{2,0},{4,6},{6,4},{8,10},{10,8},{12,14},{14,12},{1,3},{3,1},... | collective-permute-start | bytes 3981320 | tf_op jit(solution)/shard_map/ppermute | solution.py:29
  322.3 77.9 %collective-permute-start.41 = (bf16[576,1152]{1,0:T(8,128)(2,1)S(1)}, bf16[576,1152]{1,0:T(8,128)(2,1)}, u32[]{:S(2)}, u32[]{:S(2)}) collective-permute-start(bf16[576,1152]{1,0:T(8,128)(2,1)S(1)} %bitcast.775), channel_id=1, source_target_pairs={{0,1},{1,0},{2,3},{3,2},{4,5},{5,4},{6,7},{7,6},{8,9},{9,8},{10,11... | collective-permute-start | bytes 3981320 | tf_op jit(solution)/shard_map/ppermute | solution.py:29
  325.6 62.8 %collective-permute-start.45 = (bf16[4,4,1,16,1152]{4,3,1,0,2:T(8,128)(2,1)}, bf16[4,4,1,16,1152]{4,3,1,0,2:T(8,128)(2,1)S(1)}, u32[]{:S(2)}, u32[]{:S(2)}) collective-permute-start(bf16[4,4,1,16,1152]{4,3,1,0,2:T(8,128)(2,1)} %pad_maximum_fusion.53), channel_id=1, source_target_pairs={{0,12},{2,14},{4,8},{6,10},{8,4},{10,6},{12,0},{14,2},{1,13},{3,15... | collective-permute-start | bytes 1769480 | tf_op jit(solution)/shard_map/ppermute | solution.py:29
  328.9 59.7 %collective-permute-start.44 = (bf16[4,4,1,16,1152]{4,3,1,0,2:T(8,128)(2,1)}, bf16[4,4,1,16,1152]{4,3,1,0,2:T(8,128)(2,1)S(1)}, u32[]{:S(2)}, u32[]{:S(2)}) collective-permute-start(bf16[4,4,1,16,1152]{4,3,1,0,2:T(8,128)(2,1)} %pad_maximum_fusion.52), channel_id=1, source_target_pairs={{0,8},{2,10},{4,12},{6,14},{8,0},{10,2},{12,4},{14,6},{1,9},{3,11}... | collective-permute-start | bytes 1769480 | tf_op jit(solution)/shard_map/ppermute | solution.py:29
  413.5 49.7 %collective-permute-start.48 = (bf16[4,4,2,1,16,1152]{5,4,1,2,0,3:T(8,128)(2,1)}, bf16[4,4,2,1,16,1152]{5,4,1,2,0,3:T(8,128)(2,1)}, u32[]{:S(2)}, u32[]{:S(2)}) collective-permute-start(bf16[4,4,2,1,16,1152]{5,4,1,2,0,3:T(8,128)(2,1)} %get-tuple-element.457), channel_id=1, source_target_pairs={{0,2},{1,3},{2,0},{3,1},{4,6},{5,7},{6,4},{7,5},{8,10},{9,11},{10,... | collective-permute-start | bytes 3538952 | tf_op jit(solution)/shard_map/ppermute | solution.py:897
  417.3 63.4 %collective-permute-start.51 = (bf16[2,576,1152]{2,1,0:T(8,128)(2,1)S(1)}, bf16[2,576,1152]{2,1,0:T(8,128)(2,1)}, u32[]{:S(2)}, u32[]{:S(2)}) collective-permute-start(bf16[2,576,1152]{2,1,0:T(8,128)(2,1)S(1)} %bitcast.736), channel_id=1, source_target_pairs={{0,16},{16,0},{1,17},{17,1},{2,18},{18,2},{3,19},{19,3},{4,20},{20... | collective-permute-start | bytes 7962632 | tf_op jit(solution)/shard_map/ppermute | solution.py:29
  417.6 89.9 %collective-permute-start.52 = (bf16[576,2304]{1,0:T(8,128)(2,1)}, bf16[576,2304]{1,0:T(8,128)(2,1)}, u32[]{:S(2)}, u32[]{:S(2)}) collective-permute-start(bf16[576,2304]{1,0:T(8,128)(2,1)} %all-gather.7.cloned.1.call-done.refs_0_.refs_6_), channel_id=1, source_target_pairs={{0,1},{1,0},{2,3},{3,2},{4,5},{5,4},{6,7},{7,6},{8,9},{9,8},{10,11... | collective-permute-start | bytes 7962632 | tf_op jit(solution)/shard_map/ppermute | solution.py:29
  419.6 51.5 %collective-permute-start.49 = (bf16[576,1152]{1,0:T(8,128)(2,1)S(1)}, bf16[576,1152]{1,0:T(8,128)(2,1)}, u32[]{:S(2)}, u32[]{:S(2)}) collective-permute-start(bf16[576,1152]{1,0:T(8,128)(2,1)S(1)} %bitcast.776), channel_id=1, source_target_pairs={{0,16},{16,0},{1,17},{17,1},{2,18},{18,2},{3,19},{19,3},{4,20},{20... | collective-permute-start | bytes 3981320 | tf_op jit(solution)/shard_map/ppermute | solution.py:29
  419.6 60.6 %collective-permute-start.50 = (bf16[576,1152]{1,0:T(8,128)(2,1)}, bf16[576,1152]{1,0:T(8,128)(2,1)}, u32[]{:S(2)}, u32[]{:S(2)}) collective-permute-start(bf16[576,1152]{1,0:T(8,128)(2,1)} %collective-permute-done.41.refs_1_), channel_id=1, source_target_pairs={{0,16},{16,0},{1,17},{17,1},{2,18},{18,2},{3,19},{19,3},{4,20},{20... | collective-permute-start | bytes 3981320 | tf_op jit(solution)/shard_map/ppermute | solution.py:29
  466.2 41.4 %collective-permute-start.55 = (bf16[4,2,2,1,16,1152]{5,4,1,2,0,3:T(8,128)(2,1)}, bf16[4,2,2,1,16,1152]{5,4,1,2,0,3:T(8,128)(2,1)}, u32[]{:S(2)}, u32[]{:S(2)}) collective-permute-start(bf16[4,2,2,1,16,1152]{5,4,1,2,0,3:T(8,128)(2,1)} %pad_maximum_fusion.56), channel_id=1, source_target_pairs={{0,12},{2,14},{4,8},{6,10},{8,4},{10,6},{12,0},{14,2},{1,13},{3,15... | collective-permute-start | bytes 1769480 | tf_op jit(solution)/shard_map/ppermute | solution.py:29
  471.1 50.5 %collective-permute-start.54 = (bf16[4,2,2,1,16,1152]{5,4,1,2,0,3:T(8,128)(2,1)}, bf16[4,2,2,1,16,1152]{5,4,1,2,0,3:T(8,128)(2,1)S(1)}, u32[]{:S(2)}, u32[]{:S(2)}) collective-permute-start(bf16[4,2,2,1,16,1152]{5,4,1,2,0,3:T(8,128)(2,1)} %pad_maximum_fusion.55), channel_id=1, source_target_pairs={{0,8},{2,10},{4,12},{6,14},{8,0},{10,2},{12,4},{14,6},{1,9},{3,11}... | collective-permute-start | bytes 1769480 | tf_op jit(solution)/shard_map/ppermute | solution.py:29
  480.2 41.4 %collective-permute-start.53 = (bf16[4,2,2,1,16,1152]{5,4,1,2,0,3:T(8,128)(2,1)}, bf16[4,2,2,1,16,1152]{5,4,1,2,0,3:T(8,128)(2,1)S(1)}, u32[]{:S(2)}, u32[]{:S(2)}) collective-permute-start(bf16[4,2,2,1,16,1152]{5,4,1,2,0,3:T(8,128)(2,1)} %pad_maximum_fusion.54), channel_id=1, source_target_pairs={{0,4},{2,6},{4,0},{6,2},{8,12},{10,14},{12,8},{14,10},{1,5},{3,7},... | collective-permute-start | bytes 1769480 | tf_op jit(solution)/shard_map/ppermute | solution.py:29
  480.8 40.9 %collective-permute-start.56 = (bf16[576,2304]{1,0:T(8,128)(2,1)}, bf16[576,2304]{1,0:T(8,128)(2,1)S(1)}, u32[]{:S(2)}, u32[]{:S(2)}) collective-permute-start(bf16[576,2304]{1,0:T(8,128)(2,1)} %all-gather.7.cloned.1.call-done.refs_0_.refs_6_), channel_id=1, source_target_pairs={{0,16},{16,0},{1,17},{17,1},{2,18},{18,2},{3,19},{19,3},{4,20},{20... | collective-permute-start | bytes 7962632 | tf_op jit(solution)/shard_map/ppermute | solution.py:29
  553.0 49.5 %collective-permute-start.58 = (bf16[4,4,2,1,16,1152]{5,4,2,1,0,3:T(8,128)(2,1)S(1)}, bf16[4,4,2,1,16,1152]{5,4,2,1,0,3:T(8,128)(2,1)S(1)}, u32[]{:S(2)}, u32[]{:S(2)}) collective-permute-start(bf16[4,4,2,1,16,1152]{5,4,2,1,0,3:T(8,128)(2,1)S(1)} %get-tuple-element.453), channel_id=1, source_target_pairs={{0,2},{1,3},{2,0},{3,1},{4,6},{5,7},{6,4},{7,5},{8,10},{9,11},{10,... | collective-permute-start | bytes 3538952 | tf_op jit(solution)/shard_map/ppermute | solution.py:897
  636.0 77.6 %collective-permute-start.63 = (bf16[576,2304]{1,0:T(8,128)(2,1)}, bf16[576,2304]{1,0:T(8,128)(2,1)}, u32[]{:S(2)}, u32[]{:S(2)}) collective-permute-start(bf16[576,2304]{1,0:T(8,128)(2,1)} %split.72), channel_id=1, source_target_pairs={{0,1},{1,0},{2,3},{3,2},{4,5},{5,4},{6,7},{7,6},{8,9},{9,8},{10,11... | collective-permute-start | bytes 7962632 | tf_op jit(solution)/shard_map/ppermute | solution.py:29
  645.1 93.4 %collective-permute-start.67 = (bf16[576,4608]{1,0:T(8,128)(2,1)}, bf16[576,4608]{1,0:T(8,128)(2,1)}, u32[]{:S(2)}, u32[]{:S(2)}) collective-permute-start(bf16[576,4608]{1,0:T(8,128)(2,1)} %convolution_convert_fusion.2), channel_id=1, source_target_pairs={{0,16},{16,0},{1,17},{17,1},{2,18},{18,2},{3,19},{19,3},{4,20},{20... | collective-permute-start | bytes 15925256 | tf_op jit(solution)/shard_map/ppermute | solution.py:29
  646.1 67.4 %collective-permute-start.62 = (bf16[4,2,2,1,16,1152]{5,4,2,1,0,3:T(8,128)(2,1)}, bf16[4,2,2,1,16,1152]{5,4,2,1,0,3:T(8,128)(2,1)S(1)}, u32[]{:S(2)}, u32[]{:S(2)}) collective-permute-start(bf16[4,2,2,1,16,1152]{5,4,2,1,0,3:T(8,128)(2,1)} %pad_maximum_fusion.59), channel_id=1, source_target_pairs={{0,12},{2,14},{4,8},{6,10},{8,4},{10,6},{12,0},{14,2},{1,13},{3,15... | collective-permute-start | bytes 1769480 | tf_op jit(solution)/shard_map/ppermute | solution.py:29
  649.9 63.7 %collective-permute-start.61 = (bf16[4,2,2,1,16,1152]{5,4,2,1,0,3:T(8,128)(2,1)}, bf16[4,2,2,1,16,1152]{5,4,2,1,0,3:T(8,128)(2,1)}, u32[]{:S(2)}, u32[]{:S(2)}) collective-permute-start(bf16[4,2,2,1,16,1152]{5,4,2,1,0,3:T(8,128)(2,1)} %pad_maximum_fusion.58), channel_id=1, source_target_pairs={{0,8},{2,10},{4,12},{6,14},{8,0},{10,2},{12,4},{14,6},{1,9},{3,11}... | collective-permute-start | bytes 1769480 | tf_op jit(solution)/shard_map/ppermute | solution.py:29
  650.8 62.8 %collective-permute-start.60 = (bf16[4,2,2,1,16,1152]{5,4,2,1,0,3:T(8,128)(2,1)}, bf16[4,2,2,1,16,1152]{5,4,2,1,0,3:T(8,128)(2,1)}, u32[]{:S(2)}, u32[]{:S(2)}) collective-permute-start(bf16[4,2,2,1,16,1152]{5,4,2,1,0,3:T(8,128)(2,1)} %pad_maximum_fusion.57), channel_id=1, source_target_pairs={{0,4},{2,6},{4,0},{6,2},{8,12},{10,14},{12,8},{14,10},{1,5},{3,7},... | collective-permute-start | bytes 1769480 | tf_op jit(solution)/shard_map/ppermute | solution.py:29
  713.6 64.6 %collective-permute-start.74 = (bf16[576,1152]{1,0:T(8,128)(2,1)}, bf16[576,1152]{1,0:T(8,128)(2,1)}, u32[]{:S(2)}, u32[]{:S(2)}) collective-permute-start(bf16[576,1152]{1,0:T(8,128)(2,1)} %convolution_convert_fusion.5), channel_id=1, source_target_pairs={{0,16},{16,0},{1,17},{17,1},{2,18},{18,2},{3,19},{19,3},{4,20},{20... | collective-permute-start | bytes 3981320 | tf_op jit(solution)/shard_map/ppermute | solution.py:29
  727.2 486.6 %reduce-scatter.5.cloned.1.call-start = ((), (), s32[]{:S(2)}) async-start(), calls=%async_computation.5 | async-start | bytes 2985984 | tf_op jit(solution)/shard_map/reduce_scatter | solution.py:141
  738.6 105.2 %collective-permute-start.73 = (bf16[576,1728]{1,0:T(8,128)(2,1)}, bf16[576,1728]{1,0:T(8,128)(2,1)}, u32[]{:S(2)}, u32[]{:S(2)}) collective-permute-start(bf16[576,1728]{1,0:T(8,128)(2,1)} %convolution_convert_fusion.8), channel_id=1, source_target_pairs={{0,16},{16,0},{1,17},{17,1},{2,18},{18,2},{3,19},{19,3},{4,20},{20... | collective-permute-start | bytes 5971976 | tf_op jit(solution)/shard_map/ppermute | solution.py:29
  738.6 105.2 %collective-permute-start.72 = (bf16[576,1728]{1,0:T(8,128)(2,1)}, bf16[576,1728]{1,0:T(8,128)(2,1)}, u32[]{:S(2)}, u32[]{:S(2)}) collective-permute-start(bf16[576,1728]{1,0:T(8,128)(2,1)} %convolution_convert_fusion.9), channel_id=1, source_target_pairs={{0,16},{16,0},{1,17},{17,1},{2,18},{18,2},{3,19},{19,3},{4,20},{20... | collective-permute-start | bytes 5971976 | tf_op jit(solution)/shard_map/ppermute | solution.py:29
  763.6 80.1 %collective-permute-start.71 = (bf16[576,2304]{1,0:T(8,128)(2,1)S(1)}, bf16[576,2304]{1,0:T(8,128)(2,1)S(1)}, u32[]{:S(2)}, u32[]{:S(2)}) collective-permute-start(bf16[576,2304]{1,0:T(8,128)(2,1)S(1)} %split.73), channel_id=1, source_target_pairs={{0,1},{1,0},{2,3},{3,2},{4,5},{5,4},{6,7},{7,6},{8,9},{9,8},{10,11... | collective-permute-start | bytes 7962632 | tf_op jit(solution)/shard_map/ppermute | solution.py:29
  778.2 54.4 %collective-permute-start.69 = (bf16[4,4,1,16,1152]{4,3,1,0,2:T(8,128)(2,1)S(1)}, bf16[4,4,1,16,1152]{4,3,1,0,2:T(8,128)(2,1)S(1)}, u32[]{:S(2)}, u32[]{:S(2)}) collective-permute-start(bf16[4,4,1,16,1152]{4,3,1,0,2:T(8,128)(2,1)S(1)} %pad_maximum_fusion.61), channel_id=1, source_target_pairs={{0,8},{2,10},{4,12},{6,14},{8,0},{10,2},{12,4},{14,6},{1,9},{3,11}... | collective-permute-start | bytes 1769480 | tf_op jit(solution)/shard_map/ppermute | solution.py:29
  792.1 51.7 %collective-permute-start.68 = (bf16[4,4,1,16,1152]{4,3,1,0,2:T(8,128)(2,1)S(1)}, bf16[4,4,1,16,1152]{4,3,1,0,2:T(8,128)(2,1)S(1)}, u32[]{:S(2)}, u32[]{:S(2)}) collective-permute-start(bf16[4,4,1,16,1152]{4,3,1,0,2:T(8,128)(2,1)S(1)} %pad_maximum_fusion.60), channel_id=1, source_target_pairs={{0,4},{2,6},{4,0},{6,2},{8,12},{10,14},{12,8},{14,10},{1,5},{3,7},... | collective-permute-start | bytes 1769480 | tf_op jit(solution)/shard_map/ppermute | solution.py:29
  868.9 54.6 %collective-permute-start.76 = (bf16[4,72,2304]{2,1,0:T(8,128)(2,1)}, bf16[4,72,2304]{2,1,0:T(8,128)(2,1)}, u32[]{:S(2)}, u32[]{:S(2)}) collective-permute-start(bf16[4,72,2304]{2,1,0:T(8,128)(2,1)} %concatenate.691), channel_id=1, source_target_pairs={{0,2},{2,0},{4,6},{6,4},{8,10},{10,8},{12,14},{14,12},{1,3},{3,1},... | collective-permute-start | bytes 3981320 | tf_op jit(solution)/shard_map/ppermute | solution.py:29
  870.4 53.2 %collective-permute-start.75 = (bf16[576,1152]{1,0:T(8,128)(2,1)}, bf16[576,1152]{1,0:T(8,128)(2,1)}, u32[]{:S(2)}, u32[]{:S(2)}) collective-permute-start(bf16[576,1152]{1,0:T(8,128)(2,1)} %slice.1036), channel_id=1, source_target_pairs={{0,1},{1,0},{2,3},{3,2},{4,5},{5,4},{6,7},{7,6},{8,9},{9,8},{10,11... | collective-permute-start | bytes 3981320 | tf_op jit(solution)/shard_map/ppermute | solution.py:29
  934.4 42.2 %collective-permute-start.80 = (bf16[576,4608]{1,0:T(8,128)(2,1)}, bf16[576,4608]{1,0:T(8,128)(2,1)}, u32[]{:S(2)}, u32[]{:S(2)}) collective-permute-start(bf16[576,4608]{1,0:T(8,128)(2,1)} %convolution_convert_fusion), channel_id=1, source_target_pairs={{0,16},{16,0},{1,17},{17,1},{2,18},{18,2},{3,19},{19,3},{4,20},{20... | collective-permute-start | bytes 15925256 | tf_op jit(solution)/shard_map/ppermute | solution.py:29
  995.5 83.2 %collective-permute-start.85 = (bf16[4,72,4608]{2,1,0:T(8,128)(2,1)}, bf16[4,72,4608]{2,1,0:T(8,128)(2,1)}, u32[]{:S(2)}, u32[]{:S(2)}) collective-permute-start(bf16[4,72,4608]{2,1,0:T(8,128)(2,1)} %pad_maximum_fusion.3), channel_id=1, source_target_pairs={{0,2},{2,0},{4,6},{6,4},{8,10},{10,8},{12,14},{14,12},{1,3},{3,1},... | collective-permute-start | bytes 7962632 | tf_op jit(solution)/shard_map/ppermute | solution.py:29
  1007.2 71.5 %collective-permute-start.84 = (bf16[576,2304]{1,0:T(8,128)(2,1)}, bf16[576,2304]{1,0:T(8,128)(2,1)}, u32[]{:S(2)}, u32[]{:S(2)}) collective-permute-start(bf16[576,2304]{1,0:T(8,128)(2,1)} %split.78), channel_id=1, source_target_pairs={{0,1},{1,0},{2,3},{3,2},{4,5},{5,4},{6,7},{7,6},{8,9},{9,8},{10,11... | collective-permute-start | bytes 7962632 | tf_op jit(solution)/shard_map/ppermute | solution.py:29
  1013.7 65.0 %collective-permute-start.81 = (bf16[72,2304]{1,0:T(8,128)(2,1)}, bf16[72,2304]{1,0:T(8,128)(2,1)}, u32[]{:S(2)}, u32[]{:S(2)}) collective-permute-start(bf16[72,2304]{1,0:T(8,128)(2,1)} %get-tuple-element.496), channel_id=1, source_target_pairs={{0,4},{2,6},{4,0},{6,2},{8,12},{10,14},{12,8},{14,10},{1,5},{3,7},... | collective-permute-start | bytes 995336 | tf_op jit(solution)/shard_map/ppermute | solution.py:29
  1013.7 65.0 %collective-permute-start.82 = (bf16[72,2304]{1,0:T(8,128)(2,1)}, bf16[72,2304]{1,0:T(8,128)(2,1)}, u32[]{:S(2)}, u32[]{:S(2)}) collective-permute-start(bf16[72,2304]{1,0:T(8,128)(2,1)} %get-tuple-element.497), channel_id=1, source_target_pairs={{0,8},{2,10},{4,12},{6,14},{8,0},{10,2},{12,4},{14,6},{1,9},{3,11}... | collective-permute-start | bytes 995336 | tf_op jit(solution)/shard_map/ppermute | solution.py:29
  1016.2 62.5 %collective-permute-start.83 = (bf16[72,2304]{1,0:T(8,128)(2,1)}, bf16[72,2304]{1,0:T(8,128)(2,1)}, u32[]{:S(2)}, u32[]{:S(2)}) collective-permute-start(bf16[72,2304]{1,0:T(8,128)(2,1)} %get-tuple-element.495), channel_id=1, source_target_pairs={{0,12},{2,14},{4,8},{6,10},{8,4},{10,6},{12,0},{14,2},{1,13},{3,15... | collective-permute-start | bytes 995336 | tf_op jit(solution)/shard_map/ppermute | solution.py:29
  1087.6 54.4 %collective-permute-start.89 = (bf16[576,1728]{1,0:T(8,128)(2,1)}, bf16[576,1728]{1,0:T(8,128)(2,1)}, u32[]{:S(2)}, u32[]{:S(2)}) collective-permute-start(bf16[576,1728]{1,0:T(8,128)(2,1)} %convolution_convert_fusion.6), channel_id=1, source_target_pairs={{0,16},{16,0},{1,17},{17,1},{2,18},{18,2},{3,19},{19,3},{4,20},{20... | collective-permute-start | bytes 5971976 | tf_op jit(solution)/shard_map/ppermute | solution.py:29
  1091.9 50.1 %collective-permute-start.88 = (bf16[576,1728]{1,0:T(8,128)(2,1)}, bf16[576,1728]{1,0:T(8,128)(2,1)}, u32[]{:S(2)}, u32[]{:S(2)}) collective-permute-start(bf16[576,1728]{1,0:T(8,128)(2,1)} %convolution_convert_fusion.7), channel_id=1, source_target_pairs={{0,16},{16,0},{1,17},{17,1},{2,18},{18,2},{3,19},{19,3},{4,20},{20... | collective-permute-start | bytes 5971976 | tf_op jit(solution)/shard_map/ppermute | solution.py:29
  1095.8 46.2 %collective-permute-start.87 = (bf16[4,72,2304]{2,1,0:T(8,128)(2,1)}, bf16[4,72,2304]{2,1,0:T(8,128)(2,1)}, u32[]{:S(2)}, u32[]{:S(2)}) collective-permute-start(bf16[4,72,2304]{2,1,0:T(8,128)(2,1)} %split.83), channel_id=1, source_target_pairs={{0,1},{1,0},{2,3},{3,2},{4,5},{5,4},{6,7},{7,6},{8,9},{9,8},{10,11... | collective-permute-start | bytes 3981320 | tf_op jit(solution)/shard_map/ppermute | solution.py:29
  1101.9 40.1 %collective-permute-start.86 = (bf16[4,72,2304]{2,1,0:T(8,128)(2,1)}, bf16[4,72,2304]{2,1,0:T(8,128)(2,1)}, u32[]{:S(2)}, u32[]{:S(2)}) collective-permute-start(bf16[4,72,2304]{2,1,0:T(8,128)(2,1)} %dynamic-slice_bitcast_fusion.2), channel_id=1, source_target_pairs={{0,2},{2,0},{4,6},{6,4},{8,10},{10,8},{12,14},{14,12},{1,3},{3,1},... | collective-permute-start | bytes 3981320 | tf_op jit(solution)/shard_map/ppermute | solution.py:29
  1169.2 33.0 %collective-permute-start.95 = (bf16[4,72,2304]{2,1,0:T(8,128)(2,1)}, bf16[4,72,2304]{2,1,0:T(8,128)(2,1)}, u32[]{:S(2)}, u32[]{:S(2)}) collective-permute-start(bf16[4,72,2304]{2,1,0:T(8,128)(2,1)} %concatenate.701), channel_id=1, source_target_pairs={{0,2},{2,0},{4,6},{6,4},{8,10},{10,8},{12,14},{14,12},{1,3},{3,1},... | collective-permute-start | bytes 3981320 | tf_op jit(solution)/shard_map/ppermute | solution.py:29
  1169.2 33.0 %collective-permute-start.94 = (bf16[576,1152]{1,0:T(8,128)(2,1)}, bf16[576,1152]{1,0:T(8,128)(2,1)}, u32[]{:S(2)}, u32[]{:S(2)}) collective-permute-start(bf16[576,1152]{1,0:T(8,128)(2,1)} %slice.1048), channel_id=1, source_target_pairs={{0,1},{1,0},{2,3},{3,2},{4,5},{5,4},{6,7},{7,6},{8,9},{9,8},{10,11... | collective-permute-start | bytes 3981320 | tf_op jit(solution)/shard_map/ppermute | solution.py:29
  1176.8 35.7 %collective-permute-start.97 = (bf16[72,4608]{1,0:T(8,128)(2,1)}, bf16[72,4608]{1,0:T(8,128)(2,1)}, u32[]{:S(2)}, u32[]{:S(2)}) collective-permute-start(bf16[72,4608]{1,0:T(8,128)(2,1)} %get-tuple-element.407), channel_id=1, source_target_pairs={{0,4},{2,6},{4,0},{6,2},{8,12},{10,14},{12,8},{14,10},{1,5},{3,7},... | collective-permute-start | bytes 1990664 | tf_op jit(solution)/shard_map/ppermute | solution.py:29
  1183.1 48.8 %collective-permute-start.98 = (bf16[72,4608]{1,0:T(8,128)(2,1)}, bf16[72,4608]{1,0:T(8,128)(2,1)}, u32[]{:S(2)}, u32[]{:S(2)}) collective-permute-start(bf16[72,4608]{1,0:T(8,128)(2,1)} %get-tuple-element.408), channel_id=1, source_target_pairs={{0,8},{2,10},{4,12},{6,14},{8,0},{10,2},{12,4},{14,6},{1,9},{3,11}... | collective-permute-start | bytes 1990664 | tf_op jit(solution)/shard_map/ppermute | solution.py:29
  1184.1 47.7 %collective-permute-start.99 = (bf16[72,4608]{1,0:T(8,128)(2,1)}, bf16[72,4608]{1,0:T(8,128)(2,1)S(1)}, u32[]{:S(2)}, u32[]{:S(2)}) collective-permute-start(bf16[72,4608]{1,0:T(8,128)(2,1)} %get-tuple-element.406), channel_id=1, source_target_pairs={{0,12},{2,14},{4,8},{6,10},{8,4},{10,6},{12,0},{14,2},{1,13},{3,15... | collective-permute-start | bytes 1990664 | tf_op jit(solution)/shard_map/ppermute | solution.py:29
  1234.4 42.0 %collective-permute-start.107 = (bf16[4,1,128,1152]{3,2,0,1:T(8,128)(2,1)S(1)}, bf16[4,1,128,1152]{3,2,0,1:T(8,128)(2,1)S(1)}, u32[]{:S(2)}, u32[]{:S(2)}) collective-permute-start(bf16[4,1,128,1152]{3,2,0,1:T(8,128)(2,1)S(1)} %get-tuple-element.433), channel_id=1, source_target_pairs={{0,1},{1,0},{2,3},{3,2},{4,5},{5,4},{6,7},{7,6},{8,9},{9,8},{10,11... | collective-permute-start | bytes 3538952 | tf_op jit(solution)/shard_map/ppermute | solution.py:29
  (250 other events, 2715.3 us)
Sparse Core Ops, SparseCore 0:
  19.1 69.0 all-gather.8
  90.4 69.8 all-gather.4
  220.6 80.8 all-gather.6
  727.4 88.4 reduce-scatter.2
  1105.6 93.7 reduce-scatter.4
